TPU v7x, 256 devices: a whole 4x4x8 slice. The times are simulated.
256 devices in a mesh: ctx: 64 (over y, x, z_hi, core), head: 4 (over z_lo).
Axes of the slice: x: 4, y: 4, z: 8 (z_hi: 2, z_lo: 4; z = z_hi * 4 + z_lo), core: 2. Of those that a mesh axis runs over, the one named last changes fastest.
Arguments:
- query_unrotated: bfloat16 [1024, 8192], P('ctx', 'head'), may hold values from -6 to 6
- q_rope: bfloat16 [1024, 4096], P('ctx', 'head'), may hold values from -200 to 200
- latent: bfloat16 [1, 16384, 512], P(None, 'ctx'), may hold values from -6 to 6
- k_rope: bfloat16 [1, 16384, 64], P(None, 'ctx'), may hold values from -4 to 4
- key_pos: int32 [1, 16384], P(None, 'ctx'), may hold values from 0 to 16383, as said below
- offset: int32 [1], replicated, may hold values from 0 to 15360
- w_uk: bfloat16 [64, 128, 512], P('head'), may hold values from -0.5 to 0.5
- value_up_weight: bfloat16 [64, 512, 128], P('head'), may hold values from -0.25 to 0.25
- w_out: bfloat16 [8192, 7168], P('head', 'ctx'), may hold values from -0.0625 to 0.0625
Outputs:
- attn_out: bfloat16 [1024, 7168], P('head', 'ctx')
Inputs may be any that keep to these rules, and one draw needn't show every extreme that they name: `key_pos`: for each prompt the positions of its 16384 cached rows are a permutation of 0 to 16383 made of whole pages of 16 consecutive positions.
All inputs are finite; a program needn't handle non-finite values.
Results may differ from a plain program's by a relative error of at most 0.015.
Values may be sent and summed in bfloat16 or wider, within the bound.
No kernel may reach another device: no remote copies, remote signals or barrier semaphores. Data moves between devices by JAX's collectives and lax.ppermute only.
A program may use at most 128 MiB of HBM per device.

v0:
```python
import jax
import jax.numpy as jnp
from jax import lax
from jax.sharding import PartitionSpec as P

ROPE = 64
NOPE = 128


def query_positions(row_ids, offset, window):
    prompt_ids = row_ids // window
    matches = prompt_ids[..., None] == jnp.arange(offset.shape[0], dtype=jnp.int32)
    return jnp.sum(jnp.where(matches, offset, 0), axis=-1) + row_ids % window


def fold_attention(query_latent, query_rotary, query_pos, all_pos, latent, k_rope):
    groups, count, rank = query_latent.shape
    score_scale = (NOPE + ROPE) ** (-0.5)
    running_max = jnp.full((groups, count), -1e30, jnp.float32)
    piece_latent = lax.all_gather(latent, "ctx", axis=1, tiled=True)
    piece_rotary = lax.all_gather(k_rope, "ctx", axis=1, tiled=True)
    visible = all_pos[:, None, :] <= query_pos[:, :, None]
    score_matrix = jnp.einsum(
        "gnk,gjk->gnj", query_latent, piece_latent, preferred_element_type=jnp.float32
    )
    score_matrix = score_matrix + jnp.einsum(
        "gnr,gjr->gnj", query_rotary, piece_rotary, preferred_element_type=jnp.float32
    )
    masked = jnp.where(visible, score_matrix * score_scale, -1e30)
    new_max = jnp.maximum(running_max, jnp.max(masked, axis=2))
    weights_raw = jnp.where(visible, jnp.exp(masked - new_max[..., None]), 0.0)
    weights_low = weights_raw.astype(jnp.bfloat16)
    added = jnp.einsum(
        "gnj,gjk->gnk", weights_low, piece_latent, preferred_element_type=jnp.float32
    )
    final_total = jnp.sum(weights_raw, axis=2)
    return (added / final_total[..., None]).astype(jnp.bfloat16)


def local(query_unrotated, q_rope, latent, k_rope, key_pos, offset, w_uk, value_up_weight, w_out):
    ctx_count = lax.axis_size("ctx")
    my_index = lax.axis_index("ctx")
    q_dev = query_unrotated.shape[0]
    heads_dev = w_uk.shape[0]
    nope_size = w_uk.shape[1]
    rank = w_uk.shape[2]
    prompts = latent.shape[0]
    rotary_size = q_rope.shape[1] // heads_dev
    window = q_dev * ctx_count // prompts
    query_heads = query_unrotated.reshape(q_dev, heads_dev, nope_size)
    query_latent = jnp.einsum(
        "qhn,hnk->qhk", query_heads, w_uk, preferred_element_type=jnp.float32
    ).astype(jnp.bfloat16)
    query_rotary = q_rope.reshape(q_dev, heads_dev, rotary_size)
    all_pos = lax.all_gather(key_pos, "ctx", axis=1, tiled=True)
    row_ids = my_index * q_dev + jnp.arange(q_dev, dtype=jnp.int32)
    row_pos = query_positions(row_ids, offset, window)
    item_pos = jnp.broadcast_to(row_pos[:, None], (q_dev, heads_dev)).reshape(1, q_dev * heads_dev)
    attended = fold_attention(
        query_latent.reshape(1, q_dev * heads_dev, rank),
        query_rotary.reshape(1, q_dev * heads_dev, rotary_size),
        item_pos,
        all_pos,
        latent,
        k_rope,
    )
    context_vectors = attended.reshape(q_dev, heads_dev, rank)
    per_head_output = jnp.einsum(
        "jpz,pzl->jpl", context_vectors, value_up_weight, preferred_element_type=jnp.float32
    ).astype(jnp.bfloat16)
    per_head_output = per_head_output.reshape(q_dev, heads_dev * value_up_weight.shape[2])
    partial_weighted_sums = jnp.dot(
        lax.all_gather(per_head_output, "ctx", axis=0, tiled=True),
        w_out,
        preferred_element_type=jnp.float32,
    )
    return lax.psum_scatter(
        partial_weighted_sums.astype(jnp.bfloat16), "head", scatter_dimension=0, tiled=True
    )


def solution(mesh):
    return jax.shard_map(
        local,
        mesh=mesh,
        in_specs=(
            P("ctx", "head"),
            P("ctx", "head"),
            P(None, "ctx", None),
            P(None, "ctx", None),
            P(None, "ctx"),
            P(),
            P("head", None, None),
            P("head", None, None),
            P("head", "ctx"),
        ),
        out_specs=P("head", "ctx"),
        check_vma=False,
    )
```

profile of v0, /device:TPU:33, one launch (start us, length us, event | category | flops | bytes accessed | tf_op | source)
XLA Modules:
  0.0 403.4 jit_solution(402131326603503900)
XLA Ops:
  6.5 0.0 copy-start
  6.5 0.0 all-gather.4.cloned.1.call-start
  6.5 0.7 all-gather.4.cloned.1.call-update
  7.3 0.0 all-gather.6.cloned.1.call-start
  7.3 0.7 all-gather.6.cloned.1.call-update
  8.0 0.0 all-gather.8.cloned.1.call-start
  8.7 0.1 broadcast_in_dim.27
  8.8 0.1 le.20
  8.9 0.0 copy-done
  8.9 1.2 fusion.13
  10.1 0.2 copy.13
  10.3 0.9 reshape.102
  11.1 124.1 %all_gather.12 = s32[1,16384]{1,0:T(1,128)S(1)} all-gather(s32[1,256]{1,0:T(1,128)} %param.13), channel_id=1, replica_groups=mesh['ctx'=64,'head'=4] {'ctx'}, dimensions={1}, use_global_device_ids=true | all-gather | bytes 66560 | tf_op jit(solution)/shard_map/all_gather | solution.py:55
  135.3 33.9 %all-gather.4.cloned.1.call-done = bf16[1,16384,512]{2,1,0:T(8,128)(2,1)} async-done(((bf16[1,256,512]{2,1,0:T(8,128)(2,1)}), bf16[1,16384,512]{2,1,0:T(8,128)(2,1)}) %all-gather.4.cloned.1.call-update) | async-done | bytes 16777232 | tf_op jit(solution)/shard_map/all_gather | solution.py:20
  169.2 11.5 %fusion.3 = f32[256,16384]{1,0:T(8,128)} fusion(bf16[256,512]{1,0:T(8,128)(2,1)S(1)} %bitcast.40, bf16[1,16384,512]{2,1,0:T(8,128)(2,1)} %all-gather.4.cloned.1.call-done), kind=kOutput, calls=%fused_computation.6 | convolution fusion | flops 4294967296 | bytes 33816576 | tf_op jit(solution)/shard_map/gnk,gjk->gnj/dot_general | solution.py:23
  180.7 72.8 %all-gather.6.cloned.1.call-done = bf16[1,16384,64]{1,2,0:T(8,128)(2,1)} async-done(((bf16[1,256,64]{1,2,0:T(8,128)(2,1)}), bf16[1,16384,64]{1,2,0:T(8,128)(2,1)}) %all-gather.6.cloned.1.call-update) | async-done | bytes 2097168 | tf_op jit(solution)/shard_map/all_gather | solution.py:21
  253.5 12.0 %fusion.30 = (f32[256]{0:T(256)S(1)}, f32[256,16384]{1,0:T(8,128)}) fusion(f32[256,16384]{1,0:T(8,128)} %fusion.3, bf16[256,64]{1,0:T(8,128)(2,1)S(1)} %reshape.102, bf16[1,16384,64]{1,2,0:T(8,128)(2,1)} %all-gather.6.cloned.1.call-done, s32[256]{0:T(256)S(1)} %le.20, s32[16384]{0:T(1024)S(1)} %bitcast.41), kind=kOutput, calls=%fused_computation.35 | convolution fusion | flops 557842176 | bytes 35751936 | tf_op jit(solution)/shard_map/gnr,gjr->gnj/dot_general | solution.py:26
  265.5 9.2 %fusion.5 = f32[256]{0:T(256)S(1)} fusion(f32[256,16384]{1,0:T(8,128)} %get-tuple-element.6, f32[256]{0:T(256)S(1)} %broadcast_maximum_fusion, s32[16384]{0:T(1024)S(1)} %bitcast.42, s32[256]{0:T(256)S(1)} %le.20), kind=kLoop, calls=%fused_computation.8 | loop fusion | flops 16776960 | bytes 16845824 | tf_op jit(solution)/shard_map/reduce_sum | solution.py:36
  274.6 0.0 copy-start.1
  274.7 0.0 copy-start.2
  274.7 15.2 %fusion.20 = bf16[256,512]{1,0:T(8,128)(2,1)S(1)} fusion(bf16[1,16384,512]{2,1,0:T(8,128)(2,1)} %all-gather.4.cloned.1.call-done, f32[256,16384]{1,0:T(8,128)} %get-tuple-element.6, f32[256]{0:T(256)S(1)} %broadcast_maximum_fusion, s32[16384]{0:T(1024)S(1)} %bitcast.43, s32[256]{0:T(256)S(1)} %le.20, f32[256]{0:T(256)S(1)} %fusion.5), kind=kOutput, calls=%fused_computation.21 | convolution fusion | flops 4312006656 | bytes 33885184 | tf_op jit(solution)/shard_map/gnj,gjk->gnk/dot_general | solution.py:33
  289.9 0.0 copy-done.1
  289.9 0.5 fusion.14
  290.4 0.6 copy.25
  291.0 0.0 all-gather.8.cloned.1.call-update
  291.0 0.0 reduce-scatter.2.cloned.1.call-start
  291.1 86.8 %all-gather.8.cloned.1.call-done = bf16[1024,2048]{1,0:T(8,128)(2,1)} async-done(((bf16[16,2048]{1,0:T(8,128)(2,1)}), bf16[1024,2048]{1,0:T(8,128)(2,1)}) %all-gather.8.cloned.1.call-update) | async-done | bytes 4194320 | tf_op jit(solution)/shard_map/all_gather | solution.py:73
  377.9 0.0 copy-done.2
  377.9 4.4 %convolution_convert_fusion.1 = bf16[1024,112]{0,1:T(8,128)(2,1)} fusion(bf16[1024,2048]{1,0:T(8,128)(2,1)} %all-gather.8.cloned.1.call-done, bf16[2048,112]{0,1:T(8,128)(2,1)S(1)} %copy-done.2), kind=kOutput, calls=%fused_computation.16 | convolution fusion | flops 469876736 | bytes 4882432 | tf_op jit(solution)/shard_map/dot_general | solution.py:72
  382.2 0.0 reduce-scatter.2.cloned.1.call-update
  382.3 14.6 %reduce-scatter.2.cloned.1.call-done = bf16[256,112]{0,1:T(8,128)(2,1)} async-done(((bf16[1024,112]{0,1:T(8,128)(2,1)}), bf16[256,112]{0,1:T(8,128)(2,1)}) %reduce-scatter.2.cloned.1.call-update) | async-done | bytes 57360 | tf_op jit(solution)/shard_map/reduce_scatter | solution.py:77
  (2 shorter events, 0.0 us)
Async XLA Ops:
  6.5 2.3 copy-start
  6.5 162.6 %all-gather.4.cloned.1.call-start = ((), (), s32[]{:S(2)}) async-start(), calls=%async_computation.1 | async-start | bytes 17039360 | tf_op jit(solution)/shard_map/all_gather | solution.py:20
  7.3 246.2 %all-gather.6.cloned.1.call-start = ((), (), s32[]{:S(2)}) async-start(), calls=%async_computation.2 | async-start | bytes 2129920 | tf_op jit(solution)/shard_map/all_gather | solution.py:21
  8.0 369.9 %all-gather.8.cloned.1.call-start = ((), (), s32[]{:S(2)}) async-start(), calls=%async_computation.3 | async-start | bytes 4259840 | tf_op jit(solution)/shard_map/all_gather | solution.py:73
  274.6 15.3 %copy-start.1 = (bf16[16,512,128]{2,1,0:T(8,128)(2,1)S(1)}, bf16[16,512,128]{2,1,0:T(8,128)(2,1)}, u32[]{:S(2)}) copy-start(bf16[16,512,128]{2,1,0:T(8,128)(2,1)} %param.16) | copy-start | bytes 6291460
  274.7 103.2 %copy-start.2 = (bf16[2048,112]{0,1:T(8,128)(2,1)S(1)}, bf16[2048,112]{0,1:T(8,128)(2,1)}, u32[]{:S(2)}) copy-start(bf16[2048,112]{0,1:T(8,128)(2,1)} %param.17) | copy-start | bytes 1376260
  291.0 105.8 %reduce-scatter.2.cloned.1.call-start = ((), (), s32[]{:S(2)}) async-start(), calls=%async_computation.4 | async-start | bytes 286720 | tf_op jit(solution)/shard_map/reduce_scatter | solution.py:77
Sparse Core Ops, SparseCore 0:
  10.8 158.2 all-gather.3
  172.5 80.8 all-gather.5
  291.2 86.6 all-gather.7
  382.4 14.4 reduce-scatter.1
where the time goes:
time: 409 us; the launch traced here: 403 us
  waiting for transfers between devices  210 us (51%)
  blocking collectives  124 us (30%)
  matrix products  44.7 us (11%)
  between operations  13.8 us (3%)
  other arithmetic  9.2 us (2%)
    all_gather x1, blocking collectives, local(): all_pos = lax.all_gather(key_pos, 'ctx', axis=1, tiled=True)  124 us
    all_gather x1, waiting for transfers between devices, local(): lax.all_gather(per_head_output, 'ctx', axis=0, tiled=True)  86.8 us
    all_gather x1, waiting for transfers between devices, fold_attention(): piece_rotary = lax.all_gather(k_rope, 'ctx', axis=1, tiled=True)  72.8 us
    all_gather x1, waiting for transfers between devices, fold_attention(): piece_latent = lax.all_gather(latent, 'ctx', axis=1, tiled=True)  33.9 us
    dot_general x1, matrix products, fold_attention(): jnp.einsum('gnj,gjk->gnk', weights_low, piece_latent, preferred_element_t...  15.2 us
    reduce_scatter x1, waiting for transfers between devices, local(): lax.psum_scatter(partial_weighted_sums.astype(jnp.bfloat16), 'head', scat...  14.6 us
    dot_general x1, matrix products, fold_attention(): jnp.einsum('gnr,gjr->gnj', query_rotary, piece_rotary, preferred_element_...  12 us
    dot_general x1, matrix products, fold_attention(): jnp.einsum('gnk,gjk->gnj', query_latent, piece_latent, preferred_element_...  11.5 us
  transfers between devices with their start and end apart: 4, of which 4 were waited for; matrix products, arithmetic and copies ran while one was open for 3% of the time, Pallas kernels for 0%

commit v1 on v0

v1 whole, which is shorter than its diff:
```python
import functools

import jax
import jax.numpy as jnp
from jax import lax
from jax.experimental import pallas as pl
from jax.experimental.pallas import tpu as pltpu
from jax.sharding import Mesh, PartitionSpec as P

ROPE = 64
NOPE = 128
RANK = 512
VDIM = 128
HG = 16
R = 16
GROUP = 4
ROWS = GROUP * R
ITEMS = HG * ROWS
KEYW = RANK + 128
SENDW = HG * VDIM + 128
SCALE2 = (NOPE + ROPE) ** -0.5 * 1.4426950408889634
NEG = -1e30
CTX = ("y", "x", "z", "c")
SWAP = ((0, 1), (1, 0))
MIB = 1 << 20


def shift(n, d):
    return [(i, (i + d) % n) for i in range(n)]


def call(kernel, out_shape, flops, nbytes, vmem=40, **kw):
    return pl.pallas_call(
        kernel,
        out_shape=out_shape,
        compiler_params=pltpu.CompilerParams(vmem_limit_bytes=vmem * MIB),
        cost_estimate=pl.CostEstimate(flops=flops, bytes_accessed=nbytes, transcendentals=0),
        **kw,
    )


def nt_dot(a, b):
    return lax.dot_general(a, b, (((1,), (1,)), ((), ())), preferred_element_type=jnp.float32)


def absorb_kernel(q_ref, w_ref, out_ref):
    lane = lax.broadcasted_iota(jnp.int32, (ROWS, 128), 1)
    row = lax.broadcasted_iota(jnp.int32, (ROWS, 128), 0)
    eye = (lane - ROPE == row).astype(jnp.float32)
    for h in range(HG):
        latent = jnp.dot(
            q_ref[:, h * NOPE : (h + 1) * NOPE], w_ref[h], preferred_element_type=jnp.float32
        )
        out_ref[h * ROWS : (h + 1) * ROWS, :RANK] = latent.astype(jnp.bfloat16)
        start = HG * NOPE + (h // 2) * 128
        pair = q_ref[:, start : start + 128].astype(jnp.float32)
        if h % 2:
            pair = pltpu.roll(pair, ROPE, 1)
        ext = jnp.where(lane < ROPE, pair, eye)
        out_ref[h * ROWS : (h + 1) * ROWS, RANK:] = ext.astype(jnp.bfloat16)


def absorb(q, w_uk):
    return call(
        absorb_kernel,
        jax.ShapeDtypeStruct((ITEMS, KEYW), jnp.bfloat16),
        2 * ITEMS * NOPE * RANK,
        4 * MIB,
    )(q, w_uk)


def attend_kernel(pieces, first, *refs):
    q_ref, qpos_ref = refs[:2]
    key_refs = refs[2 : 2 + pieces]
    rest = refs[2 + pieces :]
    if first:
        acc_out, st_out, ext_ref = rest
    else:
        acc_in, st_in, acc_out, st_out, ext_ref = rest
    keys = key_refs[0].shape[0]

    @pl.when(pl.program_id(0) == 0)
    def _():
        qpos = qpos_ref[0:1, :]
        lane = lax.broadcasted_iota(jnp.int32, (keys, 128), 1)
        for i, key_ref in enumerate(key_refs):
            ext = key_ref[:, RANK:].astype(jnp.float32)
            pos = ext[:, ROPE : ROPE + 1] * 128.0 + ext[:, ROPE + 1 : ROPE + 2]
            bias = jnp.where(pos <= qpos, 0.0, NEG)
            ext_ref[i] = jnp.where(lane < ROPE, ext, bias).astype(jnp.bfloat16)

    tile = q_ref.shape[0]
    sub = 128
    lane = lax.broadcasted_iota(jnp.int32, (sub, 128), 1)
    for t in range(tile // sub):
        rows = slice(t * sub, (t + 1) * sub)
        q_latent, q_ext = q_ref[rows, :RANK], q_ref[rows, RANK:]
        scores = [
            (nt_dot(q_latent, key_refs[i][:, :RANK]) + nt_dot(q_ext, ext_ref[i])) * SCALE2
            for i in range(pieces)
        ]
        top = functools.reduce(jnp.maximum, [jnp.max(s, axis=1, keepdims=True) for s in scores])
        if not first:
            top = jnp.maximum(top, st_in[rows, 0:1])
        weights = [jnp.exp2(s - top) for s in scores]
        total = sum(jnp.sum(w, axis=1, keepdims=True) for w in weights)
        acc = sum(
            jnp.dot(
                w.astype(jnp.bfloat16), key_refs[i][:, :RANK], preferred_element_type=jnp.float32
            )
            for i, w in enumerate(weights)
        )
        if not first:
            keep = jnp.exp2(st_in[rows, 0:1] - top)
            total = total + keep * st_in[rows, 1:2]
            acc = acc + keep * acc_in[rows, :]
        acc_out[rows, :] = acc
        st_out[rows, :] = jnp.where(lane == 0, top, total)


def attend(q, qpos, pieces, state, tile=256):
    n, keys = len(pieces), pieces[0].shape[0]
    first = state is None
    whole = lambda shape: pl.BlockSpec(shape, lambda i: (0, 0))
    part = lambda width: pl.BlockSpec((tile, width), lambda i: (i, 0))
    carried = [part(RANK), part(128)]
    return call(
        functools.partial(attend_kernel, n, first),
        (
            jax.ShapeDtypeStruct((ITEMS, RANK), jnp.float32),
            jax.ShapeDtypeStruct((ITEMS, 128), jnp.float32),
        ),
        2 * ITEMS * n * keys * (KEYW + RANK),
        (ITEMS * (KEYW + RANK) + n * keys * KEYW) * 2,
        grid=(ITEMS // tile,),
        in_specs=[part(KEYW), whole((8, 128))]
        + [whole((keys, KEYW))] * n
        + ([] if first else carried),
        out_specs=carried,
        scratch_shapes=[pltpu.VMEM((n, keys, 128), jnp.bfloat16)],
    )(q, qpos, *pieces, *([] if first else state))


def value_kernel(acc_ref, st_ref, v_ref, keep_ref, send_ref):
    half = ROWS // 2
    lane = lax.broadcasted_iota(jnp.int32, (ROWS, 128), 1)
    stats = jnp.zeros((ROWS, 128), jnp.float32)
    for h in range(HG):
        rows = slice(h * ROWS, (h + 1) * ROWS)
        top, total = st_ref[rows, 0:1], st_ref[rows, 1:2]
        context = (acc_ref[rows, :] / total).astype(jnp.bfloat16)
        out = jnp.dot(context, v_ref[h], preferred_element_type=jnp.float32).astype(jnp.bfloat16)
        cols = slice(h * VDIM, (h + 1) * VDIM)
        keep_ref[:, cols] = out[:half]
        send_ref[:, cols] = out[half:]
        stats = jnp.where(lane == h, top + jnp.log2(total), stats)
    high = stats.astype(jnp.bfloat16).astype(jnp.float32)
    mid = (stats - high).astype(jnp.bfloat16).astype(jnp.float32)
    low = stats - high - mid
    packed = high + pltpu.roll(mid, HG, 1) + pltpu.roll(low, 2 * HG, 1)
    packed = packed.astype(jnp.bfloat16)
    keep_ref[:, HG * VDIM :] = packed[:half]
    send_ref[:, HG * VDIM :] = packed[half:]


def value_up(state, value_weight):
    half = jax.ShapeDtypeStruct((ROWS // 2, SENDW), jnp.bfloat16)
    return call(value_kernel, (half, half), 2 * ITEMS * RANK * VDIM, 5 * MIB)(
        *state, value_weight
    )


def merge(a_ref, b_ref):
    def stats(ref):
        packed = ref[:, HG * VDIM :].astype(jnp.float32)
        return (
            packed
            + pltpu.roll(packed, 128 - HG, 1)
            + pltpu.roll(packed, 128 - 2 * HG, 1)
        )

    a, b = stats(a_ref), stats(b_ref)
    top = jnp.maximum(a, b)
    wa, wb = jnp.exp2(a - top), jnp.exp2(b - top)
    total = wa + wb
    return wa / total, wb / total, top + jnp.log2(total)


def merge_core_kernel(a_ref, b_ref, own_ref, send_ref):
    wa, wb, lse = merge(a_ref, b_ref)
    for h in range(HG):
        cols = slice(h * VDIM, (h + 1) * VDIM)
        out = a_ref[:, cols].astype(jnp.float32) * wa[:, h : h + 1]
        out = out + b_ref[:, cols].astype(jnp.float32) * wb[:, h : h + 1]
        out = out.astype(jnp.bfloat16)
        own_ref[:, cols] = out[:R]
        send_ref[:, cols] = out[R:]
    lane = lax.broadcasted_iota(jnp.int32, lse.shape, 1)
    lse = jnp.where(lane < HG, lse, 0.0)
    high = lse.astype(jnp.bfloat16).astype(jnp.float32)
    mid = (lse - high).astype(jnp.bfloat16).astype(jnp.float32)
    low = lse - high - mid
    packed = high + pltpu.roll(mid, HG, 1) + pltpu.roll(low, 2 * HG, 1)
    packed = packed.astype(jnp.bfloat16)
    own_ref[:, HG * VDIM :] = packed[:R]
    send_ref[:, HG * VDIM :] = packed[R:]


def merge_zhi_kernel(a_ref, b_ref, out_ref):
    wa, wb, _ = merge(a_ref, b_ref)
    for h in range(HG):
        cols = slice(h * VDIM, (h + 1) * VDIM)
        out = a_ref[:, cols].astype(jnp.float32) * wa[:, h : h + 1]
        out = out + b_ref[:, cols].astype(jnp.float32) * wb[:, h : h + 1]
        out = out.astype(jnp.bfloat16)
        for i in range(out_ref.shape[0]):
            out_ref[i, :, cols] = out


def project_kernel(zc_ref, x_ref, *refs):
    out_ref = refs[-1]
    z, c = zc_ref[0], zc_ref[1]
    for k in range(GROUP):
        to_z = z if k % 2 == 0 else 1 - z
        to_c = c if k < 2 else 1 - c
        out_ref[to_z * 2 + to_c] = jnp.dot(
            x_ref[...], refs[k][...], preferred_element_type=jnp.float32
        ).astype(jnp.bfloat16)


def gather_keys(block):
    half = block.shape[0] // 2
    a, b = block[:half], block[half:]
    a_row = [a] + [lax.ppermute(a, "x", shift(4, d)) for d in (1, 3, 2)]
    b_row = [b] + [lax.ppermute(b, "y", shift(4, d)) for d in (1, 3, 2)]
    a_all, b_all = jnp.concatenate(a_row), jnp.concatenate(b_row)
    a_far = [lax.ppermute(a_all, "y", shift(4, d)) for d in (1, 3, 2)]
    b_far = [lax.ppermute(b_all, "x", shift(4, d)) for d in (1, 3, 2)]
    return [a_all, b_all], [a_far[0], b_far[0], a_far[1], b_far[1]], [a_far[2], b_far[2]]


def local(query_unrotated, q_rope, latent, k_rope, key_pos, offset, w_uk, value_up_weight, w_out):
    y, x, z, c = (lax.axis_index(n) for n in CTX)

    q_own = jnp.concatenate([query_unrotated, q_rope], axis=1)
    q_z = lax.ppermute(q_own, "z", SWAP)
    q_chip = jnp.concatenate([q_own, q_z])
    q_all = jnp.concatenate([q_chip, lax.ppermute(q_chip, "c", SWAP)])

    pos = key_pos.reshape(-1, 1)
    keys = jnp.concatenate(
        [
            latent[0],
            k_rope[0],
            (pos // 128).astype(jnp.bfloat16),
            (pos % 128).astype(jnp.bfloat16),
            jnp.zeros((pos.shape[0], KEYW - RANK - ROPE - 2), jnp.bfloat16),
        ],
        axis=1,
    )
    near, mid, far = gather_keys(keys)

    lane = jnp.arange(128, dtype=jnp.int32) - ROPE
    part = jnp.maximum(lane, 0) // R
    row_z = jnp.where(part % 2 == 0, z, 1 - z)
    row_c = jnp.where(part < 2, c, 1 - c)
    row = (((y * 4 + x) * 2 + row_z) * 2 + row_c) * R + lane % R
    qpos = jnp.broadcast_to((offset[0] + row).astype(jnp.float32)[None, :], (8, 128))

    q = absorb(q_all, w_uk)
    state = attend(q, qpos, near, None)
    state = attend(q, qpos, mid, state)
    state = attend(q, qpos, far, state)

    w_own, _ = lax.optimization_barrier((w_out, q_z))
    w_z = lax.ppermute(w_own, "z", SWAP)
    w_c = lax.ppermute(w_own, "c", SWAP)
    w_zc = lax.ppermute(w_z, "c", SWAP)

    keep, send = value_up(state, value_up_weight)
    both = jax.ShapeDtypeStruct((R, SENDW), jnp.bfloat16)
    own, send = call(merge_core_kernel, (both, both), MIB, MIB)(
        keep, lax.ppermute(send, "c", SWAP)
    )
    heads = call(
        merge_zhi_kernel, jax.ShapeDtypeStruct((16, R, HG * VDIM), jnp.bfloat16), MIB, MIB
    )(own, lax.ppermute(send, "z", SWAP))

    rows = lax.all_to_all(heads, ("y", "x"), 0, 0, tiled=True).reshape(16 * R, HG * VDIM)
    ncol = w_out.shape[1]
    sums = call(
        project_kernel,
        jax.ShapeDtypeStruct((GROUP, 16 * R, ncol), jnp.bfloat16),
        2 * 16 * R * HG * VDIM * GROUP * ncol,
        4 * MIB,
        in_specs=[pl.BlockSpec(memory_space=pltpu.SMEM)]
        + [pl.BlockSpec(memory_space=pltpu.VMEM)] * (1 + GROUP),
    )(jnp.stack([z, c]), rows, w_own, w_z, w_c, w_zc)
    sums = lax.all_to_all(
        sums.reshape(16, 4 * R, ncol), ("z", "c", "head"), 0, 0, tiled=True
    )
    total = jnp.sum(sums.reshape(GROUP, 4, 4, R, ncol).astype(jnp.float32), axis=1)
    return jnp.transpose(total.astype(jnp.bfloat16), (1, 0, 2, 3)).reshape(16 * R, ncol)


def solution(mesh):
    grid = Mesh(mesh.devices.reshape(4, 4, 2, 2, 4), CTX + ("head",))
    return jax.shard_map(
        local,
        mesh=grid,
        in_specs=(
            P(CTX, "head"),
            P(CTX, "head"),
            P(None, CTX, None),
            P(None, CTX, None),
            P(None, CTX),
            P(),
            P("head", None, None),
            P("head", None, None),
            P("head", CTX),
        ),
        out_specs=P("head", CTX),
        check_vma=False,
    )
```

time: 409 us -> 151 us (0.37); the launches traced: 403 us -> 151 us
  waiting for transfers between devices: 210 us -> 43.2 us
  blocking collectives: 124 us -> 16 us
  starting transfers between devices: 0.12 us -> 52.4 us
  matrix products: 44.7 us -> 0 us
  Pallas kernels: 0 us -> 34 us
  between operations: 13.8 us -> 0.87 us
  other arithmetic: 9.2 us -> 0.45 us
    all_gather x3 -> x0, waiting for transfers between devices: 194 us -> none  [the longest x1 86.8 us: local(): lax.all_gather(per_head_output, 'ctx', axis=0, tiled=True)]
    all_gather x1 -> x0, blocking collectives: 124 us -> none  [local(): all_pos = lax.all_gather(key_pos, 'ctx', axis=1, tiled=True)]
    dot_general x6 -> x0, matrix products: 44.7 us -> none  [the longest x1 15.2 us: fold_attention(): jnp.einsum('gnj,gjk->gnk', weights_low, piece_latent, preferred_element_t...]
    ppermute x0 -> x19, waiting for transfers between devices: none -> 43.2 us  [the longest x1 22.3 us: local(): w_z = lax.ppermute(w_own, 'z', SWAP)]
    ppermute x0 -> x19, starting transfers between devices: none -> 41 us  [the longest x1 6.01 us: local(): q_z = lax.ppermute(q_own, 'z', SWAP)]
    pallas_call x0 -> x8, Pallas kernels: none -> 34 us  [the longest x3 28.7 us: attend(): call(functools.partial(attend_kernel, n, first), (jax.ShapeDtypeStruct((I...]
    all_to_all x0 -> x1, blocking collectives: none -> 16 us  [local(): lax.all_to_all(sums.reshape(16, 4 * R, ncol), ('z', 'c', 'head'), 0, 0, t...]
    reduce_scatter x1 -> x0, waiting for transfers between devices: 14.6 us -> none  [local(): lax.psum_scatter(partial_weighted_sums.astype(jnp.bfloat16), 'head', scat...]
  transfers between devices with their start and end apart: 4 -> 20, of which waited for: 4 -> 9; matrix products, arithmetic and copies ran while one was open for 3% -> 0% of each run, Pallas kernels for 0% -> 14%
where the time goes in v1:
time: 151 us
  starting transfers between devices  52.4 us (35%)
  waiting for transfers between devices  43.2 us (29%)
  Pallas kernels  34 us (23%)
  blocking collectives  16 us (11%)
  local copies, waits for them, and re-layouts  3.9 us (3%)
    pallas_call x3, Pallas kernels, attend(): call(functools.partial(attend_kernel, n, first), (jax.ShapeDtypeStruct((I...  28.7 us
    ppermute x1, waiting for transfers between devices, local(): w_z = lax.ppermute(w_own, 'z', SWAP)  22.3 us
    all_to_all x1, blocking collectives, local(): lax.all_to_all(sums.reshape(16, 4 * R, ncol), ('z', 'c', 'head'), 0, 0, t...  16 us
    ppermute x3, waiting for transfers between devices, gather_keys(): a_far = [lax.ppermute(a_all, 'y', shift(4, d)) for d in (1, 3, 2)]  13.3 us
    all_to_all x1, starting transfers between devices, local(): lax.all_to_all(heads, ('y', 'x'), 0, 0, tiled=True)  11.4 us
    ppermute x1, starting transfers between devices, local(): q_z = lax.ppermute(q_own, 'z', SWAP)  6.01 us
    ppermute x1, starting transfers between devices, local(): w_z = lax.ppermute(w_own, 'z', SWAP)  5.43 us
    ppermute x1, starting transfers between devices, local(): lax.ppermute(send, 'z', SWAP)  5.19 us
  transfers between devices with their start and end apart: 20, of which 9 were waited for; matrix products, arithmetic and copies ran while one was open for 0% of the time, Pallas kernels for 14%

profile of v1, /device:TPU:33, one launch (start us, length us, event | category | flops | bytes accessed | tf_op | source)
XLA Modules:
  0.0 150.8 jit_solution(13776039931596531173)
XLA Ops:
  0.0 0.9 copy.23
  0.9 0.8 copy.24
  1.7 0.1 fusion.1
  1.9 1.1 concatenate.22
  3.0 2.8 %collective-permute-start.4 = (bf16[128,640]{1,0:T(8,128)(2,1)S(1)}, bf16[128,640]{1,0:T(8,128)(2,1)S(1)}, u32[]{:S(2)}, u32[]{:S(2)}) collective-permute-start(bf16[128,640]{1,0:T(8,128)(2,1)S(1)} %get-tuple-element.28), channel_id=1, source_target_pairs={{0,32},{16,48},{32,0},{48,16},{1,33},{17,49},{33,1},{49,17},{2,34}... | collective-permute-start | bytes 491528 | tf_op jit(solution)/shard_map/ppermute | solution.py:234
  5.9 0.9 collective-permute-start.3
  6.7 0.6 collective-permute-start.2
  7.3 2.9 %collective-permute-start.8 = (bf16[128,640]{1,0:T(8,128)(2,1)S(1)}, bf16[128,640]{1,0:T(8,128)(2,1)S(1)}, u32[]{:S(2)}, u32[]{:S(2)}) collective-permute-start(bf16[128,640]{1,0:T(8,128)(2,1)S(1)} %get-tuple-element.27), channel_id=1, source_target_pairs={{0,128},{64,192},{128,0},{192,64},{1,129},{65,193},{129,1},{193,65... | collective-permute-start | bytes 491528 | tf_op jit(solution)/shard_map/ppermute | solution.py:235
  10.2 0.8 collective-permute-start.7
  11.7 0.8 collective-permute-start.6
  12.5 0.8 collective-permute-done.3
  13.3 6.0 %collective-permute-start = (bf16[16,3072]{1,0:T(8,128)(2,1)S(1)}, bf16[16,3072]{1,0:T(8,128)(2,1)S(1)}, u32[]{:S(2)}, u32[]{:S(2)}) collective-permute-start(bf16[16,3072]{1,0:T(8,128)(2,1)S(1)} %constant_dynamic-update-slice_fusion), channel_id=1, source_target_pairs={{0,8},{8,0},{1,9},{9,1},{2,10},{10,2},{3,11},{11,3},{4,12},{12,4},... | collective-permute-start | bytes 294920 | tf_op jit(solution)/shard_map/ppermute | solution.py:246
  19.3 0.1 pad_maximum_fusion.refs_2_
  19.4 1.4 collective-permute-start.10
  20.8 0.6 collective-permute-done
  21.4 3.6 %collective-permute-start.1 = (bf16[32,3072]{1,0:T(8,128)(2,1)S(1)}, bf16[32,3072]{1,0:T(8,128)(2,1)S(1)}, u32[]{:S(2)}, u32[]{:S(2)}) collective-permute-start(bf16[32,3072]{1,0:T(8,128)(2,1)S(1)} %pad_maximum_fusion.3), channel_id=1, source_target_pairs={{0,4},{4,0},{1,5},{5,1},{2,6},{6,2},{3,7},{7,3},{8,12},{12,8},{9,1... | collective-permute-start | bytes 589832 | tf_op jit(solution)/shard_map/ppermute | solution.py:248
  25.0 2.7 %collective-permute-start.12 = (bf16[512,640]{1,0:T(8,128)(2,1)S(1)}, bf16[512,640]{1,0:T(8,128)(2,1)S(1)}, u32[]{:S(2)}, u32[]{:S(2)}) collective-permute-start(bf16[512,640]{1,0:T(8,128)(2,1)S(1)} %pad_maximum_fusion.refs_2_), channel_id=1, source_target_pairs={{0,192},{64,0},{128,64},{192,128},{1,193},{65,1},{129,65},{193,129... | collective-permute-start | bytes 1966088 | tf_op jit(solution)/shard_map/ppermute | solution.py:237
  27.7 0.1 pad_maximum_fusion.1.refs_3_
  27.8 1.8 %collective-permute-start.11 = (bf16[512,640]{1,0:T(8,128)(2,1)S(1)}, bf16[512,640]{1,0:T(8,128)(2,1)S(1)}, u32[]{:S(2)}, u32[]{:S(2)}) collective-permute-start(bf16[512,640]{1,0:T(8,128)(2,1)S(1)} %pad_maximum_fusion.1.refs_3_), channel_id=1, source_target_pairs={{0,16},{16,32},{32,48},{48,0},{1,17},{17,33},{33,49},{49,1},{2,18}... | collective-permute-start | bytes 1966088 | tf_op jit(solution)/shard_map/ppermute | solution.py:238
  29.6 1.4 collective-permute-start.13
  31.0 0.4 collective-permute-start.5
  31.5 0.4 shard_map.91.refs_0_
  31.9 3.3 %collective-permute-done.10.refs_2_ = bf16[512,640]{1,0:T(8,128)(2,1)S(1)} collective-permute-done((bf16[512,640]{1,0:T(8,128)(2,1)S(1)}, bf16[512,640]{1,0:T(8,128)(2,1)S(1)}, u32[]{:S(2)}, u32[]{:S(2)}) %collective-permute-start.10) | collective-permute-done | bytes 655392 | tf_op jit(solution)/shard_map/ppermute | solution.py:237
  35.2 1.6 %collective-permute-start.9 = (bf16[512,640]{1,0:T(8,128)(2,1)S(1)}, bf16[512,640]{1,0:T(8,128)(2,1)S(1)}, u32[]{:S(2)}, u32[]{:S(2)}) collective-permute-start(bf16[512,640]{1,0:T(8,128)(2,1)S(1)} %pad_maximum_fusion.1.refs_3_), channel_id=1, source_target_pairs={{0,32},{16,48},{32,0},{48,16},{1,33},{17,49},{33,1},{49,17},{2,34}... | collective-permute-start | bytes 1966088 | tf_op jit(solution)/shard_map/ppermute | solution.py:238
  36.8 7.2 %shard_map.92 = (f32[1024,512]{1,0:T(8,128)S(1)}, f32[1024,128]{1,0:T(8,128)S(1)}) custom-call(bf16[1024,640]{1,0:T(8,128)(2,1)S(1)} %shard_map.91.refs_0_, f32[8,128]{1,0:T(8,128)S(1)} %broadcast_in_dim.27.refs_1_, bf16[512,640]{1,0:T(8,128)(2,1)S(1)} %pad_maximum_fusion.refs_2_, bf16[512,640]{1,0:T(8,128)(2,1)S(1)} %pad_maximum_fusion.1.refs_3_), custom_call_target="tpu_custom_call" | custom-call | flops 2415919104 | bytes 3670016 | tf_op jit(solution)/shard_map/pallas_call | solution.py:127
  44.0 1.7 %collective-permute-done.11.refs_3_ = bf16[512,640]{1,0:T(8,128)(2,1)S(1)} collective-permute-done((bf16[512,640]{1,0:T(8,128)(2,1)S(1)}, bf16[512,640]{1,0:T(8,128)(2,1)S(1)}, u32[]{:S(2)}, u32[]{:S(2)}) %collective-permute-start.11) | collective-permute-done | bytes 655392 | tf_op jit(solution)/shard_map/ppermute | solution.py:238
  45.7 10.0 %collective-permute-done.12.refs_4_ = bf16[512,640]{1,0:T(8,128)(2,1)S(1)} collective-permute-done((bf16[512,640]{1,0:T(8,128)(2,1)S(1)}, bf16[512,640]{1,0:T(8,128)(2,1)S(1)}, u32[]{:S(2)}, u32[]{:S(2)}) %collective-permute-start.12) | collective-permute-done | bytes 655392 | tf_op jit(solution)/shard_map/ppermute | solution.py:237
  55.7 13.3 %shard_map.93 = (f32[1024,512]{1,0:T(8,128)S(1)}, f32[1024,128]{1,0:T(8,128)S(1)}) custom-call(bf16[1024,640]{1,0:T(8,128)(2,1)S(1)} %shard_map.91.refs_0_, f32[8,128]{1,0:T(8,128)S(1)} %broadcast_in_dim.27.refs_1_, bf16[512,640]{1,0:T(8,128)(2,1)S(1)} %collective-permute-done.10.refs_2_, bf16[512,640]{1,0:T(8,128)(2,1)S(1)} %collective-permute-done.11.refs_3_, ...), custom_call_target="tpu_custom_call" | custom-call | flops 4831838208 | bytes 4980736 | tf_op jit(solution)/shard_map/pallas_call | solution.py:127
  69.1 8.2 %shard_map.94 = (f32[1024,512]{1,0:T(8,128)S(1)}, f32[1024,128]{1,0:T(8,128)S(1)}) custom-call(bf16[1024,640]{1,0:T(8,128)(2,1)S(1)} %shard_map.91.refs_0_, f32[8,128]{1,0:T(8,128)S(1)} %broadcast_in_dim.27.refs_1_, bf16[512,640]{1,0:T(8,128)(2,1)S(1)} %collective-permute-done.5.refs_2_, bf16[512,640]{1,0:T(8,128)(2,1)S(1)} %collective-permute-done.9.refs_3_, ...), custom_call_target="tpu_custom_call" | custom-call | flops 2415919104 | bytes 3670016 | tf_op jit(solution)/shard_map/pallas_call | solution.py:127
  77.3 1.4 shard_map.95
  78.7 1.1 collective-permute-start.14
  79.8 1.0 collective-permute-done.14.b_ref
  80.8 0.3 shard_map.96
  81.1 5.2 %collective-permute-start.15 = (bf16[16,2176]{1,0:T(8,128)(2,1)S(1)}, bf16[16,2176]{1,0:T(8,128)(2,1)S(1)}, u32[]{:S(2)}, u32[]{:S(2)}) collective-permute-start(bf16[16,2176]{1,0:T(8,128)(2,1)S(1)} %get-tuple-element.25), channel_id=1, source_target_pairs={{0,8},{8,0},{1,9},{9,1},{2,10},{10,2},{3,11},{11,3},{4,12},{12,4},... | collective-permute-start | bytes 208904 | tf_op jit(solution)/shard_map/ppermute | solution.py:287
  86.3 2.0 %collective-permute-done.15.b_ref = bf16[16,2176]{1,0:T(8,128)(2,1)S(1)} collective-permute-done((bf16[16,2176]{1,0:T(8,128)(2,1)S(1)}, bf16[16,2176]{1,0:T(8,128)(2,1)S(1)}, u32[]{:S(2)}, u32[]{:S(2)}) %collective-permute-start.15) | collective-permute-done | bytes 69664 | tf_op jit(solution)/shard_map/ppermute | solution.py:287
  88.3 1.4 shard_map.97
  89.7 11.4 %all-to-all-start = ((bf16[16,16,2048]{2,1,0:T(8,128)(2,1)}), bf16[16,16,2048]{2,1,0:T(8,128)(2,1)S(1)}, u32[]{:S(2)}, u32[]{:S(2)}) async-start(bf16[16,16,2048]{2,1,0:T(8,128)(2,1)} %shard_map.97), calls=%async_computation | async-start | bytes 2097152 | tf_op jit(solution)/shard_map/all_to_all | solution.py:289
  101.1 0.3 copy.30.refs_0_
  101.4 5.4 %collective-permute-start.16 = (bf16[2048,112]{1,0:T(8,128)(2,1)S(1)}, bf16[2048,112]{1,0:T(8,128)(2,1)S(1)}, u32[]{:S(2)}, u32[]{:S(2)}) collective-permute-start(bf16[2048,112]{1,0:T(8,128)(2,1)S(1)} %copy.30.refs_0_), channel_id=1, source_target_pairs={{0,8},{8,0},{1,9},{9,1},{2,10},{10,2},{3,11},{11,3},{4,12},{12,4},... | collective-permute-start | bytes 1376264 | tf_op jit(solution)/shard_map/ppermute | solution.py:276
  106.8 1.0 collective-permute-start.17
  107.8 22.3 %collective-permute-done.16.refs_1_ = bf16[2048,112]{1,0:T(8,128)(2,1)S(1)} collective-permute-done((bf16[2048,112]{1,0:T(8,128)(2,1)S(1)}, bf16[2048,112]{1,0:T(8,128)(2,1)S(1)}, u32[]{:S(2)}, u32[]{:S(2)}) %collective-permute-start.16) | collective-permute-done | bytes 458784 | tf_op jit(solution)/shard_map/ppermute | solution.py:276
  130.2 0.5 collective-permute-start.18
  130.7 0.1 pad_add_fusion.zc_ref
  130.7 1.5 collective-permute-done.18.refs_3_
  132.2 1.8 %shard_map.98 = bf16[4,256,112]{2,1,0:T(8,128)(2,1)S(1)} custom-call(s32[2]{0:T(128)S(1)} %pad_add_fusion.zc_ref, bf16[256,2048]{1,0:T(8,128)(2,1)S(1)} %bitcast.12, bf16[2048,112]{1,0:T(8,128)(2,1)S(1)} %copy.30.refs_0_, bf16[2048,112]{1,0:T(8,128)(2,1)S(1)} %collective-permute-done.16.refs_1_, bf16[2048,112]{1,0:T(8,128)(2,1)S(1)} %collective-permute-done.17.refs_2_, ...), custom_call_target="tpu_custom_call" | custom-call | flops 469762048 | bytes 4194304 | tf_op jit(solution)/shard_map/pallas_call | solution.py:291
  134.0 16.0 %all_to_all.10 = bf16[16,64,112]{2,1,0:T(8,128)(2,1)S(1)} all-to-all(bf16[16,64,112]{2,1,0:T(8,128)(2,1)S(1)} %bitcast.13), channel_id=1, replica_groups=mesh['y'=4,'x'=4,'z'=2,'c'=2,'head'=4] {'z','c','head'}, dimensions={0} | all-to-all | bytes 458752 | tf_op jit(solution)/shard_map/all_to_all | solution.py:299
  150.0 0.1 reduce_sum.12
  150.1 0.7 copy.32
  (30 shorter events, 0.2 us)
Async XLA Ops:
  0.0 11.0 %copy-start.3 = (bf16[16,2048]{1,0:T(8,128)(2,1)S(1)}, bf16[16,2048]{1,0:T(8,128)(2,1)}, u32[]{:S(2)}) copy-start(bf16[16,2048]{1,0:T(8,128)(2,1)} %param.9) | copy-start | bytes 196612
  0.0 11.7 %copy-start.4 = (bf16[16,1024]{1,0:T(8,128)(2,1)S(1)}, bf16[16,1024]{1,0:T(8,128)(2,1)}, u32[]{:S(2)}) copy-start(bf16[16,1024]{1,0:T(8,128)(2,1)} %param.10) | copy-start | bytes 98308
  3.0 8.7 %collective-permute-start.4 = (bf16[128,640]{1,0:T(8,128)(2,1)S(1)}, bf16[128,640]{1,0:T(8,128)(2,1)S(1)}, u32[]{:S(2)}, u32[]{:S(2)}) collective-permute-start(bf16[128,640]{1,0:T(8,128)(2,1)S(1)} %get-tuple-element.28), channel_id=1, source_target_pairs={{0,32},{16,48},{32,0},{48,16},{1,33},{17,49},{33,1},{49,17},{2,34}... | collective-permute-start | bytes 491528 | tf_op jit(solution)/shard_map/ppermute | solution.py:234
  5.9 7.5 %collective-permute-start.3 = (bf16[128,640]{1,0:T(8,128)(2,1)S(1)}, bf16[128,640]{1,0:T(8,128)(2,1)S(1)}, u32[]{:S(2)}, u32[]{:S(2)}) collective-permute-start(bf16[128,640]{1,0:T(8,128)(2,1)S(1)} %get-tuple-element.28), channel_id=1, source_target_pairs={{0,48},{16,0},{32,16},{48,32},{1,49},{17,1},{33,17},{49,33},{2,50}... | collective-permute-start | bytes 491528 | tf_op jit(solution)/shard_map/ppermute | solution.py:234
  6.7 12.6 %collective-permute-start.2 = (bf16[128,640]{1,0:T(8,128)(2,1)S(1)}, bf16[128,640]{1,0:T(8,128)(2,1)S(1)}, u32[]{:S(2)}, u32[]{:S(2)}) collective-permute-start(bf16[128,640]{1,0:T(8,128)(2,1)S(1)} %get-tuple-element.28), channel_id=1, source_target_pairs={{0,16},{16,32},{32,48},{48,0},{1,17},{17,33},{33,49},{49,1},{2,18}... | collective-permute-start | bytes 491528 | tf_op jit(solution)/shard_map/ppermute | solution.py:234
  7.3 17.7 %collective-permute-start.8 = (bf16[128,640]{1,0:T(8,128)(2,1)S(1)}, bf16[128,640]{1,0:T(8,128)(2,1)S(1)}, u32[]{:S(2)}, u32[]{:S(2)}) collective-permute-start(bf16[128,640]{1,0:T(8,128)(2,1)S(1)} %get-tuple-element.27), channel_id=1, source_target_pairs={{0,128},{64,192},{128,0},{192,64},{1,129},{65,193},{129,1},{193,65... | collective-permute-start | bytes 491528 | tf_op jit(solution)/shard_map/ppermute | solution.py:235
  10.2 17.5 %collective-permute-start.7 = (bf16[128,640]{1,0:T(8,128)(2,1)S(1)}, bf16[128,640]{1,0:T(8,128)(2,1)S(1)}, u32[]{:S(2)}, u32[]{:S(2)}) collective-permute-start(bf16[128,640]{1,0:T(8,128)(2,1)S(1)} %get-tuple-element.27), channel_id=1, source_target_pairs={{0,192},{64,0},{128,64},{192,128},{1,193},{65,1},{129,65},{193,129... | collective-permute-start | bytes 491528 | tf_op jit(solution)/shard_map/ppermute | solution.py:235
  11.7 16.0 %collective-permute-start.6 = (bf16[128,640]{1,0:T(8,128)(2,1)S(1)}, bf16[128,640]{1,0:T(8,128)(2,1)S(1)}, u32[]{:S(2)}, u32[]{:S(2)}) collective-permute-start(bf16[128,640]{1,0:T(8,128)(2,1)S(1)} %get-tuple-element.27), channel_id=1, source_target_pairs={{0,64},{64,128},{128,192},{192,0},{1,65},{65,129},{129,193},{193,1... | collective-permute-start | bytes 491528 | tf_op jit(solution)/shard_map/ppermute | solution.py:235
  13.3 8.0 %collective-permute-start = (bf16[16,3072]{1,0:T(8,128)(2,1)S(1)}, bf16[16,3072]{1,0:T(8,128)(2,1)S(1)}, u32[]{:S(2)}, u32[]{:S(2)}) collective-permute-start(bf16[16,3072]{1,0:T(8,128)(2,1)S(1)} %constant_dynamic-update-slice_fusion), channel_id=1, source_target_pairs={{0,8},{8,0},{1,9},{9,1},{2,10},{10,2},{3,11},{11,3},{4,12},{12,4},... | collective-permute-start | bytes 294920 | tf_op jit(solution)/shard_map/ppermute | solution.py:246
  19.4 12.1 %copy-start = (bf16[16,128,512]{2,1,0:T(8,128)(2,1)S(1)}, bf16[16,128,512]{2,1,0:T(8,128)(2,1)}, u32[]{:S(2)}) copy-start(bf16[16,128,512]{2,1,0:T(8,128)(2,1)} %w_ref.1) | copy-start | bytes 6291460
  19.4 15.8 %collective-permute-start.10 = (bf16[512,640]{1,0:T(8,128)(2,1)S(1)}, bf16[512,640]{1,0:T(8,128)(2,1)S(1)}, u32[]{:S(2)}, u32[]{:S(2)}) collective-permute-start(bf16[512,640]{1,0:T(8,128)(2,1)S(1)} %pad_maximum_fusion.refs_2_), channel_id=1, source_target_pairs={{0,64},{64,128},{128,192},{192,0},{1,65},{65,129},{129,193},{193,1... | collective-permute-start | bytes 1966088 | tf_op jit(solution)/shard_map/ppermute | solution.py:237
  21.4 9.7 %collective-permute-start.1 = (bf16[32,3072]{1,0:T(8,128)(2,1)S(1)}, bf16[32,3072]{1,0:T(8,128)(2,1)S(1)}, u32[]{:S(2)}, u32[]{:S(2)}) collective-permute-start(bf16[32,3072]{1,0:T(8,128)(2,1)S(1)} %pad_maximum_fusion.3), channel_id=1, source_target_pairs={{0,4},{4,0},{1,5},{5,1},{2,6},{6,2},{3,7},{7,3},{8,12},{12,8},{9,1... | collective-permute-start | bytes 589832 | tf_op jit(solution)/shard_map/ppermute | solution.py:248
  25.0 30.7 %collective-permute-start.12 = (bf16[512,640]{1,0:T(8,128)(2,1)S(1)}, bf16[512,640]{1,0:T(8,128)(2,1)S(1)}, u32[]{:S(2)}, u32[]{:S(2)}) collective-permute-start(bf16[512,640]{1,0:T(8,128)(2,1)S(1)} %pad_maximum_fusion.refs_2_), channel_id=1, source_target_pairs={{0,192},{64,0},{128,64},{192,128},{1,193},{65,1},{129,65},{193,129... | collective-permute-start | bytes 1966088 | tf_op jit(solution)/shard_map/ppermute | solution.py:237
  27.8 17.9 %collective-permute-start.11 = (bf16[512,640]{1,0:T(8,128)(2,1)S(1)}, bf16[512,640]{1,0:T(8,128)(2,1)S(1)}, u32[]{:S(2)}, u32[]{:S(2)}) collective-permute-start(bf16[512,640]{1,0:T(8,128)(2,1)S(1)} %pad_maximum_fusion.1.refs_3_), channel_id=1, source_target_pairs={{0,16},{16,32},{32,48},{48,0},{1,17},{17,33},{33,49},{49,1},{2,18}... | collective-permute-start | bytes 1966088 | tf_op jit(solution)/shard_map/ppermute | solution.py:238
  29.6 26.1 %collective-permute-start.13 = (bf16[512,640]{1,0:T(8,128)(2,1)S(1)}, bf16[512,640]{1,0:T(8,128)(2,1)S(1)}, u32[]{:S(2)}, u32[]{:S(2)}) collective-permute-start(bf16[512,640]{1,0:T(8,128)(2,1)S(1)} %pad_maximum_fusion.1.refs_3_), channel_id=1, source_target_pairs={{0,48},{16,0},{32,16},{48,32},{1,49},{17,1},{33,17},{49,33},{2,50}... | collective-permute-start | bytes 1966088 | tf_op jit(solution)/shard_map/ppermute | solution.py:238
  31.0 38.0 %collective-permute-start.5 = (bf16[512,640]{1,0:T(8,128)(2,1)S(1)}, bf16[512,640]{1,0:T(8,128)(2,1)S(1)}, u32[]{:S(2)}, u32[]{:S(2)}) collective-permute-start(bf16[512,640]{1,0:T(8,128)(2,1)S(1)} %pad_maximum_fusion.refs_2_), channel_id=1, source_target_pairs={{0,128},{64,192},{128,0},{192,64},{1,129},{65,193},{129,1},{193,65... | collective-permute-start | bytes 1966088 | tf_op jit(solution)/shard_map/ppermute | solution.py:237
  35.2 33.8 %collective-permute-start.9 = (bf16[512,640]{1,0:T(8,128)(2,1)S(1)}, bf16[512,640]{1,0:T(8,128)(2,1)S(1)}, u32[]{:S(2)}, u32[]{:S(2)}) collective-permute-start(bf16[512,640]{1,0:T(8,128)(2,1)S(1)} %pad_maximum_fusion.1.refs_3_), channel_id=1, source_target_pairs={{0,32},{16,48},{32,0},{48,16},{1,33},{17,49},{33,1},{49,17},{2,34}... | collective-permute-start | bytes 1966088 | tf_op jit(solution)/shard_map/ppermute | solution.py:238
  69.1 8.2 %copy-start.1 = (bf16[16,512,128]{2,1,0:T(8,128)(2,1)S(1)}, bf16[16,512,128]{2,1,0:T(8,128)(2,1)}, u32[]{:S(2)}) copy-start(bf16[16,512,128]{2,1,0:T(8,128)(2,1)} %v_ref.1) | copy-start | bytes 6291460
  78.7 2.1 %collective-permute-start.14 = (bf16[32,2176]{1,0:T(8,128)(2,1)S(1)}, bf16[32,2176]{1,0:T(8,128)(2,1)S(1)}, u32[]{:S(2)}, u32[]{:S(2)}) collective-permute-start(bf16[32,2176]{1,0:T(8,128)(2,1)S(1)} %get-tuple-element.23), channel_id=1, source_target_pairs={{0,4},{4,0},{1,5},{5,1},{2,6},{6,2},{3,7},{7,3},{8,12},{12,8},{9,1... | collective-permute-start | bytes 417800 | tf_op jit(solution)/shard_map/ppermute | solution.py:283
  81.1 7.2 %collective-permute-start.15 = (bf16[16,2176]{1,0:T(8,128)(2,1)S(1)}, bf16[16,2176]{1,0:T(8,128)(2,1)S(1)}, u32[]{:S(2)}, u32[]{:S(2)}) collective-permute-start(bf16[16,2176]{1,0:T(8,128)(2,1)S(1)} %get-tuple-element.25), channel_id=1, source_target_pairs={{0,8},{8,0},{1,9},{9,1},{2,10},{10,2},{3,11},{11,3},{4,12},{12,4},... | collective-permute-start | bytes 208904 | tf_op jit(solution)/shard_map/ppermute | solution.py:287
  89.7 11.4 %copy-start.2 = (bf16[2048,112]{0,1:T(8,128)(2,1)S(1)}, bf16[2048,112]{0,1:T(8,128)(2,1)}, u32[]{:S(2)}) copy-start(bf16[2048,112]{0,1:T(8,128)(2,1)} %param.17) | copy-start | bytes 1376260
  89.7 42.5 %all-to-all-start = ((bf16[16,16,2048]{2,1,0:T(8,128)(2,1)}), bf16[16,16,2048]{2,1,0:T(8,128)(2,1)S(1)}, u32[]{:S(2)}, u32[]{:S(2)}) async-start(bf16[16,16,2048]{2,1,0:T(8,128)(2,1)} %shard_map.97), calls=%async_computation | async-start | bytes 2097152 | tf_op jit(solution)/shard_map/all_to_all | solution.py:289
  101.4 28.8 %collective-permute-start.16 = (bf16[2048,112]{1,0:T(8,128)(2,1)S(1)}, bf16[2048,112]{1,0:T(8,128)(2,1)S(1)}, u32[]{:S(2)}, u32[]{:S(2)}) collective-permute-start(bf16[2048,112]{1,0:T(8,128)(2,1)S(1)} %copy.30.refs_0_), channel_id=1, source_target_pairs={{0,8},{8,0},{1,9},{9,1},{2,10},{10,2},{3,11},{11,3},{4,12},{12,4},... | collective-permute-start | bytes 1376264 | tf_op jit(solution)/shard_map/ppermute | solution.py:276
  106.8 23.9 %collective-permute-start.17 = (bf16[2048,112]{1,0:T(8,128)(2,1)S(1)}, bf16[2048,112]{1,0:T(8,128)(2,1)S(1)}, u32[]{:S(2)}, u32[]{:S(2)}) collective-permute-start(bf16[2048,112]{1,0:T(8,128)(2,1)S(1)} %copy.30.refs_0_), channel_id=1, source_target_pairs={{0,4},{4,0},{1,5},{5,1},{2,6},{6,2},{3,7},{7,3},{8,12},{12,8},{9,1... | collective-permute-start | bytes 1376264 | tf_op jit(solution)/shard_map/ppermute | solution.py:277
  130.2 2.0 %collective-permute-start.18 = (bf16[2048,112]{1,0:T(8,128)(2,1)S(1)}, bf16[2048,112]{1,0:T(8,128)(2,1)S(1)}, u32[]{:S(2)}, u32[]{:S(2)}) collective-permute-start(bf16[2048,112]{1,0:T(8,128)(2,1)S(1)} %collective-permute-done.16.refs_1_), channel_id=1, source_target_pairs={{0,4},{4,0},{1,5},{5,1},{2,6},{6,2},{3,7},{7,3},{8,12},{12,8},{9,1... | collective-permute-start | bytes 1376264 | tf_op jit(solution)/shard_map/ppermute | solution.py:278

commit v2 on v0

v2 whole, which is shorter than its diff:
```python
import functools

import jax
import jax.numpy as jnp
from jax import lax
from jax.experimental import pallas as pl
from jax.experimental.pallas import tpu as pltpu
from jax.sharding import Mesh, PartitionSpec as P

ROPE = 64
NOPE = 128
RANK = 512
VDIM = 128
HG = 16
R = 16
GROUP = 8
ROWS = GROUP * R
ITEMS = HG * ROWS
KEYW = RANK + 128
ITEMW = RANK + 256
SENDW = HG * VDIM + 128
SCALE2 = (NOPE + ROPE) ** -0.5 * 1.4426950408889634
NEG = -1e30
CTX = ("y", "u", "x", "z", "c")
SWAP = ((0, 1), (1, 0))
MIB = 1 << 20


def shift(n, d):
    return [(i, (i + d) % n) for i in range(n)]


def call(kernel, out_shape, flops, nbytes, vmem=40, **kw):
    return pl.pallas_call(
        kernel,
        out_shape=out_shape,
        compiler_params=pltpu.CompilerParams(vmem_limit_bytes=vmem * MIB),
        cost_estimate=pl.CostEstimate(flops=flops, bytes_accessed=nbytes, transcendentals=0),
        **kw,
    )


def nt_dot(a, b):
    return lax.dot_general(a, b, (((1,), (1,)), ((), ())), preferred_element_type=jnp.float32)


def pack_kernel(query_ref, rope_ref, latent_ref, key_rope_ref, pos_ref, q_ref, key_ref):
    q_ref[:, : HG * NOPE] = query_ref[...]
    q_ref[:, HG * NOPE :] = rope_ref[...]
    key_ref[:, :RANK] = latent_ref[...]
    key_ref[:, RANK : RANK + ROPE] = key_rope_ref[...]
    keys = latent_ref.shape[0]
    pos = jnp.transpose(jnp.broadcast_to(pos_ref[...], (128, keys)).astype(jnp.float32))
    high = jnp.floor(pos * (1 / 128))
    lane = lax.broadcasted_iota(jnp.int32, (keys, 128), 1)
    ext = jnp.where(lane == ROPE, high, jnp.where(lane == ROPE + 1, pos - high * 128, 0.0))
    key_ref[:, RANK + ROPE :] = ext[:, ROPE:].astype(jnp.bfloat16)


def pack(query, q_rope, latent, k_rope, key_pos):
    return call(
        pack_kernel,
        (
            jax.ShapeDtypeStruct((R, HG * (NOPE + ROPE)), jnp.bfloat16),
            jax.ShapeDtypeStruct((latent.shape[0], KEYW), jnp.bfloat16),
        ),
        MIB,
        MIB,
    )(query, q_rope, latent, k_rope, key_pos)


def absorb_kernel(q_ref, w_ref, out_ref):
    lane = lax.broadcasted_iota(jnp.int32, (ROWS, 128), 1)
    row = lax.broadcasted_iota(jnp.int32, (ROWS, 128), 0)
    one_hot = (lane == row).astype(jnp.bfloat16)
    for h in range(HG):
        rows = slice(h * ROWS, (h + 1) * ROWS)
        latent = jnp.dot(
            q_ref[:, h * NOPE : (h + 1) * NOPE], w_ref[h], preferred_element_type=jnp.float32
        )
        out_ref[rows, :RANK] = latent.astype(jnp.bfloat16)
        start = HG * NOPE + (h // 2) * 128
        pair = q_ref[:, start : start + 128].astype(jnp.float32)
        if h % 2:
            pair = pltpu.roll(pair, ROPE, 1)
        rope = jnp.where(lane < ROPE, pair, 0.0)
        out_ref[rows, RANK : RANK + 128] = rope.astype(jnp.bfloat16)
        out_ref[rows, RANK + 128 :] = one_hot


def absorb(q, w_uk):
    return call(
        absorb_kernel,
        jax.ShapeDtypeStruct((ITEMS, ITEMW), jnp.bfloat16),
        2 * ITEMS * NOPE * RANK,
        6 * MIB,
    )(q, w_uk)


def pack_stats(stats):
    high = stats.astype(jnp.bfloat16).astype(jnp.float32)
    mid = (stats - high).astype(jnp.bfloat16).astype(jnp.float32)
    low = stats - high - mid
    packed = high + pltpu.roll(mid, HG, 1) + pltpu.roll(low, 2 * HG, 1)
    return packed.astype(jnp.bfloat16)


def unpack_stats(packed):
    packed = packed.astype(jnp.float32)
    return packed + pltpu.roll(packed, 128 - HG, 1) + pltpu.roll(packed, 128 - 2 * HG, 1)


def attend_kernel(pieces, last, *refs):
    q_ref, qpos_ref = refs[:2]
    key_refs = refs[2 : 2 + pieces]
    rest = refs[2 + pieces :]
    if last:
        acc_in, st_in, v_ref, keep_ref, send_ref, ext_ref, lse_ref = rest
    else:
        acc_out, st_out, ext_ref = rest
    keys = key_refs[0].shape[0]
    step = pl.program_id(0)

    @pl.when(step == 0)
    def _():
        qpos = qpos_ref[0:1, :]
        for i, key_ref in enumerate(key_refs):
            ext = key_ref[:, RANK:]
            ext_ref[i, :, :128] = ext
            ext = ext.astype(jnp.float32)
            pos = ext[:, ROPE : ROPE + 1] * 128.0 + ext[:, ROPE + 1 : ROPE + 2]
            ext_ref[i, :, 128:] = jnp.where(pos <= qpos, 0.0, NEG).astype(jnp.bfloat16)
        if last:
            lse_ref[...] = jnp.zeros_like(lse_ref)

    tile = q_ref.shape[0]
    q_latent, q_ext = q_ref[:, :RANK], q_ref[:, RANK:]
    scores = [
        (nt_dot(q_latent, key_refs[i][:, :RANK]) + nt_dot(q_ext, ext_ref[i])) * SCALE2
        for i in range(pieces)
    ]
    top = functools.reduce(jnp.maximum, [jnp.max(s, axis=1, keepdims=True) for s in scores])
    if last:
        top = jnp.maximum(top, st_in[:, 0:1])
    weights = [jnp.exp2(s - top) for s in scores]
    total = sum(jnp.sum(w, axis=1, keepdims=True) for w in weights)
    acc = sum(
        jnp.dot(w.astype(jnp.bfloat16), key_refs[i][:, :RANK], preferred_element_type=jnp.float32)
        for i, w in enumerate(weights)
    )
    if not last:
        acc_out[...] = acc
        lane = lax.broadcasted_iota(jnp.int32, (tile, 128), 1)
        st_out[...] = jnp.where(lane == 0, top, total)
        return

    keep = jnp.exp2(st_in[:, 0:1] - top)
    total = total + keep * st_in[:, 1:2]
    context = ((acc + keep * acc_in[...]) / total).astype(jnp.bfloat16)
    lse = top + jnp.log2(total)
    half = ROWS // 2
    lane = lax.broadcasted_iota(jnp.int32, (ROWS, 128), 1)
    for i in range(tile // ROWS):
        rows = slice(i * ROWS, (i + 1) * ROWS)
        head = step * (tile // ROWS) + i
        out = jnp.dot(context[rows], v_ref[i], preferred_element_type=jnp.float32)
        out = out.astype(jnp.bfloat16)
        cols = pl.ds(pl.multiple_of(head * VDIM, VDIM), VDIM)
        keep_ref[:, cols] = out[:half]
        send_ref[:, cols] = out[half:]
        lse_ref[...] = jnp.where(lane == head, lse[rows], lse_ref[...])

    @pl.when(step == pl.num_programs(0) - 1)
    def _():
        packed = pack_stats(lse_ref[...])
        keep_ref[:, HG * VDIM :] = packed[:half]
        send_ref[:, HG * VDIM :] = packed[half:]


def attend(q, qpos, pieces, state=None, value_weight=None, tile=512):
    n, keys = len(pieces), pieces[0].shape[0]
    last = state is not None
    whole = lambda shape: pl.BlockSpec(shape, lambda i: (0, 0))
    part = lambda width: pl.BlockSpec((tile, width), lambda i: (i, 0))
    carried = [part(RANK), part(128)]
    in_specs = [part(ITEMW), whole((8, 128))] + [whole((keys, KEYW))] * n
    scratch = [pltpu.VMEM((n, keys, 256), jnp.bfloat16)]
    args = [q, qpos, *pieces]
    if last:
        heads = tile // ROWS
        in_specs += carried + [pl.BlockSpec((heads, RANK, VDIM), lambda i: (i, 0, 0))]
        args += [*state, value_weight]
        half = jax.ShapeDtypeStruct((ROWS // 2, SENDW), jnp.bfloat16)
        out_shape, out_specs = (half, half), [whole((ROWS // 2, SENDW))] * 2
        scratch.append(pltpu.VMEM((ROWS, 128), jnp.float32))
    else:
        out_shape = (
            jax.ShapeDtypeStruct((ITEMS, RANK), jnp.float32),
            jax.ShapeDtypeStruct((ITEMS, 128), jnp.float32),
        )
        out_specs = carried
    return call(
        functools.partial(attend_kernel, n, last),
        out_shape,
        2 * ITEMS * n * keys * (KEYW + RANK),
        (ITEMS * (ITEMW + RANK) + n * keys * KEYW) * 2,
        grid=(ITEMS // tile,),
        in_specs=in_specs,
        out_specs=out_specs,
        scratch_shapes=scratch,
    )(*args)


def merge(a_ref, b_ref):
    a, b = (unpack_stats(ref[:, HG * VDIM :]) for ref in (a_ref, b_ref))
    top = jnp.maximum(a, b)
    wa, wb = jnp.exp2(a - top), jnp.exp2(b - top)
    total = wa + wb
    wa, wb = wa / total, wb / total
    out = []
    for h in range(HG):
        cols = slice(h * VDIM, (h + 1) * VDIM)
        head = a_ref[:, cols].astype(jnp.float32) * wa[:, h : h + 1]
        head = head + b_ref[:, cols].astype(jnp.float32) * wb[:, h : h + 1]
        out.append((cols, head.astype(jnp.bfloat16)))
    return out, top + jnp.log2(total)


def merge_kernel(a_ref, b_ref, own_ref, send_ref):
    heads, lse = merge(a_ref, b_ref)
    half = own_ref.shape[0]
    lane = lax.broadcasted_iota(jnp.int32, lse.shape, 1)
    packed = pack_stats(jnp.where(lane < HG, lse, 0.0))
    for cols, head in heads + [(slice(HG * VDIM, SENDW), packed)]:
        own_ref[:, cols] = head[:half]
        send_ref[:, cols] = head[half:]


def merge_last_kernel(a_ref, b_ref, out_ref):
    heads, _ = merge(a_ref, b_ref)
    for cols, head in heads:
        for i in range(out_ref.shape[0]):
            out_ref[i, :, cols] = head


def merge_over(axis, own, send):
    half = jax.ShapeDtypeStruct((own.shape[0] // 2, SENDW), jnp.bfloat16)
    return call(merge_kernel, (half, half), MIB, MIB)(own, lax.ppermute(send, axis, SWAP))


def project_kernel(zc_ref, x_ref, *refs):
    out_ref = refs[-1]
    z, c = zc_ref[0], zc_ref[1]
    for k in range(4):
        to_z = z if k % 2 == 0 else 1 - z
        to_c = c if k < 2 else 1 - c
        out_ref[to_z * 2 + to_c] = jnp.dot(
            x_ref[...], refs[k][...], preferred_element_type=jnp.float32
        ).astype(jnp.bfloat16)


def local(query_unrotated, q_rope, latent, k_rope, key_pos, offset, w_uk, value_up_weight, w_out):
    y, u, x, z, c = (lax.axis_index(n) for n in CTX)

    q_own, keys = pack(query_unrotated, q_rope, latent[0], k_rope[0], key_pos)

    keys_u = lax.ppermute(keys, "u", SWAP)
    keys_up = lax.ppermute(keys, "y", shift(4, 1))
    keys_down = lax.ppermute(keys, "y", shift(4, 3))
    near = [jnp.concatenate([keys, keys_u]), jnp.concatenate([keys_up, keys_down])]
    far = [lax.ppermute(near[0], "y", shift(4, 2)), lax.ppermute(near[1], "u", SWAP)]

    q_z = lax.ppermute(q_own, "z", SWAP)
    q_all = jnp.concatenate([q_own, q_z])
    q_all = jnp.concatenate([q_all, lax.ppermute(q_all, "x", SWAP)])
    q_all = jnp.concatenate([q_all, lax.ppermute(q_all, "c", SWAP)])

    w_own, _ = lax.optimization_barrier((w_out, q_z))
    w_z = lax.ppermute(w_own, "z", SWAP)
    w_c = lax.ppermute(w_own, "c", SWAP)
    w_zc = lax.ppermute(w_z, "c", SWAP)

    row = jnp.arange(ROWS, dtype=jnp.int32)
    part = row // R
    row_z = jnp.where(part % 2 == 0, z, 1 - z)
    row_x = jnp.where(part // 2 % 2 == 0, x, 1 - x)
    row_c = jnp.where(part < 4, c, 1 - c)
    row = ((((y * 2 + u) * 2 + row_x) * 2 + row_z) * 2 + row_c) * R + row % R
    qpos = jnp.broadcast_to((offset[0] + row).astype(jnp.float32)[None, :], (8, ROWS))

    q = absorb(q_all, w_uk)
    state = attend(q, qpos, near)
    state, w_z = lax.optimization_barrier((state, w_z))
    own, send = attend(q, qpos, far, state, value_up_weight)
    own, send = merge_over("c", own, send)
    own, send = merge_over("x", own, send)
    heads = call(
        merge_last_kernel, jax.ShapeDtypeStruct((16, R, HG * VDIM), jnp.bfloat16), MIB, MIB
    )(own, lax.ppermute(send, "z", SWAP))

    rows = lax.all_to_all(heads, ("y", "u", "x"), 0, 0, tiled=True).reshape(16 * R, HG * VDIM)
    ncol = w_out.shape[1]
    sums = call(
        project_kernel,
        jax.ShapeDtypeStruct((4, 16 * R, ncol), jnp.bfloat16),
        2 * 16 * R * HG * VDIM * 4 * ncol,
        4 * MIB,
        in_specs=[pl.BlockSpec(memory_space=pltpu.SMEM)]
        + [pl.BlockSpec(memory_space=pltpu.VMEM)] * 5,
    )(jnp.stack([z, c]), rows, w_own, w_z, w_c, w_zc)
    sums = lax.all_to_all(
        sums.reshape(16, 4 * R, ncol), ("z", "c", "head"), 0, 0, tiled=True
    )
    total = jnp.sum(sums.reshape(4, 4, 4, R, ncol).astype(jnp.float32), axis=1)
    return jnp.transpose(total.astype(jnp.bfloat16), (1, 0, 2, 3)).reshape(16 * R, ncol)


def solution(mesh):
    grid = Mesh(mesh.devices.reshape(4, 2, 2, 2, 2, 4), CTX + ("head",))
    return jax.shard_map(
        local,
        mesh=grid,
        in_specs=(
            P(CTX, "head"),
            P(CTX, "head"),
            P(None, CTX, None),
            P(None, CTX, None),
            P(None, CTX),
            P(),
            P("head", None, None),
            P("head", None, None),
            P("head", CTX),
        ),
        out_specs=P("head", CTX),
        check_vma=False,
    )
```

time: 409 us -> 127 us (0.31); the launches traced: 403 us -> 127 us
  waiting for transfers between devices: 210 us -> 32 us
  blocking collectives: 124 us -> 22 us
  matrix products: 44.7 us -> 0 us
  starting transfers between devices: 0.12 us -> 41 us
  Pallas kernels: 0 us -> 23.2 us
  between operations: 13.8 us -> 0.84 us
  other arithmetic: 9.2 us -> 0.25 us
  local copies, waits for them, and re-layouts: 1.84 us -> 7.21 us
    all_gather x3 -> x0, waiting for transfers between devices: 194 us -> none  [the longest x1 86.8 us: local(): lax.all_gather(per_head_output, 'ctx', axis=0, tiled=True)]
    all_gather x1 -> x0, blocking collectives: 124 us -> none  [local(): all_pos = lax.all_gather(key_pos, 'ctx', axis=1, tiled=True)]
    dot_general x6 -> x0, matrix products: 44.7 us -> none  [the longest x1 15.2 us: fold_attention(): jnp.einsum('gnj,gjk->gnk', weights_low, piece_latent, preferred_element_t...]
    ppermute x0 -> x14, starting transfers between devices: none -> 36.1 us  [the longest x1 6.16 us: local(): w_z = lax.ppermute(w_own, 'z', SWAP)]
    pallas_call x0 -> x8, Pallas kernels: none -> 23.2 us  [the longest x2 18.3 us: attend(): call(functools.partial(attend_kernel, n, last), out_shape, 2 * ITEMS * n...]
    all_to_all x0 -> x1, blocking collectives: none -> 22 us  [local(): lax.all_to_all(sums.reshape(16, 4 * R, ncol), ('z', 'c', 'head'), 0, 0, t...]
    ppermute x0 -> x14, waiting for transfers between devices: none -> 21.8 us  [the longest x1 8.31 us: local(): w_z = lax.ppermute(w_own, 'z', SWAP)]
    reduce_scatter x1 -> x0, waiting for transfers between devices: 14.6 us -> none  [local(): lax.psum_scatter(partial_weighted_sums.astype(jnp.bfloat16), 'head', scat...]
  transfers between devices with their start and end apart: 4 -> 15, of which waited for: 4 -> 8; matrix products, arithmetic and copies ran while one was open for 3% -> 2% of each run, Pallas kernels for 0% -> 7%
where the time goes in v2:
time: 127 us
  starting transfers between devices  41 us (32%)
  waiting for transfers between devices  32 us (25%)
  Pallas kernels  23.2 us (18%)
  blocking collectives  22 us (17%)
  local copies, waits for them, and re-layouts  7.21 us (6%)
    all_to_all x1, blocking collectives, local(): lax.all_to_all(sums.reshape(16, 4 * R, ncol), ('z', 'c', 'head'), 0, 0, t...  22 us
    pallas_call x2, Pallas kernels, attend(): call(functools.partial(attend_kernel, n, last), out_shape, 2 * ITEMS * n...  18.3 us
    all_to_all x1, waiting for transfers between devices, local(): lax.all_to_all(heads, ('y', 'u', 'x'), 0, 0, tiled=True)  10.3 us
    ppermute x1, waiting for transfers between devices, local(): w_z = lax.ppermute(w_own, 'z', SWAP)  8.31 us
    ppermute x1, starting transfers between devices, local(): w_z = lax.ppermute(w_own, 'z', SWAP)  6.16 us
    ppermute x1, starting transfers between devices, local(): q_z = lax.ppermute(q_own, 'z', SWAP)  6.1 us
    ppermute x2, waiting for transfers between devices, merge_over(): lax.ppermute(send, axis, SWAP)  5.65 us
    ppermute x1, starting transfers between devices, local(): lax.ppermute(send, 'z', SWAP)  5.19 us
  transfers between devices with their start and end apart: 15, of which 8 were waited for; matrix products, arithmetic and copies ran while one was open for 2% of the time, Pallas kernels for 7%

profile of v2, /device:TPU:33, one launch (start us, length us, event | category | flops | bytes accessed | tf_op | source)
XLA Modules:
  0.0 126.6 jit_solution(17043978719734169347)
XLA Ops:
  0.0 0.9 copy.19
  0.9 0.0 copy-start.1
  0.9 0.9 copy-done.1
  1.8 0.8 copy-done.2
  2.7 0.8 copy-done.3
  3.4 0.7 copy-done.4
  4.1 0.1 shard_map.91
  4.2 6.1 %collective-permute-start = (bf16[16,3072]{1,0:T(8,128)(2,1)S(1)}, bf16[16,3072]{1,0:T(8,128)(2,1)S(1)}, u32[]{:S(2)}, u32[]{:S(2)}) collective-permute-start(bf16[16,3072]{1,0:T(8,128)(2,1)S(1)} %get-tuple-element.19), channel_id=1, source_target_pairs={{0,8},{8,0},{1,9},{9,1},{2,10},{10,2},{3,11},{11,3},{4,12},{12,4},... | collective-permute-start | bytes 294920 | tf_op jit(solution)/shard_map/ppermute | solution.py:273
  10.3 2.5 %collective-permute-done = bf16[16,3072]{1,0:T(8,128)(2,1)S(1)} collective-permute-done((bf16[16,3072]{1,0:T(8,128)(2,1)S(1)}, bf16[16,3072]{1,0:T(8,128)(2,1)S(1)}, u32[]{:S(2)}, u32[]{:S(2)}) %collective-permute-start) | collective-permute-done | bytes 98336 | tf_op jit(solution)/shard_map/ppermute | solution.py:273
  12.9 1.3 %collective-permute-start.1 = (bf16[32,3072]{1,0:T(8,128)(2,1)S(1)}, bf16[32,3072]{1,0:T(8,128)(2,1)S(1)}, u32[]{:S(2)}, u32[]{:S(2)}) collective-permute-start(bf16[32,3072]{1,0:T(8,128)(2,1)S(1)} %pad_maximum_fusion.2), channel_id=1, source_target_pairs={{0,16},{16,0},{1,17},{17,1},{2,18},{18,2},{3,19},{19,3},{4,20},{20... | collective-permute-start | bytes 589832 | tf_op jit(solution)/shard_map/ppermute | solution.py:275
  14.2 2.5 %collective-permute-start.3 = (bf16[256,640]{1,0:T(8,128)(2,1)S(1)}, bf16[256,640]{1,0:T(8,128)(2,1)}, u32[]{:S(2)}, u32[]{:S(2)}) collective-permute-start(bf16[256,640]{1,0:T(8,128)(2,1)S(1)} %get-tuple-element.20), channel_id=1, source_target_pairs={{0,32},{32,0},{1,33},{33,1},{2,34},{34,2},{3,35},{35,3},{4,36},{36... | collective-permute-start | bytes 983048 | tf_op jit(solution)/shard_map/ppermute | solution.py:267
  16.6 1.3 %collective-permute-start.5 = (bf16[256,640]{1,0:T(8,128)(2,1)S(1)}, bf16[256,640]{1,0:T(8,128)(2,1)}, u32[]{:S(2)}, u32[]{:S(2)}) collective-permute-start(bf16[256,640]{1,0:T(8,128)(2,1)S(1)} %get-tuple-element.20), channel_id=1, source_target_pairs={{0,64},{64,128},{128,192},{192,0},{1,65},{65,129},{129,193},{193,1... | collective-permute-start | bytes 983048 | tf_op jit(solution)/shard_map/ppermute | solution.py:268
  17.9 1.4 %collective-permute-start.6 = (bf16[256,640]{1,0:T(8,128)(2,1)S(1)}, bf16[256,640]{1,0:T(8,128)(2,1)S(1)}, u32[]{:S(2)}, u32[]{:S(2)}) collective-permute-start(bf16[256,640]{1,0:T(8,128)(2,1)S(1)} %get-tuple-element.20), channel_id=1, source_target_pairs={{0,192},{64,0},{128,64},{192,128},{1,193},{65,1},{129,65},{193,129... | collective-permute-start | bytes 983048 | tf_op jit(solution)/shard_map/ppermute | solution.py:269
  20.0 0.0 collective-permute-done.1
  20.1 3.8 %collective-permute-start.2 = (bf16[64,3072]{1,0:T(8,128)(2,1)S(1)}, bf16[64,3072]{1,0:T(8,128)(2,1)S(1)}, u32[]{:S(2)}, u32[]{:S(2)}) collective-permute-start(bf16[64,3072]{1,0:T(8,128)(2,1)S(1)} %pad_maximum_fusion.1), channel_id=1, source_target_pairs={{0,4},{4,0},{1,5},{5,1},{2,6},{6,2},{3,7},{7,3},{8,12},{12,8},{9,1... | collective-permute-start | bytes 1179656 | tf_op jit(solution)/shard_map/ppermute | solution.py:276
  23.9 0.3 copy.20.refs_0_
  24.2 6.2 %collective-permute-start.8 = (bf16[2048,112]{1,0:T(8,128)(2,1)S(1)}, bf16[2048,112]{1,0:T(8,128)(2,1)S(1)}, u32[]{:S(2)}, u32[]{:S(2)}) collective-permute-start(bf16[2048,112]{1,0:T(8,128)(2,1)S(1)} %copy.20.refs_0_), channel_id=1, source_target_pairs={{0,8},{8,0},{1,9},{9,1},{2,10},{10,2},{3,11},{11,3},{4,12},{12,4},... | collective-permute-start | bytes 1376264 | tf_op jit(solution)/shard_map/ppermute | solution.py:279
  30.4 1.0 constant_dynamic-update-slice_fusion.refs_2_
  31.4 0.0 copy-start
  31.4 1.8 %collective-permute-start.4 = (bf16[512,640]{1,0:T(8,128)(2,1)S(1)}, bf16[512,640]{1,0:T(8,128)(2,1)S(1)}, u32[]{:S(2)}, u32[]{:S(2)}) collective-permute-start(bf16[512,640]{1,0:T(8,128)(2,1)S(1)} %constant_dynamic-update-slice_fusion.refs_2_), channel_id=1, source_target_pairs={{0,128},{64,192},{128,0},{192,64},{1,129},{65,193},{129,1},{193,65... | collective-permute-start | bytes 1966088 | tf_op jit(solution)/shard_map/ppermute | solution.py:271
  33.2 1.0 constant_dynamic-update-slice_fusion.3
  34.3 2.8 %collective-permute-start.7 = (bf16[512,640]{1,0:T(8,128)(2,1)S(1)}, bf16[512,640]{1,0:T(8,128)(2,1)S(1)}, u32[]{:S(2)}, u32[]{:S(2)}) collective-permute-start(bf16[512,640]{1,0:T(8,128)(2,1)S(1)} %constant_dynamic-update-slice_fusion.2.refs_3_), channel_id=1, source_target_pairs={{0,32},{32,0},{1,33},{33,1},{2,34},{34,2},{3,35},{35,3},{4,36},{36... | collective-permute-start | bytes 1966088 | tf_op jit(solution)/shard_map/ppermute | solution.py:271
  37.1 0.1 pad_maximum_fusion.q_ref
  37.2 0.8 shard_map.92.refs_0_
  38.0 0.0 copy-start.5
  38.0 7.7 %shard_map.93 = (f32[2048,512]{1,0:T(8,128)S(1)}, f32[2048,128]{1,0:T(8,128)S(1)}) custom-call(bf16[2048,768]{1,0:T(8,128)(2,1)S(1)} %shard_map.92.refs_0_, f32[8,128]{1,0:T(8,128)S(1)} %broadcast_in_dim.32.refs_1_, bf16[512,640]{1,0:T(8,128)(2,1)S(1)} %constant_dynamic-update-slice_fusion.refs_2_, ...), custom_call_target="tpu_custom_call" | custom-call | flops 4831838208 | bytes 6553600 | tf_op jit(solution)/shard_map/pallas_call | solution.py:202
  45.8 8.3 %collective-permute-done.8.refs_1_ = bf16[2048,112]{1,0:T(8,128)(2,1)S(1)} collective-permute-done((bf16[2048,112]{1,0:T(8,128)(2,1)S(1)}, bf16[2048,112]{1,0:T(8,128)(2,1)S(1)}, u32[]{:S(2)}, u32[]{:S(2)}) %collective-permute-start.8) | collective-permute-done | bytes 458784 | tf_op jit(solution)/shard_map/ppermute | solution.py:279
  54.1 10.5 %shard_map.94 = (bf16[64,2176]{1,0:T(8,128)(2,1)S(1)}, bf16[64,2176]{1,0:T(8,128)(2,1)S(1)}) custom-call(bf16[2048,768]{1,0:T(8,128)(2,1)S(1)} %shard_map.92.refs_0_, f32[8,128]{1,0:T(8,128)S(1)} %broadcast_in_dim.32.refs_1_, bf16[512,640]{1,0:T(8,128)(2,1)S(1)} %collective-permute-done.4.refs_2_, bf16[512,640]{1,0:T(8,128)(2,1)S(1)} %collective-permute-done.7.refs_3_, ...), custom_call_target="tpu_custom_call" | custom-call | flops 4831838208 | bytes 6553600 | tf_op jit(solution)/shard_map/pallas_call | solution.py:202
  64.6 0.6 collective-permute-start.9
  65.2 1.2 collective-permute-done.9.b_ref
  66.4 0.5 shard_map.95
  66.9 0.7 collective-permute-start.10
  67.6 4.5 %collective-permute-done.10.b_ref = bf16[32,2176]{1,0:T(8,128)(2,1)S(1)} collective-permute-done((bf16[32,2176]{1,0:T(8,128)(2,1)S(1)}, bf16[32,2176]{1,0:T(8,128)(2,1)S(1)}, u32[]{:S(2)}, u32[]{:S(2)}) %collective-permute-start.10) | collective-permute-done | bytes 139296 | tf_op jit(solution)/shard_map/ppermute | solution.py:248
  72.0 0.3 shard_map.96
  72.3 5.2 %collective-permute-start.11 = (bf16[16,2176]{1,0:T(8,128)(2,1)S(1)}, bf16[16,2176]{1,0:T(8,128)(2,1)S(1)}, u32[]{:S(2)}, u32[]{:S(2)}) collective-permute-start(bf16[16,2176]{1,0:T(8,128)(2,1)S(1)} %get-tuple-element.31), channel_id=1, source_target_pairs={{0,8},{8,0},{1,9},{9,1},{2,10},{10,2},{3,11},{11,3},{4,12},{12,4},... | collective-permute-start | bytes 208904 | tf_op jit(solution)/shard_map/ppermute | solution.py:299
  77.5 3.2 %collective-permute-done.11.b_ref = bf16[16,2176]{1,0:T(8,128)(2,1)S(1)} collective-permute-done((bf16[16,2176]{1,0:T(8,128)(2,1)S(1)}, bf16[16,2176]{1,0:T(8,128)(2,1)S(1)}, u32[]{:S(2)}, u32[]{:S(2)}) %collective-permute-start.11) | collective-permute-done | bytes 69664 | tf_op jit(solution)/shard_map/ppermute | solution.py:299
  80.7 1.4 %shard_map.97 = bf16[16,16,2048]{2,1,0:T(8,128)(2,1)} custom-call(bf16[16,2176]{1,0:T(8,128)(2,1)S(1)} %get-tuple-element.30.a_ref, bf16[16,2176]{1,0:T(8,128)(2,1)S(1)} %collective-permute-done.11.b_ref), custom_call_target="tpu_custom_call" | custom-call | flops 1048576 | bytes 1048576 | tf_op jit(solution)/shard_map/pallas_call | solution.py:297
  82.1 4.9 %all-to-all-start = ((bf16[16,16,2048]{2,1,0:T(8,128)(2,1)}), bf16[16,16,2048]{2,1,0:T(8,128)(2,1)S(1)}, u32[]{:S(2)}, u32[]{:S(2)}) async-start(bf16[16,16,2048]{2,1,0:T(8,128)(2,1)} %shard_map.97), calls=%async_computation | async-start | bytes 2097152 | tf_op jit(solution)/shard_map/all_to_all | solution.py:301
  87.0 2.4 %collective-permute-start.12 = (bf16[2048,112]{1,0:T(8,128)(2,1)S(1)}, bf16[2048,112]{1,0:T(8,128)(2,1)S(1)}, u32[]{:S(2)}, u32[]{:S(2)}) collective-permute-start(bf16[2048,112]{1,0:T(8,128)(2,1)S(1)} %copy.20.refs_0_), channel_id=1, source_target_pairs={{0,4},{4,0},{1,5},{5,1},{2,6},{6,2},{3,7},{7,3},{8,12},{12,8},{9,1... | collective-permute-start | bytes 1376264 | tf_op jit(solution)/shard_map/ppermute | solution.py:280
  89.4 0.1 collective-permute-start.13
  89.5 0.1 pad_add_fusion.zc_ref
  89.6 1.4 %collective-permute-done.12.refs_2_ = bf16[2048,112]{1,0:T(8,128)(2,1)S(1)} collective-permute-done((bf16[2048,112]{1,0:T(8,128)(2,1)S(1)}, bf16[2048,112]{1,0:T(8,128)(2,1)S(1)}, u32[]{:S(2)}, u32[]{:S(2)}) %collective-permute-start.12) | collective-permute-done | bytes 458784 | tf_op jit(solution)/shard_map/ppermute | solution.py:280
  90.9 0.7 collective-permute-done.13.refs_3_
  91.7 10.3 %all-to-all-done = bf16[16,16,2048]{2,1,0:T(8,128)(2,1)S(1)} async-done(((bf16[16,16,2048]{2,1,0:T(8,128)(2,1)}), bf16[16,16,2048]{2,1,0:T(8,128)(2,1)S(1)}, u32[]{:S(2)}, u32[]{:S(2)}) %all-to-all-start) | async-done | bytes 1048608 | tf_op jit(solution)/shard_map/all_to_all | solution.py:301
  102.0 1.8 %shard_map.98 = bf16[4,256,112]{2,1,0:T(8,128)(2,1)S(1)} custom-call(s32[2]{0:T(128)S(1)} %pad_add_fusion.zc_ref, bf16[256,2048]{1,0:T(8,128)(2,1)S(1)} %bitcast.11, bf16[2048,112]{1,0:T(8,128)(2,1)S(1)} %copy.20.refs_0_, bf16[2048,112]{1,0:T(8,128)(2,1)S(1)} %collective-permute-done.8.refs_1_, bf16[2048,112]{1,0:T(8,128)(2,1)S(1)} %collective-permute-done.12.refs_2_, ...), custom_call_target="tpu_custom_call" | custom-call | flops 469762048 | bytes 4194304 | tf_op jit(solution)/shard_map/pallas_call | solution.py:303
  103.8 22.0 %all_to_all.10 = bf16[16,64,112]{2,1,0:T(8,128)(2,1)S(1)} all-to-all(bf16[16,64,112]{2,1,0:T(8,128)(2,1)S(1)} %bitcast.12), channel_id=1, replica_groups=mesh['y'=4,'u'=2,'x'=2,'z'=2,'c'=2,'head'=4] {'z','c','head'}, dimensions={0} | all-to-all | bytes 458752 | tf_op jit(solution)/shard_map/all_to_all | solution.py:311
  125.8 0.1 reduce_sum.12
  125.8 0.7 copy.24
  (20 shorter events, 0.2 us)
Async XLA Ops:
  0.9 1.0 copy-start.1
  1.8 0.8 copy-start.2
  2.7 0.8 copy-start.3
  3.4 0.7 copy-start.4
  4.1 19.8 %copy-start.6 = (bf16[2048,112]{0,1:T(8,128)(2,1)S(1)}, bf16[2048,112]{0,1:T(8,128)(2,1)}, u32[]{:S(2)}) copy-start(bf16[2048,112]{0,1:T(8,128)(2,1)} %param.17) | copy-start | bytes 1376260
  4.2 8.6 %collective-permute-start = (bf16[16,3072]{1,0:T(8,128)(2,1)S(1)}, bf16[16,3072]{1,0:T(8,128)(2,1)S(1)}, u32[]{:S(2)}, u32[]{:S(2)}) collective-permute-start(bf16[16,3072]{1,0:T(8,128)(2,1)S(1)} %get-tuple-element.19), channel_id=1, source_target_pairs={{0,8},{8,0},{1,9},{9,1},{2,10},{10,2},{3,11},{11,3},{4,12},{12,4},... | collective-permute-start | bytes 294920 | tf_op jit(solution)/shard_map/ppermute | solution.py:273
  12.9 7.2 %collective-permute-start.1 = (bf16[32,3072]{1,0:T(8,128)(2,1)S(1)}, bf16[32,3072]{1,0:T(8,128)(2,1)S(1)}, u32[]{:S(2)}, u32[]{:S(2)}) collective-permute-start(bf16[32,3072]{1,0:T(8,128)(2,1)S(1)} %pad_maximum_fusion.2), channel_id=1, source_target_pairs={{0,16},{16,0},{1,17},{17,1},{2,18},{18,2},{3,19},{19,3},{4,20},{20... | collective-permute-start | bytes 589832 | tf_op jit(solution)/shard_map/ppermute | solution.py:275
  14.2 16.2 %collective-permute-start.3 = (bf16[256,640]{1,0:T(8,128)(2,1)S(1)}, bf16[256,640]{1,0:T(8,128)(2,1)}, u32[]{:S(2)}, u32[]{:S(2)}) collective-permute-start(bf16[256,640]{1,0:T(8,128)(2,1)S(1)} %get-tuple-element.20), channel_id=1, source_target_pairs={{0,32},{32,0},{1,33},{33,1},{2,34},{34,2},{3,35},{35,3},{4,36},{36... | collective-permute-start | bytes 983048 | tf_op jit(solution)/shard_map/ppermute | solution.py:267
  16.6 16.6 %collective-permute-start.5 = (bf16[256,640]{1,0:T(8,128)(2,1)S(1)}, bf16[256,640]{1,0:T(8,128)(2,1)}, u32[]{:S(2)}, u32[]{:S(2)}) collective-permute-start(bf16[256,640]{1,0:T(8,128)(2,1)S(1)} %get-tuple-element.20), channel_id=1, source_target_pairs={{0,64},{64,128},{128,192},{192,0},{1,65},{65,129},{129,193},{193,1... | collective-permute-start | bytes 983048 | tf_op jit(solution)/shard_map/ppermute | solution.py:268
  17.9 16.3 %collective-permute-start.6 = (bf16[256,640]{1,0:T(8,128)(2,1)S(1)}, bf16[256,640]{1,0:T(8,128)(2,1)S(1)}, u32[]{:S(2)}, u32[]{:S(2)}) collective-permute-start(bf16[256,640]{1,0:T(8,128)(2,1)S(1)} %get-tuple-element.20), channel_id=1, source_target_pairs={{0,192},{64,0},{128,64},{192,128},{1,193},{65,1},{129,65},{193,129... | collective-permute-start | bytes 983048 | tf_op jit(solution)/shard_map/ppermute | solution.py:269
  20.1 17.0 %collective-permute-start.2 = (bf16[64,3072]{1,0:T(8,128)(2,1)S(1)}, bf16[64,3072]{1,0:T(8,128)(2,1)S(1)}, u32[]{:S(2)}, u32[]{:S(2)}) collective-permute-start(bf16[64,3072]{1,0:T(8,128)(2,1)S(1)} %pad_maximum_fusion.1), channel_id=1, source_target_pairs={{0,4},{4,0},{1,5},{5,1},{2,6},{6,2},{3,7},{7,3},{8,12},{12,8},{9,1... | collective-permute-start | bytes 1179656 | tf_op jit(solution)/shard_map/ppermute | solution.py:276
  24.2 29.8 %collective-permute-start.8 = (bf16[2048,112]{1,0:T(8,128)(2,1)S(1)}, bf16[2048,112]{1,0:T(8,128)(2,1)S(1)}, u32[]{:S(2)}, u32[]{:S(2)}) collective-permute-start(bf16[2048,112]{1,0:T(8,128)(2,1)S(1)} %copy.20.refs_0_), channel_id=1, source_target_pairs={{0,8},{8,0},{1,9},{9,1},{2,10},{10,2},{3,11},{11,3},{4,12},{12,4},... | collective-permute-start | bytes 1376264 | tf_op jit(solution)/shard_map/ppermute | solution.py:279
  31.4 5.7 %copy-start = (bf16[16,128,512]{2,1,0:T(8,128)(2,1)S(1)}, bf16[16,128,512]{2,1,0:T(8,128)(2,1)}, u32[]{:S(2)}) copy-start(bf16[16,128,512]{2,1,0:T(8,128)(2,1)} %w_ref.1) | copy-start | bytes 6291460
  31.4 22.6 %collective-permute-start.4 = (bf16[512,640]{1,0:T(8,128)(2,1)S(1)}, bf16[512,640]{1,0:T(8,128)(2,1)S(1)}, u32[]{:S(2)}, u32[]{:S(2)}) collective-permute-start(bf16[512,640]{1,0:T(8,128)(2,1)S(1)} %constant_dynamic-update-slice_fusion.refs_2_), channel_id=1, source_target_pairs={{0,128},{64,192},{128,0},{192,64},{1,129},{65,193},{129,1},{193,65... | collective-permute-start | bytes 1966088 | tf_op jit(solution)/shard_map/ppermute | solution.py:271
  34.3 19.8 %collective-permute-start.7 = (bf16[512,640]{1,0:T(8,128)(2,1)S(1)}, bf16[512,640]{1,0:T(8,128)(2,1)S(1)}, u32[]{:S(2)}, u32[]{:S(2)}) collective-permute-start(bf16[512,640]{1,0:T(8,128)(2,1)S(1)} %constant_dynamic-update-slice_fusion.2.refs_3_), channel_id=1, source_target_pairs={{0,32},{32,0},{1,33},{33,1},{2,34},{34,2},{3,35},{35,3},{4,36},{36... | collective-permute-start | bytes 1966088 | tf_op jit(solution)/shard_map/ppermute | solution.py:271
  38.0 16.1 %copy-start.5 = (bf16[16,512,128]{2,1,0:T(8,128)(2,1)S(1)}, bf16[16,512,128]{2,1,0:T(8,128)(2,1)}, u32[]{:S(2)}) copy-start(bf16[16,512,128]{2,1,0:T(8,128)(2,1)} %refs_6_.1) | copy-start | bytes 6291460
  64.6 1.7 %collective-permute-start.9 = (bf16[64,2176]{1,0:T(8,128)(2,1)S(1)}, bf16[64,2176]{1,0:T(8,128)(2,1)S(1)}, u32[]{:S(2)}, u32[]{:S(2)}) collective-permute-start(bf16[64,2176]{1,0:T(8,128)(2,1)S(1)} %get-tuple-element.27), channel_id=1, source_target_pairs={{0,4},{4,0},{1,5},{5,1},{2,6},{6,2},{3,7},{7,3},{8,12},{12,8},{9,1... | collective-permute-start | bytes 835592 | tf_op jit(solution)/shard_map/ppermute | solution.py:248
  66.9 5.2 %collective-permute-start.10 = (bf16[32,2176]{1,0:T(8,128)(2,1)S(1)}, bf16[32,2176]{1,0:T(8,128)(2,1)S(1)}, u32[]{:S(2)}, u32[]{:S(2)}) collective-permute-start(bf16[32,2176]{1,0:T(8,128)(2,1)S(1)} %get-tuple-element.29), channel_id=1, source_target_pairs={{0,16},{16,0},{1,17},{17,1},{2,18},{18,2},{3,19},{19,3},{4,20},{20... | collective-permute-start | bytes 417800 | tf_op jit(solution)/shard_map/ppermute | solution.py:248
  72.3 8.3 %collective-permute-start.11 = (bf16[16,2176]{1,0:T(8,128)(2,1)S(1)}, bf16[16,2176]{1,0:T(8,128)(2,1)S(1)}, u32[]{:S(2)}, u32[]{:S(2)}) collective-permute-start(bf16[16,2176]{1,0:T(8,128)(2,1)S(1)} %get-tuple-element.31), channel_id=1, source_target_pairs={{0,8},{8,0},{1,9},{9,1},{2,10},{10,2},{3,11},{11,3},{4,12},{12,4},... | collective-permute-start | bytes 208904 | tf_op jit(solution)/shard_map/ppermute | solution.py:299
  82.1 19.9 %all-to-all-start = ((bf16[16,16,2048]{2,1,0:T(8,128)(2,1)}), bf16[16,16,2048]{2,1,0:T(8,128)(2,1)S(1)}, u32[]{:S(2)}, u32[]{:S(2)}) async-start(bf16[16,16,2048]{2,1,0:T(8,128)(2,1)} %shard_map.97), calls=%async_computation | async-start | bytes 2097152 | tf_op jit(solution)/shard_map/all_to_all | solution.py:301
  87.0 4.0 %collective-permute-start.12 = (bf16[2048,112]{1,0:T(8,128)(2,1)S(1)}, bf16[2048,112]{1,0:T(8,128)(2,1)S(1)}, u32[]{:S(2)}, u32[]{:S(2)}) collective-permute-start(bf16[2048,112]{1,0:T(8,128)(2,1)S(1)} %copy.20.refs_0_), channel_id=1, source_target_pairs={{0,4},{4,0},{1,5},{5,1},{2,6},{6,2},{3,7},{7,3},{8,12},{12,8},{9,1... | collective-permute-start | bytes 1376264 | tf_op jit(solution)/shard_map/ppermute | solution.py:280
  89.4 2.3 %collective-permute-start.13 = (bf16[2048,112]{1,0:T(8,128)(2,1)S(1)}, bf16[2048,112]{1,0:T(8,128)(2,1)S(1)}, u32[]{:S(2)}, u32[]{:S(2)}) collective-permute-start(bf16[2048,112]{1,0:T(8,128)(2,1)S(1)} %collective-permute-done.8.refs_1_), channel_id=1, source_target_pairs={{0,4},{4,0},{1,5},{5,1},{2,6},{6,2},{3,7},{7,3},{8,12},{12,8},{9,1... | collective-permute-start | bytes 1376264 | tf_op jit(solution)/shard_map/ppermute | solution.py:281

commit v3 on v2

--- a/solution.py
+++ b/solution.py
@@ -45,16 +45,15 @@
 
 
 def pack_kernel(query_ref, rope_ref, latent_ref, key_rope_ref, pos_ref, q_ref, key_ref):
+    key_ref[:, :RANK] = latent_ref[...]
+    pos = pos_ref[...].astype(jnp.float32)
+    high = jnp.floor(pos * (1 / 128))
+    row = lax.broadcasted_iota(jnp.int32, key_rope_ref.shape, 0)
+    ext = jnp.where(row == 0, high, jnp.where(row == 1, pos - high * 128, 0.0))
+    ext = jnp.concatenate([key_rope_ref[...].astype(jnp.float32), ext], axis=0)
+    key_ref[:, RANK:] = jnp.transpose(ext).astype(jnp.bfloat16)
     q_ref[:, : HG * NOPE] = query_ref[...]
     q_ref[:, HG * NOPE :] = rope_ref[...]
-    key_ref[:, :RANK] = latent_ref[...]
-    key_ref[:, RANK : RANK + ROPE] = key_rope_ref[...]
-    keys = latent_ref.shape[0]
-    pos = jnp.transpose(jnp.broadcast_to(pos_ref[...], (128, keys)).astype(jnp.float32))
-    high = jnp.floor(pos * (1 / 128))
-    lane = lax.broadcasted_iota(jnp.int32, (keys, 128), 1)
-    ext = jnp.where(lane == ROPE, high, jnp.where(lane == ROPE + 1, pos - high * 128, 0.0))
-    key_ref[:, RANK + ROPE :] = ext[:, ROPE:].astype(jnp.bfloat16)
 
 
 def pack(query, q_rope, latent, k_rope, key_pos):
@@ -66,7 +65,8 @@
         ),
         MIB,
         MIB,
-    )(query, q_rope, latent, k_rope, key_pos)
+        vmem=60,
+    )(query, q_rope, latent, jnp.transpose(k_rope), key_pos)
 
 
 def absorb_kernel(q_ref, w_ref, out_ref):
@@ -254,9 +254,18 @@
     for k in range(4):
         to_z = z if k % 2 == 0 else 1 - z
         to_c = c if k < 2 else 1 - c
-        out_ref[to_z * 2 + to_c] = jnp.dot(
-            x_ref[...], refs[k][...], preferred_element_type=jnp.float32
-        ).astype(jnp.bfloat16)
+        out_ref[to_z * 2 + to_c] = nt_dot(x_ref[...], refs[k][...]).astype(jnp.bfloat16)
+
+
+def finish_kernel(sums_ref, out_ref, row_ref):
+    ncol = sums_ref.shape[2]
+    row_ref[...] = jnp.zeros_like(row_ref)
+    for zc in range(4):
+        total = sum(sums_ref[zc * 4 + h].astype(jnp.float32) for h in range(4))
+        for i in range(4):
+            start = (i * 4 + zc) * R
+            row_ref[start : start + R, :ncol] = total[i * R : (i + 1) * R]
+    out_ref[...] = jnp.transpose(row_ref[...])[:ncol].astype(jnp.bfloat16)
 
 
 def local(query_unrotated, q_rope, latent, k_rope, key_pos, offset, w_uk, value_up_weight, w_out):
@@ -264,21 +273,24 @@
 
     q_own, keys = pack(query_unrotated, q_rope, latent[0], k_rope[0], key_pos)
 
-    keys_u = lax.ppermute(keys, "u", SWAP)
-    keys_up = lax.ppermute(keys, "y", shift(4, 1))
-    keys_down = lax.ppermute(keys, "y", shift(4, 3))
+    phase = (
+        lax.ppermute(keys, "u", SWAP),
+        lax.ppermute(keys, "y", shift(4, 1)),
+        lax.ppermute(keys, "y", shift(4, 3)),
+        lax.ppermute(q_own, "z", SWAP),
+        lax.ppermute(q_own, "x", SWAP),
+        lax.ppermute(q_own, ("x", "z"), [(i, 3 - i) for i in range(4)]),
+    )
+    keys_u, keys_up, keys_down, q_z, q_x, q_xz, w_own = lax.optimization_barrier(
+        phase + (jnp.transpose(w_out),)
+    )
+
     near = [jnp.concatenate([keys, keys_u]), jnp.concatenate([keys_up, keys_down])]
     far = [lax.ppermute(near[0], "y", shift(4, 2)), lax.ppermute(near[1], "u", SWAP)]
-
-    q_z = lax.ppermute(q_own, "z", SWAP)
-    q_all = jnp.concatenate([q_own, q_z])
-    q_all = jnp.concatenate([q_all, lax.ppermute(q_all, "x", SWAP)])
+    q_all = jnp.concatenate([q_own, q_z, q_x, q_xz])
     q_all = jnp.concatenate([q_all, lax.ppermute(q_all, "c", SWAP)])
-
-    w_own, _ = lax.optimization_barrier((w_out, q_z))
     w_z = lax.ppermute(w_own, "z", SWAP)
     w_c = lax.ppermute(w_own, "c", SWAP)
-    w_zc = lax.ppermute(w_z, "c", SWAP)
 
     row = jnp.arange(ROWS, dtype=jnp.int32)
     part = row // R
@@ -291,6 +303,8 @@
     q = absorb(q_all, w_uk)
     state = attend(q, qpos, near)
     state, w_z = lax.optimization_barrier((state, w_z))
+    w_zc = lax.ppermute(w_z, "c", SWAP)
+    state, far, w_c, w_zc = lax.optimization_barrier((state, far, w_c, w_zc))
     own, send = attend(q, qpos, far, state, value_up_weight)
     own, send = merge_over("c", own, send)
     own, send = merge_over("x", own, send)
@@ -311,8 +325,14 @@
     sums = lax.all_to_all(
         sums.reshape(16, 4 * R, ncol), ("z", "c", "head"), 0, 0, tiled=True
     )
-    total = jnp.sum(sums.reshape(4, 4, 4, R, ncol).astype(jnp.float32), axis=1)
-    return jnp.transpose(total.astype(jnp.bfloat16), (1, 0, 2, 3)).reshape(16 * R, ncol)
+    out = call(
+        finish_kernel,
+        jax.ShapeDtypeStruct((ncol, 16 * R), jnp.bfloat16),
+        MIB,
+        MIB,
+        scratch_shapes=[pltpu.VMEM((16 * R, 128), jnp.float32)],
+    )(sums)
+    return jnp.transpose(out)
 
 
 def solution(mesh):

time: 127 us -> 126 us (level)
  blocking collectives: 22 us -> 17.5 us
  waiting for transfers between devices: 32 us -> 35.8 us
  starting transfers between devices: 41 us -> 38.3 us
  Pallas kernels: 23.2 us -> 25.6 us
    ppermute x1, waiting for transfers between devices: 8.31 us -> 0.01 us  [local(): w_z = lax.ppermute(w_own, 'z', SWAP)]
    ppermute x1, starting transfers between devices: 5.19 us -> 0.09 us  [local(): lax.ppermute(send, 'z', SWAP)]
    ppermute x5 -> x6, starting transfers between devices: 12.6 us -> 17 us  [the longest x1 6.01 us: local(): lax.ppermute(q_own, 'z', SWAP)]
    all_to_all x1, blocking collectives: 22 us -> 17.5 us  [local(): lax.all_to_all(sums.reshape(16, 4 * R, ncol), ('z', 'c', 'head'), 0, 0, t...]
    all_to_all x1, waiting for transfers between devices: 10.3 us -> 14.5 us  [local(): lax.all_to_all(heads, ('y', 'u', 'x'), 0, 0, tiled=True)]
    ppermute x1, waiting for transfers between devices: 0.01 us -> 4.06 us  [local(): lax.ppermute(near[0], 'y', shift(4, 2))]
    ppermute x1, waiting for transfers between devices: 3.16 us -> 7.06 us  [local(): lax.ppermute(send, 'z', SWAP)]
    ppermute x1, starting transfers between devices: 3.83 us -> 0.1 us  [local(): q_all = jnp.concatenate([q_all, lax.ppermute(q_all, 'c', SWAP)])]
  transfers between devices with their start and end apart: 15 -> 16, of which waited for: 8 -> 7; matrix products, arithmetic and copies ran while one was open for 2% -> 5% of each run, Pallas kernels for 7% -> 7%
where the time goes in v3:
time: 126 us
  starting transfers between devices  38.3 us (30%)
  waiting for transfers between devices  35.8 us (28%)
  Pallas kernels  25.6 us (20%)
  blocking collectives  17.5 us (14%)
  local copies, waits for them, and re-layouts  6.52 us (5%)
    pallas_call x2, Pallas kernels, attend(): call(functools.partial(attend_kernel, n, last), out_shape, 2 * ITEMS * n...  18 us
    all_to_all x1, blocking collectives, local(): lax.all_to_all(sums.reshape(16, 4 * R, ncol), ('z', 'c', 'head'), 0, 0, t...  17.5 us
    all_to_all x1, waiting for transfers between devices, local(): lax.all_to_all(heads, ('y', 'u', 'x'), 0, 0, tiled=True)  14.5 us
    ppermute x1, waiting for transfers between devices, local(): lax.ppermute(send, 'z', SWAP)  7.06 us
    ppermute x1, starting transfers between devices, local(): w_c = lax.ppermute(w_own, 'c', SWAP)  6.1 us
    ppermute x1, starting transfers between devices, local(): lax.ppermute(q_own, 'z', SWAP)  6.01 us
    ppermute x2, waiting for transfers between devices, merge_over(): lax.ppermute(send, axis, SWAP)  5.8 us
    ppermute x1, starting transfers between devices, local(): lax.ppermute(q_own, ('x', 'z'), [(i, 3 - i) for i in range(4)])  5.24 us
  transfers between devices with their start and end apart: 16, of which 7 were waited for; matrix products, arithmetic and copies ran while one was open for 5% of the time, Pallas kernels for 7%

profile of v3, /device:TPU:33, one launch (start us, length us, event | category | flops | bytes accessed | tf_op | source)
XLA Modules:
  0.0 125.6 jit_solution(18370905134701607107)
XLA Ops:
  0.0 2.0 %shard_map.91 = (bf16[16,3072]{1,0:T(8,128)(2,1)}, bf16[256,640]{1,0:T(8,128)(2,1)}) custom-call(bf16[16,2048]{1,0:T(8,128)(2,1)} %query_ref.1, bf16[16,1024]{1,0:T(8,128)(2,1)} %rope_ref.1, bf16[256,512]{1,0:T(8,128)(2,1)} %bitcast.17, bf16[64,256]{1,0:T(8,128)(2,1)} %bitcast.18, s32[1,256]{1,0:T(1,128)} %pos_ref.1), custom_call_target="tpu_custom_call" | custom-call | flops 1048576 | bytes 1048576 | tf_op jit(solution)/shard_map/pallas_call | solution.py:60
  2.0 2.7 %collective-permute-start = (bf16[256,640]{1,0:T(8,128)(2,1)}, bf16[256,640]{1,0:T(8,128)(2,1)S(1)}, u32[]{:S(2)}, u32[]{:S(2)}) collective-permute-start(bf16[256,640]{1,0:T(8,128)(2,1)} %get-tuple-element.32), channel_id=1, source_target_pairs={{0,32},{32,0},{1,33},{33,1},{2,34},{34,2},{3,35},{35,3},{4,36},{36... | collective-permute-start | bytes 983048 | tf_op jit(solution)/shard_map/ppermute | solution.py:277
  4.7 1.3 %collective-permute-start.1 = (bf16[256,640]{1,0:T(8,128)(2,1)}, bf16[256,640]{1,0:T(8,128)(2,1)}, u32[]{:S(2)}, u32[]{:S(2)}) collective-permute-start(bf16[256,640]{1,0:T(8,128)(2,1)} %get-tuple-element.32), channel_id=1, source_target_pairs={{0,64},{64,128},{128,192},{192,0},{1,65},{65,129},{129,193},{193,1... | collective-permute-start | bytes 983048 | tf_op jit(solution)/shard_map/ppermute | solution.py:278
  6.0 1.4 %collective-permute-start.2 = (bf16[256,640]{1,0:T(8,128)(2,1)}, bf16[256,640]{1,0:T(8,128)(2,1)}, u32[]{:S(2)}, u32[]{:S(2)}) collective-permute-start(bf16[256,640]{1,0:T(8,128)(2,1)} %get-tuple-element.32), channel_id=1, source_target_pairs={{0,192},{64,0},{128,64},{192,128},{1,193},{65,1},{129,65},{193,129... | collective-permute-start | bytes 983048 | tf_op jit(solution)/shard_map/ppermute | solution.py:279
  7.5 6.0 %collective-permute-start.3 = (bf16[16,3072]{1,0:T(8,128)(2,1)}, bf16[16,3072]{1,0:T(8,128)(2,1)S(1)}, u32[]{:S(2)}, u32[]{:S(2)}) collective-permute-start(bf16[16,3072]{1,0:T(8,128)(2,1)} %get-tuple-element.31), channel_id=1, source_target_pairs={{0,8},{8,0},{1,9},{9,1},{2,10},{10,2},{3,11},{11,3},{4,12},{12,4},... | collective-permute-start | bytes 294920 | tf_op jit(solution)/shard_map/ppermute | solution.py:280
  13.5 0.3 collective-permute-start.4
  13.8 0.9 constant_dynamic-update-slice_fusion.4
  15.4 1.0 constant_dynamic-update-slice_fusion.6
  16.4 5.2 %collective-permute-start.5 = (bf16[16,3072]{1,0:T(8,128)(2,1)}, bf16[16,3072]{1,0:T(8,128)(2,1)S(1)}, u32[]{:S(2)}, u32[]{:S(2)}) collective-permute-start(bf16[16,3072]{1,0:T(8,128)(2,1)} %get-tuple-element.31), channel_id=1, source_target_pairs={{0,24},{8,16},{16,8},{24,0},{1,25},{9,17},{17,9},{25,1},{2,26},{10... | collective-permute-start | bytes 294920 | tf_op jit(solution)/shard_map/ppermute | solution.py:282
  21.7 3.3 %collective-permute-done.5 = bf16[16,3072]{1,0:T(8,128)(2,1)S(1)} collective-permute-done((bf16[16,3072]{1,0:T(8,128)(2,1)}, bf16[16,3072]{1,0:T(8,128)(2,1)S(1)}, u32[]{:S(2)}, u32[]{:S(2)}) %collective-permute-start.5) | collective-permute-done | bytes 98336 | tf_op jit(solution)/shard_map/ppermute | solution.py:282
  25.0 0.0 collective-permute-done
  25.0 0.0 collective-permute-done.2
  25.0 0.7 copy-done.5
  25.7 5.2 %collective-permute-start.7 = (bf16[112,2048]{1,0:T(8,128)(2,1)}, bf16[112,2048]{1,0:T(8,128)(2,1)S(1)}, u32[]{:S(2)}, u32[]{:S(2)}) collective-permute-start(bf16[112,2048]{1,0:T(8,128)(2,1)} %bitcast.14), channel_id=1, source_target_pairs={{0,8},{8,0},{1,9},{9,1},{2,10},{10,2},{3,11},{11,3},{4,12},{12,4},... | collective-permute-start | bytes 1376264 | tf_op jit(solution)/shard_map/ppermute | solution.py:292
  30.9 6.1 %collective-permute-start.10 = (bf16[112,2048]{1,0:T(8,128)(2,1)}, bf16[112,2048]{1,0:T(8,128)(2,1)S(1)}, u32[]{:S(2)}, u32[]{:S(2)}) collective-permute-start(bf16[112,2048]{1,0:T(8,128)(2,1)} %bitcast.15), channel_id=1, source_target_pairs={{0,4},{4,0},{1,5},{5,1},{2,6},{6,2},{3,7},{7,3},{8,12},{12,8},{9,1... | collective-permute-start | bytes 1376264 | tf_op jit(solution)/shard_map/ppermute | solution.py:293
  37.0 0.9 pad_maximum_fusion
  38.0 0.1 collective-permute-start.6
  38.1 1.0 constant_dynamic-update-slice_fusion.8
  39.1 1.0 constant_dynamic-update-slice_fusion.5.refs_2_
  40.1 0.1 collective-permute-start.8
  40.2 1.0 constant_dynamic-update-slice_fusion.7.refs_3_
  41.2 0.1 collective-permute-start.9
  41.3 0.0 collective-permute-done.6
  41.4 0.8 shard_map.92.refs_0_
  42.2 0.0 copy-start.4
  42.2 7.7 %shard_map.93 = (f32[2048,512]{1,0:T(8,128)S(1)}, f32[2048,128]{1,0:T(8,128)S(1)}) custom-call(bf16[2048,768]{1,0:T(8,128)(2,1)S(1)} %shard_map.92.refs_0_, f32[8,128]{1,0:T(8,128)S(1)} %broadcast_in_dim.32.refs_1_, bf16[512,640]{1,0:T(8,128)(2,1)S(1)} %constant_dynamic-update-slice_fusion.5.refs_2_, ...), custom_call_target="tpu_custom_call" | custom-call | flops 4831838208 | bytes 6553600 | tf_op jit(solution)/shard_map/pallas_call | solution.py:202
  50.0 2.7 %collective-permute-start.11 = (bf16[112,2048]{1,0:T(8,128)(2,1)S(1)}, bf16[112,2048]{1,0:T(8,128)(2,1)S(1)}, u32[]{:S(2)}, u32[]{:S(2)}) collective-permute-start(bf16[112,2048]{1,0:T(8,128)(2,1)S(1)} %collective-permute-done.7.refs_1_), channel_id=1, source_target_pairs={{0,4},{4,0},{1,5},{5,1},{2,6},{6,2},{3,7},{7,3},{8,12},{12,8},{9,1... | collective-permute-start | bytes 1376264 | tf_op jit(solution)/shard_map/ppermute | solution.py:306
  52.7 0.8 copy-done.2
  53.4 4.1 %collective-permute-done.8.refs_2_ = bf16[512,640]{1,0:T(8,128)(2,1)S(1)} collective-permute-done((bf16[512,640]{1,0:T(8,128)(2,1)S(1)}, bf16[512,640]{1,0:T(8,128)(2,1)S(1)}, u32[]{:S(2)}, u32[]{:S(2)}) %collective-permute-start.8) | collective-permute-done | bytes 655392 | tf_op jit(solution)/shard_map/ppermute | solution.py:289
  57.5 1.1 collective-permute-done.9.refs_3_
  58.6 0.0 collective-permute-done.11.refs_3_
  58.6 10.3 %shard_map.94 = (bf16[64,2176]{1,0:T(8,128)(2,1)S(1)}, bf16[64,2176]{1,0:T(8,128)(2,1)S(1)}) custom-call(bf16[2048,768]{1,0:T(8,128)(2,1)S(1)} %shard_map.92.refs_0_, f32[8,128]{1,0:T(8,128)S(1)} %broadcast_in_dim.32.refs_1_, bf16[512,640]{1,0:T(8,128)(2,1)S(1)} %collective-permute-done.8.refs_2_, bf16[512,640]{1,0:T(8,128)(2,1)S(1)} %collective-permute-done.9.refs_3_, ...), custom_call_target="tpu_custom_call" | custom-call | flops 4831838208 | bytes 6553600 | tf_op jit(solution)/shard_map/pallas_call | solution.py:202
  68.9 0.0 copy-start.1
  68.9 1.4 %collective-permute-start.12 = (bf16[64,2176]{1,0:T(8,128)(2,1)S(1)}, bf16[64,2176]{1,0:T(8,128)(2,1)S(1)}, u32[]{:S(2)}, u32[]{:S(2)}) collective-permute-start(bf16[64,2176]{1,0:T(8,128)(2,1)S(1)} %get-tuple-element.50), channel_id=1, source_target_pairs={{0,4},{4,0},{1,5},{5,1},{2,6},{6,2},{3,7},{7,3},{8,12},{12,8},{9,1... | collective-permute-start | bytes 835592 | tf_op jit(solution)/shard_map/ppermute | solution.py:248
  70.4 1.2 collective-permute-done.12.b_ref
  71.5 0.5 shard_map.95
  72.0 0.4 collective-permute-start.13
  72.4 4.6 %collective-permute-done.13.b_ref = bf16[32,2176]{1,0:T(8,128)(2,1)S(1)} collective-permute-done((bf16[32,2176]{1,0:T(8,128)(2,1)S(1)}, bf16[32,2176]{1,0:T(8,128)(2,1)S(1)}, u32[]{:S(2)}, u32[]{:S(2)}) %collective-permute-start.13) | collective-permute-done | bytes 139296 | tf_op jit(solution)/shard_map/ppermute | solution.py:248
  77.0 0.3 shard_map.96
  77.3 0.1 collective-permute-start.14
  77.4 7.1 %collective-permute-done.14.b_ref = bf16[16,2176]{1,0:T(8,128)(2,1)S(1)} collective-permute-done((bf16[16,2176]{1,0:T(8,128)(2,1)S(1)}, bf16[16,2176]{1,0:T(8,128)(2,1)S(1)}, u32[]{:S(2)}, u32[]{:S(2)}) %collective-permute-start.14) | collective-permute-done | bytes 69664 | tf_op jit(solution)/shard_map/ppermute | solution.py:313
  84.5 1.4 %shard_map.97 = bf16[16,16,2048]{2,1,0:T(8,128)(2,1)} custom-call(bf16[16,2176]{1,0:T(8,128)(2,1)S(1)} %get-tuple-element.53.a_ref, bf16[16,2176]{1,0:T(8,128)(2,1)S(1)} %collective-permute-done.14.b_ref), custom_call_target="tpu_custom_call" | custom-call | flops 1048576 | bytes 1048576 | tf_op jit(solution)/shard_map/pallas_call | solution.py:311
  85.9 5.1 %all-to-all-start = ((bf16[16,16,2048]{2,1,0:T(8,128)(2,1)}), bf16[16,16,2048]{2,1,0:T(8,128)(2,1)S(1)}, u32[]{:S(2)}, u32[]{:S(2)}) async-start(bf16[16,16,2048]{2,1,0:T(8,128)(2,1)} %shard_map.97), calls=%async_computation | async-start | bytes 2097152 | tf_op jit(solution)/shard_map/all_to_all | solution.py:315
  91.0 0.1 pad_add_fusion.zc_ref
  91.1 14.5 %all-to-all-done = bf16[16,16,2048]{2,1,0:T(8,128)(2,1)S(1)} async-done(((bf16[16,16,2048]{2,1,0:T(8,128)(2,1)}), bf16[16,16,2048]{2,1,0:T(8,128)(2,1)S(1)}, u32[]{:S(2)}, u32[]{:S(2)}) %all-to-all-start) | async-done | bytes 1048608 | tf_op jit(solution)/shard_map/all_to_all | solution.py:315
  105.6 1.8 %shard_map.98 = bf16[4,256,112]{2,1,0:T(8,128)(2,1)S(1)} custom-call(s32[2]{0:T(128)S(1)} %pad_add_fusion.zc_ref, bf16[256,2048]{1,0:T(8,128)(2,1)S(1)} %bitcast.12, bf16[112,2048]{1,0:T(8,128)(2,1)S(1)} %bitcast.16, bf16[112,2048]{1,0:T(8,128)(2,1)S(1)} %collective-permute-done.7.refs_1_, bf16[112,2048]{1,0:T(8,128)(2,1)S(1)} %copy-done.3, ...), custom_call_target="tpu_custom_call" | custom-call | flops 469762048 | bytes 4194304 | tf_op jit(solution)/shard_map/pallas_call | solution.py:317
  107.4 17.5 %all_to_all.10.sums_ref = bf16[16,64,112]{2,1,0:T(8,128)(2,1)S(1)} all-to-all(bf16[16,64,112]{2,1,0:T(8,128)(2,1)S(1)} %bitcast.13), channel_id=1, replica_groups=mesh['y'=4,'u'=2,'x'=2,'z'=2,'c'=2,'head'=4] {'z','c','head'}, dimensions={0} | all-to-all | bytes 458752 | tf_op jit(solution)/shard_map/all_to_all | solution.py:325
  124.9 0.7 shard_map.99
  (19 shorter events, 0.1 us)
Async XLA Ops:
  0.0 41.4 %copy-start = (bf16[16,128,512]{2,1,0:T(8,128)(2,1)S(1)}, bf16[16,128,512]{2,1,0:T(8,128)(2,1)}, u32[]{:S(2)}) copy-start(bf16[16,128,512]{2,1,0:T(8,128)(2,1)} %w_ref.1) | copy-start | bytes 6291460
  2.0 23.0 %collective-permute-start = (bf16[256,640]{1,0:T(8,128)(2,1)}, bf16[256,640]{1,0:T(8,128)(2,1)S(1)}, u32[]{:S(2)}, u32[]{:S(2)}) collective-permute-start(bf16[256,640]{1,0:T(8,128)(2,1)} %get-tuple-element.32), channel_id=1, source_target_pairs={{0,32},{32,0},{1,33},{33,1},{2,34},{34,2},{3,35},{35,3},{4,36},{36... | collective-permute-start | bytes 983048 | tf_op jit(solution)/shard_map/ppermute | solution.py:277
  4.7 20.3 %collective-permute-start.1 = (bf16[256,640]{1,0:T(8,128)(2,1)}, bf16[256,640]{1,0:T(8,128)(2,1)}, u32[]{:S(2)}, u32[]{:S(2)}) collective-permute-start(bf16[256,640]{1,0:T(8,128)(2,1)} %get-tuple-element.32), channel_id=1, source_target_pairs={{0,64},{64,128},{128,192},{192,0},{1,65},{65,129},{129,193},{193,1... | collective-permute-start | bytes 983048 | tf_op jit(solution)/shard_map/ppermute | solution.py:278
  6.0 19.0 %collective-permute-start.2 = (bf16[256,640]{1,0:T(8,128)(2,1)}, bf16[256,640]{1,0:T(8,128)(2,1)}, u32[]{:S(2)}, u32[]{:S(2)}) collective-permute-start(bf16[256,640]{1,0:T(8,128)(2,1)} %get-tuple-element.32), channel_id=1, source_target_pairs={{0,192},{64,0},{128,64},{192,128},{1,193},{65,1},{129,65},{193,129... | collective-permute-start | bytes 983048 | tf_op jit(solution)/shard_map/ppermute | solution.py:279
  7.5 8.9 %collective-permute-start.3 = (bf16[16,3072]{1,0:T(8,128)(2,1)}, bf16[16,3072]{1,0:T(8,128)(2,1)S(1)}, u32[]{:S(2)}, u32[]{:S(2)}) collective-permute-start(bf16[16,3072]{1,0:T(8,128)(2,1)} %get-tuple-element.31), channel_id=1, source_target_pairs={{0,8},{8,0},{1,9},{9,1},{2,10},{10,2},{3,11},{11,3},{4,12},{12,4},... | collective-permute-start | bytes 294920 | tf_op jit(solution)/shard_map/ppermute | solution.py:280
  13.5 8.2 %collective-permute-start.4 = (bf16[16,3072]{1,0:T(8,128)(2,1)}, bf16[16,3072]{1,0:T(8,128)(2,1)S(1)}, u32[]{:S(2)}, u32[]{:S(2)}) collective-permute-start(bf16[16,3072]{1,0:T(8,128)(2,1)} %get-tuple-element.31), channel_id=1, source_target_pairs={{0,16},{16,0},{1,17},{17,1},{2,18},{18,2},{3,19},{19,3},{4,20},{20... | collective-permute-start | bytes 294920 | tf_op jit(solution)/shard_map/ppermute | solution.py:281
  16.4 8.6 %collective-permute-start.5 = (bf16[16,3072]{1,0:T(8,128)(2,1)}, bf16[16,3072]{1,0:T(8,128)(2,1)S(1)}, u32[]{:S(2)}, u32[]{:S(2)}) collective-permute-start(bf16[16,3072]{1,0:T(8,128)(2,1)} %get-tuple-element.31), channel_id=1, source_target_pairs={{0,24},{8,16},{16,8},{24,0},{1,25},{9,17},{17,9},{25,1},{2,26},{10... | collective-permute-start | bytes 294920 | tf_op jit(solution)/shard_map/ppermute | solution.py:282
  25.0 0.7 copy-start.5
  25.7 24.2 %collective-permute-start.7 = (bf16[112,2048]{1,0:T(8,128)(2,1)}, bf16[112,2048]{1,0:T(8,128)(2,1)S(1)}, u32[]{:S(2)}, u32[]{:S(2)}) collective-permute-start(bf16[112,2048]{1,0:T(8,128)(2,1)} %bitcast.14), channel_id=1, source_target_pairs={{0,8},{8,0},{1,9},{9,1},{2,10},{10,2},{3,11},{11,3},{4,12},{12,4},... | collective-permute-start | bytes 1376264 | tf_op jit(solution)/shard_map/ppermute | solution.py:292
  30.9 21.7 %collective-permute-start.10 = (bf16[112,2048]{1,0:T(8,128)(2,1)}, bf16[112,2048]{1,0:T(8,128)(2,1)S(1)}, u32[]{:S(2)}, u32[]{:S(2)}) collective-permute-start(bf16[112,2048]{1,0:T(8,128)(2,1)} %bitcast.15), channel_id=1, source_target_pairs={{0,4},{4,0},{1,5},{5,1},{2,6},{6,2},{3,7},{7,3},{8,12},{12,8},{9,1... | collective-permute-start | bytes 1376264 | tf_op jit(solution)/shard_map/ppermute | solution.py:293
  38.0 3.4 %collective-permute-start.6 = (bf16[64,3072]{1,0:T(8,128)(2,1)S(1)}, bf16[64,3072]{1,0:T(8,128)(2,1)S(1)}, u32[]{:S(2)}, u32[]{:S(2)}) collective-permute-start(bf16[64,3072]{1,0:T(8,128)(2,1)S(1)} %pad_maximum_fusion), channel_id=1, source_target_pairs={{0,4},{4,0},{1,5},{5,1},{2,6},{6,2},{3,7},{7,3},{8,12},{12,8},{9,1... | collective-permute-start | bytes 1179656 | tf_op jit(solution)/shard_map/ppermute | solution.py:291
  40.1 17.4 %collective-permute-start.8 = (bf16[512,640]{1,0:T(8,128)(2,1)S(1)}, bf16[512,640]{1,0:T(8,128)(2,1)S(1)}, u32[]{:S(2)}, u32[]{:S(2)}) collective-permute-start(bf16[512,640]{1,0:T(8,128)(2,1)S(1)} %constant_dynamic-update-slice_fusion.5.refs_2_), channel_id=1, source_target_pairs={{0,128},{64,192},{128,0},{192,64},{1,129},{65,193},{129,1},{193,65... | collective-permute-start | bytes 1966088 | tf_op jit(solution)/shard_map/ppermute | solution.py:289
  41.2 17.4 %collective-permute-start.9 = (bf16[512,640]{1,0:T(8,128)(2,1)S(1)}, bf16[512,640]{1,0:T(8,128)(2,1)S(1)}, u32[]{:S(2)}, u32[]{:S(2)}) collective-permute-start(bf16[512,640]{1,0:T(8,128)(2,1)S(1)} %constant_dynamic-update-slice_fusion.7.refs_3_), channel_id=1, source_target_pairs={{0,32},{32,0},{1,33},{33,1},{2,34},{34,2},{3,35},{35,3},{4,36},{36... | collective-permute-start | bytes 1966088 | tf_op jit(solution)/shard_map/ppermute | solution.py:289
  42.2 16.4 %copy-start.4 = (bf16[16,512,128]{2,1,0:T(8,128)(2,1)S(1)}, bf16[16,512,128]{2,1,0:T(8,128)(2,1)}, u32[]{:S(2)}) copy-start(bf16[16,512,128]{2,1,0:T(8,128)(2,1)} %refs_6_.1) | copy-start | bytes 6291460
  50.0 8.6 %collective-permute-start.11 = (bf16[112,2048]{1,0:T(8,128)(2,1)S(1)}, bf16[112,2048]{1,0:T(8,128)(2,1)S(1)}, u32[]{:S(2)}, u32[]{:S(2)}) collective-permute-start(bf16[112,2048]{1,0:T(8,128)(2,1)S(1)} %collective-permute-done.7.refs_1_), channel_id=1, source_target_pairs={{0,4},{4,0},{1,5},{5,1},{2,6},{6,2},{3,7},{7,3},{8,12},{12,8},{9,1... | collective-permute-start | bytes 1376264 | tf_op jit(solution)/shard_map/ppermute | solution.py:306
  52.7 0.8 copy-start.2
  68.9 36.6 %copy-start.1 = (bf16[2048,112]{0,1:T(8,128)(2,1)S(1)}, bf16[2048,112]{0,1:T(8,128)(2,1)}, u32[]{:S(2)}) copy-start(bf16[2048,112]{0,1:T(8,128)(2,1)} %param.17) | copy-start | bytes 1376260
  68.9 36.6 %copy-start.3 = (bf16[112,2048]{1,0:T(8,128)(2,1)S(1)}, bf16[112,2048]{1,0:T(8,128)(2,1)}, u32[]{:S(2)}) copy-start(bf16[112,2048]{1,0:T(8,128)(2,1)} %copy-done.2) | copy-start | bytes 1376260
  68.9 2.6 %collective-permute-start.12 = (bf16[64,2176]{1,0:T(8,128)(2,1)S(1)}, bf16[64,2176]{1,0:T(8,128)(2,1)S(1)}, u32[]{:S(2)}, u32[]{:S(2)}) collective-permute-start(bf16[64,2176]{1,0:T(8,128)(2,1)S(1)} %get-tuple-element.50), channel_id=1, source_target_pairs={{0,4},{4,0},{1,5},{5,1},{2,6},{6,2},{3,7},{7,3},{8,12},{12,8},{9,1... | collective-permute-start | bytes 835592 | tf_op jit(solution)/shard_map/ppermute | solution.py:248
  72.0 5.0 %collective-permute-start.13 = (bf16[32,2176]{1,0:T(8,128)(2,1)S(1)}, bf16[32,2176]{1,0:T(8,128)(2,1)S(1)}, u32[]{:S(2)}, u32[]{:S(2)}) collective-permute-start(bf16[32,2176]{1,0:T(8,128)(2,1)S(1)} %get-tuple-element.52), channel_id=1, source_target_pairs={{0,16},{16,0},{1,17},{17,1},{2,18},{18,2},{3,19},{19,3},{4,20},{20... | collective-permute-start | bytes 417800 | tf_op jit(solution)/shard_map/ppermute | solution.py:248
  77.3 7.2 %collective-permute-start.14 = (bf16[16,2176]{1,0:T(8,128)(2,1)S(1)}, bf16[16,2176]{1,0:T(8,128)(2,1)S(1)}, u32[]{:S(2)}, u32[]{:S(2)}) collective-permute-start(bf16[16,2176]{1,0:T(8,128)(2,1)S(1)} %get-tuple-element.54), channel_id=1, source_target_pairs={{0,8},{8,0},{1,9},{9,1},{2,10},{10,2},{3,11},{11,3},{4,12},{12,4},... | collective-permute-start | bytes 208904 | tf_op jit(solution)/shard_map/ppermute | solution.py:313
  85.9 19.6 %all-to-all-start = ((bf16[16,16,2048]{2,1,0:T(8,128)(2,1)}), bf16[16,16,2048]{2,1,0:T(8,128)(2,1)S(1)}, u32[]{:S(2)}, u32[]{:S(2)}) async-start(bf16[16,16,2048]{2,1,0:T(8,128)(2,1)} %shard_map.97), calls=%async_computation | async-start | bytes 2097152 | tf_op jit(solution)/shard_map/all_to_all | solution.py:315

commit v4 on v3

--- a/solution.py
+++ b/solution.py
@@ -30,12 +30,12 @@
     return [(i, (i + d) % n) for i in range(n)]
 
 
-def call(kernel, out_shape, flops, nbytes, vmem=40, **kw):
+def call(kernel, out_shape, vmem=40, **kw):
     return pl.pallas_call(
         kernel,
         out_shape=out_shape,
         compiler_params=pltpu.CompilerParams(vmem_limit_bytes=vmem * MIB),
-        cost_estimate=pl.CostEstimate(flops=flops, bytes_accessed=nbytes, transcendentals=0),
+        cost_estimate=pl.CostEstimate(flops=1, bytes_accessed=1, transcendentals=0),
         **kw,
     )
 
@@ -44,7 +44,7 @@
     return lax.dot_general(a, b, (((1,), (1,)), ((), ())), preferred_element_type=jnp.float32)
 
 
-def pack_kernel(query_ref, rope_ref, latent_ref, key_rope_ref, pos_ref, q_ref, key_ref):
+def pack_keys_kernel(latent_ref, key_rope_ref, pos_ref, key_ref):
     key_ref[:, :RANK] = latent_ref[...]
     pos = pos_ref[...].astype(jnp.float32)
     high = jnp.floor(pos * (1 / 128))
@@ -52,35 +52,61 @@
     ext = jnp.where(row == 0, high, jnp.where(row == 1, pos - high * 128, 0.0))
     ext = jnp.concatenate([key_rope_ref[...].astype(jnp.float32), ext], axis=0)
     key_ref[:, RANK:] = jnp.transpose(ext).astype(jnp.bfloat16)
-    q_ref[:, : HG * NOPE] = query_ref[...]
-    q_ref[:, HG * NOPE :] = rope_ref[...]
-
-
-def pack(query, q_rope, latent, k_rope, key_pos):
+
+
+def pack_keys(latent, k_rope, key_pos):
     return call(
-        pack_kernel,
-        (
-            jax.ShapeDtypeStruct((R, HG * (NOPE + ROPE)), jnp.bfloat16),
-            jax.ShapeDtypeStruct((latent.shape[0], KEYW), jnp.bfloat16),
-        ),
-        MIB,
-        MIB,
+        pack_keys_kernel,
+        jax.ShapeDtypeStruct((latent.shape[0], KEYW), jnp.bfloat16),
         vmem=60,
-    )(query, q_rope, latent, jnp.transpose(k_rope), key_pos)
-
-
-def absorb_kernel(q_ref, w_ref, out_ref):
+    )(latent, jnp.transpose(k_rope), key_pos)
+
+
+def pack_far_kernel(w_ref, query_ref, rope_ref, out_ref):
+    ncol = w_ref.shape[0]
+    out_ref[:ncol] = w_ref[...]
+    out_ref[ncol : ncol + R] = query_ref[...]
+    out_ref[ncol + R :, : HG * ROPE] = rope_ref[...]
+    out_ref[ncol + R :, HG * ROPE :] = jnp.zeros((R, HG * (NOPE - ROPE)), jnp.bfloat16)
+
+
+def pack_far(w_out, query, q_rope):
+    ncol = w_out.shape[1]
+    return call(
+        pack_far_kernel,
+        jax.ShapeDtypeStruct((ncol + 2 * R, HG * VDIM), jnp.bfloat16),
+        vmem=60,
+    )(jnp.transpose(w_out), query, q_rope)
+
+
+def unpack_queries_kernel(own_ref, far_ref, out_ref):
+    ncol = own_ref.shape[0] - 2 * R
+    for i, ref in enumerate((own_ref, far_ref)):
+        out_ref[i * R : (i + 1) * R, : HG * NOPE] = ref[ncol : ncol + R]
+        out_ref[i * R : (i + 1) * R, HG * NOPE :] = ref[ncol + R :, : HG * ROPE]
+
+
+def unpack_queries(own, far):
+    return call(
+        unpack_queries_kernel,
+        jax.ShapeDtypeStruct((2 * R, HG * (NOPE + ROPE)), jnp.bfloat16),
+    )(own, far)
+
+
+def absorb_kernel(*refs):
+    q_refs, (w_ref, out_ref) = refs[:4], refs[4:]
     lane = lax.broadcasted_iota(jnp.int32, (ROWS, 128), 1)
     row = lax.broadcasted_iota(jnp.int32, (ROWS, 128), 0)
     one_hot = (lane == row).astype(jnp.bfloat16)
+
+    def columns(start):
+        return jnp.concatenate([ref[:, start : start + 128] for ref in q_refs], axis=0)
+
     for h in range(HG):
         rows = slice(h * ROWS, (h + 1) * ROWS)
-        latent = jnp.dot(
-            q_ref[:, h * NOPE : (h + 1) * NOPE], w_ref[h], preferred_element_type=jnp.float32
-        )
+        latent = jnp.dot(columns(h * NOPE), w_ref[h], preferred_element_type=jnp.float32)
         out_ref[rows, :RANK] = latent.astype(jnp.bfloat16)
-        start = HG * NOPE + (h // 2) * 128
-        pair = q_ref[:, start : start + 128].astype(jnp.float32)
+        pair = columns(HG * NOPE + (h // 2) * 128).astype(jnp.float32)
         if h % 2:
             pair = pltpu.roll(pair, ROPE, 1)
         rope = jnp.where(lane < ROPE, pair, 0.0)
@@ -88,13 +114,10 @@
         out_ref[rows, RANK + 128 :] = one_hot
 
 
-def absorb(q, w_uk):
-    return call(
-        absorb_kernel,
-        jax.ShapeDtypeStruct((ITEMS, ITEMW), jnp.bfloat16),
-        2 * ITEMS * NOPE * RANK,
-        6 * MIB,
-    )(q, w_uk)
+def absorb(queries, w_uk):
+    return call(absorb_kernel, jax.ShapeDtypeStruct((ITEMS, ITEMW), jnp.bfloat16))(
+        *queries, w_uk
+    )
 
 
 def pack_stats(stats):
@@ -202,8 +225,6 @@
     return call(
         functools.partial(attend_kernel, n, last),
         out_shape,
-        2 * ITEMS * n * keys * (KEYW + RANK),
-        (ITEMS * (ITEMW + RANK) + n * keys * KEYW) * 2,
         grid=(ITEMS // tile,),
         in_specs=in_specs,
         out_specs=out_specs,
@@ -243,18 +264,20 @@
             out_ref[i, :, cols] = head
 
 
-def merge_over(axis, own, send):
+def merge_over(axis, own, send, *beside):
     half = jax.ShapeDtypeStruct((own.shape[0] // 2, SENDW), jnp.bfloat16)
-    return call(merge_kernel, (half, half), MIB, MIB)(own, lax.ppermute(send, axis, SWAP))
+    received, *beside = lax.optimization_barrier((lax.ppermute(send, axis, SWAP), *beside))
+    return *call(merge_kernel, (half, half))(own, received), *beside
 
 
 def project_kernel(zc_ref, x_ref, *refs):
     out_ref = refs[-1]
     z, c = zc_ref[0], zc_ref[1]
+    ncol = out_ref.shape[2]
     for k in range(4):
         to_z = z if k % 2 == 0 else 1 - z
         to_c = c if k < 2 else 1 - c
-        out_ref[to_z * 2 + to_c] = nt_dot(x_ref[...], refs[k][...]).astype(jnp.bfloat16)
+        out_ref[to_z * 2 + to_c] = nt_dot(x_ref[...], refs[k][:ncol]).astype(jnp.bfloat16)
 
 
 def finish_kernel(sums_ref, out_ref, row_ref):
@@ -271,26 +294,21 @@
 def local(query_unrotated, q_rope, latent, k_rope, key_pos, offset, w_uk, value_up_weight, w_out):
     y, u, x, z, c = (lax.axis_index(n) for n in CTX)
 
-    q_own, keys = pack(query_unrotated, q_rope, latent[0], k_rope[0], key_pos)
-
-    phase = (
-        lax.ppermute(keys, "u", SWAP),
-        lax.ppermute(keys, "y", shift(4, 1)),
-        lax.ppermute(keys, "y", shift(4, 3)),
-        lax.ppermute(q_own, "z", SWAP),
-        lax.ppermute(q_own, "x", SWAP),
-        lax.ppermute(q_own, ("x", "z"), [(i, 3 - i) for i in range(4)]),
-    )
-    keys_u, keys_up, keys_down, q_z, q_x, q_xz, w_own = lax.optimization_barrier(
-        phase + (jnp.transpose(w_out),)
-    )
-
-    near = [jnp.concatenate([keys, keys_u]), jnp.concatenate([keys_up, keys_down])]
-    far = [lax.ppermute(near[0], "y", shift(4, 2)), lax.ppermute(near[1], "u", SWAP)]
-    q_all = jnp.concatenate([q_own, q_z, q_x, q_xz])
-    q_all = jnp.concatenate([q_all, lax.ppermute(q_all, "c", SWAP)])
-    w_z = lax.ppermute(w_own, "z", SWAP)
-    w_c = lax.ppermute(w_own, "c", SWAP)
+    keys = pack_keys(latent[0], k_rope[0], key_pos)
+    keys_u = lax.ppermute(keys, "u", SWAP)
+    keys_up = lax.ppermute(keys, "y", shift(4, 1))
+    keys_down = lax.ppermute(keys, "y", shift(4, 3))
+    keys_far = lax.ppermute(keys, "y", shift(4, 2))
+    keys_u, keys_up, keys_down = lax.optimization_barrier((keys_u, keys_up, keys_down))
+    far_u = lax.ppermute(keys_u, "y", shift(4, 2))
+    up_u = lax.ppermute(keys_up, "u", SWAP)
+    down_u = lax.ppermute(keys_down, "u", SWAP)
+
+    own_w = pack_far(w_out, query_unrotated, q_rope)
+    z_w = lax.ppermute(own_w, "z", SWAP)
+    q_z = unpack_queries(own_w, z_w)
+    q_x = lax.ppermute(q_z, "x", SWAP)
+    queries = (q_z, q_x, lax.ppermute(q_z, "c", SWAP), lax.ppermute(q_x, "c", SWAP))
 
     row = jnp.arange(ROWS, dtype=jnp.int32)
     part = row // R
@@ -300,36 +318,35 @@
     row = ((((y * 2 + u) * 2 + row_x) * 2 + row_z) * 2 + row_c) * R + row % R
     qpos = jnp.broadcast_to((offset[0] + row).astype(jnp.float32)[None, :], (8, ROWS))
 
-    q = absorb(q_all, w_uk)
-    state = attend(q, qpos, near)
-    state, w_z = lax.optimization_barrier((state, w_z))
-    w_zc = lax.ppermute(w_z, "c", SWAP)
-    state, far, w_c, w_zc = lax.optimization_barrier((state, far, w_c, w_zc))
+    q = absorb(queries, w_uk)
+    state = attend(q, qpos, [keys, keys_u, keys_up, keys_down, keys_far])
+    state, far = lax.optimization_barrier((state, [far_u, up_u, down_u]))
     own, send = attend(q, qpos, far, state, value_up_weight)
     own, send = merge_over("c", own, send)
-    own, send = merge_over("x", own, send)
-    heads = call(
-        merge_last_kernel, jax.ShapeDtypeStruct((16, R, HG * VDIM), jnp.bfloat16), MIB, MIB
-    )(own, lax.ppermute(send, "z", SWAP))
+    send, own_w, z_w = lax.optimization_barrier((send, own_w, z_w))
+    own, send, c_w = merge_over("x", own, send, lax.ppermute(own_w, "c", SWAP))
+    send, z_w = lax.optimization_barrier((send, z_w))
+    send, zc_w = lax.optimization_barrier(
+        (lax.ppermute(send, "z", SWAP), lax.ppermute(z_w, "c", SWAP))
+    )
+    heads = call(merge_last_kernel, jax.ShapeDtypeStruct((16, R, HG * VDIM), jnp.bfloat16))(
+        own, send
+    )
 
     rows = lax.all_to_all(heads, ("y", "u", "x"), 0, 0, tiled=True).reshape(16 * R, HG * VDIM)
     ncol = w_out.shape[1]
     sums = call(
         project_kernel,
         jax.ShapeDtypeStruct((4, 16 * R, ncol), jnp.bfloat16),
-        2 * 16 * R * HG * VDIM * 4 * ncol,
-        4 * MIB,
         in_specs=[pl.BlockSpec(memory_space=pltpu.SMEM)]
         + [pl.BlockSpec(memory_space=pltpu.VMEM)] * 5,
-    )(jnp.stack([z, c]), rows, w_own, w_z, w_c, w_zc)
+    )(jnp.stack([z, c]), rows, own_w, z_w, c_w, zc_w)
     sums = lax.all_to_all(
         sums.reshape(16, 4 * R, ncol), ("z", "c", "head"), 0, 0, tiled=True
     )
     out = call(
         finish_kernel,
         jax.ShapeDtypeStruct((ncol, 16 * R), jnp.bfloat16),
-        MIB,
-        MIB,
         scratch_shapes=[pltpu.VMEM((16 * R, 128), jnp.float32)],
     )(sums)
     return jnp.transpose(out)

time: 126 us -> 143 us (1.13)
  Pallas kernels: 25.6 us -> 36.6 us
  waiting for transfers between devices: 35.8 us -> 45.5 us
  starting transfers between devices: 38.3 us -> 35.5 us
  blocking collectives: 17.5 us -> 20 us
  local copies, waits for them, and re-layouts: 6.52 us -> 4.27 us
    pallas_call x7 -> x9, Pallas kernels: 22.4 us -> 33.4 us  [the longest x2 26.3 us: attend(): call(functools.partial(attend_kernel, n, last), out_shape, grid=(ITEMS //...]
    ppermute x12 -> x13, waiting for transfers between devices: 8.51 us -> 19.4 us  [the longest x1 18.6 us: local(): z_w = lax.ppermute(own_w, 'z', SWAP)]
    ppermute x12 -> x13, starting transfers between devices: 31.3 us -> 23.5 us  [the longest x1 6.01 us: local(): z_w = lax.ppermute(own_w, 'z', SWAP)]
    ppermute x1, starting transfers between devices: 0.09 us -> 5.02 us  [local(): lax.ppermute(send, 'z', SWAP)]
    ppermute x1, waiting for transfers between devices: 7.06 us -> 4.06 us  [local(): lax.ppermute(send, 'z', SWAP)]
    all_to_all x1, blocking collectives: 17.5 us -> 20 us  [local(): lax.all_to_all(sums.reshape(16, 4 * R, ncol), ('z', 'c', 'head'), 0, 0, t...]
    concatenate x3 -> x0, local copies, waits for them, and re-layouts: 2.06 us -> none  [the longest x1 1.01 us: local(): jnp.concatenate([keys, keys_u])]
    all_to_all x1, waiting for transfers between devices: 14.5 us -> 16.1 us  [local(): lax.all_to_all(heads, ('y', 'u', 'x'), 0, 0, tiled=True)]
  transfers between devices with their start and end apart: 16 -> 17, of which waited for: 7 -> 6; matrix products, arithmetic and copies ran while one was open for 5% -> 0% of each run, Pallas kernels for 7% -> 13%
where the time goes in v4:
time: 143 us
  waiting for transfers between devices  45.5 us (32%)
  Pallas kernels  36.6 us (26%)
  starting transfers between devices  35.5 us (25%)
  blocking collectives  20 us (14%)
  local copies, waits for them, and re-layouts  4.27 us (3%)
    pallas_call x2, Pallas kernels, attend(): call(functools.partial(attend_kernel, n, last), out_shape, grid=(ITEMS //...  26.3 us
    all_to_all x1, blocking collectives, local(): lax.all_to_all(sums.reshape(16, 4 * R, ncol), ('z', 'c', 'head'), 0, 0, t...  20 us
    ppermute x1, waiting for transfers between devices, local(): z_w = lax.ppermute(own_w, 'z', SWAP)  18.6 us
    all_to_all x1, waiting for transfers between devices, local(): lax.all_to_all(heads, ('y', 'u', 'x'), 0, 0, tiled=True)  16.1 us
    all_to_all x1, starting transfers between devices, local(): lax.all_to_all(heads, ('y', 'u', 'x'), 0, 0, tiled=True)  6.24 us
    ppermute x1, starting transfers between devices, local(): z_w = lax.ppermute(own_w, 'z', SWAP)  6.01 us
    ppermute x2, waiting for transfers between devices, merge_over(): lax.ppermute(send, axis, SWAP)  6 us
    ppermute x1, starting transfers between devices, local(): lax.ppermute(send, 'z', SWAP)  5.02 us
  transfers between devices with their start and end apart: 17, of which 6 were waited for; matrix products, arithmetic and copies ran while one was open for 0% of the time, Pallas kernels for 13%

profile of v4, /device:TPU:33, one launch (start us, length us, event | category | flops | bytes accessed | tf_op | source)
XLA Modules:
  0.0 142.7 jit_solution(5281015768849501368)
XLA Ops:
  0.0 1.9 %shard_map.91.own_ref.refs_0_ = bf16[144,2048]{1,0:T(8,128)(2,1)} custom-call(bf16[112,2048]{1,0:T(8,128)(2,1)} %bitcast.14, bf16[16,2048]{1,0:T(8,128)(2,1)} %query_ref.1, bf16[16,1024]{1,0:T(8,128)(2,1)} %rope_ref.1), custom_call_target="tpu_custom_call" | custom-call | flops 1 | bytes 1 | tf_op jit(solution)/shard_map/pallas_call | solution.py:75
  1.9 6.0 %collective-permute-start = (bf16[144,2048]{1,0:T(8,128)(2,1)}, bf16[144,2048]{1,0:T(8,128)(2,1)S(1)}, u32[]{:S(2)}, u32[]{:S(2)}) collective-permute-start(bf16[144,2048]{1,0:T(8,128)(2,1)} %shard_map.91.own_ref.refs_0_), channel_id=1, source_target_pairs={{0,8},{8,0},{1,9},{9,1},{2,10},{10,2},{3,11},{11,3},{4,12},{12,4},... | collective-permute-start | bytes 1769480 | tf_op jit(solution)/shard_map/ppermute | solution.py:308
  8.0 1.8 %shard_map.94.refs_2_ = bf16[256,640]{1,0:T(8,128)(2,1)} custom-call(bf16[256,512]{1,0:T(8,128)(2,1)} %bitcast.15, bf16[64,256]{1,0:T(8,128)(2,1)} %bitcast.16, s32[1,256]{1,0:T(1,128)} %pos_ref.1), custom_call_target="tpu_custom_call" | custom-call | flops 1 | bytes 1 | tf_op jit(solution)/shard_map/pallas_call | solution.py:58
  9.8 2.7 %collective-permute-start.4 = (bf16[256,640]{1,0:T(8,128)(2,1)}, bf16[256,640]{1,0:T(8,128)(2,1)S(1)}, u32[]{:S(2)}, u32[]{:S(2)}) collective-permute-start(bf16[256,640]{1,0:T(8,128)(2,1)} %shard_map.94.refs_2_), channel_id=1, source_target_pairs={{0,32},{32,0},{1,33},{33,1},{2,34},{34,2},{3,35},{35,3},{4,36},{36... | collective-permute-start | bytes 983048 | tf_op jit(solution)/shard_map/ppermute | solution.py:298
  12.5 1.3 collective-permute-start.5
  13.8 1.4 %collective-permute-start.6 = (bf16[256,640]{1,0:T(8,128)(2,1)}, bf16[256,640]{1,0:T(8,128)(2,1)S(1)}, u32[]{:S(2)}, u32[]{:S(2)}) collective-permute-start(bf16[256,640]{1,0:T(8,128)(2,1)} %shard_map.94.refs_2_), channel_id=1, source_target_pairs={{0,192},{64,0},{128,64},{192,128},{1,193},{65,1},{129,65},{193,129... | collective-permute-start | bytes 983048 | tf_op jit(solution)/shard_map/ppermute | solution.py:300
  15.2 18.6 %collective-permute-done.far_ref.refs_1_ = bf16[144,2048]{1,0:T(8,128)(2,1)S(1)} collective-permute-done((bf16[144,2048]{1,0:T(8,128)(2,1)}, bf16[144,2048]{1,0:T(8,128)(2,1)S(1)}, u32[]{:S(2)}, u32[]{:S(2)}) %collective-permute-start) | collective-permute-done | bytes 589856 | tf_op jit(solution)/shard_map/ppermute | solution.py:308
  33.9 1.1 copy-done
  34.9 1.3 collective-permute-start.1
  36.2 1.6 %collective-permute-start.2 = (bf16[32,3072]{1,0:T(8,128)(2,1)S(1)}, bf16[32,3072]{1,0:T(8,128)(2,1)S(1)}, u32[]{:S(2)}, u32[]{:S(2)}) collective-permute-start(bf16[32,3072]{1,0:T(8,128)(2,1)S(1)} %shard_map.92.refs_0_), channel_id=1, source_target_pairs={{0,4},{4,0},{1,5},{5,1},{2,6},{6,2},{3,7},{7,3},{8,12},{12,8},{9,1... | collective-permute-start | bytes 589832 | tf_op jit(solution)/shard_map/ppermute | solution.py:311
  37.8 0.0 collective-permute-done.4.refs_3_
  37.8 2.9 %collective-permute-start.7 = (bf16[256,640]{1,0:T(8,128)(2,1)}, bf16[256,640]{1,0:T(8,128)(2,1)S(1)}, u32[]{:S(2)}, u32[]{:S(2)}) collective-permute-start(bf16[256,640]{1,0:T(8,128)(2,1)} %shard_map.94.refs_2_), channel_id=1, source_target_pairs={{0,128},{64,192},{128,0},{192,64},{1,129},{65,193},{129,1},{193,65... | collective-permute-start | bytes 983048 | tf_op jit(solution)/shard_map/ppermute | solution.py:301
  40.7 0.0 collective-permute-done.5.refs_4_
  40.7 0.0 collective-permute-done.6.refs_5_
  40.7 0.1 collective-permute-start.8
  40.8 2.5 %collective-permute-start.9 = (bf16[256,640]{1,0:T(8,128)(2,1)S(1)}, bf16[256,640]{1,0:T(8,128)(2,1)S(1)}, u32[]{:S(2)}, u32[]{:S(2)}) collective-permute-start(bf16[256,640]{1,0:T(8,128)(2,1)S(1)} %collective-permute-done.5.refs_4_), channel_id=1, source_target_pairs={{0,32},{32,0},{1,33},{33,1},{2,34},{34,2},{3,35},{35,3},{4,36},{36... | collective-permute-start | bytes 983048 | tf_op jit(solution)/shard_map/ppermute | solution.py:304
  43.3 0.0 collective-permute-done.1.refs_1_
  43.3 0.5 collective-permute-start.10
  43.8 0.0 collective-permute-done.2.refs_2_
  43.8 0.7 copy-done.5
  44.5 1.7 %collective-permute-start.3 = (bf16[32,3072]{1,0:T(8,128)(2,1)}, bf16[32,3072]{1,0:T(8,128)(2,1)}, u32[]{:S(2)}, u32[]{:S(2)}) collective-permute-start(bf16[32,3072]{1,0:T(8,128)(2,1)} %collective-permute-done.1.refs_1_), channel_id=1, source_target_pairs={{0,4},{4,0},{1,5},{5,1},{2,6},{6,2},{3,7},{7,3},{8,12},{12,8},{9,1... | collective-permute-start | bytes 589832 | tf_op jit(solution)/shard_map/ppermute | solution.py:311
  46.8 0.7 collective-permute-done.3.refs_3_
  47.6 1.6 %copy-done.2 = bf16[16,128,512]{2,1,0:T(8,128)(2,1)S(1)} copy-done((bf16[16,128,512]{2,1,0:T(8,128)(2,1)S(1)}, bf16[16,128,512]{2,1,0:T(8,128)(2,1)}, u32[]{:S(2)}) %copy-start.2) | copy-done | bytes 2097176
  49.2 0.9 copy-done.6
  50.1 1.8 %shard_map.93.refs_0_ = bf16[2048,768]{1,0:T(8,128)(2,1)S(1)} custom-call(bf16[32,3072]{1,0:T(8,128)(2,1)S(1)} %shard_map.92.refs_0_, bf16[32,3072]{1,0:T(8,128)(2,1)} %collective-permute-done.1.refs_1_, bf16[32,3072]{1,0:T(8,128)(2,1)S(1)} %copy-done.6, bf16[32,3072]{1,0:T(8,128)(2,1)} %collective-permute-done.3.refs_3_, bf16[16,128,512]{2,1,0:T(8,128)(2,1)S(1)} %copy-done.2), custom_call_target="tpu_custom_call" | custom-call | flops 1 | bytes 1 | tf_op jit(solution)/shard_map/pallas_call | solution.py:118
  51.9 0.0 copy-start.3
  52.0 14.2 %shard_map.95 = (f32[2048,512]{1,0:T(8,128)S(1)}, f32[2048,128]{1,0:T(8,128)S(1)}) custom-call(bf16[2048,768]{1,0:T(8,128)(2,1)S(1)} %shard_map.93.refs_0_, f32[8,128]{1,0:T(8,128)S(1)} %broadcast_in_dim.32.refs_1_, bf16[256,640]{1,0:T(8,128)(2,1)S(1)} %copy-done.4, bf16[256,640]{1,0:T(8,128)(2,1)S(1)} %collective-permute-done.4.refs_3_, ...), custom_call_target="tpu_custom_call" | custom-call | flops 1 | bytes 1 | tf_op jit(solution)/shard_map/pallas_call | solution.py:225
  66.2 0.0 collective-permute-done.8.refs_2_
  66.2 0.0 collective-permute-done.9.refs_3_
  66.2 12.0 %shard_map.96 = (bf16[64,2176]{1,0:T(8,128)(2,1)S(1)}, bf16[64,2176]{1,0:T(8,128)(2,1)S(1)}) custom-call(bf16[2048,768]{1,0:T(8,128)(2,1)S(1)} %shard_map.93.refs_0_, f32[8,128]{1,0:T(8,128)S(1)} %broadcast_in_dim.32.refs_1_, bf16[256,640]{1,0:T(8,128)(2,1)S(1)} %collective-permute-done.8.refs_2_, bf16[256,640]{1,0:T(8,128)(2,1)S(1)} %collective-permute-done.9.refs_3_, ...), custom_call_target="tpu_custom_call" | custom-call | flops 1 | bytes 1 | tf_op jit(solution)/shard_map/pallas_call | solution.py:225
  78.3 0.4 collective-permute-start.11
  78.7 1.2 collective-permute-done.11.b_ref
  79.9 0.5 shard_map.97
  80.4 0.4 collective-permute-start.13
  80.9 0.3 collective-permute-start.12
  81.2 4.8 %collective-permute-done.12.b_ref = bf16[32,2176]{1,0:T(8,128)(2,1)S(1)} collective-permute-done((bf16[32,2176]{1,0:T(8,128)(2,1)S(1)}, bf16[32,2176]{1,0:T(8,128)(2,1)S(1)}, u32[]{:S(2)}, u32[]{:S(2)}) %collective-permute-start.12) | collective-permute-done | bytes 139296 | tf_op jit(solution)/shard_map/ppermute | solution.py:269
  86.0 0.0 collective-permute-done.13.refs_2_
  86.0 0.3 shard_map.98
  86.3 1.1 collective-permute-start.15
  87.4 5.0 %collective-permute-start.14 = (bf16[16,2176]{1,0:T(8,128)(2,1)S(1)}, bf16[16,2176]{1,0:T(8,128)(2,1)S(1)}, u32[]{:S(2)}, u32[]{:S(2)}) collective-permute-start(bf16[16,2176]{1,0:T(8,128)(2,1)S(1)} %get-tuple-element.50), channel_id=1, source_target_pairs={{0,8},{8,0},{1,9},{9,1},{2,10},{10,2},{3,11},{11,3},{4,12},{12,4},... | collective-permute-start | bytes 208904 | tf_op jit(solution)/shard_map/ppermute | solution.py:330
  92.4 4.1 %collective-permute-done.14.b_ref = bf16[16,2176]{1,0:T(8,128)(2,1)S(1)} collective-permute-done((bf16[16,2176]{1,0:T(8,128)(2,1)S(1)}, bf16[16,2176]{1,0:T(8,128)(2,1)S(1)}, u32[]{:S(2)}, u32[]{:S(2)}) %collective-permute-start.14) | collective-permute-done | bytes 69664 | tf_op jit(solution)/shard_map/ppermute | solution.py:330
  96.5 1.4 shard_map.99
  97.9 6.2 %all-to-all-start = ((bf16[16,16,2048]{2,1,0:T(8,128)(2,1)}), bf16[16,16,2048]{2,1,0:T(8,128)(2,1)S(1)}, u32[]{:S(2)}, u32[]{:S(2)}) async-start(bf16[16,16,2048]{2,1,0:T(8,128)(2,1)} %shard_map.99), calls=%async_computation | async-start | bytes 2097152 | tf_op jit(solution)/shard_map/all_to_all | solution.py:336
  104.1 0.1 pad_add_fusion.zc_ref
  104.2 16.1 %all-to-all-done = bf16[16,16,2048]{2,1,0:T(8,128)(2,1)S(1)} async-done(((bf16[16,16,2048]{2,1,0:T(8,128)(2,1)}), bf16[16,16,2048]{2,1,0:T(8,128)(2,1)S(1)}, u32[]{:S(2)}, u32[]{:S(2)}) %all-to-all-start) | async-done | bytes 1048608 | tf_op jit(solution)/shard_map/all_to_all | solution.py:336
  120.3 1.8 %shard_map.100 = bf16[4,256,112]{2,1,0:T(8,128)(2,1)S(1)} custom-call(s32[2]{0:T(128)S(1)} %pad_add_fusion.zc_ref, bf16[256,2048]{1,0:T(8,128)(2,1)S(1)} %bitcast.12, bf16[144,2048]{1,0:T(8,128)(2,1)S(1)} %copy-done.1, bf16[144,2048]{1,0:T(8,128)(2,1)S(1)} %collective-permute-done.far_ref.refs_1_, bf16[144,2048]{1,0:T(8,128)(2,1)S(1)} %collective-permute-done.13.refs_2_, ...), custom_call_target="tpu_custom_call" | custom-call | flops 1 | bytes 1 | tf_op jit(solution)/shard_map/pallas_call | solution.py:338
  122.0 20.0 %all_to_all.10.sums_ref = bf16[16,64,112]{2,1,0:T(8,128)(2,1)S(1)} all-to-all(bf16[16,64,112]{2,1,0:T(8,128)(2,1)S(1)} %bitcast.13), channel_id=1, replica_groups=mesh['y'=4,'u'=2,'x'=2,'z'=2,'c'=2,'head'=4] {'z','c','head'}, dimensions={0} | all-to-all | bytes 458752 | tf_op jit(solution)/shard_map/all_to_all | solution.py:344
  142.0 0.7 shard_map.101
  (15 shorter events, 0.1 us)
Async XLA Ops:
  1.9 31.9 %collective-permute-start = (bf16[144,2048]{1,0:T(8,128)(2,1)}, bf16[144,2048]{1,0:T(8,128)(2,1)S(1)}, u32[]{:S(2)}, u32[]{:S(2)}) collective-permute-start(bf16[144,2048]{1,0:T(8,128)(2,1)} %shard_map.91.own_ref.refs_0_), channel_id=1, source_target_pairs={{0,8},{8,0},{1,9},{9,1},{2,10},{10,2},{3,11},{11,3},{4,12},{12,4},... | collective-permute-start | bytes 1769480 | tf_op jit(solution)/shard_map/ppermute | solution.py:308
  9.8 28.1 %collective-permute-start.4 = (bf16[256,640]{1,0:T(8,128)(2,1)}, bf16[256,640]{1,0:T(8,128)(2,1)S(1)}, u32[]{:S(2)}, u32[]{:S(2)}) collective-permute-start(bf16[256,640]{1,0:T(8,128)(2,1)} %shard_map.94.refs_2_), channel_id=1, source_target_pairs={{0,32},{32,0},{1,33},{33,1},{2,34},{34,2},{3,35},{35,3},{4,36},{36... | collective-permute-start | bytes 983048 | tf_op jit(solution)/shard_map/ppermute | solution.py:298
  12.5 28.2 %collective-permute-start.5 = (bf16[256,640]{1,0:T(8,128)(2,1)}, bf16[256,640]{1,0:T(8,128)(2,1)S(1)}, u32[]{:S(2)}, u32[]{:S(2)}) collective-permute-start(bf16[256,640]{1,0:T(8,128)(2,1)} %shard_map.94.refs_2_), channel_id=1, source_target_pairs={{0,64},{64,128},{128,192},{192,0},{1,65},{65,129},{129,193},{193,1... | collective-permute-start | bytes 983048 | tf_op jit(solution)/shard_map/ppermute | solution.py:299
  13.8 26.9 %collective-permute-start.6 = (bf16[256,640]{1,0:T(8,128)(2,1)}, bf16[256,640]{1,0:T(8,128)(2,1)S(1)}, u32[]{:S(2)}, u32[]{:S(2)}) collective-permute-start(bf16[256,640]{1,0:T(8,128)(2,1)} %shard_map.94.refs_2_), channel_id=1, source_target_pairs={{0,192},{64,0},{128,64},{192,128},{1,193},{65,1},{129,65},{193,129... | collective-permute-start | bytes 983048 | tf_op jit(solution)/shard_map/ppermute | solution.py:300
  33.9 1.1 copy-start
  34.9 17.0 %copy-start.4 = (bf16[256,640]{1,0:T(8,128)(2,1)S(1)}, bf16[256,640]{1,0:T(8,128)(2,1)}, u32[]{:S(2)}) copy-start(bf16[256,640]{1,0:T(8,128)(2,1)} %shard_map.94.refs_2_) | copy-start | bytes 983044
  34.9 8.4 %collective-permute-start.1 = (bf16[32,3072]{1,0:T(8,128)(2,1)S(1)}, bf16[32,3072]{1,0:T(8,128)(2,1)}, u32[]{:S(2)}, u32[]{:S(2)}) collective-permute-start(bf16[32,3072]{1,0:T(8,128)(2,1)S(1)} %shard_map.92.refs_0_), channel_id=1, source_target_pairs={{0,16},{16,0},{1,17},{17,1},{2,18},{18,2},{3,19},{19,3},{4,20},{20... | collective-permute-start | bytes 589832 | tf_op jit(solution)/shard_map/ppermute | solution.py:310
  36.2 7.6 %collective-permute-start.2 = (bf16[32,3072]{1,0:T(8,128)(2,1)S(1)}, bf16[32,3072]{1,0:T(8,128)(2,1)S(1)}, u32[]{:S(2)}, u32[]{:S(2)}) collective-permute-start(bf16[32,3072]{1,0:T(8,128)(2,1)S(1)} %shard_map.92.refs_0_), channel_id=1, source_target_pairs={{0,4},{4,0},{1,5},{5,1},{2,6},{6,2},{3,7},{7,3},{8,12},{12,8},{9,1... | collective-permute-start | bytes 589832 | tf_op jit(solution)/shard_map/ppermute | solution.py:311
  37.8 14.1 %collective-permute-start.7 = (bf16[256,640]{1,0:T(8,128)(2,1)}, bf16[256,640]{1,0:T(8,128)(2,1)S(1)}, u32[]{:S(2)}, u32[]{:S(2)}) collective-permute-start(bf16[256,640]{1,0:T(8,128)(2,1)} %shard_map.94.refs_2_), channel_id=1, source_target_pairs={{0,128},{64,192},{128,0},{192,64},{1,129},{65,193},{129,1},{193,65... | collective-permute-start | bytes 983048 | tf_op jit(solution)/shard_map/ppermute | solution.py:301
  40.7 25.4 %collective-permute-start.8 = (bf16[256,640]{1,0:T(8,128)(2,1)S(1)}, bf16[256,640]{1,0:T(8,128)(2,1)S(1)}, u32[]{:S(2)}, u32[]{:S(2)}) collective-permute-start(bf16[256,640]{1,0:T(8,128)(2,1)S(1)} %collective-permute-done.4.refs_3_), channel_id=1, source_target_pairs={{0,128},{64,192},{128,0},{192,64},{1,129},{65,193},{129,1},{193,65... | collective-permute-start | bytes 983048 | tf_op jit(solution)/shard_map/ppermute | solution.py:303
  40.8 25.4 %collective-permute-start.9 = (bf16[256,640]{1,0:T(8,128)(2,1)S(1)}, bf16[256,640]{1,0:T(8,128)(2,1)S(1)}, u32[]{:S(2)}, u32[]{:S(2)}) collective-permute-start(bf16[256,640]{1,0:T(8,128)(2,1)S(1)} %collective-permute-done.5.refs_4_), channel_id=1, source_target_pairs={{0,32},{32,0},{1,33},{33,1},{2,34},{34,2},{3,35},{35,3},{4,36},{36... | collective-permute-start | bytes 983048 | tf_op jit(solution)/shard_map/ppermute | solution.py:304
  43.3 22.9 %collective-permute-start.10 = (bf16[256,640]{1,0:T(8,128)(2,1)S(1)}, bf16[256,640]{1,0:T(8,128)(2,1)S(1)}, u32[]{:S(2)}, u32[]{:S(2)}) collective-permute-start(bf16[256,640]{1,0:T(8,128)(2,1)S(1)} %collective-permute-done.6.refs_5_), channel_id=1, source_target_pairs={{0,32},{32,0},{1,33},{33,1},{2,34},{34,2},{3,35},{35,3},{4,36},{36... | collective-permute-start | bytes 983048 | tf_op jit(solution)/shard_map/ppermute | solution.py:305
  43.8 0.7 copy-start.5
  44.5 3.1 %collective-permute-start.3 = (bf16[32,3072]{1,0:T(8,128)(2,1)}, bf16[32,3072]{1,0:T(8,128)(2,1)}, u32[]{:S(2)}, u32[]{:S(2)}) collective-permute-start(bf16[32,3072]{1,0:T(8,128)(2,1)} %collective-permute-done.1.refs_1_), channel_id=1, source_target_pairs={{0,4},{4,0},{1,5},{5,1},{2,6},{6,2},{3,7},{7,3},{8,12},{12,8},{9,1... | collective-permute-start | bytes 589832 | tf_op jit(solution)/shard_map/ppermute | solution.py:311
  47.6 1.6 %copy-start.2 = (bf16[16,128,512]{2,1,0:T(8,128)(2,1)S(1)}, bf16[16,128,512]{2,1,0:T(8,128)(2,1)}, u32[]{:S(2)}) copy-start(bf16[16,128,512]{2,1,0:T(8,128)(2,1)} %refs_4_.1) | copy-start | bytes 6291460
  49.2 0.9 copy-start.6
  51.9 14.3 %copy-start.3 = (bf16[16,512,128]{2,1,0:T(8,128)(2,1)S(1)}, bf16[16,512,128]{2,1,0:T(8,128)(2,1)}, u32[]{:S(2)}) copy-start(bf16[16,512,128]{2,1,0:T(8,128)(2,1)} %refs_7_.1) | copy-start | bytes 6291460
  66.2 14.2 %copy-start.1 = (bf16[144,2048]{1,0:T(8,128)(2,1)S(1)}, bf16[144,2048]{1,0:T(8,128)(2,1)}, u32[]{:S(2)}) copy-start(bf16[144,2048]{1,0:T(8,128)(2,1)} %shard_map.91.own_ref.refs_0_) | copy-start | bytes 1769476
  78.3 1.6 %collective-permute-start.11 = (bf16[64,2176]{1,0:T(8,128)(2,1)S(1)}, bf16[64,2176]{1,0:T(8,128)(2,1)S(1)}, u32[]{:S(2)}, u32[]{:S(2)}) collective-permute-start(bf16[64,2176]{1,0:T(8,128)(2,1)S(1)} %get-tuple-element.41), channel_id=1, source_target_pairs={{0,4},{4,0},{1,5},{5,1},{2,6},{6,2},{3,7},{7,3},{8,12},{12,8},{9,1... | collective-permute-start | bytes 835592 | tf_op jit(solution)/shard_map/ppermute | solution.py:269
  80.4 5.6 %collective-permute-start.13 = (bf16[144,2048]{1,0:T(8,128)(2,1)S(1)}, bf16[144,2048]{1,0:T(8,128)(2,1)S(1)}, u32[]{:S(2)}, u32[]{:S(2)}) collective-permute-start(bf16[144,2048]{1,0:T(8,128)(2,1)S(1)} %copy-done.1), channel_id=1, source_target_pairs={{0,4},{4,0},{1,5},{5,1},{2,6},{6,2},{3,7},{7,3},{8,12},{12,8},{9,1... | collective-permute-start | bytes 1769480 | tf_op jit(solution)/shard_map/ppermute | solution.py:327
  80.9 5.1 %collective-permute-start.12 = (bf16[32,2176]{1,0:T(8,128)(2,1)S(1)}, bf16[32,2176]{1,0:T(8,128)(2,1)S(1)}, u32[]{:S(2)}, u32[]{:S(2)}) collective-permute-start(bf16[32,2176]{1,0:T(8,128)(2,1)S(1)} %get-tuple-element.44), channel_id=1, source_target_pairs={{0,16},{16,0},{1,17},{17,1},{2,18},{18,2},{3,19},{19,3},{4,20},{20... | collective-permute-start | bytes 417800 | tf_op jit(solution)/shard_map/ppermute | solution.py:269
  86.3 10.1 %collective-permute-start.15 = (bf16[144,2048]{1,0:T(8,128)(2,1)S(1)}, bf16[144,2048]{1,0:T(8,128)(2,1)S(1)}, u32[]{:S(2)}, u32[]{:S(2)}) collective-permute-start(bf16[144,2048]{1,0:T(8,128)(2,1)S(1)} %collective-permute-done.far_ref.refs_1_), channel_id=1, source_target_pairs={{0,4},{4,0},{1,5},{5,1},{2,6},{6,2},{3,7},{7,3},{8,12},{12,8},{9,1... | collective-permute-start | bytes 1769480 | tf_op jit(solution)/shard_map/ppermute | solution.py:330
  87.4 9.1 %collective-permute-start.14 = (bf16[16,2176]{1,0:T(8,128)(2,1)S(1)}, bf16[16,2176]{1,0:T(8,128)(2,1)S(1)}, u32[]{:S(2)}, u32[]{:S(2)}) collective-permute-start(bf16[16,2176]{1,0:T(8,128)(2,1)S(1)} %get-tuple-element.50), channel_id=1, source_target_pairs={{0,8},{8,0},{1,9},{9,1},{2,10},{10,2},{3,11},{11,3},{4,12},{12,4},... | collective-permute-start | bytes 208904 | tf_op jit(solution)/shard_map/ppermute | solution.py:330
  97.9 22.4 %all-to-all-start = ((bf16[16,16,2048]{2,1,0:T(8,128)(2,1)}), bf16[16,16,2048]{2,1,0:T(8,128)(2,1)S(1)}, u32[]{:S(2)}, u32[]{:S(2)}) async-start(bf16[16,16,2048]{2,1,0:T(8,128)(2,1)} %shard_map.99), calls=%async_computation | async-start | bytes 2097152 | tf_op jit(solution)/shard_map/all_to_all | solution.py:336

commit v5 on v4

v5 whole, which is shorter than its diff:
```python
import functools

import jax
import jax.numpy as jnp
from jax import lax
from jax.experimental import pallas as pl
from jax.experimental.pallas import tpu as pltpu
from jax.sharding import Mesh, PartitionSpec as P

ROPE = 64
NOPE = 128
RANK = 512
VDIM = 128
HG = 16
R = 16
GROUP = 8
ROWS = GROUP * R
ITEMS = HG * ROWS
KEYW = RANK + 128
ITEMW = RANK + 256
SENDW = HG * VDIM + 128
SCALE2 = (NOPE + ROPE) ** -0.5 * 1.4426950408889634
NEG = -1e30
CTX = ("y", "x", "z", "c")
RING = (0, 1, 3, 2)
SWAP = ((0, 1), (1, 0))
MIB = 1 << 20


def shift(d):
    return [(i, (i + d) % 4) for i in range(4)]


def call(kernel, out_shape, vmem=40, **kw):
    return pl.pallas_call(
        kernel,
        out_shape=out_shape,
        compiler_params=pltpu.CompilerParams(vmem_limit_bytes=vmem * MIB),
        cost_estimate=pl.CostEstimate(flops=1, bytes_accessed=1, transcendentals=0),
        **kw,
    )


def nt_dot(a, b):
    return lax.dot_general(a, b, (((1,), (1,)), ((), ())), preferred_element_type=jnp.float32)


def pack_keys_kernel(latent_ref, key_rope_ref, pos_ref, key_ref):
    key_ref[:, :RANK] = latent_ref[...]
    pos = pos_ref[...].astype(jnp.float32)
    high = jnp.floor(pos * (1 / 128))
    row = lax.broadcasted_iota(jnp.int32, key_rope_ref.shape, 0)
    ext = jnp.where(row == 0, high, jnp.where(row == 1, pos - high * 128, 0.0))
    ext = jnp.concatenate([key_rope_ref[...].astype(jnp.float32), ext], axis=0)
    key_ref[:, RANK:] = jnp.transpose(ext).astype(jnp.bfloat16)


def pack_keys(latent, k_rope, key_pos):
    return call(
        pack_keys_kernel,
        jax.ShapeDtypeStruct((latent.shape[0], KEYW), jnp.bfloat16),
        vmem=60,
    )(latent, jnp.transpose(k_rope), key_pos)


def pack_queries_kernel(query_ref, rope_ref, out_ref):
    out_ref[:, : HG * NOPE] = query_ref[...]
    out_ref[:, HG * NOPE :] = rope_ref[...]


def pack_queries(query, q_rope):
    return call(
        pack_queries_kernel,
        jax.ShapeDtypeStruct((R, HG * (NOPE + ROPE)), jnp.bfloat16),
        vmem=60,
    )(query, q_rope)


def join_kernel(*refs):
    start = 0
    for ref in refs[:-1]:
        refs[-1][start : start + ref.shape[0]] = ref[...]
        start += ref.shape[0]


def join(parts):
    shape = (sum(part.shape[0] for part in parts), parts[0].shape[1])
    return call(join_kernel, jax.ShapeDtypeStruct(shape, jnp.bfloat16))(*parts)


def absorb_kernel(*refs):
    q_refs, (w_ref, out_ref) = refs[:2], refs[2:]
    lane = lax.broadcasted_iota(jnp.int32, (ROWS, 128), 1)
    row = lax.broadcasted_iota(jnp.int32, (ROWS, 128), 0)
    one_hot = (lane == row).astype(jnp.bfloat16)

    def columns(start):
        return jnp.concatenate([ref[:, start : start + 128] for ref in q_refs], axis=0)

    for h in range(HG):
        rows = slice(h * ROWS, (h + 1) * ROWS)
        latent = jnp.dot(columns(h * NOPE), w_ref[h], preferred_element_type=jnp.float32)
        out_ref[rows, :RANK] = latent.astype(jnp.bfloat16)
        pair = columns(HG * NOPE + (h // 2) * 128).astype(jnp.float32)
        if h % 2:
            pair = pltpu.roll(pair, ROPE, 1)
        rope = jnp.where(lane < ROPE, pair, 0.0)
        out_ref[rows, RANK : RANK + 128] = rope.astype(jnp.bfloat16)
        out_ref[rows, RANK + 128 :] = one_hot


def absorb(queries, w_uk):
    return call(absorb_kernel, jax.ShapeDtypeStruct((ITEMS, ITEMW), jnp.bfloat16))(
        *queries, w_uk
    )


def pack_stats(stats):
    high = stats.astype(jnp.bfloat16).astype(jnp.float32)
    mid = (stats - high).astype(jnp.bfloat16).astype(jnp.float32)
    low = stats - high - mid
    packed = high + pltpu.roll(mid, HG, 1) + pltpu.roll(low, 2 * HG, 1)
    return packed.astype(jnp.bfloat16)


def unpack_stats(packed):
    packed = packed.astype(jnp.float32)
    return packed + pltpu.roll(packed, 128 - HG, 1) + pltpu.roll(packed, 128 - 2 * HG, 1)


def attend_kernel(pieces, last, *refs):
    q_ref, qpos_ref = refs[:2]
    piece_refs = refs[2 : 2 + pieces]
    rest = refs[2 + pieces :]
    if last:
        acc_in, st_in, v_ref, keep_ref, send_ref, key_ref, lse_ref = rest
    else:
        acc_out, st_out, key_ref = rest
    step = pl.program_id(0)

    @pl.when(step == 0)
    def _():
        qpos = qpos_ref[0:1, :]
        start = 0
        for ref in piece_refs:
            rows = slice(start, start + ref.shape[0])
            start += ref.shape[0]
            key_ref[rows, :KEYW] = ref[...]
            ext = ref[:, RANK:].astype(jnp.float32)
            pos = ext[:, ROPE : ROPE + 1] * 128.0 + ext[:, ROPE + 1 : ROPE + 2]
            key_ref[rows, KEYW:] = jnp.where(pos <= qpos, 0.0, NEG).astype(jnp.bfloat16)
        if last:
            lse_ref[...] = jnp.zeros_like(lse_ref)

    tile = q_ref.shape[0]
    scores = nt_dot(q_ref[...], key_ref[...]) * SCALE2
    top = jnp.max(scores, axis=1, keepdims=True)
    if last:
        top = jnp.maximum(top, st_in[:, 0:1])
    weights = jnp.exp2(scores - top)
    total = jnp.sum(weights, axis=1, keepdims=True)
    acc = jnp.dot(
        weights.astype(jnp.bfloat16), key_ref[:, :RANK], preferred_element_type=jnp.float32
    )
    if not last:
        acc_out[...] = acc
        lane = lax.broadcasted_iota(jnp.int32, (tile, 128), 1)
        st_out[...] = jnp.where(lane == 0, top, total)
        return

    keep = jnp.exp2(st_in[:, 0:1] - top)
    total = total + keep * st_in[:, 1:2]
    context = ((acc + keep * acc_in[...]) / total).astype(jnp.bfloat16)
    lse = top + jnp.log2(total)
    half = ROWS // 2
    lane = lax.broadcasted_iota(jnp.int32, (ROWS, 128), 1)
    for i in range(tile // ROWS):
        rows = slice(i * ROWS, (i + 1) * ROWS)
        head = step * (tile // ROWS) + i
        out = jnp.dot(context[rows], v_ref[i], preferred_element_type=jnp.float32)
        out = out.astype(jnp.bfloat16)
        cols = pl.ds(pl.multiple_of(head * VDIM, VDIM), VDIM)
        keep_ref[:, cols] = out[:half]
        send_ref[:, cols] = out[half:]
        lse_ref[...] = jnp.where(lane == head, lse[rows], lse_ref[...])

    @pl.when(step == pl.num_programs(0) - 1)
    def _():
        packed = pack_stats(lse_ref[...])
        keep_ref[:, HG * VDIM :] = packed[:half]
        send_ref[:, HG * VDIM :] = packed[half:]


def attend(q, qpos, pieces, state=None, value_weight=None, tile=512):
    n, keys = len(pieces), sum(piece.shape[0] for piece in pieces)
    last = state is not None
    whole = lambda shape: pl.BlockSpec(shape, lambda i: (0, 0))
    part = lambda width: pl.BlockSpec((tile, width), lambda i: (i, 0))
    carried = [part(RANK), part(128)]
    in_specs = [part(ITEMW), whole((8, 128))] + [whole(piece.shape) for piece in pieces]
    scratch = [pltpu.VMEM((keys, ITEMW), jnp.bfloat16)]
    args = [q, qpos, *pieces]
    if last:
        heads = tile // ROWS
        in_specs += carried + [pl.BlockSpec((heads, RANK, VDIM), lambda i: (i, 0, 0))]
        args += [*state, value_weight]
        half = jax.ShapeDtypeStruct((ROWS // 2, SENDW), jnp.bfloat16)
        out_shape, out_specs = (half, half), [whole((ROWS // 2, SENDW))] * 2
        scratch.append(pltpu.VMEM((ROWS, 128), jnp.float32))
    else:
        out_shape = (
            jax.ShapeDtypeStruct((ITEMS, RANK), jnp.float32),
            jax.ShapeDtypeStruct((ITEMS, 128), jnp.float32),
        )
        out_specs = carried
    return call(
        functools.partial(attend_kernel, n, last),
        out_shape,
        grid=(ITEMS // tile,),
        in_specs=in_specs,
        out_specs=out_specs,
        scratch_shapes=scratch,
    )(*args)


def merge(refs):
    stats = [unpack_stats(ref[:, HG * VDIM :]) for ref in refs]
    top = functools.reduce(jnp.maximum, stats)
    weights = [jnp.exp2(s - top) for s in stats]
    total = sum(weights)
    weights = [w / total for w in weights]
    out = []
    for h in range(HG):
        cols = slice(h * VDIM, (h + 1) * VDIM)
        head = sum(
            ref[:, cols].astype(jnp.float32) * w[:, h : h + 1] for ref, w in zip(refs, weights)
        )
        out.append((cols, head.astype(jnp.bfloat16)))
    return out, top + jnp.log2(total)


def merge_core_kernel(a_ref, b_ref, *out_refs):
    heads, lse = merge((a_ref, b_ref))
    lane = lax.broadcasted_iota(jnp.int32, lse.shape, 1)
    packed = pack_stats(jnp.where(lane < HG, lse, 0.0))
    for cols, head in heads + [(slice(HG * VDIM, SENDW), packed)]:
        for i, ref in enumerate(out_refs):
            ref[:, cols] = head[i * R : (i + 1) * R]


def merge_ring_kernel(*refs):
    heads, _ = merge(refs[:-1])
    for cols, head in heads:
        for i in range(refs[-1].shape[0]):
            refs[-1][i, :, cols] = head


def project_kernel(zc_ref, x_ref, *refs):
    out_ref = refs[-1]
    z, c = zc_ref[0], zc_ref[1]
    for k in range(4):
        to_z = z if k % 2 == 0 else 1 - z
        to_c = c if k < 2 else 1 - c
        out_ref[to_z * 2 + to_c] = nt_dot(x_ref[...], refs[k][...]).astype(jnp.bfloat16)


def finish_kernel(sums_ref, out_ref, row_ref):
    ncol = sums_ref.shape[2]
    row_ref[...] = jnp.zeros_like(row_ref)
    for zc in range(4):
        total = sum(sums_ref[zc * 4 + h].astype(jnp.float32) for h in range(4))
        for i in range(4):
            start = (i * 4 + zc) * R
            row_ref[start : start + R, :ncol] = total[i * R : (i + 1) * R]
    out_ref[...] = jnp.transpose(row_ref[...])[:ncol].astype(jnp.bfloat16)


def local(query_unrotated, q_rope, latent, k_rope, key_pos, offset, w_uk, value_up_weight, w_out):
    y, x, z, c = (lax.axis_index(n) for n in CTX)

    keys = pack_keys(latent[0], k_rope[0], key_pos)
    q_own = pack_queries(query_unrotated, q_rope)
    z_keys = lax.ppermute(keys, "z", SWAP)
    up, down = (lax.ppermute(keys, "y", shift(d)) for d in (1, 3))
    q_ring = [lax.ppermute(q_own, "x", shift(d)) for d in RING[1:]]
    z_keys, up, down, q_ring, keys, q_own = lax.optimization_barrier(
        (z_keys, up, down, q_ring, keys, q_own)
    )
    near = [join([keys, z_keys]), up, down]
    far = [lax.ppermute(near[0], "y", shift(2))]
    far += [lax.ppermute(z_keys, "y", shift(d)) for d in (1, 3)]
    q_chip = join([q_own, *q_ring])
    q_core = lax.ppermute(q_chip, "c", SWAP)
    q_core, w_own = lax.optimization_barrier((q_core, jnp.transpose(w_out)))
    z_w = lax.ppermute(w_own, "z", SWAP)

    row = jnp.arange(ROWS, dtype=jnp.int32)
    part = row // R
    row_x = (x - jnp.array(RING, jnp.int32)[part % 4]) % 4
    row_c = jnp.where(part < 4, c, 1 - c)
    row = (((y * 4 + row_x) * 2 + z) * 2 + row_c) * R + row % R
    qpos = jnp.broadcast_to((offset[0] + row).astype(jnp.float32)[None, :], (8, ROWS))

    q = absorb((q_chip, q_core), w_uk)
    state = attend(q, qpos, near)
    state, far = lax.optimization_barrier((state, far))
    keep, send = attend(q, qpos, far, state, value_up_weight)

    z_w, send = lax.optimization_barrier((z_w, send))
    parts = call(
        merge_core_kernel, [jax.ShapeDtypeStruct((R, SENDW), jnp.bfloat16)] * 4
    )(keep, lax.ppermute(send, "c", SWAP))
    parts = [parts[0]] + [
        lax.ppermute(part, "x", shift(-d % 4)) for part, d in zip(parts[1:], RING[1:])
    ]
    heads = call(merge_ring_kernel, jax.ShapeDtypeStruct((16, R, HG * VDIM), jnp.bfloat16))(
        *parts
    )

    rows = lax.all_to_all(heads, ("y", "x"), 0, 0, tiled=True).reshape(16 * R, HG * VDIM)
    c_w = lax.ppermute(w_own, "c", SWAP)
    zc_w = lax.ppermute(z_w, "c", SWAP)
    ncol = w_out.shape[1]
    sums = call(
        project_kernel,
        jax.ShapeDtypeStruct((4, 16 * R, ncol), jnp.bfloat16),
        in_specs=[pl.BlockSpec(memory_space=pltpu.SMEM)]
        + [pl.BlockSpec(memory_space=pltpu.VMEM)] * 5,
    )(jnp.stack([z, c]), rows, w_own, z_w, c_w, zc_w)
    sums = lax.all_to_all(
        sums.reshape(16, 4 * R, ncol), ("z", "c", "head"), 0, 0, tiled=True
    )
    out = call(
        finish_kernel,
        jax.ShapeDtypeStruct((ncol, 16 * R), jnp.bfloat16),
        scratch_shapes=[pltpu.VMEM((16 * R, 128), jnp.float32)],
    )(sums)
    return jnp.transpose(out)


def solution(mesh):
    grid = Mesh(mesh.devices.reshape(4, 4, 2, 2, 4), CTX + ("head",))
    return jax.shard_map(
        local,
        mesh=grid,
        in_specs=(
            P(CTX, "head"),
            P(CTX, "head"),
            P(None, CTX, None),
            P(None, CTX, None),
            P(None, CTX),
            P(),
            P("head", None, None),
            P("head", None, None),
            P("head", CTX),
        ),
        out_specs=P("head", CTX),
        check_vma=False,
    )
```

time: 143 us -> 122 us (0.85)
  waiting for transfers between devices: 45.5 us -> 30.6 us
  Pallas kernels: 36.6 us -> 29.5 us
  local copies, waits for them, and re-layouts: 4.27 us -> 2.83 us
    ppermute x16 -> x17, waiting for transfers between devices: 29.4 us -> 20.4 us  [the longest x2 6.75 us: local(): far += [lax.ppermute(z_keys, 'y', shift(d)) for d in (1, 3)]]
    pallas_call x2, Pallas kernels: 26.3 us -> 19.3 us  [attend(): call(functools.partial(attend_kernel, n, last), out_shape, grid=(ITEMS //...]
    all_to_all x1, waiting for transfers between devices: 16.1 us -> 10.2 us  [local(): lax.all_to_all(heads, ('y', 'x'), 0, 0, tiled=True)]
    ppermute x16 -> x17, starting transfers between devices: 29.3 us -> 31.2 us  [the longest x1 6.01 us: local(): z_keys = lax.ppermute(keys, 'z', SWAP)]
    unnamed x14 -> x18, local copies, waits for them, and re-layouts: 4.27 us -> 2.83 us
  transfers between devices with their start and end apart: 17 -> 18, of which waited for: 6 -> 10; matrix products, arithmetic and copies ran while one was open for 0% -> 0% of each run, Pallas kernels for 13% -> 19%
where the time goes in v5:
time: 122 us; the launch traced here: 121 us
  starting transfers between devices  36.4 us (30%)
  waiting for transfers between devices  30.6 us (25%)
  Pallas kernels  29.5 us (24%)
  blocking collectives  20.9 us (17%)
  local copies, waits for them, and re-layouts  2.83 us (2%)
    all_to_all x1, blocking collectives, local(): lax.all_to_all(sums.reshape(16, 4 * R, ncol), ('z', 'c', 'head'), 0, 0, t...  20.9 us
    pallas_call x2, Pallas kernels, attend(): call(functools.partial(attend_kernel, n, last), out_shape, grid=(ITEMS //...  19.3 us
    all_to_all x1, waiting for transfers between devices, local(): lax.all_to_all(heads, ('y', 'x'), 0, 0, tiled=True)  10.2 us
    ppermute x2, waiting for transfers between devices, local(): far += [lax.ppermute(z_keys, 'y', shift(d)) for d in (1, 3)]  6.75 us
    ppermute x3, waiting for transfers between devices, local(): q_ring = [lax.ppermute(q_own, 'x', shift(d)) for d in RING[1:]]  6.66 us
    ppermute x1, starting transfers between devices, local(): z_keys = lax.ppermute(keys, 'z', SWAP)  6.01 us
    all_to_all x1, starting transfers between devices, local(): lax.all_to_all(heads, ('y', 'x'), 0, 0, tiled=True)  5.18 us
    ppermute x1, starting transfers between devices, local(): z_w = lax.ppermute(w_own, 'z', SWAP)  4.5 us
  transfers between devices with their start and end apart: 18, of which 10 were waited for; matrix products, arithmetic and copies ran while one was open for 0% of the time, Pallas kernels for 19%

profile of v5, /device:TPU:33, one launch (start us, length us, event | category | flops | bytes accessed | tf_op | source)
XLA Modules:
  0.0 121.2 jit_solution(1977802985880428874)
XLA Ops:
  0.0 1.9 %shard_map.100.refs_0_ = bf16[256,640]{1,0:T(8,128)(2,1)} custom-call(bf16[256,512]{1,0:T(8,128)(2,1)} %bitcast.23, bf16[64,256]{1,0:T(8,128)(2,1)} %bitcast.24, s32[1,256]{1,0:T(1,128)} %pos_ref.1), custom_call_target="tpu_custom_call" | custom-call | flops 1 | bytes 1 | tf_op jit(solution)/shard_map/pallas_call | solution.py:59
  1.9 6.0 %collective-permute-start = (bf16[256,640]{1,0:T(8,128)(2,1)}, bf16[256,640]{1,0:T(8,128)(2,1)}, u32[]{:S(2)}, u32[]{:S(2)}) collective-permute-start(bf16[256,640]{1,0:T(8,128)(2,1)} %shard_map.100.refs_0_), channel_id=1, source_target_pairs={{0,8},{8,0},{1,9},{9,1},{2,10},{10,2},{3,11},{11,3},{4,12},{12,4},... | collective-permute-start | bytes 983048 | tf_op jit(solution)/shard_map/ppermute | solution.py:283
  8.0 1.3 %collective-permute-start.1 = (bf16[256,640]{1,0:T(8,128)(2,1)}, bf16[256,640]{1,0:T(8,128)(2,1)S(1)}, u32[]{:S(2)}, u32[]{:S(2)}) collective-permute-start(bf16[256,640]{1,0:T(8,128)(2,1)} %shard_map.100.refs_0_), channel_id=1, source_target_pairs={{0,64},{64,128},{128,192},{192,0},{1,65},{65,129},{129,193},{193,1... | collective-permute-start | bytes 983048 | tf_op jit(solution)/shard_map/ppermute | solution.py:284
  9.3 1.4 %collective-permute-start.2 = (bf16[256,640]{1,0:T(8,128)(2,1)}, bf16[256,640]{1,0:T(8,128)(2,1)S(1)}, u32[]{:S(2)}, u32[]{:S(2)}) collective-permute-start(bf16[256,640]{1,0:T(8,128)(2,1)} %shard_map.100.refs_0_), channel_id=1, source_target_pairs={{0,192},{64,0},{128,64},{192,128},{1,193},{65,1},{129,65},{193,129... | collective-permute-start | bytes 983048 | tf_op jit(solution)/shard_map/ppermute | solution.py:284
  10.7 1.5 %shard_map.101.refs_0_ = bf16[16,3072]{1,0:T(8,128)(2,1)} custom-call(bf16[16,2048]{1,0:T(8,128)(2,1)} %query_ref.1, bf16[16,1024]{1,0:T(8,128)(2,1)} %rope_ref.1), custom_call_target="tpu_custom_call" | custom-call | flops 1 | bytes 1 | tf_op jit(solution)/shard_map/pallas_call | solution.py:72
  12.2 1.2 collective-permute-start.3
  13.4 1.5 %collective-permute-start.4 = (bf16[16,3072]{1,0:T(8,128)(2,1)}, bf16[16,3072]{1,0:T(8,128)(2,1)S(1)}, u32[]{:S(2)}, u32[]{:S(2)}) collective-permute-start(bf16[16,3072]{1,0:T(8,128)(2,1)} %shard_map.101.refs_0_), channel_id=1, source_target_pairs={{0,48},{16,0},{32,16},{48,32},{1,49},{17,1},{33,17},{49,33},{2,50}... | collective-permute-start | bytes 294920 | tf_op jit(solution)/shard_map/ppermute | solution.py:285
  14.9 2.6 %collective-permute-done.3.refs_1_ = bf16[16,3072]{1,0:T(8,128)(2,1)S(1)} collective-permute-done((bf16[16,3072]{1,0:T(8,128)(2,1)}, bf16[16,3072]{1,0:T(8,128)(2,1)S(1)}, u32[]{:S(2)}, u32[]{:S(2)}) %collective-permute-start.3) | collective-permute-done | bytes 98336 | tf_op jit(solution)/shard_map/ppermute | solution.py:285
  17.5 1.5 %collective-permute-start.5 = (bf16[16,3072]{1,0:T(8,128)(2,1)}, bf16[16,3072]{1,0:T(8,128)(2,1)S(1)}, u32[]{:S(2)}, u32[]{:S(2)}) collective-permute-start(bf16[16,3072]{1,0:T(8,128)(2,1)} %shard_map.101.refs_0_), channel_id=1, source_target_pairs={{0,32},{16,48},{32,0},{48,16},{1,33},{17,49},{33,1},{49,17},{2,34}... | collective-permute-start | bytes 294920 | tf_op jit(solution)/shard_map/ppermute | solution.py:285
  19.0 0.0 collective-permute-done.4.refs_2_
  19.0 4.0 %collective-permute-done.5.refs_3_ = bf16[16,3072]{1,0:T(8,128)(2,1)S(1)} collective-permute-done((bf16[16,3072]{1,0:T(8,128)(2,1)}, bf16[16,3072]{1,0:T(8,128)(2,1)S(1)}, u32[]{:S(2)}, u32[]{:S(2)}) %collective-permute-start.5) | collective-permute-done | bytes 98336 | tf_op jit(solution)/shard_map/ppermute | solution.py:285
  23.1 0.8 copy-done.7
  23.9 0.9 copy-done.4
  24.8 3.0 %collective-permute-start.6 = (bf16[64,3072]{1,0:T(8,128)(2,1)S(1)}, bf16[64,3072]{1,0:T(8,128)(2,1)S(1)}, u32[]{:S(2)}, u32[]{:S(2)}) collective-permute-start(bf16[64,3072]{1,0:T(8,128)(2,1)S(1)} %shard_map.102.refs_0_), channel_id=1, source_target_pairs={{0,4},{4,0},{1,5},{5,1},{2,6},{6,2},{3,7},{7,3},{8,12},{12,8},{9,1... | collective-permute-start | bytes 1179656 | tf_op jit(solution)/shard_map/ppermute | solution.py:293
  27.8 1.0 copy-done.2
  28.8 1.0 shard_map.104.refs_2_
  29.8 1.8 %collective-permute-start.7 = (bf16[512,640]{1,0:T(8,128)(2,1)S(1)}, bf16[512,640]{1,0:T(8,128)(2,1)}, u32[]{:S(2)}, u32[]{:S(2)}) collective-permute-start(bf16[512,640]{1,0:T(8,128)(2,1)S(1)} %shard_map.104.refs_2_), channel_id=1, source_target_pairs={{0,128},{64,192},{128,0},{192,64},{1,129},{65,193},{129,1},{193,65... | collective-permute-start | bytes 1966088 | tf_op jit(solution)/shard_map/ppermute | solution.py:290
  31.6 4.5 %collective-permute-start.10 = (bf16[112,2048]{1,0:T(8,128)(2,1)}, bf16[112,2048]{1,0:T(8,128)(2,1)}, u32[]{:S(2)}, u32[]{:S(2)}) collective-permute-start(bf16[112,2048]{1,0:T(8,128)(2,1)} %bitcast.20), channel_id=1, source_target_pairs={{0,8},{8,0},{1,9},{9,1},{2,10},{10,2},{3,11},{11,3},{4,12},{12,4},... | collective-permute-start | bytes 1376264 | tf_op jit(solution)/shard_map/ppermute | solution.py:295
  36.1 0.4 collective-permute-start.8
  36.5 2.3 %collective-permute-start.9 = (bf16[256,640]{1,0:T(8,128)(2,1)}, bf16[256,640]{1,0:T(8,128)(2,1)}, u32[]{:S(2)}, u32[]{:S(2)}) collective-permute-start(bf16[256,640]{1,0:T(8,128)(2,1)} %collective-permute-done.refs_1_), channel_id=1, source_target_pairs={{0,192},{64,0},{128,64},{192,128},{1,193},{65,1},{129,65},{193,129... | collective-permute-start | bytes 983048 | tf_op jit(solution)/shard_map/ppermute | solution.py:291
  39.5 0.8 shard_map.103.refs_0_
  40.3 0.0 copy-start.1
  40.3 0.1 copy-done.6
  40.4 0.1 copy-done.8
  40.5 7.9 %shard_map.105 = (f32[2048,512]{1,0:T(8,128)S(1)}, f32[2048,128]{1,0:T(8,128)S(1)}) custom-call(bf16[2048,768]{1,0:T(8,128)(2,1)S(1)} %shard_map.103.refs_0_, f32[8,128]{1,0:T(8,128)S(1)} %broadcast_in_dim.17.refs_1_, bf16[512,640]{1,0:T(8,128)(2,1)S(1)} %shard_map.104.refs_2_, bf16[256,640]{1,0:T(8,128)(2,1)S(1)} %copy-done.6, bf16[256,640]{1,0:T(8,128)(2,1)S(1)} %copy-done.8), custom_call_target="tpu_custom_call" | custom-call | flops 1 | bytes 1 | tf_op jit(solution)/shard_map/pallas_call | solution.py:216
  48.4 6.7 %collective-permute-done.8.refs_3_ = bf16[256,640]{1,0:T(8,128)(2,1)} collective-permute-done((bf16[256,640]{1,0:T(8,128)(2,1)}, bf16[256,640]{1,0:T(8,128)(2,1)}, u32[]{:S(2)}, u32[]{:S(2)}) %collective-permute-start.8) | collective-permute-done | bytes 327712 | tf_op jit(solution)/shard_map/ppermute | solution.py:291
  55.2 11.4 %shard_map.106 = (bf16[64,2176]{1,0:T(8,128)(2,1)S(1)}, bf16[64,2176]{1,0:T(8,128)(2,1)S(1)}) custom-call(bf16[2048,768]{1,0:T(8,128)(2,1)S(1)} %shard_map.103.refs_0_, f32[8,128]{1,0:T(8,128)S(1)} %broadcast_in_dim.17.refs_1_, bf16[512,640]{1,0:T(8,128)(2,1)} %collective-permute-done.7.refs_2_, bf16[256,640]{1,0:T(8,128)(2,1)} %collective-permute-done.8.refs_3_, ...), custom_call_target="tpu_custom_call" | custom-call | flops 1 | bytes 1 | tf_op jit(solution)/shard_map/pallas_call | solution.py:216
  66.6 0.0 copy-start.3
  66.6 0.6 collective-permute-start.11
  67.2 1.2 collective-permute-done.11.b_ref
  68.4 0.5 shard_map.107
  68.8 1.3 %collective-permute-start.12 = (bf16[16,2176]{1,0:T(8,128)(2,1)S(1)}, bf16[16,2176]{1,0:T(8,128)(2,1)S(1)}, u32[]{:S(2)}, u32[]{:S(2)}) collective-permute-start(bf16[16,2176]{1,0:T(8,128)(2,1)S(1)} %get-tuple-element.51), channel_id=1, source_target_pairs={{0,48},{16,0},{32,16},{48,32},{1,49},{17,1},{33,17},{49,33},{2,50}... | collective-permute-start | bytes 208904 | tf_op jit(solution)/shard_map/ppermute | solution.py:314
  70.2 0.2 collective-permute-start.13
  70.4 1.5 %collective-permute-start.14 = (bf16[16,2176]{1,0:T(8,128)(2,1)S(1)}, bf16[16,2176]{1,0:T(8,128)(2,1)S(1)}, u32[]{:S(2)}, u32[]{:S(2)}) collective-permute-start(bf16[16,2176]{1,0:T(8,128)(2,1)S(1)} %get-tuple-element.53), channel_id=1, source_target_pairs={{0,32},{16,48},{32,0},{48,16},{1,33},{17,49},{33,1},{49,17},{2,34}... | collective-permute-start | bytes 208904 | tf_op jit(solution)/shard_map/ppermute | solution.py:314
  71.9 0.2 collective-permute-done.12.refs_1_
  72.1 2.7 %collective-permute-done.13.refs_2_ = bf16[16,2176]{1,0:T(8,128)(2,1)S(1)} collective-permute-done((bf16[16,2176]{1,0:T(8,128)(2,1)S(1)}, bf16[16,2176]{1,0:T(8,128)(2,1)S(1)}, u32[]{:S(2)}, u32[]{:S(2)}) %collective-permute-start.13) | collective-permute-done | bytes 69664 | tf_op jit(solution)/shard_map/ppermute | solution.py:314
  74.8 0.8 collective-permute-done.14.refs_3_
  75.6 1.5 %shard_map.108 = bf16[16,16,2048]{2,1,0:T(8,128)(2,1)} custom-call(bf16[16,2176]{1,0:T(8,128)(2,1)S(1)} %get-tuple-element.50.refs_0_, bf16[16,2176]{1,0:T(8,128)(2,1)S(1)} %collective-permute-done.12.refs_1_, bf16[16,2176]{1,0:T(8,128)(2,1)S(1)} %collective-permute-done.13.refs_2_, bf16[16,2176]{1,0:T(8,128)(2,1)S(1)} %collective-permute-done.14.refs_3_), custom_call_target="tpu_custom_call" | custom-call | flops 1 | bytes 1 | tf_op jit(solution)/shard_map/pallas_call | solution.py:316
  77.0 5.2 %all-to-all-start = ((bf16[16,16,2048]{2,1,0:T(8,128)(2,1)}), bf16[16,16,2048]{2,1,0:T(8,128)(2,1)S(1)}, u32[]{:S(2)}, u32[]{:S(2)}) async-start(bf16[16,16,2048]{2,1,0:T(8,128)(2,1)} %shard_map.108), calls=%async_computation | async-start | bytes 2097152 | tf_op jit(solution)/shard_map/all_to_all | solution.py:320
  82.2 2.5 %collective-permute-start.15 = (bf16[112,2048]{1,0:T(8,128)(2,1)S(1)}, bf16[112,2048]{1,0:T(8,128)(2,1)S(1)}, u32[]{:S(2)}, u32[]{:S(2)}) collective-permute-start(bf16[112,2048]{1,0:T(8,128)(2,1)S(1)} %bitcast.21), channel_id=1, source_target_pairs={{0,4},{4,0},{1,5},{5,1},{2,6},{6,2},{3,7},{7,3},{8,12},{12,8},{9,1... | collective-permute-start | bytes 1376264 | tf_op jit(solution)/shard_map/ppermute | solution.py:321
  84.7 0.1 collective-permute-start.16
  84.8 0.1 pad_add_fusion.zc_ref
  84.9 1.3 %collective-permute-done.15.refs_2_ = bf16[112,2048]{1,0:T(8,128)(2,1)S(1)} collective-permute-done((bf16[112,2048]{1,0:T(8,128)(2,1)S(1)}, bf16[112,2048]{1,0:T(8,128)(2,1)S(1)}, u32[]{:S(2)}, u32[]{:S(2)}) %collective-permute-start.15) | collective-permute-done | bytes 458784 | tf_op jit(solution)/shard_map/ppermute | solution.py:321
  86.1 0.9 collective-permute-done.16.refs_3_
  87.0 10.2 %all-to-all-done = bf16[16,16,2048]{2,1,0:T(8,128)(2,1)S(1)} async-done(((bf16[16,16,2048]{2,1,0:T(8,128)(2,1)}), bf16[16,16,2048]{2,1,0:T(8,128)(2,1)S(1)}, u32[]{:S(2)}, u32[]{:S(2)}) %all-to-all-start) | async-done | bytes 1048608 | tf_op jit(solution)/shard_map/all_to_all | solution.py:320
  97.2 2.3 %shard_map.109 = bf16[4,256,112]{2,1,0:T(8,128)(2,1)S(1)} custom-call(s32[2]{0:T(128)S(1)} %pad_add_fusion.zc_ref, bf16[256,2048]{1,0:T(8,128)(2,1)S(1)} %bitcast.18, bf16[112,2048]{1,0:T(8,128)(2,1)S(1)} %bitcast.22, bf16[112,2048]{1,0:T(8,128)(2,1)} %collective-permute-done.10.refs_1_, bf16[112,2048]{1,0:T(8,128)(2,1)S(1)} %collective-permute-done.15.refs_2_, ...), custom_call_target="tpu_custom_call" | custom-call | flops 1 | bytes 1 | tf_op jit(solution)/shard_map/pallas_call | solution.py:324
  99.5 20.9 %all_to_all.10.sums_ref = bf16[16,64,112]{2,1,0:T(8,128)(2,1)S(1)} all-to-all(bf16[16,64,112]{2,1,0:T(8,128)(2,1)S(1)} %bitcast.19), channel_id=1, replica_groups=mesh['y'=4,'x'=4,'z'=2,'c'=2,'head'=4] {'z','c','head'}, dimensions={0} | all-to-all | bytes 458752 | tf_op jit(solution)/shard_map/all_to_all | solution.py:330
  120.4 0.7 shard_map.110
  (21 shorter events, 0.1 us)
Async XLA Ops:
  0.0 39.5 %copy-start = (bf16[16,128,512]{2,1,0:T(8,128)(2,1)S(1)}, bf16[16,128,512]{2,1,0:T(8,128)(2,1)}, u32[]{:S(2)}) copy-start(bf16[16,128,512]{2,1,0:T(8,128)(2,1)} %refs_2_.1) | copy-start | bytes 6291460
  1.9 21.1 %collective-permute-start = (bf16[256,640]{1,0:T(8,128)(2,1)}, bf16[256,640]{1,0:T(8,128)(2,1)}, u32[]{:S(2)}, u32[]{:S(2)}) collective-permute-start(bf16[256,640]{1,0:T(8,128)(2,1)} %shard_map.100.refs_0_), channel_id=1, source_target_pairs={{0,8},{8,0},{1,9},{9,1},{2,10},{10,2},{3,11},{11,3},{4,12},{12,4},... | collective-permute-start | bytes 983048 | tf_op jit(solution)/shard_map/ppermute | solution.py:283
  8.0 15.1 %collective-permute-start.1 = (bf16[256,640]{1,0:T(8,128)(2,1)}, bf16[256,640]{1,0:T(8,128)(2,1)S(1)}, u32[]{:S(2)}, u32[]{:S(2)}) collective-permute-start(bf16[256,640]{1,0:T(8,128)(2,1)} %shard_map.100.refs_0_), channel_id=1, source_target_pairs={{0,64},{64,128},{128,192},{192,0},{1,65},{65,129},{129,193},{193,1... | collective-permute-start | bytes 983048 | tf_op jit(solution)/shard_map/ppermute | solution.py:284
  9.3 13.8 %collective-permute-start.2 = (bf16[256,640]{1,0:T(8,128)(2,1)}, bf16[256,640]{1,0:T(8,128)(2,1)S(1)}, u32[]{:S(2)}, u32[]{:S(2)}) collective-permute-start(bf16[256,640]{1,0:T(8,128)(2,1)} %shard_map.100.refs_0_), channel_id=1, source_target_pairs={{0,192},{64,0},{128,64},{192,128},{1,193},{65,1},{129,65},{193,129... | collective-permute-start | bytes 983048 | tf_op jit(solution)/shard_map/ppermute | solution.py:284
  12.2 5.3 %collective-permute-start.3 = (bf16[16,3072]{1,0:T(8,128)(2,1)}, bf16[16,3072]{1,0:T(8,128)(2,1)S(1)}, u32[]{:S(2)}, u32[]{:S(2)}) collective-permute-start(bf16[16,3072]{1,0:T(8,128)(2,1)} %shard_map.101.refs_0_), channel_id=1, source_target_pairs={{0,16},{16,32},{32,48},{48,0},{1,17},{17,33},{33,49},{49,1},{2,18}... | collective-permute-start | bytes 294920 | tf_op jit(solution)/shard_map/ppermute | solution.py:285
  13.4 5.6 %collective-permute-start.4 = (bf16[16,3072]{1,0:T(8,128)(2,1)}, bf16[16,3072]{1,0:T(8,128)(2,1)S(1)}, u32[]{:S(2)}, u32[]{:S(2)}) collective-permute-start(bf16[16,3072]{1,0:T(8,128)(2,1)} %shard_map.101.refs_0_), channel_id=1, source_target_pairs={{0,48},{16,0},{32,16},{48,32},{1,49},{17,1},{33,17},{49,33},{2,50}... | collective-permute-start | bytes 294920 | tf_op jit(solution)/shard_map/ppermute | solution.py:285
  17.5 5.6 %collective-permute-start.5 = (bf16[16,3072]{1,0:T(8,128)(2,1)}, bf16[16,3072]{1,0:T(8,128)(2,1)S(1)}, u32[]{:S(2)}, u32[]{:S(2)}) collective-permute-start(bf16[16,3072]{1,0:T(8,128)(2,1)} %shard_map.101.refs_0_), channel_id=1, source_target_pairs={{0,32},{16,48},{32,0},{48,16},{1,33},{17,49},{33,1},{49,17},{2,34}... | collective-permute-start | bytes 294920 | tf_op jit(solution)/shard_map/ppermute | solution.py:285
  23.1 8.5 %copy-start.5 = (bf16[256,640]{1,0:T(8,128)(2,1)}, bf16[256,640]{1,0:T(8,128)(2,1)S(1)}, u32[]{:S(2)}) copy-start(bf16[256,640]{1,0:T(8,128)(2,1)S(1)} %collective-permute-done.1.refs_3_) | copy-start | bytes 983044
  23.1 0.8 copy-start.7
  23.9 0.9 copy-start.4
  24.8 6.8 %collective-permute-start.6 = (bf16[64,3072]{1,0:T(8,128)(2,1)S(1)}, bf16[64,3072]{1,0:T(8,128)(2,1)S(1)}, u32[]{:S(2)}, u32[]{:S(2)}) collective-permute-start(bf16[64,3072]{1,0:T(8,128)(2,1)S(1)} %shard_map.102.refs_0_), channel_id=1, source_target_pairs={{0,4},{4,0},{1,5},{5,1},{2,6},{6,2},{3,7},{7,3},{8,12},{12,8},{9,1... | collective-permute-start | bytes 1179656 | tf_op jit(solution)/shard_map/ppermute | solution.py:293
  27.8 1.0 copy-start.2
  29.8 25.4 %collective-permute-start.7 = (bf16[512,640]{1,0:T(8,128)(2,1)S(1)}, bf16[512,640]{1,0:T(8,128)(2,1)}, u32[]{:S(2)}, u32[]{:S(2)}) collective-permute-start(bf16[512,640]{1,0:T(8,128)(2,1)S(1)} %shard_map.104.refs_2_), channel_id=1, source_target_pairs={{0,128},{64,192},{128,0},{192,64},{1,129},{65,193},{129,1},{193,65... | collective-permute-start | bytes 1966088 | tf_op jit(solution)/shard_map/ppermute | solution.py:290
  31.6 35.0 %collective-permute-start.10 = (bf16[112,2048]{1,0:T(8,128)(2,1)}, bf16[112,2048]{1,0:T(8,128)(2,1)}, u32[]{:S(2)}, u32[]{:S(2)}) collective-permute-start(bf16[112,2048]{1,0:T(8,128)(2,1)} %bitcast.20), channel_id=1, source_target_pairs={{0,8},{8,0},{1,9},{9,1},{2,10},{10,2},{3,11},{11,3},{4,12},{12,4},... | collective-permute-start | bytes 1376264 | tf_op jit(solution)/shard_map/ppermute | solution.py:295
  36.1 19.1 %collective-permute-start.8 = (bf16[256,640]{1,0:T(8,128)(2,1)}, bf16[256,640]{1,0:T(8,128)(2,1)}, u32[]{:S(2)}, u32[]{:S(2)}) collective-permute-start(bf16[256,640]{1,0:T(8,128)(2,1)} %collective-permute-done.refs_1_), channel_id=1, source_target_pairs={{0,64},{64,128},{128,192},{192,0},{1,65},{65,129},{129,193},{193,1... | collective-permute-start | bytes 983048 | tf_op jit(solution)/shard_map/ppermute | solution.py:291
  36.5 18.7 %collective-permute-start.9 = (bf16[256,640]{1,0:T(8,128)(2,1)}, bf16[256,640]{1,0:T(8,128)(2,1)}, u32[]{:S(2)}, u32[]{:S(2)}) collective-permute-start(bf16[256,640]{1,0:T(8,128)(2,1)} %collective-permute-done.refs_1_), channel_id=1, source_target_pairs={{0,192},{64,0},{128,64},{192,128},{1,193},{65,1},{129,65},{193,129... | collective-permute-start | bytes 983048 | tf_op jit(solution)/shard_map/ppermute | solution.py:291
  39.4 1.0 copy-start.6
  39.5 1.1 copy-start.8
  40.3 14.9 %copy-start.1 = (bf16[16,512,128]{2,1,0:T(8,128)(2,1)S(1)}, bf16[16,512,128]{2,1,0:T(8,128)(2,1)}, u32[]{:S(2)}) copy-start(bf16[16,512,128]{2,1,0:T(8,128)(2,1)} %refs_7_.1) | copy-start | bytes 6291460
  66.6 15.7 %copy-start.3 = (bf16[2048,112]{0,1:T(8,128)(2,1)S(1)}, bf16[2048,112]{0,1:T(8,128)(2,1)}, u32[]{:S(2)}) copy-start(bf16[2048,112]{0,1:T(8,128)(2,1)} %param.18) | copy-start | bytes 1376260
  66.6 1.8 %collective-permute-start.11 = (bf16[64,2176]{1,0:T(8,128)(2,1)S(1)}, bf16[64,2176]{1,0:T(8,128)(2,1)S(1)}, u32[]{:S(2)}, u32[]{:S(2)}) collective-permute-start(bf16[64,2176]{1,0:T(8,128)(2,1)S(1)} %get-tuple-element.49), channel_id=1, source_target_pairs={{0,4},{4,0},{1,5},{5,1},{2,6},{6,2},{3,7},{7,3},{8,12},{12,8},{9,1... | collective-permute-start | bytes 835592 | tf_op jit(solution)/shard_map/ppermute | solution.py:312
  68.8 3.2 %collective-permute-start.12 = (bf16[16,2176]{1,0:T(8,128)(2,1)S(1)}, bf16[16,2176]{1,0:T(8,128)(2,1)S(1)}, u32[]{:S(2)}, u32[]{:S(2)}) collective-permute-start(bf16[16,2176]{1,0:T(8,128)(2,1)S(1)} %get-tuple-element.51), channel_id=1, source_target_pairs={{0,48},{16,0},{32,16},{48,32},{1,49},{17,1},{33,17},{49,33},{2,50}... | collective-permute-start | bytes 208904 | tf_op jit(solution)/shard_map/ppermute | solution.py:314
  70.2 4.6 %collective-permute-start.13 = (bf16[16,2176]{1,0:T(8,128)(2,1)S(1)}, bf16[16,2176]{1,0:T(8,128)(2,1)S(1)}, u32[]{:S(2)}, u32[]{:S(2)}) collective-permute-start(bf16[16,2176]{1,0:T(8,128)(2,1)S(1)} %get-tuple-element.52), channel_id=1, source_target_pairs={{0,16},{16,32},{32,48},{48,0},{1,17},{17,33},{33,49},{49,1},{2,18}... | collective-permute-start | bytes 208904 | tf_op jit(solution)/shard_map/ppermute | solution.py:314
  70.4 5.2 %collective-permute-start.14 = (bf16[16,2176]{1,0:T(8,128)(2,1)S(1)}, bf16[16,2176]{1,0:T(8,128)(2,1)S(1)}, u32[]{:S(2)}, u32[]{:S(2)}) collective-permute-start(bf16[16,2176]{1,0:T(8,128)(2,1)S(1)} %get-tuple-element.53), channel_id=1, source_target_pairs={{0,32},{16,48},{32,0},{48,16},{1,33},{17,49},{33,1},{49,17},{2,34}... | collective-permute-start | bytes 208904 | tf_op jit(solution)/shard_map/ppermute | solution.py:314
  77.0 20.2 %all-to-all-start = ((bf16[16,16,2048]{2,1,0:T(8,128)(2,1)}), bf16[16,16,2048]{2,1,0:T(8,128)(2,1)S(1)}, u32[]{:S(2)}, u32[]{:S(2)}) async-start(bf16[16,16,2048]{2,1,0:T(8,128)(2,1)} %shard_map.108), calls=%async_computation | async-start | bytes 2097152 | tf_op jit(solution)/shard_map/all_to_all | solution.py:320
  82.2 3.9 %collective-permute-start.15 = (bf16[112,2048]{1,0:T(8,128)(2,1)S(1)}, bf16[112,2048]{1,0:T(8,128)(2,1)S(1)}, u32[]{:S(2)}, u32[]{:S(2)}) collective-permute-start(bf16[112,2048]{1,0:T(8,128)(2,1)S(1)} %bitcast.21), channel_id=1, source_target_pairs={{0,4},{4,0},{1,5},{5,1},{2,6},{6,2},{3,7},{7,3},{8,12},{12,8},{9,1... | collective-permute-start | bytes 1376264 | tf_op jit(solution)/shard_map/ppermute | solution.py:321
  84.7 2.3 %collective-permute-start.16 = (bf16[112,2048]{1,0:T(8,128)(2,1)}, bf16[112,2048]{1,0:T(8,128)(2,1)S(1)}, u32[]{:S(2)}, u32[]{:S(2)}) collective-permute-start(bf16[112,2048]{1,0:T(8,128)(2,1)} %collective-permute-done.10.refs_1_), channel_id=1, source_target_pairs={{0,4},{4,0},{1,5},{5,1},{2,6},{6,2},{3,7},{7,3},{8,12},{12,8},{9,1... | collective-permute-start | bytes 1376264 | tf_op jit(solution)/shard_map/ppermute | solution.py:322

commit v6 on v5

--- a/solution.py
+++ b/solution.py
@@ -45,35 +45,65 @@
     return lax.dot_general(a, b, (((1,), (1,)), ((), ())), preferred_element_type=jnp.float32)
 
 
-def pack_keys_kernel(latent_ref, key_rope_ref, pos_ref, key_ref):
-    key_ref[:, :RANK] = latent_ref[...]
-    pos = pos_ref[...].astype(jnp.float32)
-    high = jnp.floor(pos * (1 / 128))
-    row = lax.broadcasted_iota(jnp.int32, key_rope_ref.shape, 0)
-    ext = jnp.where(row == 0, high, jnp.where(row == 1, pos - high * 128, 0.0))
-    ext = jnp.concatenate([key_rope_ref[...].astype(jnp.float32), ext], axis=0)
+HBM = pl.BlockSpec(memory_space=pltpu.HBM)
+
+
+def in_hbm(*arrays):
+    return [pltpu.with_memory_space_constraint(a, pltpu.HBM) for a in arrays]
+
+
+def pack_keys_kernel(latent_ref, key_rope_ref, pos_ref, key_ref, rope, pos, sems):
+    copies = [
+        pltpu.make_async_copy(key_rope_ref, rope, sems.at[0]),
+        pltpu.make_async_copy(pos_ref, pos, sems.at[1]),
+        pltpu.make_async_copy(latent_ref, key_ref.at[:, :RANK], sems.at[2]),
+    ]
+    for copy in copies:
+        copy.start()
+    copies[0].wait()
+    copies[1].wait()
+    where = pos[...].astype(jnp.float32)
+    high = jnp.floor(where * (1 / 128))
+    row = lax.broadcasted_iota(jnp.int32, rope.shape, 0)
+    ext = jnp.where(row == 0, high, jnp.where(row == 1, where - high * 128, 0.0))
+    ext = jnp.concatenate([rope[...].astype(jnp.float32), ext], axis=0)
     key_ref[:, RANK:] = jnp.transpose(ext).astype(jnp.bfloat16)
+    copies[2].wait()
 
 
 def pack_keys(latent, k_rope, key_pos):
     return call(
         pack_keys_kernel,
         jax.ShapeDtypeStruct((latent.shape[0], KEYW), jnp.bfloat16),
-        vmem=60,
-    )(latent, jnp.transpose(k_rope), key_pos)
-
-
-def pack_queries_kernel(query_ref, rope_ref, out_ref):
-    out_ref[:, : HG * NOPE] = query_ref[...]
-    out_ref[:, HG * NOPE :] = rope_ref[...]
+        vmem=16,
+        in_specs=[HBM] * 3,
+        scratch_shapes=[
+            pltpu.VMEM((k_rope.shape[1], k_rope.shape[0]), jnp.bfloat16),
+            pltpu.VMEM(key_pos.shape, jnp.int32),
+            pltpu.SemaphoreType.DMA((3,)),
+        ],
+    )(*in_hbm(latent, jnp.transpose(k_rope), key_pos))
+
+
+def pack_queries_kernel(query_ref, rope_ref, out_ref, sems):
+    copies = [
+        pltpu.make_async_copy(query_ref, out_ref.at[:, : HG * NOPE], sems.at[0]),
+        pltpu.make_async_copy(rope_ref, out_ref.at[:, HG * NOPE :], sems.at[1]),
+    ]
+    for copy in copies:
+        copy.start()
+    for copy in copies:
+        copy.wait()
 
 
 def pack_queries(query, q_rope):
     return call(
         pack_queries_kernel,
         jax.ShapeDtypeStruct((R, HG * (NOPE + ROPE)), jnp.bfloat16),
-        vmem=60,
-    )(query, q_rope)
+        vmem=16,
+        in_specs=[HBM] * 2,
+        scratch_shapes=[pltpu.SemaphoreType.DMA((2,))],
+    )(*in_hbm(query, q_rope))
 
 
 def join_kernel(*refs):
@@ -170,7 +200,7 @@
 
     keep = jnp.exp2(st_in[:, 0:1] - top)
     total = total + keep * st_in[:, 1:2]
-    context = ((acc + keep * acc_in[...]) / total).astype(jnp.bfloat16)
+    context = ((acc + keep * acc_in[...]) * (1.0 / total)).astype(jnp.bfloat16)
     lse = top + jnp.log2(total)
     half = ROWS // 2
     lane = lax.broadcasted_iota(jnp.int32, (ROWS, 128), 1)
@@ -255,13 +285,23 @@
             refs[-1][i, :, cols] = head
 
 
-def project_kernel(zc_ref, x_ref, *refs):
-    out_ref = refs[-1]
+def columns_kernel(zc_ref, *refs):
     z, c = zc_ref[0], zc_ref[1]
+    out_ref = refs[4]
+    ncol, depth = refs[0].shape
     for k in range(4):
         to_z = z if k % 2 == 0 else 1 - z
         to_c = c if k < 2 else 1 - c
-        out_ref[to_z * 2 + to_c] = nt_dot(x_ref[...], refs[k][...]).astype(jnp.bfloat16)
+        padded = jnp.concatenate(
+            [refs[k][...], jnp.zeros((128 - ncol, depth), jnp.bfloat16)], axis=0
+        )
+        out_ref[to_z * 2 + to_c] = jnp.transpose(padded)
+
+
+def project_kernel(x_ref, w_ref, out_ref):
+    for k in range(4):
+        out = jnp.dot(x_ref[...], w_ref[k], preferred_element_type=jnp.float32)
+        out_ref[k] = out[:, : out_ref.shape[2]].astype(jnp.bfloat16)
 
 
 def finish_kernel(sums_ref, out_ref, row_ref):
@@ -283,9 +323,7 @@
     z_keys = lax.ppermute(keys, "z", SWAP)
     up, down = (lax.ppermute(keys, "y", shift(d)) for d in (1, 3))
     q_ring = [lax.ppermute(q_own, "x", shift(d)) for d in RING[1:]]
-    z_keys, up, down, q_ring, keys, q_own = lax.optimization_barrier(
-        (z_keys, up, down, q_ring, keys, q_own)
-    )
+    z_keys, up, down, keys = lax.optimization_barrier((z_keys, up, down, keys))
     near = [join([keys, z_keys]), up, down]
     far = [lax.ppermute(near[0], "y", shift(2))]
     far += [lax.ppermute(z_keys, "y", shift(d)) for d in (1, 3)]
@@ -313,20 +351,24 @@
     parts = [parts[0]] + [
         lax.ppermute(part, "x", shift(-d % 4)) for part, d in zip(parts[1:], RING[1:])
     ]
+    c_w = lax.ppermute(w_own, "c", SWAP)
+    zc_w = lax.ppermute(z_w, "c", SWAP)
+    parts, c_w, zc_w = lax.optimization_barrier((parts, c_w, zc_w))
     heads = call(merge_ring_kernel, jax.ShapeDtypeStruct((16, R, HG * VDIM), jnp.bfloat16))(
         *parts
     )
 
     rows = lax.all_to_all(heads, ("y", "x"), 0, 0, tiled=True).reshape(16 * R, HG * VDIM)
-    c_w = lax.ppermute(w_own, "c", SWAP)
-    zc_w = lax.ppermute(z_w, "c", SWAP)
     ncol = w_out.shape[1]
-    sums = call(
-        project_kernel,
-        jax.ShapeDtypeStruct((4, 16 * R, ncol), jnp.bfloat16),
+    columns = call(
+        columns_kernel,
+        jax.ShapeDtypeStruct((4, HG * VDIM, 128), jnp.bfloat16),
         in_specs=[pl.BlockSpec(memory_space=pltpu.SMEM)]
-        + [pl.BlockSpec(memory_space=pltpu.VMEM)] * 5,
-    )(jnp.stack([z, c]), rows, w_own, z_w, c_w, zc_w)
+        + [pl.BlockSpec(memory_space=pltpu.VMEM)] * 4,
+    )(jnp.stack([z, c]), w_own, z_w, c_w, zc_w)
+    sums = call(project_kernel, jax.ShapeDtypeStruct((4, 16 * R, ncol), jnp.bfloat16))(
+        rows, columns
+    )
     sums = lax.all_to_all(
         sums.reshape(16, 4 * R, ncol), ("z", "c", "head"), 0, 0, tiled=True
     )

time: 122 us -> 118 us (0.967)
  waiting for transfers between devices: 30.6 us -> 21.1 us
  starting transfers between devices: 36.4 us -> 41.4 us
    ppermute x2, waiting for transfers between devices: 6.75 us -> 1.03 us  [local(): far += [lax.ppermute(z_keys, 'y', shift(d)) for d in (1, 3)]]
    ppermute x3, waiting for transfers between devices: 6.66 us -> 3.84 us  [local(): q_ring = [lax.ppermute(q_own, 'x', shift(d)) for d in RING[1:]]]
    ppermute x1, starting transfers between devices: 2.45 us -> 3.92 us  [local(): c_w = lax.ppermute(w_own, 'c', SWAP)]
    ppermute x3, waiting for transfers between devices: 3.66 us -> 2.24 us  [local(): lax.ppermute(part, 'x', shift(-d % 4))]
    ppermute x1, waiting for transfers between devices: 1.27 us -> 0.01 us  [local(): c_w = lax.ppermute(w_own, 'c', SWAP)]
    unnamed x18 -> x20, local copies, waits for them, and re-layouts: 2.83 us -> 3.63 us
    pallas_call x1 -> x2, Pallas kernels: 2.27 us -> 3.03 us  [the longest x1 1.79 us: local(): call(columns_kernel, jax.ShapeDtypeStruct((4, HG * VDIM, 128), jnp.bfloat...]
  transfers between devices with their start and end apart: 18 -> 18, of which waited for: 10 -> 7; matrix products, arithmetic and copies ran while one was open for 0% -> 0% of each run, Pallas kernels for 19% -> 21%
where the time goes in v6:
time: 118 us
  starting transfers between devices  41.4 us (35%)
  Pallas kernels  29.3 us (25%)
  blocking collectives  21.4 us (18%)
  waiting for transfers between devices  21.1 us (18%)
  local copies, waits for them, and re-layouts  3.63 us (3%)
    all_to_all x1, blocking collectives, local(): lax.all_to_all(sums.reshape(16, 4 * R, ncol), ('z', 'c', 'head'), 0, 0, t...  21.4 us
    pallas_call x2, Pallas kernels, attend(): call(functools.partial(attend_kernel, n, last), out_shape, grid=(ITEMS //...  19.5 us
    all_to_all x1, waiting for transfers between devices, local(): lax.all_to_all(heads, ('y', 'x'), 0, 0, tiled=True)  11.1 us
    ppermute x1, starting transfers between devices, local(): z_keys = lax.ppermute(keys, 'z', SWAP)  6.1 us
    all_to_all x1, starting transfers between devices, local(): lax.all_to_all(heads, ('y', 'x'), 0, 0, tiled=True)  5.51 us
    ppermute x1, starting transfers between devices, local(): z_w = lax.ppermute(w_own, 'z', SWAP)  5.15 us
    ppermute x3, starting transfers between devices, local(): q_ring = [lax.ppermute(q_own, 'x', shift(d)) for d in RING[1:]]  4.29 us
    ppermute x3, starting transfers between devices, local(): lax.ppermute(part, 'x', shift(-d % 4))  4 us
  transfers between devices with their start and end apart: 18, of which 7 were waited for; matrix products, arithmetic and copies ran while one was open for 0% of the time, Pallas kernels for 21%

profile of v6, /device:TPU:33, one launch (start us, length us, event | category | flops | bytes accessed | tf_op | source)
XLA Modules:
  0.0 117.8 jit_solution(16806614296585856086)
XLA Ops:
  0.0 1.0 shard_map.100.refs_0_
  1.0 1.3 %collective-permute-start = (bf16[16,3072]{1,0:T(8,128)(2,1)S(1)}, bf16[16,3072]{1,0:T(8,128)(2,1)S(1)}, u32[]{:S(2)}, u32[]{:S(2)}) collective-permute-start(bf16[16,3072]{1,0:T(8,128)(2,1)S(1)} %shard_map.100.refs_0_), channel_id=1, source_target_pairs={{0,16},{16,32},{32,48},{48,0},{1,17},{17,33},{33,49},{49,1},{2,18}... | collective-permute-start | bytes 294920 | tf_op jit(solution)/shard_map/ppermute | solution.py:325
  2.3 1.0 shard_map.103.refs_0_
  3.3 6.1 %collective-permute-start.4 = (bf16[256,640]{1,0:T(8,128)(2,1)S(1)}, bf16[256,640]{1,0:T(8,128)(2,1)}, u32[]{:S(2)}, u32[]{:S(2)}) collective-permute-start(bf16[256,640]{1,0:T(8,128)(2,1)S(1)} %shard_map.103.refs_0_), channel_id=1, source_target_pairs={{0,8},{8,0},{1,9},{9,1},{2,10},{10,2},{3,11},{11,3},{4,12},{12,4},... | collective-permute-start | bytes 983048 | tf_op jit(solution)/shard_map/ppermute | solution.py:323
  9.4 1.3 %collective-permute-start.5 = (bf16[256,640]{1,0:T(8,128)(2,1)S(1)}, bf16[256,640]{1,0:T(8,128)(2,1)S(1)}, u32[]{:S(2)}, u32[]{:S(2)}) collective-permute-start(bf16[256,640]{1,0:T(8,128)(2,1)S(1)} %shard_map.103.refs_0_), channel_id=1, source_target_pairs={{0,64},{64,128},{128,192},{192,0},{1,65},{65,129},{129,193},{193,1... | collective-permute-start | bytes 983048 | tf_op jit(solution)/shard_map/ppermute | solution.py:324
  10.7 1.4 %collective-permute-start.6 = (bf16[256,640]{1,0:T(8,128)(2,1)S(1)}, bf16[256,640]{1,0:T(8,128)(2,1)S(1)}, u32[]{:S(2)}, u32[]{:S(2)}) collective-permute-start(bf16[256,640]{1,0:T(8,128)(2,1)S(1)} %shard_map.103.refs_0_), channel_id=1, source_target_pairs={{0,192},{64,0},{128,64},{192,128},{1,193},{65,1},{129,65},{193,129... | collective-permute-start | bytes 983048 | tf_op jit(solution)/shard_map/ppermute | solution.py:324
  12.2 1.5 %collective-permute-start.1 = (bf16[16,3072]{1,0:T(8,128)(2,1)S(1)}, bf16[16,3072]{1,0:T(8,128)(2,1)S(1)}, u32[]{:S(2)}, u32[]{:S(2)}) collective-permute-start(bf16[16,3072]{1,0:T(8,128)(2,1)S(1)} %shard_map.100.refs_0_), channel_id=1, source_target_pairs={{0,48},{16,0},{32,16},{48,32},{1,49},{17,1},{33,17},{49,33},{2,50}... | collective-permute-start | bytes 294920 | tf_op jit(solution)/shard_map/ppermute | solution.py:325
  13.6 1.5 %collective-permute-start.2 = (bf16[16,3072]{1,0:T(8,128)(2,1)S(1)}, bf16[16,3072]{1,0:T(8,128)(2,1)S(1)}, u32[]{:S(2)}, u32[]{:S(2)}) collective-permute-start(bf16[16,3072]{1,0:T(8,128)(2,1)S(1)} %shard_map.100.refs_0_), channel_id=1, source_target_pairs={{0,32},{16,48},{32,0},{48,16},{1,33},{17,49},{33,1},{49,17},{2,34}... | collective-permute-start | bytes 294920 | tf_op jit(solution)/shard_map/ppermute | solution.py:325
  15.2 0.9 collective-permute-done.1.refs_2_
  16.0 3.0 %collective-permute-done.2.refs_3_ = bf16[16,3072]{1,0:T(8,128)(2,1)S(1)} collective-permute-done((bf16[16,3072]{1,0:T(8,128)(2,1)S(1)}, bf16[16,3072]{1,0:T(8,128)(2,1)S(1)}, u32[]{:S(2)}, u32[]{:S(2)}) %collective-permute-start.2) | collective-permute-done | bytes 98336 | tf_op jit(solution)/shard_map/ppermute | solution.py:325
  19.0 2.9 %collective-permute-start.3 = (bf16[64,3072]{1,0:T(8,128)(2,1)S(1)}, bf16[64,3072]{1,0:T(8,128)(2,1)S(1)}, u32[]{:S(2)}, u32[]{:S(2)}) collective-permute-start(bf16[64,3072]{1,0:T(8,128)(2,1)S(1)} %shard_map.101.refs_0_), channel_id=1, source_target_pairs={{0,4},{4,0},{1,5},{5,1},{2,6},{6,2},{3,7},{7,3},{8,12},{12,8},{9,1... | collective-permute-start | bytes 1179656 | tf_op jit(solution)/shard_map/ppermute | solution.py:331
  21.9 1.1 collective-permute-done.4.refs_1_
  23.0 0.0 collective-permute-done.5.refs_3_
  23.0 0.0 collective-permute-done.6.refs_4_
  23.0 1.3 %shard_map.104.refs_2_ = bf16[512,640]{1,0:T(8,128)(2,1)S(1)} custom-call(bf16[256,640]{1,0:T(8,128)(2,1)S(1)} %shard_map.103.refs_0_, bf16[256,640]{1,0:T(8,128)(2,1)} %collective-permute-done.4.refs_1_), custom_call_target="tpu_custom_call" | custom-call | flops 1 | bytes 1 | tf_op jit(solution)/shard_map/pallas_call | solution.py:118
  24.3 3.0 %collective-permute-start.7 = (bf16[512,640]{1,0:T(8,128)(2,1)S(1)}, bf16[512,640]{1,0:T(8,128)(2,1)}, u32[]{:S(2)}, u32[]{:S(2)}) collective-permute-start(bf16[512,640]{1,0:T(8,128)(2,1)S(1)} %shard_map.104.refs_2_), channel_id=1, source_target_pairs={{0,128},{64,192},{128,0},{192,64},{1,129},{65,193},{129,1},{193,65... | collective-permute-start | bytes 1966088 | tf_op jit(solution)/shard_map/ppermute | solution.py:328
  27.3 5.2 %collective-permute-start.10 = (bf16[112,2048]{1,0:T(8,128)(2,1)}, bf16[112,2048]{1,0:T(8,128)(2,1)}, u32[]{:S(2)}, u32[]{:S(2)}) collective-permute-start(bf16[112,2048]{1,0:T(8,128)(2,1)} %bitcast.refs_0_), channel_id=1, source_target_pairs={{0,8},{8,0},{1,9},{9,1},{2,10},{10,2},{3,11},{11,3},{4,12},{12,4},... | collective-permute-start | bytes 1376264 | tf_op jit(solution)/shard_map/ppermute | solution.py:333
  32.4 0.4 collective-permute-start.8
  32.8 2.3 %collective-permute-start.9 = (bf16[256,640]{1,0:T(8,128)(2,1)}, bf16[256,640]{1,0:T(8,128)(2,1)}, u32[]{:S(2)}, u32[]{:S(2)}) collective-permute-start(bf16[256,640]{1,0:T(8,128)(2,1)} %collective-permute-done.4.refs_1_), channel_id=1, source_target_pairs={{0,192},{64,0},{128,64},{192,128},{1,193},{65,1},{129,65},{193,129... | collective-permute-start | bytes 983048 | tf_op jit(solution)/shard_map/ppermute | solution.py:329
  35.8 3.9 %collective-permute-start.15 = (bf16[112,2048]{1,0:T(8,128)(2,1)}, bf16[112,2048]{1,0:T(8,128)(2,1)S(1)}, u32[]{:S(2)}, u32[]{:S(2)}) collective-permute-start(bf16[112,2048]{1,0:T(8,128)(2,1)} %bitcast.refs_0_), channel_id=1, source_target_pairs={{0,4},{4,0},{1,5},{5,1},{2,6},{6,2},{3,7},{7,3},{8,12},{12,8},{9,1... | collective-permute-start | bytes 1376264 | tf_op jit(solution)/shard_map/ppermute | solution.py:354
  39.7 0.8 shard_map.102.refs_0_
  40.6 0.0 copy-start.1
  40.6 7.9 %shard_map.105 = (f32[2048,512]{1,0:T(8,128)S(1)}, f32[2048,128]{1,0:T(8,128)S(1)}) custom-call(bf16[2048,768]{1,0:T(8,128)(2,1)S(1)} %shard_map.102.refs_0_, f32[8,128]{1,0:T(8,128)S(1)} %broadcast_in_dim.17.refs_1_, bf16[512,640]{1,0:T(8,128)(2,1)S(1)} %shard_map.104.refs_2_, bf16[256,640]{1,0:T(8,128)(2,1)S(1)} %copy-done.7, bf16[256,640]{1,0:T(8,128)(2,1)S(1)} %copy-done.9), custom_call_target="tpu_custom_call" | custom-call | flops 1 | bytes 1 | tf_op jit(solution)/shard_map/pallas_call | solution.py:246
  48.5 1.0 collective-permute-done.8.refs_3_
  49.6 11.6 %shard_map.106 = (bf16[64,2176]{1,0:T(8,128)(2,1)S(1)}, bf16[64,2176]{1,0:T(8,128)(2,1)S(1)}) custom-call(bf16[2048,768]{1,0:T(8,128)(2,1)S(1)} %shard_map.102.refs_0_, f32[8,128]{1,0:T(8,128)S(1)} %broadcast_in_dim.17.refs_1_, bf16[512,640]{1,0:T(8,128)(2,1)} %collective-permute-done.7.refs_2_, bf16[256,640]{1,0:T(8,128)(2,1)} %collective-permute-done.8.refs_3_, ...), custom_call_target="tpu_custom_call" | custom-call | flops 1 | bytes 1 | tf_op jit(solution)/shard_map/pallas_call | solution.py:246
  61.2 0.0 collective-permute-done.10.refs_1_
  61.2 1.0 collective-permute-start.16
  62.2 0.1 collective-permute-start.11
  62.3 1.7 %collective-permute-done.11.b_ref = bf16[64,2176]{1,0:T(8,128)(2,1)S(1)} collective-permute-done((bf16[64,2176]{1,0:T(8,128)(2,1)S(1)}, bf16[64,2176]{1,0:T(8,128)(2,1)S(1)}, u32[]{:S(2)}, u32[]{:S(2)}) %collective-permute-start.11) | collective-permute-done | bytes 278560 | tf_op jit(solution)/shard_map/ppermute | solution.py:350
  64.1 0.5 shard_map.107
  64.5 1.5 %collective-permute-start.12 = (bf16[16,2176]{1,0:T(8,128)(2,1)S(1)}, bf16[16,2176]{1,0:T(8,128)(2,1)S(1)}, u32[]{:S(2)}, u32[]{:S(2)}) collective-permute-start(bf16[16,2176]{1,0:T(8,128)(2,1)S(1)} %get-tuple-element.49), channel_id=1, source_target_pairs={{0,48},{16,0},{32,16},{48,32},{1,49},{17,1},{33,17},{49,33},{2,50}... | collective-permute-start | bytes 208904 | tf_op jit(solution)/shard_map/ppermute | solution.py:352
  66.1 2.4 %collective-permute-start.14 = (bf16[16,2176]{1,0:T(8,128)(2,1)S(1)}, bf16[16,2176]{1,0:T(8,128)(2,1)S(1)}, u32[]{:S(2)}, u32[]{:S(2)}) collective-permute-start(bf16[16,2176]{1,0:T(8,128)(2,1)S(1)} %get-tuple-element.51), channel_id=1, source_target_pairs={{0,32},{16,48},{32,0},{48,16},{1,33},{17,49},{33,1},{49,17},{2,34}... | collective-permute-start | bytes 208904 | tf_op jit(solution)/shard_map/ppermute | solution.py:352
  68.5 0.0 collective-permute-done.15.refs_2_
  68.6 0.8 copy-done.2
  69.3 0.0 collective-permute-done.12.refs_1_
  69.3 2.2 %collective-permute-done.13.refs_2_ = bf16[16,2176]{1,0:T(8,128)(2,1)S(1)} collective-permute-done((bf16[16,2176]{1,0:T(8,128)(2,1)S(1)}, bf16[16,2176]{1,0:T(8,128)(2,1)S(1)}, u32[]{:S(2)}, u32[]{:S(2)}) %collective-permute-start.13) | collective-permute-done | bytes 69664 | tf_op jit(solution)/shard_map/ppermute | solution.py:352
  71.6 0.0 collective-permute-done.14.refs_3_
  71.6 0.8 copy-done.4
  72.4 1.4 %shard_map.108 = bf16[16,16,2048]{2,1,0:T(8,128)(2,1)} custom-call(bf16[16,2176]{1,0:T(8,128)(2,1)S(1)} %get-tuple-element.53.refs_0_, bf16[16,2176]{1,0:T(8,128)(2,1)S(1)} %collective-permute-done.12.refs_1_, bf16[16,2176]{1,0:T(8,128)(2,1)S(1)} %collective-permute-done.13.refs_2_, bf16[16,2176]{1,0:T(8,128)(2,1)S(1)} %collective-permute-done.14.refs_3_), custom_call_target="tpu_custom_call" | custom-call | flops 1 | bytes 1 | tf_op jit(solution)/shard_map/pallas_call | solution.py:357
  73.8 5.5 %all-to-all-start = ((bf16[16,16,2048]{2,1,0:T(8,128)(2,1)}), bf16[16,16,2048]{2,1,0:T(8,128)(2,1)S(1)}, u32[]{:S(2)}, u32[]{:S(2)}) async-start(bf16[16,16,2048]{2,1,0:T(8,128)(2,1)} %shard_map.108), calls=%async_computation | async-start | bytes 2097152 | tf_op jit(solution)/shard_map/all_to_all | solution.py:361
  79.3 0.1 pad_add_fusion.zc_ref
  79.4 1.0 copy-done.3
  80.4 1.0 copy-done.5
  81.4 1.8 %shard_map.109.w_ref = bf16[4,2048,128]{2,1,0:T(8,128)(2,1)S(1)} custom-call(s32[2]{0:T(128)S(1)} %pad_add_fusion.zc_ref, bf16[112,2048]{1,0:T(8,128)(2,1)} %bitcast.refs_0_, bf16[112,2048]{1,0:T(8,128)(2,1)} %collective-permute-done.10.refs_1_, bf16[112,2048]{1,0:T(8,128)(2,1)S(1)} %copy-done.3, bf16[112,2048]{1,0:T(8,128)(2,1)S(1)} %copy-done.5), custom_call_target="tpu_custom_call" | custom-call | flops 1 | bytes 1 | tf_op jit(solution)/shard_map/pallas_call | solution.py:363
  83.2 11.1 %all-to-all-done = bf16[16,16,2048]{2,1,0:T(8,128)(2,1)S(1)} async-done(((bf16[16,16,2048]{2,1,0:T(8,128)(2,1)}), bf16[16,16,2048]{2,1,0:T(8,128)(2,1)S(1)}, u32[]{:S(2)}, u32[]{:S(2)}) %all-to-all-start) | async-done | bytes 1048608 | tf_op jit(solution)/shard_map/all_to_all | solution.py:361
  94.3 1.2 %shard_map.110 = bf16[4,256,112]{2,1,0:T(8,128)(2,1)S(1)} custom-call(bf16[256,2048]{1,0:T(8,128)(2,1)S(1)} %bitcast.18, bf16[4,2048,128]{2,1,0:T(8,128)(2,1)S(1)} %shard_map.109.w_ref), custom_call_target="tpu_custom_call" | custom-call | flops 1 | bytes 1 | tf_op jit(solution)/shard_map/pallas_call | solution.py:369
  95.6 21.4 %all_to_all.10.sums_ref = bf16[16,64,112]{2,1,0:T(8,128)(2,1)S(1)} all-to-all(bf16[16,64,112]{2,1,0:T(8,128)(2,1)S(1)} %bitcast.19), channel_id=1, replica_groups=mesh['y'=4,'x'=4,'z'=2,'c'=2,'head'=4] {'z','c','head'}, dimensions={0} | all-to-all | bytes 458752 | tf_op jit(solution)/shard_map/all_to_all | solution.py:372
  117.0 0.7 shard_map.111
  (24 shorter events, 0.1 us)
Async XLA Ops:
  0.0 39.7 %copy-start = (bf16[16,128,512]{2,1,0:T(8,128)(2,1)S(1)}, bf16[16,128,512]{2,1,0:T(8,128)(2,1)}, u32[]{:S(2)}) copy-start(bf16[16,128,512]{2,1,0:T(8,128)(2,1)} %refs_2_.1) | copy-start | bytes 6291460
  1.0 12.6 %collective-permute-start = (bf16[16,3072]{1,0:T(8,128)(2,1)S(1)}, bf16[16,3072]{1,0:T(8,128)(2,1)S(1)}, u32[]{:S(2)}, u32[]{:S(2)}) collective-permute-start(bf16[16,3072]{1,0:T(8,128)(2,1)S(1)} %shard_map.100.refs_0_), channel_id=1, source_target_pairs={{0,16},{16,32},{32,48},{48,0},{1,17},{17,33},{33,49},{49,1},{2,18}... | collective-permute-start | bytes 294920 | tf_op jit(solution)/shard_map/ppermute | solution.py:325
  3.3 19.7 %collective-permute-start.4 = (bf16[256,640]{1,0:T(8,128)(2,1)S(1)}, bf16[256,640]{1,0:T(8,128)(2,1)}, u32[]{:S(2)}, u32[]{:S(2)}) collective-permute-start(bf16[256,640]{1,0:T(8,128)(2,1)S(1)} %shard_map.103.refs_0_), channel_id=1, source_target_pairs={{0,8},{8,0},{1,9},{9,1},{2,10},{10,2},{3,11},{11,3},{4,12},{12,4},... | collective-permute-start | bytes 983048 | tf_op jit(solution)/shard_map/ppermute | solution.py:323
  9.4 13.6 %collective-permute-start.5 = (bf16[256,640]{1,0:T(8,128)(2,1)S(1)}, bf16[256,640]{1,0:T(8,128)(2,1)S(1)}, u32[]{:S(2)}, u32[]{:S(2)}) collective-permute-start(bf16[256,640]{1,0:T(8,128)(2,1)S(1)} %shard_map.103.refs_0_), channel_id=1, source_target_pairs={{0,64},{64,128},{128,192},{192,0},{1,65},{65,129},{129,193},{193,1... | collective-permute-start | bytes 983048 | tf_op jit(solution)/shard_map/ppermute | solution.py:324
  10.7 12.3 %collective-permute-start.6 = (bf16[256,640]{1,0:T(8,128)(2,1)S(1)}, bf16[256,640]{1,0:T(8,128)(2,1)S(1)}, u32[]{:S(2)}, u32[]{:S(2)}) collective-permute-start(bf16[256,640]{1,0:T(8,128)(2,1)S(1)} %shard_map.103.refs_0_), channel_id=1, source_target_pairs={{0,192},{64,0},{128,64},{192,128},{1,193},{65,1},{129,65},{193,129... | collective-permute-start | bytes 983048 | tf_op jit(solution)/shard_map/ppermute | solution.py:324
  12.2 3.9 %collective-permute-start.1 = (bf16[16,3072]{1,0:T(8,128)(2,1)S(1)}, bf16[16,3072]{1,0:T(8,128)(2,1)S(1)}, u32[]{:S(2)}, u32[]{:S(2)}) collective-permute-start(bf16[16,3072]{1,0:T(8,128)(2,1)S(1)} %shard_map.100.refs_0_), channel_id=1, source_target_pairs={{0,48},{16,0},{32,16},{48,32},{1,49},{17,1},{33,17},{49,33},{2,50}... | collective-permute-start | bytes 294920 | tf_op jit(solution)/shard_map/ppermute | solution.py:325
  13.6 5.4 %collective-permute-start.2 = (bf16[16,3072]{1,0:T(8,128)(2,1)S(1)}, bf16[16,3072]{1,0:T(8,128)(2,1)S(1)}, u32[]{:S(2)}, u32[]{:S(2)}) collective-permute-start(bf16[16,3072]{1,0:T(8,128)(2,1)S(1)} %shard_map.100.refs_0_), channel_id=1, source_target_pairs={{0,32},{16,48},{32,0},{48,16},{1,33},{17,49},{33,1},{49,17},{2,34}... | collective-permute-start | bytes 294920 | tf_op jit(solution)/shard_map/ppermute | solution.py:325
  19.0 8.2 %collective-permute-start.3 = (bf16[64,3072]{1,0:T(8,128)(2,1)S(1)}, bf16[64,3072]{1,0:T(8,128)(2,1)S(1)}, u32[]{:S(2)}, u32[]{:S(2)}) collective-permute-start(bf16[64,3072]{1,0:T(8,128)(2,1)S(1)} %shard_map.101.refs_0_), channel_id=1, source_target_pairs={{0,4},{4,0},{1,5},{5,1},{2,6},{6,2},{3,7},{7,3},{8,12},{12,8},{9,1... | collective-permute-start | bytes 1179656 | tf_op jit(solution)/shard_map/ppermute | solution.py:331
  23.0 4.3 %copy-start.6 = (bf16[256,640]{1,0:T(8,128)(2,1)}, bf16[256,640]{1,0:T(8,128)(2,1)S(1)}, u32[]{:S(2)}) copy-start(bf16[256,640]{1,0:T(8,128)(2,1)S(1)} %collective-permute-done.5.refs_3_) | copy-start | bytes 983044
  23.0 4.3 %copy-start.8 = (bf16[256,640]{1,0:T(8,128)(2,1)}, bf16[256,640]{1,0:T(8,128)(2,1)S(1)}, u32[]{:S(2)}) copy-start(bf16[256,640]{1,0:T(8,128)(2,1)S(1)} %collective-permute-done.6.refs_4_) | copy-start | bytes 983044
  24.3 25.3 %collective-permute-start.7 = (bf16[512,640]{1,0:T(8,128)(2,1)S(1)}, bf16[512,640]{1,0:T(8,128)(2,1)}, u32[]{:S(2)}, u32[]{:S(2)}) collective-permute-start(bf16[512,640]{1,0:T(8,128)(2,1)S(1)} %shard_map.104.refs_2_), channel_id=1, source_target_pairs={{0,128},{64,192},{128,0},{192,64},{1,129},{65,193},{129,1},{193,65... | collective-permute-start | bytes 1966088 | tf_op jit(solution)/shard_map/ppermute | solution.py:328
  27.3 33.9 %collective-permute-start.10 = (bf16[112,2048]{1,0:T(8,128)(2,1)}, bf16[112,2048]{1,0:T(8,128)(2,1)}, u32[]{:S(2)}, u32[]{:S(2)}) collective-permute-start(bf16[112,2048]{1,0:T(8,128)(2,1)} %bitcast.refs_0_), channel_id=1, source_target_pairs={{0,8},{8,0},{1,9},{9,1},{2,10},{10,2},{3,11},{11,3},{4,12},{12,4},... | collective-permute-start | bytes 1376264 | tf_op jit(solution)/shard_map/ppermute | solution.py:333
  32.4 17.1 %collective-permute-start.8 = (bf16[256,640]{1,0:T(8,128)(2,1)}, bf16[256,640]{1,0:T(8,128)(2,1)}, u32[]{:S(2)}, u32[]{:S(2)}) collective-permute-start(bf16[256,640]{1,0:T(8,128)(2,1)} %collective-permute-done.4.refs_1_), channel_id=1, source_target_pairs={{0,64},{64,128},{128,192},{192,0},{1,65},{65,129},{129,193},{193,1... | collective-permute-start | bytes 983048 | tf_op jit(solution)/shard_map/ppermute | solution.py:329
  32.8 16.7 %collective-permute-start.9 = (bf16[256,640]{1,0:T(8,128)(2,1)}, bf16[256,640]{1,0:T(8,128)(2,1)}, u32[]{:S(2)}, u32[]{:S(2)}) collective-permute-start(bf16[256,640]{1,0:T(8,128)(2,1)} %collective-permute-done.4.refs_1_), channel_id=1, source_target_pairs={{0,192},{64,0},{128,64},{192,128},{1,193},{65,1},{129,65},{193,129... | collective-permute-start | bytes 983048 | tf_op jit(solution)/shard_map/ppermute | solution.py:329
  35.8 4.8 %copy-start.7 = (bf16[256,640]{1,0:T(8,128)(2,1)S(1)}, bf16[256,640]{1,0:T(8,128)(2,1)}, u32[]{:S(2)}) copy-start(bf16[256,640]{1,0:T(8,128)(2,1)} %copy-done.6) | copy-start | bytes 983044
  35.8 4.8 %copy-start.9 = (bf16[256,640]{1,0:T(8,128)(2,1)S(1)}, bf16[256,640]{1,0:T(8,128)(2,1)}, u32[]{:S(2)}) copy-start(bf16[256,640]{1,0:T(8,128)(2,1)} %copy-done.8) | copy-start | bytes 983044
  35.8 32.7 %collective-permute-start.15 = (bf16[112,2048]{1,0:T(8,128)(2,1)}, bf16[112,2048]{1,0:T(8,128)(2,1)S(1)}, u32[]{:S(2)}, u32[]{:S(2)}) collective-permute-start(bf16[112,2048]{1,0:T(8,128)(2,1)} %bitcast.refs_0_), channel_id=1, source_target_pairs={{0,4},{4,0},{1,5},{5,1},{2,6},{6,2},{3,7},{7,3},{8,12},{12,8},{9,1... | collective-permute-start | bytes 1376264 | tf_op jit(solution)/shard_map/ppermute | solution.py:354
  40.6 9.0 %copy-start.1 = (bf16[16,512,128]{2,1,0:T(8,128)(2,1)S(1)}, bf16[16,512,128]{2,1,0:T(8,128)(2,1)}, u32[]{:S(2)}) copy-start(bf16[16,512,128]{2,1,0:T(8,128)(2,1)} %refs_7_.1) | copy-start | bytes 6291460
  61.2 10.4 %collective-permute-start.16 = (bf16[112,2048]{1,0:T(8,128)(2,1)}, bf16[112,2048]{1,0:T(8,128)(2,1)S(1)}, u32[]{:S(2)}, u32[]{:S(2)}) collective-permute-start(bf16[112,2048]{1,0:T(8,128)(2,1)} %collective-permute-done.10.refs_1_), channel_id=1, source_target_pairs={{0,4},{4,0},{1,5},{5,1},{2,6},{6,2},{3,7},{7,3},{8,12},{12,8},{9,1... | collective-permute-start | bytes 1376264 | tf_op jit(solution)/shard_map/ppermute | solution.py:355
  62.2 1.8 %collective-permute-start.11 = (bf16[64,2176]{1,0:T(8,128)(2,1)S(1)}, bf16[64,2176]{1,0:T(8,128)(2,1)S(1)}, u32[]{:S(2)}, u32[]{:S(2)}) collective-permute-start(bf16[64,2176]{1,0:T(8,128)(2,1)S(1)} %get-tuple-element.47), channel_id=1, source_target_pairs={{0,4},{4,0},{1,5},{5,1},{2,6},{6,2},{3,7},{7,3},{8,12},{12,8},{9,1... | collective-permute-start | bytes 835592 | tf_op jit(solution)/shard_map/ppermute | solution.py:350
  64.5 4.8 %collective-permute-start.12 = (bf16[16,2176]{1,0:T(8,128)(2,1)S(1)}, bf16[16,2176]{1,0:T(8,128)(2,1)S(1)}, u32[]{:S(2)}, u32[]{:S(2)}) collective-permute-start(bf16[16,2176]{1,0:T(8,128)(2,1)S(1)} %get-tuple-element.49), channel_id=1, source_target_pairs={{0,48},{16,0},{32,16},{48,32},{1,49},{17,1},{33,17},{49,33},{2,50}... | collective-permute-start | bytes 208904 | tf_op jit(solution)/shard_map/ppermute | solution.py:352
  66.1 5.5 %collective-permute-start.13 = (bf16[16,2176]{1,0:T(8,128)(2,1)S(1)}, bf16[16,2176]{1,0:T(8,128)(2,1)S(1)}, u32[]{:S(2)}, u32[]{:S(2)}) collective-permute-start(bf16[16,2176]{1,0:T(8,128)(2,1)S(1)} %get-tuple-element.50), channel_id=1, source_target_pairs={{0,16},{16,32},{32,48},{48,0},{1,17},{17,33},{33,49},{49,1},{2,18}... | collective-permute-start | bytes 208904 | tf_op jit(solution)/shard_map/ppermute | solution.py:352
  66.1 5.5 %collective-permute-start.14 = (bf16[16,2176]{1,0:T(8,128)(2,1)S(1)}, bf16[16,2176]{1,0:T(8,128)(2,1)S(1)}, u32[]{:S(2)}, u32[]{:S(2)}) collective-permute-start(bf16[16,2176]{1,0:T(8,128)(2,1)S(1)} %get-tuple-element.51), channel_id=1, source_target_pairs={{0,32},{16,48},{32,0},{48,16},{1,33},{17,49},{33,1},{49,17},{2,34}... | collective-permute-start | bytes 208904 | tf_op jit(solution)/shard_map/ppermute | solution.py:352
  68.6 0.8 copy-start.2
  71.6 0.8 copy-start.4
  73.8 20.5 %all-to-all-start = ((bf16[16,16,2048]{2,1,0:T(8,128)(2,1)}), bf16[16,16,2048]{2,1,0:T(8,128)(2,1)S(1)}, u32[]{:S(2)}, u32[]{:S(2)}) async-start(bf16[16,16,2048]{2,1,0:T(8,128)(2,1)} %shard_map.108), calls=%async_computation | async-start | bytes 2097152 | tf_op jit(solution)/shard_map/all_to_all | solution.py:361
  79.4 1.0 copy-start.3
  80.4 1.0 copy-start.5

commit v7 on v6

--- a/solution.py
+++ b/solution.py
@@ -159,13 +159,13 @@
 
 
 def attend_kernel(pieces, last, *refs):
-    q_ref, qpos_ref = refs[:2]
-    piece_refs = refs[2 : 2 + pieces]
-    rest = refs[2 + pieces :]
+    q_ref, qpos_ref, v_ref = refs[:3]
+    piece_refs = refs[3 : 3 + pieces]
+    rest = refs[3 + pieces :]
     if last:
-        acc_in, st_in, v_ref, keep_ref, send_ref, key_ref, lse_ref = rest
+        part_in, lse_in, keep_ref, send_ref, key_ref, lse_ref = rest
     else:
-        acc_out, st_out, key_ref = rest
+        part_out, lse_out, key_ref = rest
     step = pl.program_id(0)
 
     @pl.when(step == 0)
@@ -185,61 +185,70 @@
     tile = q_ref.shape[0]
     scores = nt_dot(q_ref[...], key_ref[...]) * SCALE2
     top = jnp.max(scores, axis=1, keepdims=True)
-    if last:
-        top = jnp.maximum(top, st_in[:, 0:1])
     weights = jnp.exp2(scores - top)
     total = jnp.sum(weights, axis=1, keepdims=True)
     acc = jnp.dot(
         weights.astype(jnp.bfloat16), key_ref[:, :RANK], preferred_element_type=jnp.float32
     )
-    if not last:
-        acc_out[...] = acc
-        lane = lax.broadcasted_iota(jnp.int32, (tile, 128), 1)
-        st_out[...] = jnp.where(lane == 0, top, total)
-        return
-
-    keep = jnp.exp2(st_in[:, 0:1] - top)
-    total = total + keep * st_in[:, 1:2]
-    context = ((acc + keep * acc_in[...]) * (1.0 / total)).astype(jnp.bfloat16)
+    context = (acc * (1.0 / total)).astype(jnp.bfloat16)
     lse = top + jnp.log2(total)
+    if last:
+        earlier = lse_in[:, 0:1]
+        top = jnp.maximum(lse, earlier)
+        here, there = jnp.exp2(lse - top), jnp.exp2(earlier - top)
+        total = here + there
+        lse = top + jnp.log2(total)
+        inverse = 1.0 / total
+        here, there = here * inverse, there * inverse
+    else:
+        lse_out[...] = jnp.broadcast_to(lse, lse_out.shape)
+
     half = ROWS // 2
     lane = lax.broadcasted_iota(jnp.int32, (ROWS, 128), 1)
     for i in range(tile // ROWS):
         rows = slice(i * ROWS, (i + 1) * ROWS)
         head = step * (tile // ROWS) + i
+        cols = pl.ds(pl.multiple_of(head * VDIM, VDIM), VDIM)
         out = jnp.dot(context[rows], v_ref[i], preferred_element_type=jnp.float32)
-        out = out.astype(jnp.bfloat16)
-        cols = pl.ds(pl.multiple_of(head * VDIM, VDIM), VDIM)
-        keep_ref[:, cols] = out[:half]
-        send_ref[:, cols] = out[half:]
-        lse_ref[...] = jnp.where(lane == head, lse[rows], lse_ref[...])
-
-    @pl.when(step == pl.num_programs(0) - 1)
-    def _():
-        packed = pack_stats(lse_ref[...])
-        keep_ref[:, HG * VDIM :] = packed[:half]
-        send_ref[:, HG * VDIM :] = packed[half:]
-
-
-def attend(q, qpos, pieces, state=None, value_weight=None, tile=512):
+        if last:
+            out = out * here[rows] + part_in[:, i * VDIM : (i + 1) * VDIM] * there[rows]
+            out = out.astype(jnp.bfloat16)
+            keep_ref[:, cols] = out[:half]
+            send_ref[:, cols] = out[half:]
+            lse_ref[...] = jnp.where(lane == head, lse[rows], lse_ref[...])
+        else:
+            part_out[:, i * VDIM : (i + 1) * VDIM] = out
+
+    if last:
+
+        @pl.when(step == pl.num_programs(0) - 1)
+        def _():
+            packed = pack_stats(lse_ref[...])
+            keep_ref[:, HG * VDIM :] = packed[:half]
+            send_ref[:, HG * VDIM :] = packed[half:]
+
+
+def attend(q, qpos, value_weight, pieces, earlier=None, tile=512):
     n, keys = len(pieces), sum(piece.shape[0] for piece in pieces)
-    last = state is not None
+    last = earlier is not None
+    heads = tile // ROWS
     whole = lambda shape: pl.BlockSpec(shape, lambda i: (0, 0))
     part = lambda width: pl.BlockSpec((tile, width), lambda i: (i, 0))
-    carried = [part(RANK), part(128)]
-    in_specs = [part(ITEMW), whole((8, 128))] + [whole(piece.shape) for piece in pieces]
+    carried = [pl.BlockSpec((ROWS, heads * VDIM), lambda i: (0, i)), part(128)]
+    in_specs = [part(ITEMW), whole((8, 128))]
+    in_specs += [pl.BlockSpec((heads, RANK, VDIM), lambda i: (i, 0, 0))]
+    in_specs += [whole(piece.shape) for piece in pieces]
     scratch = [pltpu.VMEM((keys, ITEMW), jnp.bfloat16)]
-    args = [q, qpos, *pieces]
+    args = [q, qpos, value_weight, *pieces]
     if last:
-        heads = tile // ROWS
-        in_specs += carried + [pl.BlockSpec((heads, RANK, VDIM), lambda i: (i, 0, 0))]
-        args += [*state, value_weight]
+        in_specs += carried
+        args += earlier
         half = jax.ShapeDtypeStruct((ROWS // 2, SENDW), jnp.bfloat16)
         out_shape, out_specs = (half, half), [whole((ROWS // 2, SENDW))] * 2
         scratch.append(pltpu.VMEM((ROWS, 128), jnp.float32))
     else:
         out_shape = (
-            jax.ShapeDtypeStruct((ITEMS, RANK), jnp.float32),
+            jax.ShapeDtypeStruct((ROWS, HG * VDIM), jnp.float32),
             jax.ShapeDtypeStruct((ITEMS, 128), jnp.float32),
         )
         out_specs = carried
@@ -287,15 +296,33 @@
 
 def columns_kernel(zc_ref, *refs):
     z, c = zc_ref[0], zc_ref[1]
-    out_ref = refs[4]
-    ncol, depth = refs[0].shape
+    w_refs, (out_ref, held, sems) = refs[:4], refs[4:]
+    ncol, depth = w_refs[0].shape
+    copies = [pltpu.make_async_copy(w_refs[k], held.at[k], sems.at[k]) for k in range(4)]
+    for copy in copies:
+        copy.start()
     for k in range(4):
         to_z = z if k % 2 == 0 else 1 - z
         to_c = c if k < 2 else 1 - c
+        copies[k].wait()
         padded = jnp.concatenate(
-            [refs[k][...], jnp.zeros((128 - ncol, depth), jnp.bfloat16)], axis=0
+            [held[k], jnp.zeros((128 - ncol, depth), jnp.bfloat16)], axis=0
         )
         out_ref[to_z * 2 + to_c] = jnp.transpose(padded)
+
+
+def columns_of(zc, pieces):
+    ncol, depth = pieces[0].shape
+    return call(
+        columns_kernel,
+        jax.ShapeDtypeStruct((4, depth, 128), jnp.bfloat16),
+        vmem=16,
+        in_specs=[pl.BlockSpec(memory_space=pltpu.SMEM)] + [HBM] * 4,
+        scratch_shapes=[
+            pltpu.VMEM((4, ncol, depth), jnp.bfloat16),
+            pltpu.SemaphoreType.DMA((4,)),
+        ],
+    )(zc, *in_hbm(pieces[0]), *pieces[1:])
 
 
 def project_kernel(x_ref, w_ref, out_ref):
@@ -319,17 +346,16 @@
     y, x, z, c = (lax.axis_index(n) for n in CTX)
 
     keys = pack_keys(latent[0], k_rope[0], key_pos)
+    keys, query_unrotated = lax.optimization_barrier((keys, query_unrotated))
     q_own = pack_queries(query_unrotated, q_rope)
     z_keys = lax.ppermute(keys, "z", SWAP)
-    up, down = (lax.ppermute(keys, "y", shift(d)) for d in (1, 3))
-    q_ring = [lax.ppermute(q_own, "x", shift(d)) for d in RING[1:]]
-    z_keys, up, down, keys = lax.optimization_barrier((z_keys, up, down, keys))
-    near = [join([keys, z_keys]), up, down]
-    far = [lax.ppermute(near[0], "y", shift(2))]
-    far += [lax.ppermute(z_keys, "y", shift(d)) for d in (1, 3)]
-    q_chip = join([q_own, *q_ring])
+    near = [keys] + [lax.ppermute(keys, "y", shift(d)) for d in RING[1:]]
+    z_keys, near = lax.optimization_barrier((z_keys, near))
+    far = [z_keys] + [lax.ppermute(z_keys, "y", shift(d)) for d in RING[1:]]
+
+    q_chip = join([q_own] + [lax.ppermute(q_own, "x", shift(d)) for d in RING[1:]])
+    q_chip, w_own = lax.optimization_barrier((q_chip, jnp.transpose(w_out)))
     q_core = lax.ppermute(q_chip, "c", SWAP)
-    q_core, w_own = lax.optimization_barrier((q_core, jnp.transpose(w_out)))
     z_w = lax.ppermute(w_own, "z", SWAP)
 
     row = jnp.arange(ROWS, dtype=jnp.int32)
@@ -340,9 +366,9 @@
     qpos = jnp.broadcast_to((offset[0] + row).astype(jnp.float32)[None, :], (8, ROWS))
 
     q = absorb((q_chip, q_core), w_uk)
-    state = attend(q, qpos, near)
-    state, far = lax.optimization_barrier((state, far))
-    keep, send = attend(q, qpos, far, state, value_up_weight)
+    earlier = attend(q, qpos, value_up_weight, near)
+    earlier, far = lax.optimization_barrier((earlier, far))
+    keep, send = attend(q, qpos, value_up_weight, far, earlier)
 
     z_w, send = lax.optimization_barrier((z_w, send))
     parts = call(
@@ -360,12 +386,7 @@
 
     rows = lax.all_to_all(heads, ("y", "x"), 0, 0, tiled=True).reshape(16 * R, HG * VDIM)
     ncol = w_out.shape[1]
-    columns = call(
-        columns_kernel,
-        jax.ShapeDtypeStruct((4, HG * VDIM, 128), jnp.bfloat16),
-        in_specs=[pl.BlockSpec(memory_space=pltpu.SMEM)]
-        + [pl.BlockSpec(memory_space=pltpu.VMEM)] * 4,
-    )(jnp.stack([z, c]), w_own, z_w, c_w, zc_w)
+    columns = columns_of(jnp.stack([z, c]), (w_own, z_w, c_w, zc_w))
     sums = call(project_kernel, jax.ShapeDtypeStruct((4, 16 * R, ncol), jnp.bfloat16))(
         rows, columns
     )

time: 118 us -> 114 us (0.966)
  starting transfers between devices: 41.4 us -> 38.3 us
  waiting for transfers between devices: 21.1 us -> 18.5 us
  local copies, waits for them, and re-layouts: 3.63 us -> 6.23 us
  Pallas kernels: 29.3 us -> 27.4 us
    ppermute x1, starting transfers between devices: 5.15 us -> 0.09 us  [local(): z_w = lax.ppermute(w_own, 'z', SWAP)]
    ppermute x8 -> x9, starting transfers between devices: 12.7 us -> 16.7 us  [the longest x3 7.15 us: local(): far = [z_keys] + [lax.ppermute(z_keys, 'y', shift(d)) for d in RING[1:]]]
    ppermute x1, starting transfers between devices: 3.92 us -> 1.12 us  [local(): c_w = lax.ppermute(w_own, 'c', SWAP)]
    unnamed x20 -> x16, local copies, waits for them, and re-layouts: 3.63 us -> 6.23 us
    all_to_all x1, waiting for transfers between devices: 11.1 us -> 9.45 us  [local(): lax.all_to_all(heads, ('y', 'x'), 0, 0, tiled=True)]
    pallas_call x2 -> x1, Pallas kernels: 1.29 us -> 0.03 us  [join(): return call(join_kernel, jax.ShapeDtypeStruct(shape, jnp.bfloat16))(*parts)]
    ppermute x8 -> x9, waiting for transfers between devices: 4.88 us -> 5.3 us  [the longest x3 5.11 us: local(): lax.ppermute(q_own, 'x', shift(d))]
  transfers between devices with their start and end apart: 18 -> 19, of which waited for: 7 -> 6; matrix products, arithmetic and copies ran while one was open for 0% -> 0% of each run, Pallas kernels for 21% -> 19%
where the time goes in v7:
time: 114 us
  starting transfers between devices  38.3 us (34%)
  Pallas kernels  27.4 us (24%)
  blocking collectives  22.2 us (19%)
  waiting for transfers between devices  18.5 us (16%)
  local copies, waits for them, and re-layouts  6.23 us (5%)
    all_to_all x1, blocking collectives, local(): lax.all_to_all(sums.reshape(16, 4 * R, ncol), ('z', 'c', 'head'), 0, 0, t...  22.2 us
    pallas_call x2, Pallas kernels, attend(): call(functools.partial(attend_kernel, n, last), out_shape, grid=(ITEMS //...  18.4 us
    all_to_all x1, waiting for transfers between devices, local(): lax.all_to_all(heads, ('y', 'x'), 0, 0, tiled=True)  9.45 us
    ppermute x3, starting transfers between devices, local(): far = [z_keys] + [lax.ppermute(z_keys, 'y', shift(d)) for d in RING[1:]]  7.15 us
    unnamed x16, local copies, waits for them, and re-layouts  6.23 us
    ppermute x1, starting transfers between devices, local(): z_keys = lax.ppermute(keys, 'z', SWAP)  6.01 us
    all_to_all x1, starting transfers between devices, local(): lax.all_to_all(heads, ('y', 'x'), 0, 0, tiled=True)  5.3 us
    ppermute x3, starting transfers between devices, local(): lax.ppermute(q_own, 'x', shift(d))  5.2 us
  transfers between devices with their start and end apart: 19, of which 6 were waited for; matrix products, arithmetic and copies ran while one was open for 0% of the time, Pallas kernels for 19%

profile of v7, /device:TPU:33, one launch (start us, length us, event | category | flops | bytes accessed | tf_op | source)
XLA Modules:
  0.0 113.6 jit_solution(897974035041740536)
XLA Ops:
  0.0 1.0 shard_map.100.refs_3_
  1.0 0.9 shard_map.101.refs_0_
  1.9 1.3 %collective-permute-start = (bf16[16,3072]{1,0:T(8,128)(2,1)S(1)}, bf16[16,3072]{1,0:T(8,128)(2,1)S(1)}, u32[]{:S(2)}, u32[]{:S(2)}) collective-permute-start(bf16[16,3072]{1,0:T(8,128)(2,1)S(1)} %shard_map.101.refs_0_), channel_id=1, source_target_pairs={{0,16},{16,32},{32,48},{48,0},{1,17},{17,33},{33,49},{49,1},{2,18}... | collective-permute-start | bytes 294920 | tf_op jit(solution)/shard_map/ppermute | solution.py:356
  3.2 6.0 %collective-permute-start.4 = (bf16[256,640]{1,0:T(8,128)(2,1)S(1)}, bf16[256,640]{1,0:T(8,128)(2,1)S(1)}, u32[]{:S(2)}, u32[]{:S(2)}) collective-permute-start(bf16[256,640]{1,0:T(8,128)(2,1)S(1)} %shard_map.100.refs_3_), channel_id=1, source_target_pairs={{0,8},{8,0},{1,9},{9,1},{2,10},{10,2},{3,11},{11,3},{4,12},{12,4},... | collective-permute-start | bytes 983048 | tf_op jit(solution)/shard_map/ppermute | solution.py:351
  9.2 1.3 %collective-permute-start.5 = (bf16[256,640]{1,0:T(8,128)(2,1)S(1)}, bf16[256,640]{1,0:T(8,128)(2,1)S(1)}, u32[]{:S(2)}, u32[]{:S(2)}) collective-permute-start(bf16[256,640]{1,0:T(8,128)(2,1)S(1)} %shard_map.100.refs_3_), channel_id=1, source_target_pairs={{0,64},{64,128},{128,192},{192,0},{1,65},{65,129},{129,193},{193,1... | collective-permute-start | bytes 983048 | tf_op jit(solution)/shard_map/ppermute | solution.py:352
  10.5 1.4 %collective-permute-start.6 = (bf16[256,640]{1,0:T(8,128)(2,1)S(1)}, bf16[256,640]{1,0:T(8,128)(2,1)S(1)}, u32[]{:S(2)}, u32[]{:S(2)}) collective-permute-start(bf16[256,640]{1,0:T(8,128)(2,1)S(1)} %shard_map.100.refs_3_), channel_id=1, source_target_pairs={{0,192},{64,0},{128,64},{192,128},{1,193},{65,1},{129,65},{193,129... | collective-permute-start | bytes 983048 | tf_op jit(solution)/shard_map/ppermute | solution.py:352
  11.9 1.6 %collective-permute-start.7 = (bf16[256,640]{1,0:T(8,128)(2,1)S(1)}, bf16[256,640]{1,0:T(8,128)(2,1)S(1)}, u32[]{:S(2)}, u32[]{:S(2)}) collective-permute-start(bf16[256,640]{1,0:T(8,128)(2,1)S(1)} %shard_map.100.refs_3_), channel_id=1, source_target_pairs={{0,128},{64,192},{128,0},{192,64},{1,129},{65,193},{129,1},{193,65... | collective-permute-start | bytes 983048 | tf_op jit(solution)/shard_map/ppermute | solution.py:352
  13.6 0.0 collective-permute-done.refs_1_
  13.6 1.5 %collective-permute-start.1 = (bf16[16,3072]{1,0:T(8,128)(2,1)S(1)}, bf16[16,3072]{1,0:T(8,128)(2,1)S(1)}, u32[]{:S(2)}, u32[]{:S(2)}) collective-permute-start(bf16[16,3072]{1,0:T(8,128)(2,1)S(1)} %shard_map.101.refs_0_), channel_id=1, source_target_pairs={{0,48},{16,0},{32,16},{48,32},{1,49},{17,1},{33,17},{49,33},{2,50}... | collective-permute-start | bytes 294920 | tf_op jit(solution)/shard_map/ppermute | solution.py:356
  15.0 2.3 %collective-permute-done.1.refs_2_ = bf16[16,3072]{1,0:T(8,128)(2,1)S(1)} collective-permute-done((bf16[16,3072]{1,0:T(8,128)(2,1)S(1)}, bf16[16,3072]{1,0:T(8,128)(2,1)S(1)}, u32[]{:S(2)}, u32[]{:S(2)}) %collective-permute-start.1) | collective-permute-done | bytes 98336 | tf_op jit(solution)/shard_map/ppermute | solution.py:356
  17.3 2.5 %collective-permute-start.2 = (bf16[16,3072]{1,0:T(8,128)(2,1)S(1)}, bf16[16,3072]{1,0:T(8,128)(2,1)S(1)}, u32[]{:S(2)}, u32[]{:S(2)}) collective-permute-start(bf16[16,3072]{1,0:T(8,128)(2,1)S(1)} %shard_map.101.refs_0_), channel_id=1, source_target_pairs={{0,32},{16,48},{32,0},{48,16},{1,33},{17,49},{33,1},{49,17},{2,34}... | collective-permute-start | bytes 294920 | tf_op jit(solution)/shard_map/ppermute | solution.py:356
  19.8 2.8 %collective-permute-done.2.refs_3_ = bf16[16,3072]{1,0:T(8,128)(2,1)S(1)} collective-permute-done((bf16[16,3072]{1,0:T(8,128)(2,1)S(1)}, bf16[16,3072]{1,0:T(8,128)(2,1)S(1)}, u32[]{:S(2)}, u32[]{:S(2)}) %collective-permute-start.2) | collective-permute-done | bytes 98336 | tf_op jit(solution)/shard_map/ppermute | solution.py:356
  22.6 0.1 collective-permute-start.11
  22.7 0.0 collective-permute-done.4.refs_3_
  22.7 3.9 %collective-permute-start.3 = (bf16[64,3072]{1,0:T(8,128)(2,1)S(1)}, bf16[64,3072]{1,0:T(8,128)(2,1)S(1)}, u32[]{:S(2)}, u32[]{:S(2)}) collective-permute-start(bf16[64,3072]{1,0:T(8,128)(2,1)S(1)} %shard_map.102.refs_0_), channel_id=1, source_target_pairs={{0,4},{4,0},{1,5},{5,1},{2,6},{6,2},{3,7},{7,3},{8,12},{12,8},{9,1... | collective-permute-start | bytes 1179656 | tf_op jit(solution)/shard_map/ppermute | solution.py:358
  26.6 0.0 collective-permute-done.5.refs_4_
  26.6 4.5 %collective-permute-start.10 = (bf16[256,640]{1,0:T(8,128)(2,1)S(1)}, bf16[256,640]{1,0:T(8,128)(2,1)S(1)}, u32[]{:S(2)}, u32[]{:S(2)}) collective-permute-start(bf16[256,640]{1,0:T(8,128)(2,1)S(1)} %collective-permute-done.4.refs_3_), channel_id=1, source_target_pairs={{0,128},{64,192},{128,0},{192,64},{1,129},{65,193},{129,1},{193,65... | collective-permute-start | bytes 983048 | tf_op jit(solution)/shard_map/ppermute | solution.py:354
  31.1 0.6 collective-permute-start.8
  31.8 2.0 %collective-permute-start.9 = (bf16[256,640]{1,0:T(8,128)(2,1)S(1)}, bf16[256,640]{1,0:T(8,128)(2,1)}, u32[]{:S(2)}, u32[]{:S(2)}) collective-permute-start(bf16[256,640]{1,0:T(8,128)(2,1)S(1)} %collective-permute-done.4.refs_3_), channel_id=1, source_target_pairs={{0,192},{64,0},{128,64},{192,128},{1,193},{65,1},{129,65},{193,129... | collective-permute-start | bytes 983048 | tf_op jit(solution)/shard_map/ppermute | solution.py:354
  34.5 0.0 collective-permute-done.3.refs_1_
  34.5 1.1 collective-permute-start.16
  35.6 1.6 %copy-done.1 = bf16[16,128,512]{2,1,0:T(8,128)(2,1)S(1)} copy-done((bf16[16,128,512]{2,1,0:T(8,128)(2,1)S(1)}, bf16[16,128,512]{2,1,0:T(8,128)(2,1)}, u32[]{:S(2)}) %copy-start.1) | copy-done | bytes 2097176
  37.2 0.8 shard_map.103.refs_0_
  38.0 8.6 %shard_map.104 = (f32[128,2048]{1,0:T(8,128)S(1)}, f32[2048,128]{1,0:T(8,128)S(1)}) custom-call(bf16[2048,768]{1,0:T(8,128)(2,1)S(1)} %shard_map.103.refs_0_, f32[8,128]{1,0:T(8,128)S(1)} %broadcast_in_dim.17.refs_1_, bf16[16,512,128]{2,1,0:T(8,128)(2,1)S(1)} %copy-done, bf16[256,640]{1,0:T(8,128)(2,1)S(1)} %shard_map.100.refs_3_, ...), custom_call_target="tpu_custom_call" | custom-call | flops 1 | bytes 1 | tf_op jit(solution)/shard_map/pallas_call | solution.py:255
  46.6 0.0 collective-permute-done.10.refs_6_
  46.6 0.2 collective-permute-done.9.refs_5_
  46.8 9.9 %shard_map.105 = (bf16[64,2176]{1,0:T(8,128)(2,1)S(1)}, bf16[64,2176]{1,0:T(8,128)(2,1)S(1)}) custom-call(bf16[2048,768]{1,0:T(8,128)(2,1)S(1)} %shard_map.103.refs_0_, f32[8,128]{1,0:T(8,128)S(1)} %broadcast_in_dim.17.refs_1_, bf16[16,512,128]{2,1,0:T(8,128)(2,1)S(1)} %copy-done, bf16[256,640]{1,0:T(8,128)(2,1)S(1)} %collective-permute-done.4.refs_3_, ...), custom_call_target="tpu_custom_call" | custom-call | flops 1 | bytes 1 | tf_op jit(solution)/shard_map/pallas_call | solution.py:255
  56.7 0.9 collective-permute-start.17
  57.6 0.1 collective-permute-start.12
  57.7 1.7 %collective-permute-done.12.b_ref = bf16[64,2176]{1,0:T(8,128)(2,1)S(1)} collective-permute-done((bf16[64,2176]{1,0:T(8,128)(2,1)S(1)}, bf16[64,2176]{1,0:T(8,128)(2,1)S(1)}, u32[]{:S(2)}, u32[]{:S(2)}) %collective-permute-start.12) | collective-permute-done | bytes 278560 | tf_op jit(solution)/shard_map/ppermute | solution.py:376
  59.4 0.5 shard_map.106
  59.9 0.5 collective-permute-start.13
  60.4 1.0 collective-permute-start.14
  61.5 2.6 %collective-permute-start.15 = (bf16[16,2176]{1,0:T(8,128)(2,1)S(1)}, bf16[16,2176]{1,0:T(8,128)(2,1)S(1)}, u32[]{:S(2)}, u32[]{:S(2)}) collective-permute-start(bf16[16,2176]{1,0:T(8,128)(2,1)S(1)} %get-tuple-element.59), channel_id=1, source_target_pairs={{0,32},{16,48},{32,0},{48,16},{1,33},{17,49},{33,1},{49,17},{2,34}... | collective-permute-start | bytes 208904 | tf_op jit(solution)/shard_map/ppermute | solution.py:378
  64.1 0.8 copy-done.4
  64.9 2.0 %collective-permute-done.15.refs_3_ = bf16[16,2176]{1,0:T(8,128)(2,1)S(1)} collective-permute-done((bf16[16,2176]{1,0:T(8,128)(2,1)S(1)}, bf16[16,2176]{1,0:T(8,128)(2,1)S(1)}, u32[]{:S(2)}, u32[]{:S(2)}) %collective-permute-start.15) | collective-permute-done | bytes 69664 | tf_op jit(solution)/shard_map/ppermute | solution.py:378
  66.9 0.8 copy-done.6
  67.7 1.4 %shard_map.107 = bf16[16,16,2048]{2,1,0:T(8,128)(2,1)} custom-call(bf16[16,2176]{1,0:T(8,128)(2,1)S(1)} %get-tuple-element.61.refs_0_, bf16[16,2176]{1,0:T(8,128)(2,1)S(1)} %collective-permute-done.13.refs_1_, bf16[16,2176]{1,0:T(8,128)(2,1)S(1)} %collective-permute-done.14.refs_2_, bf16[16,2176]{1,0:T(8,128)(2,1)S(1)} %collective-permute-done.15.refs_3_), custom_call_target="tpu_custom_call" | custom-call | flops 1 | bytes 1 | tf_op jit(solution)/shard_map/pallas_call | solution.py:383
  69.1 5.3 %all-to-all-start = ((bf16[16,16,2048]{2,1,0:T(8,128)(2,1)}), bf16[16,16,2048]{2,1,0:T(8,128)(2,1)S(1)}, u32[]{:S(2)}, u32[]{:S(2)}) async-start(bf16[16,16,2048]{2,1,0:T(8,128)(2,1)} %shard_map.107), calls=%async_computation | async-start | bytes 2097152 | tf_op jit(solution)/shard_map/all_to_all | solution.py:387
  74.4 0.1 pad_add_fusion.zc_ref
  74.5 1.0 copy-done.3
  75.5 1.0 copy-done.5
  76.5 1.0 copy-done.7
  77.5 2.4 %shard_map.108.w_ref = bf16[4,2048,128]{2,1,0:T(8,128)(2,1)S(1)} custom-call(s32[2]{0:T(128)S(1)} %pad_add_fusion.zc_ref, bf16[112,2048]{1,0:T(8,128)(2,1)} %bitcast.22, bf16[112,2048]{1,0:T(8,128)(2,1)S(1)} %copy-done.3, bf16[112,2048]{1,0:T(8,128)(2,1)S(1)} %copy-done.5, bf16[112,2048]{1,0:T(8,128)(2,1)S(1)} %copy-done.7), custom_call_target="tpu_custom_call" | custom-call | flops 1 | bytes 1 | tf_op jit(solution)/shard_map/pallas_call | solution.py:316
  80.0 9.4 %all-to-all-done = bf16[16,16,2048]{2,1,0:T(8,128)(2,1)S(1)} async-done(((bf16[16,16,2048]{2,1,0:T(8,128)(2,1)}), bf16[16,16,2048]{2,1,0:T(8,128)(2,1)S(1)}, u32[]{:S(2)}, u32[]{:S(2)}) %all-to-all-start) | async-done | bytes 1048608 | tf_op jit(solution)/shard_map/all_to_all | solution.py:387
  89.4 1.2 %shard_map.109 = bf16[4,256,112]{2,1,0:T(8,128)(2,1)S(1)} custom-call(bf16[256,2048]{1,0:T(8,128)(2,1)S(1)} %bitcast.18, bf16[4,2048,128]{2,1,0:T(8,128)(2,1)S(1)} %shard_map.108.w_ref), custom_call_target="tpu_custom_call" | custom-call | flops 1 | bytes 1 | tf_op jit(solution)/shard_map/pallas_call | solution.py:390
  90.7 22.2 %all_to_all.10.sums_ref = bf16[16,64,112]{2,1,0:T(8,128)(2,1)S(1)} all-to-all(bf16[16,64,112]{2,1,0:T(8,128)(2,1)S(1)} %bitcast.19), channel_id=1, replica_groups=mesh['y'=4,'x'=4,'z'=2,'c'=2,'head'=4] {'z','c','head'}, dimensions={0} | all-to-all | bytes 458752 | tf_op jit(solution)/shard_map/all_to_all | solution.py:393
  112.9 0.7 shard_map.110
  (21 shorter events, 0.1 us)
Async XLA Ops:
  1.9 11.7 %collective-permute-start = (bf16[16,3072]{1,0:T(8,128)(2,1)S(1)}, bf16[16,3072]{1,0:T(8,128)(2,1)S(1)}, u32[]{:S(2)}, u32[]{:S(2)}) collective-permute-start(bf16[16,3072]{1,0:T(8,128)(2,1)S(1)} %shard_map.101.refs_0_), channel_id=1, source_target_pairs={{0,16},{16,32},{32,48},{48,0},{1,17},{17,33},{33,49},{49,1},{2,18}... | collective-permute-start | bytes 294920 | tf_op jit(solution)/shard_map/ppermute | solution.py:356
  3.2 19.6 %collective-permute-start.4 = (bf16[256,640]{1,0:T(8,128)(2,1)S(1)}, bf16[256,640]{1,0:T(8,128)(2,1)S(1)}, u32[]{:S(2)}, u32[]{:S(2)}) collective-permute-start(bf16[256,640]{1,0:T(8,128)(2,1)S(1)} %shard_map.100.refs_3_), channel_id=1, source_target_pairs={{0,8},{8,0},{1,9},{9,1},{2,10},{10,2},{3,11},{11,3},{4,12},{12,4},... | collective-permute-start | bytes 983048 | tf_op jit(solution)/shard_map/ppermute | solution.py:351
  9.2 17.4 %collective-permute-start.5 = (bf16[256,640]{1,0:T(8,128)(2,1)S(1)}, bf16[256,640]{1,0:T(8,128)(2,1)S(1)}, u32[]{:S(2)}, u32[]{:S(2)}) collective-permute-start(bf16[256,640]{1,0:T(8,128)(2,1)S(1)} %shard_map.100.refs_3_), channel_id=1, source_target_pairs={{0,64},{64,128},{128,192},{192,0},{1,65},{65,129},{129,193},{193,1... | collective-permute-start | bytes 983048 | tf_op jit(solution)/shard_map/ppermute | solution.py:352
  10.5 16.1 %collective-permute-start.6 = (bf16[256,640]{1,0:T(8,128)(2,1)S(1)}, bf16[256,640]{1,0:T(8,128)(2,1)S(1)}, u32[]{:S(2)}, u32[]{:S(2)}) collective-permute-start(bf16[256,640]{1,0:T(8,128)(2,1)S(1)} %shard_map.100.refs_3_), channel_id=1, source_target_pairs={{0,192},{64,0},{128,64},{192,128},{1,193},{65,1},{129,65},{193,129... | collective-permute-start | bytes 983048 | tf_op jit(solution)/shard_map/ppermute | solution.py:352
  11.9 14.7 %collective-permute-start.7 = (bf16[256,640]{1,0:T(8,128)(2,1)S(1)}, bf16[256,640]{1,0:T(8,128)(2,1)S(1)}, u32[]{:S(2)}, u32[]{:S(2)}) collective-permute-start(bf16[256,640]{1,0:T(8,128)(2,1)S(1)} %shard_map.100.refs_3_), channel_id=1, source_target_pairs={{0,128},{64,192},{128,0},{192,64},{1,129},{65,193},{129,1},{193,65... | collective-permute-start | bytes 983048 | tf_op jit(solution)/shard_map/ppermute | solution.py:352
  13.6 3.8 %collective-permute-start.1 = (bf16[16,3072]{1,0:T(8,128)(2,1)S(1)}, bf16[16,3072]{1,0:T(8,128)(2,1)S(1)}, u32[]{:S(2)}, u32[]{:S(2)}) collective-permute-start(bf16[16,3072]{1,0:T(8,128)(2,1)S(1)} %shard_map.101.refs_0_), channel_id=1, source_target_pairs={{0,48},{16,0},{32,16},{48,32},{1,49},{17,1},{33,17},{49,33},{2,50}... | collective-permute-start | bytes 294920 | tf_op jit(solution)/shard_map/ppermute | solution.py:356
  17.3 5.3 %collective-permute-start.2 = (bf16[16,3072]{1,0:T(8,128)(2,1)S(1)}, bf16[16,3072]{1,0:T(8,128)(2,1)S(1)}, u32[]{:S(2)}, u32[]{:S(2)}) collective-permute-start(bf16[16,3072]{1,0:T(8,128)(2,1)S(1)} %shard_map.101.refs_0_), channel_id=1, source_target_pairs={{0,32},{16,48},{32,0},{48,16},{1,33},{17,49},{33,1},{49,17},{2,34}... | collective-permute-start | bytes 294920 | tf_op jit(solution)/shard_map/ppermute | solution.py:356
  22.6 34.0 %collective-permute-start.11 = (bf16[112,2048]{1,0:T(8,128)(2,1)}, bf16[112,2048]{1,0:T(8,128)(2,1)S(1)}, u32[]{:S(2)}, u32[]{:S(2)}) collective-permute-start(bf16[112,2048]{1,0:T(8,128)(2,1)} %bitcast.20), channel_id=1, source_target_pairs={{0,8},{8,0},{1,9},{9,1},{2,10},{10,2},{3,11},{11,3},{4,12},{12,4},... | collective-permute-start | bytes 1376264 | tf_op jit(solution)/shard_map/ppermute | solution.py:359
  22.7 11.7 %collective-permute-start.3 = (bf16[64,3072]{1,0:T(8,128)(2,1)S(1)}, bf16[64,3072]{1,0:T(8,128)(2,1)S(1)}, u32[]{:S(2)}, u32[]{:S(2)}) collective-permute-start(bf16[64,3072]{1,0:T(8,128)(2,1)S(1)} %shard_map.102.refs_0_), channel_id=1, source_target_pairs={{0,4},{4,0},{1,5},{5,1},{2,6},{6,2},{3,7},{7,3},{8,12},{12,8},{9,1... | collective-permute-start | bytes 1179656 | tf_op jit(solution)/shard_map/ppermute | solution.py:358
  26.6 20.0 %collective-permute-start.10 = (bf16[256,640]{1,0:T(8,128)(2,1)S(1)}, bf16[256,640]{1,0:T(8,128)(2,1)S(1)}, u32[]{:S(2)}, u32[]{:S(2)}) collective-permute-start(bf16[256,640]{1,0:T(8,128)(2,1)S(1)} %collective-permute-done.4.refs_3_), channel_id=1, source_target_pairs={{0,128},{64,192},{128,0},{192,64},{1,129},{65,193},{129,1},{193,65... | collective-permute-start | bytes 983048 | tf_op jit(solution)/shard_map/ppermute | solution.py:354
  31.1 15.5 %collective-permute-start.8 = (bf16[256,640]{1,0:T(8,128)(2,1)S(1)}, bf16[256,640]{1,0:T(8,128)(2,1)S(1)}, u32[]{:S(2)}, u32[]{:S(2)}) collective-permute-start(bf16[256,640]{1,0:T(8,128)(2,1)S(1)} %collective-permute-done.4.refs_3_), channel_id=1, source_target_pairs={{0,64},{64,128},{128,192},{192,0},{1,65},{65,129},{129,193},{193,1... | collective-permute-start | bytes 983048 | tf_op jit(solution)/shard_map/ppermute | solution.py:354
  31.8 15.0 %collective-permute-start.9 = (bf16[256,640]{1,0:T(8,128)(2,1)S(1)}, bf16[256,640]{1,0:T(8,128)(2,1)}, u32[]{:S(2)}, u32[]{:S(2)}) collective-permute-start(bf16[256,640]{1,0:T(8,128)(2,1)S(1)} %collective-permute-done.4.refs_3_), channel_id=1, source_target_pairs={{0,192},{64,0},{128,64},{192,128},{1,193},{65,1},{129,65},{193,129... | collective-permute-start | bytes 983048 | tf_op jit(solution)/shard_map/ppermute | solution.py:354
  34.5 3.5 %copy-start = (bf16[16,512,128]{2,1,0:T(8,128)(2,1)S(1)}, bf16[16,512,128]{2,1,0:T(8,128)(2,1)}, u32[]{:S(2)}) copy-start(bf16[16,512,128]{2,1,0:T(8,128)(2,1)} %refs_2_.5) | copy-start | bytes 6291460
  34.5 29.6 %collective-permute-start.16 = (bf16[112,2048]{1,0:T(8,128)(2,1)}, bf16[112,2048]{1,0:T(8,128)(2,1)S(1)}, u32[]{:S(2)}, u32[]{:S(2)}) collective-permute-start(bf16[112,2048]{1,0:T(8,128)(2,1)} %bitcast.21), channel_id=1, source_target_pairs={{0,4},{4,0},{1,5},{5,1},{2,6},{6,2},{3,7},{7,3},{8,12},{12,8},{9,1... | collective-permute-start | bytes 1376264 | tf_op jit(solution)/shard_map/ppermute | solution.py:380
  35.6 1.6 %copy-start.1 = (bf16[16,128,512]{2,1,0:T(8,128)(2,1)S(1)}, bf16[16,128,512]{2,1,0:T(8,128)(2,1)}, u32[]{:S(2)}) copy-start(bf16[16,128,512]{2,1,0:T(8,128)(2,1)} %refs_2_.3) | copy-start | bytes 6291460
  56.7 17.7 %copy-start.2 = (bf16[112,2048]{1,0:T(8,128)(2,1)}, bf16[112,2048]{1,0:T(8,128)(2,1)S(1)}, u32[]{:S(2)}) copy-start(bf16[112,2048]{1,0:T(8,128)(2,1)S(1)} %collective-permute-done.11.refs_1_) | copy-start | bytes 1376260
  56.7 10.2 %collective-permute-start.17 = (bf16[112,2048]{1,0:T(8,128)(2,1)S(1)}, bf16[112,2048]{1,0:T(8,128)(2,1)S(1)}, u32[]{:S(2)}, u32[]{:S(2)}) collective-permute-start(bf16[112,2048]{1,0:T(8,128)(2,1)S(1)} %collective-permute-done.11.refs_1_), channel_id=1, source_target_pairs={{0,4},{4,0},{1,5},{5,1},{2,6},{6,2},{3,7},{7,3},{8,12},{12,8},{9,1... | collective-permute-start | bytes 1376264 | tf_op jit(solution)/shard_map/ppermute | solution.py:381
  57.6 1.8 %collective-permute-start.12 = (bf16[64,2176]{1,0:T(8,128)(2,1)S(1)}, bf16[64,2176]{1,0:T(8,128)(2,1)S(1)}, u32[]{:S(2)}, u32[]{:S(2)}) collective-permute-start(bf16[64,2176]{1,0:T(8,128)(2,1)S(1)} %get-tuple-element.55), channel_id=1, source_target_pairs={{0,4},{4,0},{1,5},{5,1},{2,6},{6,2},{3,7},{7,3},{8,12},{12,8},{9,1... | collective-permute-start | bytes 835592 | tf_op jit(solution)/shard_map/ppermute | solution.py:376
  59.9 5.0 %collective-permute-start.13 = (bf16[16,2176]{1,0:T(8,128)(2,1)S(1)}, bf16[16,2176]{1,0:T(8,128)(2,1)S(1)}, u32[]{:S(2)}, u32[]{:S(2)}) collective-permute-start(bf16[16,2176]{1,0:T(8,128)(2,1)S(1)} %get-tuple-element.57), channel_id=1, source_target_pairs={{0,48},{16,0},{32,16},{48,32},{1,49},{17,1},{33,17},{49,33},{2,50}... | collective-permute-start | bytes 208904 | tf_op jit(solution)/shard_map/ppermute | solution.py:378
  60.4 4.5 %collective-permute-start.14 = (bf16[16,2176]{1,0:T(8,128)(2,1)S(1)}, bf16[16,2176]{1,0:T(8,128)(2,1)S(1)}, u32[]{:S(2)}, u32[]{:S(2)}) collective-permute-start(bf16[16,2176]{1,0:T(8,128)(2,1)S(1)} %get-tuple-element.58), channel_id=1, source_target_pairs={{0,16},{16,32},{32,48},{48,0},{1,17},{17,33},{33,49},{49,1},{2,18}... | collective-permute-start | bytes 208904 | tf_op jit(solution)/shard_map/ppermute | solution.py:378
  61.5 5.4 %collective-permute-start.15 = (bf16[16,2176]{1,0:T(8,128)(2,1)S(1)}, bf16[16,2176]{1,0:T(8,128)(2,1)S(1)}, u32[]{:S(2)}, u32[]{:S(2)}) collective-permute-start(bf16[16,2176]{1,0:T(8,128)(2,1)S(1)} %get-tuple-element.59), channel_id=1, source_target_pairs={{0,32},{16,48},{32,0},{48,16},{1,33},{17,49},{33,1},{49,17},{2,34}... | collective-permute-start | bytes 208904 | tf_op jit(solution)/shard_map/ppermute | solution.py:378
  64.1 0.8 copy-start.4
  66.9 0.8 copy-start.6
  69.1 20.3 %all-to-all-start = ((bf16[16,16,2048]{2,1,0:T(8,128)(2,1)}), bf16[16,16,2048]{2,1,0:T(8,128)(2,1)S(1)}, u32[]{:S(2)}, u32[]{:S(2)}) async-start(bf16[16,16,2048]{2,1,0:T(8,128)(2,1)} %shard_map.107), calls=%async_computation | async-start | bytes 2097152 | tf_op jit(solution)/shard_map/all_to_all | solution.py:387
  74.5 1.0 copy-start.3
  75.5 1.0 copy-start.5
  76.5 1.0 copy-start.7

commit v8 on v7

--- a/solution.py
+++ b/solution.py
@@ -31,7 +31,7 @@
     return [(i, (i + d) % 4) for i in range(4)]
 
 
-def call(kernel, out_shape, vmem=40, **kw):
+def call(kernel, out_shape, vmem=8, **kw):
     return pl.pallas_call(
         kernel,
         out_shape=out_shape,
@@ -52,11 +52,15 @@
     return [pltpu.with_memory_space_constraint(a, pltpu.HBM) for a in arrays]
 
 
-def pack_keys_kernel(latent_ref, key_rope_ref, pos_ref, key_ref, rope, pos, sems):
+def pack_kernel(
+    latent_ref, key_rope_ref, pos_ref, query_ref, q_rope_ref, key_ref, q_ref, rope, pos, sems
+):
     copies = [
         pltpu.make_async_copy(key_rope_ref, rope, sems.at[0]),
         pltpu.make_async_copy(pos_ref, pos, sems.at[1]),
         pltpu.make_async_copy(latent_ref, key_ref.at[:, :RANK], sems.at[2]),
+        pltpu.make_async_copy(query_ref, q_ref.at[:, : HG * NOPE], sems.at[3]),
+        pltpu.make_async_copy(q_rope_ref, q_ref.at[:, HG * NOPE :], sems.at[4]),
     ]
     for copy in copies:
         copy.start()
@@ -68,42 +72,24 @@
     ext = jnp.where(row == 0, high, jnp.where(row == 1, where - high * 128, 0.0))
     ext = jnp.concatenate([rope[...].astype(jnp.float32), ext], axis=0)
     key_ref[:, RANK:] = jnp.transpose(ext).astype(jnp.bfloat16)
-    copies[2].wait()
-
-
-def pack_keys(latent, k_rope, key_pos):
+    for copy in copies[2:]:
+        copy.wait()
+
+
+def pack(latent, k_rope, key_pos, query, q_rope):
     return call(
-        pack_keys_kernel,
-        jax.ShapeDtypeStruct((latent.shape[0], KEYW), jnp.bfloat16),
-        vmem=16,
-        in_specs=[HBM] * 3,
+        pack_kernel,
+        (
+            jax.ShapeDtypeStruct((latent.shape[0], KEYW), jnp.bfloat16),
+            jax.ShapeDtypeStruct((R, HG * (NOPE + ROPE)), jnp.bfloat16),
+        ),
+        in_specs=[HBM] * 5,
         scratch_shapes=[
             pltpu.VMEM((k_rope.shape[1], k_rope.shape[0]), jnp.bfloat16),
             pltpu.VMEM(key_pos.shape, jnp.int32),
-            pltpu.SemaphoreType.DMA((3,)),
+            pltpu.SemaphoreType.DMA((5,)),
         ],
-    )(*in_hbm(latent, jnp.transpose(k_rope), key_pos))
-
-
-def pack_queries_kernel(query_ref, rope_ref, out_ref, sems):
-    copies = [
-        pltpu.make_async_copy(query_ref, out_ref.at[:, : HG * NOPE], sems.at[0]),
-        pltpu.make_async_copy(rope_ref, out_ref.at[:, HG * NOPE :], sems.at[1]),
-    ]
-    for copy in copies:
-        copy.start()
-    for copy in copies:
-        copy.wait()
-
-
-def pack_queries(query, q_rope):
-    return call(
-        pack_queries_kernel,
-        jax.ShapeDtypeStruct((R, HG * (NOPE + ROPE)), jnp.bfloat16),
-        vmem=16,
-        in_specs=[HBM] * 2,
-        scratch_shapes=[pltpu.SemaphoreType.DMA((2,))],
-    )(*in_hbm(query, q_rope))
+    )(*in_hbm(latent, jnp.transpose(k_rope), key_pos, query, q_rope))
 
 
 def join_kernel(*refs):
@@ -119,7 +105,18 @@
 
 
 def absorb_kernel(*refs):
-    q_refs, (w_ref, out_ref) = refs[:2], refs[2:]
+    q_refs, (w_hbm, out_ref, w_ref, sems) = refs[:2], refs[2:]
+    step = HG // 4
+    copies = [
+        pltpu.make_async_copy(
+            w_hbm.at[i * step : (i + 1) * step],
+            w_ref.at[i * step : (i + 1) * step],
+            sems.at[i],
+        )
+        for i in range(4)
+    ]
+    for copy in copies:
+        copy.start()
     lane = lax.broadcasted_iota(jnp.int32, (ROWS, 128), 1)
     row = lax.broadcasted_iota(jnp.int32, (ROWS, 128), 0)
     one_hot = (lane == row).astype(jnp.bfloat16)
@@ -128,6 +125,8 @@
         return jnp.concatenate([ref[:, start : start + 128] for ref in q_refs], axis=0)
 
     for h in range(HG):
+        if h % step == 0:
+            copies[h // step].wait()
         rows = slice(h * ROWS, (h + 1) * ROWS)
         latent = jnp.dot(columns(h * NOPE), w_ref[h], preferred_element_type=jnp.float32)
         out_ref[rows, :RANK] = latent.astype(jnp.bfloat16)
@@ -140,9 +139,16 @@
 
 
 def absorb(queries, w_uk):
-    return call(absorb_kernel, jax.ShapeDtypeStruct((ITEMS, ITEMW), jnp.bfloat16))(
-        *queries, w_uk
-    )
+    return call(
+        absorb_kernel,
+        jax.ShapeDtypeStruct((ITEMS, ITEMW), jnp.bfloat16),
+        vmem=16,
+        in_specs=[pl.BlockSpec(memory_space=pltpu.VMEM)] * 2 + [HBM],
+        scratch_shapes=[
+            pltpu.VMEM(w_uk.shape, jnp.bfloat16),
+            pltpu.SemaphoreType.DMA((4,)),
+        ],
+    )(*queries, *in_hbm(w_uk))
 
 
 def pack_stats(stats):
@@ -255,6 +261,7 @@
     return call(
         functools.partial(attend_kernel, n, last),
         out_shape,
+        vmem=32,
         grid=(ITEMS // tile,),
         in_specs=in_specs,
         out_specs=out_specs,
@@ -345,16 +352,16 @@
 def local(query_unrotated, q_rope, latent, k_rope, key_pos, offset, w_uk, value_up_weight, w_out):
     y, x, z, c = (lax.axis_index(n) for n in CTX)
 
-    keys = pack_keys(latent[0], k_rope[0], key_pos)
-    keys, query_unrotated = lax.optimization_barrier((keys, query_unrotated))
-    q_own = pack_queries(query_unrotated, q_rope)
+    keys, q_own = pack(latent[0], k_rope[0], key_pos, query_unrotated, q_rope)
     z_keys = lax.ppermute(keys, "z", SWAP)
-    near = [keys] + [lax.ppermute(keys, "y", shift(d)) for d in RING[1:]]
-    z_keys, near = lax.optimization_barrier((z_keys, near))
-    far = [z_keys] + [lax.ppermute(z_keys, "y", shift(d)) for d in RING[1:]]
-
-    q_chip = join([q_own] + [lax.ppermute(q_own, "x", shift(d)) for d in RING[1:]])
-    q_chip, w_own = lax.optimization_barrier((q_chip, jnp.transpose(w_out)))
+    up, down, across = (lax.ppermute(keys, "y", shift(d)) for d in (1, 3, 2))
+    q_ring = [lax.ppermute(q_own, "x", shift(1)), lax.ppermute(q_own, "x", shift(3))]
+    q_ring, q_own, w_own = lax.optimization_barrier((q_ring, q_own, jnp.transpose(w_out)))
+    q_ring.append(lax.ppermute(q_own, "x", shift(2)))
+    z_keys, up, down, across, q_ring[0] = lax.optimization_barrier((z_keys, up, down, across, q_ring[0]))
+    near = [keys, z_keys, up, down, across]
+    far = [lax.ppermute(z_keys, "y", shift(d)) for d in RING[1:]]
+    q_chip = join([q_own, *q_ring])
     q_core = lax.ppermute(q_chip, "c", SWAP)
     z_w = lax.ppermute(w_own, "z", SWAP)
 
@@ -379,7 +386,7 @@
     ]
     c_w = lax.ppermute(w_own, "c", SWAP)
     zc_w = lax.ppermute(z_w, "c", SWAP)
-    parts, c_w, zc_w = lax.optimization_barrier((parts, c_w, zc_w))
+    parts, c_w = lax.optimization_barrier((parts, c_w))
     heads = call(merge_ring_kernel, jax.ShapeDtypeStruct((16, R, HG * VDIM), jnp.bfloat16))(
         *parts
     )
@@ -387,9 +394,9 @@
     rows = lax.all_to_all(heads, ("y", "x"), 0, 0, tiled=True).reshape(16 * R, HG * VDIM)
     ncol = w_out.shape[1]
     columns = columns_of(jnp.stack([z, c]), (w_own, z_w, c_w, zc_w))
-    sums = call(project_kernel, jax.ShapeDtypeStruct((4, 16 * R, ncol), jnp.bfloat16))(
-        rows, columns
-    )
+    sums = call(
+        project_kernel, jax.ShapeDtypeStruct((4, 16 * R, ncol), jnp.bfloat16), vmem=16
+    )(rows, columns)
     sums = lax.all_to_all(
         sums.reshape(16, 4 * R, ncol), ("z", "c", "head"), 0, 0, tiled=True
     )

time: 114 us -> 115 us (level)
  waiting for transfers between devices: 18.5 us -> 25.6 us
  starting transfers between devices: 38.3 us -> 33.5 us
  local copies, waits for them, and re-layouts: 6.23 us -> 2.85 us
  Pallas kernels: 27.4 us -> 30.7 us
  blocking collectives: 22.2 us -> 21 us
    ppermute x9, waiting for transfers between devices: 5.3 us -> 9.99 us  [the longest x1 3.76 us: local(): lax.ppermute(q_own, 'x', shift(1))]
    ppermute x9, starting transfers between devices: 16.7 us -> 12.3 us  [the longest x3 4.38 us: local(): up, down, across = (lax.ppermute(keys, 'y', shift(d)) for d in (1, 3, 2))]
    unnamed x16 -> x10, local copies, waits for them, and re-layouts: 6.23 us -> 2.85 us
    pallas_call x6 -> x5, Pallas kernels: 22.3 us -> 25.6 us  [the longest x2 20.9 us: attend(): call(functools.partial(attend_kernel, n, last), out_shape, vmem=32, grid=...]
    ppermute x3, waiting for transfers between devices: 2 us -> 3.77 us  [local(): lax.ppermute(part, 'x', shift(-d % 4))]
    all_to_all x1, starting transfers between devices: 5.3 us -> 3.65 us  [local(): lax.all_to_all(heads, ('y', 'x'), 0, 0, tiled=True)]
    ppermute x1, waiting for transfers between devices: 0.01 us -> 1.37 us  [local(): zc_w = lax.ppermute(z_w, 'c', SWAP)]
    all_to_all x1, blocking collectives: 22.2 us -> 21 us  [local(): lax.all_to_all(sums.reshape(16, 4 * R, ncol), ('z', 'c', 'head'), 0, 0, t...]
  transfers between devices with their start and end apart: 19 -> 19, of which waited for: 6 -> 8; matrix products, arithmetic and copies ran while one was open for 0% -> 0% of each run, Pallas kernels for 19% -> 23%
where the time goes in v8:
time: 115 us
  starting transfers between devices  33.5 us (29%)
  Pallas kernels  30.7 us (27%)
  waiting for transfers between devices  25.6 us (22%)
  blocking collectives  21 us (18%)
  local copies, waits for them, and re-layouts  2.85 us (2%)
    all_to_all x1, blocking collectives, local(): lax.all_to_all(sums.reshape(16, 4 * R, ncol), ('z', 'c', 'head'), 0, 0, t...  21 us
    pallas_call x2, Pallas kernels, attend(): call(functools.partial(attend_kernel, n, last), out_shape, vmem=32, grid=...  20.9 us
    all_to_all x1, waiting for transfers between devices, local(): lax.all_to_all(heads, ('y', 'x'), 0, 0, tiled=True)  8.96 us
    ppermute x1, starting transfers between devices, local(): z_keys = lax.ppermute(keys, 'z', SWAP)  6.1 us
    ppermute x1, starting transfers between devices, local(): q_core = lax.ppermute(q_chip, 'c', SWAP)  4.45 us
    ppermute x3, starting transfers between devices, local(): up, down, across = (lax.ppermute(keys, 'y', shift(d)) for d in (1, 3, 2))  4.38 us
    ppermute x3, starting transfers between devices, local(): lax.ppermute(part, 'x', shift(-d % 4))  4.29 us
    ppermute x3, starting transfers between devices, local(): far = [lax.ppermute(z_keys, 'y', shift(d)) for d in RING[1:]]  3.95 us
  transfers between devices with their start and end apart: 19, of which 8 were waited for; matrix products, arithmetic and copies ran while one was open for 0% of the time, Pallas kernels for 23%

profile of v8, /device:TPU:33, one launch (start us, length us, event | category | flops | bytes accessed | tf_op | source)
XLA Modules:
  0.0 114.6 jit_solution(10568273794540315612)
XLA Ops:
  0.0 1.0 shard_map.100
  1.0 6.1 %collective-permute-start.2 = (bf16[256,640]{1,0:T(8,128)(2,1)S(1)}, bf16[256,640]{1,0:T(8,128)(2,1)S(1)}, u32[]{:S(2)}, u32[]{:S(2)}) collective-permute-start(bf16[256,640]{1,0:T(8,128)(2,1)S(1)} %get-tuple-element.38.refs_3_), channel_id=1, source_target_pairs={{0,8},{8,0},{1,9},{9,1},{2,10},{10,2},{3,11},{11,3},{4,12},{12,4},... | collective-permute-start | bytes 983048 | tf_op jit(solution)/shard_map/ppermute | solution.py:356
  7.1 1.3 %collective-permute-start.3 = (bf16[256,640]{1,0:T(8,128)(2,1)S(1)}, bf16[256,640]{1,0:T(8,128)(2,1)S(1)}, u32[]{:S(2)}, u32[]{:S(2)}) collective-permute-start(bf16[256,640]{1,0:T(8,128)(2,1)S(1)} %get-tuple-element.38.refs_3_), channel_id=1, source_target_pairs={{0,64},{64,128},{128,192},{192,0},{1,65},{65,129},{129,193},{193,1... | collective-permute-start | bytes 983048 | tf_op jit(solution)/shard_map/ppermute | solution.py:357
  8.4 1.4 %collective-permute-start.4 = (bf16[256,640]{1,0:T(8,128)(2,1)S(1)}, bf16[256,640]{1,0:T(8,128)(2,1)S(1)}, u32[]{:S(2)}, u32[]{:S(2)}) collective-permute-start(bf16[256,640]{1,0:T(8,128)(2,1)S(1)} %get-tuple-element.38.refs_3_), channel_id=1, source_target_pairs={{0,192},{64,0},{128,64},{192,128},{1,193},{65,1},{129,65},{193,129... | collective-permute-start | bytes 983048 | tf_op jit(solution)/shard_map/ppermute | solution.py:357
  9.9 1.6 %collective-permute-start.5 = (bf16[256,640]{1,0:T(8,128)(2,1)S(1)}, bf16[256,640]{1,0:T(8,128)(2,1)S(1)}, u32[]{:S(2)}, u32[]{:S(2)}) collective-permute-start(bf16[256,640]{1,0:T(8,128)(2,1)S(1)} %get-tuple-element.38.refs_3_), channel_id=1, source_target_pairs={{0,128},{64,192},{128,0},{192,64},{1,129},{65,193},{129,1},{193,65... | collective-permute-start | bytes 983048 | tf_op jit(solution)/shard_map/ppermute | solution.py:357
  11.5 1.2 %collective-permute-start = (bf16[16,3072]{1,0:T(8,128)(2,1)S(1)}, bf16[16,3072]{1,0:T(8,128)(2,1)S(1)}, u32[]{:S(2)}, u32[]{:S(2)}) collective-permute-start(bf16[16,3072]{1,0:T(8,128)(2,1)S(1)} %get-tuple-element.37.refs_0_), channel_id=1, source_target_pairs={{0,16},{16,32},{32,48},{48,0},{1,17},{17,33},{33,49},{49,1},{2,18}... | collective-permute-start | bytes 294920 | tf_op jit(solution)/shard_map/ppermute | solution.py:358
  12.7 3.8 %collective-permute-done.refs_1_ = bf16[16,3072]{1,0:T(8,128)(2,1)S(1)} collective-permute-done((bf16[16,3072]{1,0:T(8,128)(2,1)S(1)}, bf16[16,3072]{1,0:T(8,128)(2,1)S(1)}, u32[]{:S(2)}, u32[]{:S(2)}) %collective-permute-start) | collective-permute-done | bytes 98336 | tf_op jit(solution)/shard_map/ppermute | solution.py:358
  16.5 1.3 %collective-permute-start.1 = (bf16[16,3072]{1,0:T(8,128)(2,1)S(1)}, bf16[16,3072]{1,0:T(8,128)(2,1)S(1)}, u32[]{:S(2)}, u32[]{:S(2)}) collective-permute-start(bf16[16,3072]{1,0:T(8,128)(2,1)S(1)} %get-tuple-element.37.refs_0_), channel_id=1, source_target_pairs={{0,48},{16,0},{32,16},{48,32},{1,49},{17,1},{33,17},{49,33},{2,50}... | collective-permute-start | bytes 294920 | tf_op jit(solution)/shard_map/ppermute | solution.py:358
  17.8 2.5 %collective-permute-done.1.refs_2_ = bf16[16,3072]{1,0:T(8,128)(2,1)S(1)} collective-permute-done((bf16[16,3072]{1,0:T(8,128)(2,1)S(1)}, bf16[16,3072]{1,0:T(8,128)(2,1)S(1)}, u32[]{:S(2)}, u32[]{:S(2)}) %collective-permute-start.1) | collective-permute-done | bytes 98336 | tf_op jit(solution)/shard_map/ppermute | solution.py:358
  20.3 1.5 %collective-permute-start.6 = (bf16[16,3072]{1,0:T(8,128)(2,1)S(1)}, bf16[16,3072]{1,0:T(8,128)(2,1)S(1)}, u32[]{:S(2)}, u32[]{:S(2)}) collective-permute-start(bf16[16,3072]{1,0:T(8,128)(2,1)S(1)} %get-tuple-element.37.refs_0_), channel_id=1, source_target_pairs={{0,32},{16,48},{32,0},{48,16},{1,33},{17,49},{33,1},{49,17},{2,34}... | collective-permute-start | bytes 294920 | tf_op jit(solution)/shard_map/ppermute | solution.py:360
  21.8 0.0 collective-permute-done.2.refs_4_
  21.8 0.0 collective-permute-done.3.refs_5_
  21.8 0.0 collective-permute-done.4.refs_6_
  21.8 3.1 %collective-permute-done.5.refs_7_ = bf16[256,640]{1,0:T(8,128)(2,1)S(1)} collective-permute-done((bf16[256,640]{1,0:T(8,128)(2,1)S(1)}, bf16[256,640]{1,0:T(8,128)(2,1)S(1)}, u32[]{:S(2)}, u32[]{:S(2)}) %collective-permute-start.5) | collective-permute-done | bytes 327712 | tf_op jit(solution)/shard_map/ppermute | solution.py:357
  24.9 0.6 collective-permute-done.6.refs_3_
  25.6 4.4 %collective-permute-start.7 = (bf16[64,3072]{1,0:T(8,128)(2,1)S(1)}, bf16[64,3072]{1,0:T(8,128)(2,1)S(1)}, u32[]{:S(2)}, u32[]{:S(2)}) collective-permute-start(bf16[64,3072]{1,0:T(8,128)(2,1)S(1)} %shard_map.101.refs_0_), channel_id=1, source_target_pairs={{0,4},{4,0},{1,5},{5,1},{2,6},{6,2},{3,7},{7,3},{8,12},{12,8},{9,1... | collective-permute-start | bytes 1179656 | tf_op jit(solution)/shard_map/ppermute | solution.py:365
  30.0 1.3 %collective-permute-start.10 = (bf16[256,640]{1,0:T(8,128)(2,1)S(1)}, bf16[256,640]{1,0:T(8,128)(2,1)S(1)}, u32[]{:S(2)}, u32[]{:S(2)}) collective-permute-start(bf16[256,640]{1,0:T(8,128)(2,1)S(1)} %collective-permute-done.2.refs_4_), channel_id=1, source_target_pairs={{0,128},{64,192},{128,0},{192,64},{1,129},{65,193},{129,1},{193,65... | collective-permute-start | bytes 983048 | tf_op jit(solution)/shard_map/ppermute | solution.py:363
  31.3 0.4 collective-permute-start.8
  31.7 2.3 %collective-permute-start.9 = (bf16[256,640]{1,0:T(8,128)(2,1)S(1)}, bf16[256,640]{1,0:T(8,128)(2,1)}, u32[]{:S(2)}, u32[]{:S(2)}) collective-permute-start(bf16[256,640]{1,0:T(8,128)(2,1)S(1)} %collective-permute-done.2.refs_4_), channel_id=1, source_target_pairs={{0,192},{64,0},{128,64},{192,128},{1,193},{65,1},{129,65},{193,129... | collective-permute-start | bytes 983048 | tf_op jit(solution)/shard_map/ppermute | solution.py:363
  34.6 0.0 collective-permute-done.7.refs_1_
  34.6 1.5 %collective-permute-start.16 = (bf16[112,2048]{1,0:T(8,128)(2,1)}, bf16[112,2048]{1,0:T(8,128)(2,1)S(1)}, u32[]{:S(2)}, u32[]{:S(2)}) collective-permute-start(bf16[112,2048]{1,0:T(8,128)(2,1)} %bitcast.21), channel_id=1, source_target_pairs={{0,4},{4,0},{1,5},{5,1},{2,6},{6,2},{3,7},{7,3},{8,12},{12,8},{9,1... | collective-permute-start | bytes 1376264 | tf_op jit(solution)/shard_map/ppermute | solution.py:387
  36.1 2.5 %shard_map.102.refs_0_ = bf16[2048,768]{1,0:T(8,128)(2,1)S(1)} custom-call(bf16[64,3072]{1,0:T(8,128)(2,1)S(1)} %shard_map.101.refs_0_, bf16[64,3072]{1,0:T(8,128)(2,1)S(1)} %collective-permute-done.7.refs_1_, bf16[16,128,512]{2,1,0:T(8,128)(2,1)} %refs_2_.3), custom_call_target="tpu_custom_call" | custom-call | flops 1 | bytes 1 | tf_op jit(solution)/shard_map/pallas_call | solution.py:142
  38.6 11.7 %shard_map.103 = (f32[128,2048]{1,0:T(8,128)S(1)}, f32[2048,128]{1,0:T(8,128)S(1)}) custom-call(bf16[2048,768]{1,0:T(8,128)(2,1)S(1)} %shard_map.102.refs_0_, f32[8,128]{1,0:T(8,128)S(1)} %broadcast_in_dim.17.refs_1_, bf16[16,512,128]{2,1,0:T(8,128)(2,1)S(1)} %copy-done, bf16[256,640]{1,0:T(8,128)(2,1)S(1)} %get-tuple-element.38.refs_3_, ...), custom_call_target="tpu_custom_call" | custom-call | flops 1 | bytes 1 | tf_op jit(solution)/shard_map/pallas_call | solution.py:261
  50.3 0.0 collective-permute-done.8.refs_3_
  50.3 0.0 collective-permute-done.9.refs_4_
  50.4 9.2 %shard_map.104 = (bf16[64,2176]{1,0:T(8,128)(2,1)S(1)}, bf16[64,2176]{1,0:T(8,128)(2,1)S(1)}) custom-call(bf16[2048,768]{1,0:T(8,128)(2,1)S(1)} %shard_map.102.refs_0_, f32[8,128]{1,0:T(8,128)S(1)} %broadcast_in_dim.17.refs_1_, bf16[16,512,128]{2,1,0:T(8,128)(2,1)S(1)} %copy-done, bf16[256,640]{1,0:T(8,128)(2,1)S(1)} %collective-permute-done.8.refs_3_, ...), custom_call_target="tpu_custom_call" | custom-call | flops 1 | bytes 1 | tf_op jit(solution)/shard_map/pallas_call | solution.py:261
  59.5 0.0 collective-permute-done.11.refs_1_
  59.5 0.1 collective-permute-start.12
  59.7 1.5 %collective-permute-done.12.b_ref = bf16[64,2176]{1,0:T(8,128)(2,1)S(1)} collective-permute-done((bf16[64,2176]{1,0:T(8,128)(2,1)S(1)}, bf16[64,2176]{1,0:T(8,128)(2,1)S(1)}, u32[]{:S(2)}, u32[]{:S(2)}) %collective-permute-start.12) | collective-permute-done | bytes 278560 | tf_op jit(solution)/shard_map/ppermute | solution.py:383
  61.2 0.5 shard_map.105
  61.7 2.5 %collective-permute-start.13 = (bf16[16,2176]{1,0:T(8,128)(2,1)S(1)}, bf16[16,2176]{1,0:T(8,128)(2,1)S(1)}, u32[]{:S(2)}, u32[]{:S(2)}) collective-permute-start(bf16[16,2176]{1,0:T(8,128)(2,1)S(1)} %get-tuple-element.58), channel_id=1, source_target_pairs={{0,48},{16,0},{32,16},{48,32},{1,49},{17,1},{33,17},{49,33},{2,50}... | collective-permute-start | bytes 208904 | tf_op jit(solution)/shard_map/ppermute | solution.py:385
  64.2 0.0 collective-permute-start.14
  64.2 1.7 %collective-permute-start.15 = (bf16[16,2176]{1,0:T(8,128)(2,1)S(1)}, bf16[16,2176]{1,0:T(8,128)(2,1)S(1)}, u32[]{:S(2)}, u32[]{:S(2)}) collective-permute-start(bf16[16,2176]{1,0:T(8,128)(2,1)S(1)} %get-tuple-element.60), channel_id=1, source_target_pairs={{0,32},{16,48},{32,0},{48,16},{1,33},{17,49},{33,1},{49,17},{2,34}... | collective-permute-start | bytes 208904 | tf_op jit(solution)/shard_map/ppermute | solution.py:385
  66.0 0.8 copy-done.3
  66.8 3.8 %collective-permute-done.14.refs_2_ = bf16[16,2176]{1,0:T(8,128)(2,1)S(1)} collective-permute-done((bf16[16,2176]{1,0:T(8,128)(2,1)S(1)}, bf16[16,2176]{1,0:T(8,128)(2,1)S(1)}, u32[]{:S(2)}, u32[]{:S(2)}) %collective-permute-start.14) | collective-permute-done | bytes 69664 | tf_op jit(solution)/shard_map/ppermute | solution.py:385
  70.5 0.0 collective-permute-done.15.refs_3_
  70.5 1.4 %shard_map.106 = bf16[16,16,2048]{2,1,0:T(8,128)(2,1)} custom-call(bf16[16,2176]{1,0:T(8,128)(2,1)S(1)} %get-tuple-element.61.refs_0_, bf16[16,2176]{1,0:T(8,128)(2,1)S(1)} %collective-permute-done.13.refs_1_, bf16[16,2176]{1,0:T(8,128)(2,1)S(1)} %collective-permute-done.14.refs_2_, bf16[16,2176]{1,0:T(8,128)(2,1)S(1)} %collective-permute-done.15.refs_3_), custom_call_target="tpu_custom_call" | custom-call | flops 1 | bytes 1 | tf_op jit(solution)/shard_map/pallas_call | solution.py:390
  72.0 3.7 %all-to-all-start = ((bf16[16,16,2048]{2,1,0:T(8,128)(2,1)}), bf16[16,16,2048]{2,1,0:T(8,128)(2,1)S(1)}, u32[]{:S(2)}, u32[]{:S(2)}) async-start(bf16[16,16,2048]{2,1,0:T(8,128)(2,1)} %shard_map.106), calls=%async_computation | async-start | bytes 2097152 | tf_op jit(solution)/shard_map/all_to_all | solution.py:394
  75.7 1.1 collective-permute-start.17
  76.7 0.1 pad_add_fusion.zc_ref
  76.8 1.4 %collective-permute-done.17.refs_3_ = bf16[112,2048]{1,0:T(8,128)(2,1)S(1)} collective-permute-done((bf16[112,2048]{1,0:T(8,128)(2,1)S(1)}, bf16[112,2048]{1,0:T(8,128)(2,1)S(1)}, u32[]{:S(2)}, u32[]{:S(2)}) %collective-permute-start.17) | collective-permute-done | bytes 458784 | tf_op jit(solution)/shard_map/ppermute | solution.py:388
  78.2 1.0 copy-done.2
  79.2 1.0 copy-done.4
  80.2 2.4 %shard_map.107.w_ref = bf16[4,2048,128]{2,1,0:T(8,128)(2,1)S(1)} custom-call(s32[2]{0:T(128)S(1)} %pad_add_fusion.zc_ref, bf16[112,2048]{1,0:T(8,128)(2,1)} %bitcast.22, bf16[112,2048]{1,0:T(8,128)(2,1)S(1)} %copy-done.2, bf16[112,2048]{1,0:T(8,128)(2,1)S(1)} %copy-done.4, bf16[112,2048]{1,0:T(8,128)(2,1)S(1)} %collective-permute-done.17.refs_3_), custom_call_target="tpu_custom_call" | custom-call | flops 1 | bytes 1 | tf_op jit(solution)/shard_map/pallas_call | solution.py:323
  82.6 9.0 %all-to-all-done = bf16[16,16,2048]{2,1,0:T(8,128)(2,1)S(1)} async-done(((bf16[16,16,2048]{2,1,0:T(8,128)(2,1)}), bf16[16,16,2048]{2,1,0:T(8,128)(2,1)S(1)}, u32[]{:S(2)}, u32[]{:S(2)}) %all-to-all-start) | async-done | bytes 1048608 | tf_op jit(solution)/shard_map/all_to_all | solution.py:394
  91.6 1.2 %shard_map.108 = bf16[4,256,112]{2,1,0:T(8,128)(2,1)S(1)} custom-call(bf16[256,2048]{1,0:T(8,128)(2,1)S(1)} %bitcast.18, bf16[4,2048,128]{2,1,0:T(8,128)(2,1)S(1)} %shard_map.107.w_ref), custom_call_target="tpu_custom_call" | custom-call | flops 1 | bytes 1 | tf_op jit(solution)/shard_map/pallas_call | solution.py:397
  92.8 21.0 %all_to_all.10.sums_ref = bf16[16,64,112]{2,1,0:T(8,128)(2,1)S(1)} all-to-all(bf16[16,64,112]{2,1,0:T(8,128)(2,1)S(1)} %bitcast.19), channel_id=1, replica_groups=mesh['y'=4,'x'=4,'z'=2,'c'=2,'head'=4] {'z','c','head'}, dimensions={0} | all-to-all | bytes 458752 | tf_op jit(solution)/shard_map/all_to_all | solution.py:400
  113.8 0.7 shard_map.109
  (14 shorter events, 0.1 us)
Async XLA Ops:
  1.0 20.8 %collective-permute-start.2 = (bf16[256,640]{1,0:T(8,128)(2,1)S(1)}, bf16[256,640]{1,0:T(8,128)(2,1)S(1)}, u32[]{:S(2)}, u32[]{:S(2)}) collective-permute-start(bf16[256,640]{1,0:T(8,128)(2,1)S(1)} %get-tuple-element.38.refs_3_), channel_id=1, source_target_pairs={{0,8},{8,0},{1,9},{9,1},{2,10},{10,2},{3,11},{11,3},{4,12},{12,4},... | collective-permute-start | bytes 983048 | tf_op jit(solution)/shard_map/ppermute | solution.py:356
  7.1 14.7 %collective-permute-start.3 = (bf16[256,640]{1,0:T(8,128)(2,1)S(1)}, bf16[256,640]{1,0:T(8,128)(2,1)S(1)}, u32[]{:S(2)}, u32[]{:S(2)}) collective-permute-start(bf16[256,640]{1,0:T(8,128)(2,1)S(1)} %get-tuple-element.38.refs_3_), channel_id=1, source_target_pairs={{0,64},{64,128},{128,192},{192,0},{1,65},{65,129},{129,193},{193,1... | collective-permute-start | bytes 983048 | tf_op jit(solution)/shard_map/ppermute | solution.py:357
  8.4 13.4 %collective-permute-start.4 = (bf16[256,640]{1,0:T(8,128)(2,1)S(1)}, bf16[256,640]{1,0:T(8,128)(2,1)S(1)}, u32[]{:S(2)}, u32[]{:S(2)}) collective-permute-start(bf16[256,640]{1,0:T(8,128)(2,1)S(1)} %get-tuple-element.38.refs_3_), channel_id=1, source_target_pairs={{0,192},{64,0},{128,64},{192,128},{1,193},{65,1},{129,65},{193,129... | collective-permute-start | bytes 983048 | tf_op jit(solution)/shard_map/ppermute | solution.py:357
  9.9 15.0 %collective-permute-start.5 = (bf16[256,640]{1,0:T(8,128)(2,1)S(1)}, bf16[256,640]{1,0:T(8,128)(2,1)S(1)}, u32[]{:S(2)}, u32[]{:S(2)}) collective-permute-start(bf16[256,640]{1,0:T(8,128)(2,1)S(1)} %get-tuple-element.38.refs_3_), channel_id=1, source_target_pairs={{0,128},{64,192},{128,0},{192,64},{1,129},{65,193},{129,1},{193,65... | collective-permute-start | bytes 983048 | tf_op jit(solution)/shard_map/ppermute | solution.py:357
  11.5 5.0 %collective-permute-start = (bf16[16,3072]{1,0:T(8,128)(2,1)S(1)}, bf16[16,3072]{1,0:T(8,128)(2,1)S(1)}, u32[]{:S(2)}, u32[]{:S(2)}) collective-permute-start(bf16[16,3072]{1,0:T(8,128)(2,1)S(1)} %get-tuple-element.37.refs_0_), channel_id=1, source_target_pairs={{0,16},{16,32},{32,48},{48,0},{1,17},{17,33},{33,49},{49,1},{2,18}... | collective-permute-start | bytes 294920 | tf_op jit(solution)/shard_map/ppermute | solution.py:358
  16.5 3.8 %collective-permute-start.1 = (bf16[16,3072]{1,0:T(8,128)(2,1)S(1)}, bf16[16,3072]{1,0:T(8,128)(2,1)S(1)}, u32[]{:S(2)}, u32[]{:S(2)}) collective-permute-start(bf16[16,3072]{1,0:T(8,128)(2,1)S(1)} %get-tuple-element.37.refs_0_), channel_id=1, source_target_pairs={{0,48},{16,0},{32,16},{48,32},{1,49},{17,1},{33,17},{49,33},{2,50}... | collective-permute-start | bytes 294920 | tf_op jit(solution)/shard_map/ppermute | solution.py:358
  20.3 5.3 %collective-permute-start.6 = (bf16[16,3072]{1,0:T(8,128)(2,1)S(1)}, bf16[16,3072]{1,0:T(8,128)(2,1)S(1)}, u32[]{:S(2)}, u32[]{:S(2)}) collective-permute-start(bf16[16,3072]{1,0:T(8,128)(2,1)S(1)} %get-tuple-element.37.refs_0_), channel_id=1, source_target_pairs={{0,32},{16,48},{32,0},{48,16},{1,33},{17,49},{33,1},{49,17},{2,34}... | collective-permute-start | bytes 294920 | tf_op jit(solution)/shard_map/ppermute | solution.py:360
  25.6 9.1 %collective-permute-start.7 = (bf16[64,3072]{1,0:T(8,128)(2,1)S(1)}, bf16[64,3072]{1,0:T(8,128)(2,1)S(1)}, u32[]{:S(2)}, u32[]{:S(2)}) collective-permute-start(bf16[64,3072]{1,0:T(8,128)(2,1)S(1)} %shard_map.101.refs_0_), channel_id=1, source_target_pairs={{0,4},{4,0},{1,5},{5,1},{2,6},{6,2},{3,7},{7,3},{8,12},{12,8},{9,1... | collective-permute-start | bytes 1179656 | tf_op jit(solution)/shard_map/ppermute | solution.py:365
  30.0 29.5 %collective-permute-start.11 = (bf16[112,2048]{1,0:T(8,128)(2,1)}, bf16[112,2048]{1,0:T(8,128)(2,1)S(1)}, u32[]{:S(2)}, u32[]{:S(2)}) collective-permute-start(bf16[112,2048]{1,0:T(8,128)(2,1)} %bitcast.20), channel_id=1, source_target_pairs={{0,8},{8,0},{1,9},{9,1},{2,10},{10,2},{3,11},{11,3},{4,12},{12,4},... | collective-permute-start | bytes 1376264 | tf_op jit(solution)/shard_map/ppermute | solution.py:366
  30.0 20.3 %collective-permute-start.10 = (bf16[256,640]{1,0:T(8,128)(2,1)S(1)}, bf16[256,640]{1,0:T(8,128)(2,1)S(1)}, u32[]{:S(2)}, u32[]{:S(2)}) collective-permute-start(bf16[256,640]{1,0:T(8,128)(2,1)S(1)} %collective-permute-done.2.refs_4_), channel_id=1, source_target_pairs={{0,128},{64,192},{128,0},{192,64},{1,129},{65,193},{129,1},{193,65... | collective-permute-start | bytes 983048 | tf_op jit(solution)/shard_map/ppermute | solution.py:363
  31.3 19.1 %collective-permute-start.8 = (bf16[256,640]{1,0:T(8,128)(2,1)S(1)}, bf16[256,640]{1,0:T(8,128)(2,1)S(1)}, u32[]{:S(2)}, u32[]{:S(2)}) collective-permute-start(bf16[256,640]{1,0:T(8,128)(2,1)S(1)} %collective-permute-done.2.refs_4_), channel_id=1, source_target_pairs={{0,64},{64,128},{128,192},{192,0},{1,65},{65,129},{129,193},{193,1... | collective-permute-start | bytes 983048 | tf_op jit(solution)/shard_map/ppermute | solution.py:363
  31.7 18.7 %collective-permute-start.9 = (bf16[256,640]{1,0:T(8,128)(2,1)S(1)}, bf16[256,640]{1,0:T(8,128)(2,1)}, u32[]{:S(2)}, u32[]{:S(2)}) collective-permute-start(bf16[256,640]{1,0:T(8,128)(2,1)S(1)} %collective-permute-done.2.refs_4_), channel_id=1, source_target_pairs={{0,192},{64,0},{128,64},{192,128},{1,193},{65,1},{129,65},{193,129... | collective-permute-start | bytes 983048 | tf_op jit(solution)/shard_map/ppermute | solution.py:363
  34.6 31.3 %collective-permute-start.16 = (bf16[112,2048]{1,0:T(8,128)(2,1)}, bf16[112,2048]{1,0:T(8,128)(2,1)S(1)}, u32[]{:S(2)}, u32[]{:S(2)}) collective-permute-start(bf16[112,2048]{1,0:T(8,128)(2,1)} %bitcast.21), channel_id=1, source_target_pairs={{0,4},{4,0},{1,5},{5,1},{2,6},{6,2},{3,7},{7,3},{8,12},{12,8},{9,1... | collective-permute-start | bytes 1376264 | tf_op jit(solution)/shard_map/ppermute | solution.py:387
  36.1 2.5 %copy-start = (bf16[16,512,128]{2,1,0:T(8,128)(2,1)S(1)}, bf16[16,512,128]{2,1,0:T(8,128)(2,1)}, u32[]{:S(2)}) copy-start(bf16[16,512,128]{2,1,0:T(8,128)(2,1)} %refs_2_.5) | copy-start | bytes 6291460
  59.5 17.3 %copy-start.1 = (bf16[112,2048]{1,0:T(8,128)(2,1)}, bf16[112,2048]{1,0:T(8,128)(2,1)S(1)}, u32[]{:S(2)}) copy-start(bf16[112,2048]{1,0:T(8,128)(2,1)S(1)} %collective-permute-done.11.refs_1_) | copy-start | bytes 1376260
  59.5 1.6 %collective-permute-start.12 = (bf16[64,2176]{1,0:T(8,128)(2,1)S(1)}, bf16[64,2176]{1,0:T(8,128)(2,1)S(1)}, u32[]{:S(2)}, u32[]{:S(2)}) collective-permute-start(bf16[64,2176]{1,0:T(8,128)(2,1)S(1)} %get-tuple-element.56), channel_id=1, source_target_pairs={{0,4},{4,0},{1,5},{5,1},{2,6},{6,2},{3,7},{7,3},{8,12},{12,8},{9,1... | collective-permute-start | bytes 835592 | tf_op jit(solution)/shard_map/ppermute | solution.py:383
  61.7 5.1 %collective-permute-start.13 = (bf16[16,2176]{1,0:T(8,128)(2,1)S(1)}, bf16[16,2176]{1,0:T(8,128)(2,1)S(1)}, u32[]{:S(2)}, u32[]{:S(2)}) collective-permute-start(bf16[16,2176]{1,0:T(8,128)(2,1)S(1)} %get-tuple-element.58), channel_id=1, source_target_pairs={{0,48},{16,0},{32,16},{48,32},{1,49},{17,1},{33,17},{49,33},{2,50}... | collective-permute-start | bytes 208904 | tf_op jit(solution)/shard_map/ppermute | solution.py:385
  64.2 6.3 %collective-permute-start.14 = (bf16[16,2176]{1,0:T(8,128)(2,1)S(1)}, bf16[16,2176]{1,0:T(8,128)(2,1)S(1)}, u32[]{:S(2)}, u32[]{:S(2)}) collective-permute-start(bf16[16,2176]{1,0:T(8,128)(2,1)S(1)} %get-tuple-element.59), channel_id=1, source_target_pairs={{0,16},{16,32},{32,48},{48,0},{1,17},{17,33},{33,49},{49,1},{2,18}... | collective-permute-start | bytes 208904 | tf_op jit(solution)/shard_map/ppermute | solution.py:385
  64.2 6.3 %collective-permute-start.15 = (bf16[16,2176]{1,0:T(8,128)(2,1)S(1)}, bf16[16,2176]{1,0:T(8,128)(2,1)S(1)}, u32[]{:S(2)}, u32[]{:S(2)}) collective-permute-start(bf16[16,2176]{1,0:T(8,128)(2,1)S(1)} %get-tuple-element.60), channel_id=1, source_target_pairs={{0,32},{16,48},{32,0},{48,16},{1,33},{17,49},{33,1},{49,17},{2,34}... | collective-permute-start | bytes 208904 | tf_op jit(solution)/shard_map/ppermute | solution.py:385
  66.0 0.8 copy-start.3
  72.0 19.6 %all-to-all-start = ((bf16[16,16,2048]{2,1,0:T(8,128)(2,1)}), bf16[16,16,2048]{2,1,0:T(8,128)(2,1)S(1)}, u32[]{:S(2)}, u32[]{:S(2)}) async-start(bf16[16,16,2048]{2,1,0:T(8,128)(2,1)} %shard_map.106), calls=%async_computation | async-start | bytes 2097152 | tf_op jit(solution)/shard_map/all_to_all | solution.py:394
  75.7 2.5 %collective-permute-start.17 = (bf16[112,2048]{1,0:T(8,128)(2,1)S(1)}, bf16[112,2048]{1,0:T(8,128)(2,1)S(1)}, u32[]{:S(2)}, u32[]{:S(2)}) collective-permute-start(bf16[112,2048]{1,0:T(8,128)(2,1)S(1)} %collective-permute-done.11.refs_1_), channel_id=1, source_target_pairs={{0,4},{4,0},{1,5},{5,1},{2,6},{6,2},{3,7},{7,3},{8,12},{12,8},{9,1... | collective-permute-start | bytes 1376264 | tf_op jit(solution)/shard_map/ppermute | solution.py:388
  78.2 1.0 copy-start.2
  79.2 1.0 copy-start.4

commit v9 on v8

--- a/solution.py
+++ b/solution.py
@@ -164,109 +164,93 @@
     return packed + pltpu.roll(packed, 128 - HG, 1) + pltpu.roll(packed, 128 - 2 * HG, 1)
 
 
-def attend_kernel(pieces, last, *refs):
+def attend_kernel(pieces, last, tile, unroll, *refs):
     q_ref, qpos_ref, v_ref = refs[:3]
     piece_refs = refs[3 : 3 + pieces]
     rest = refs[3 + pieces :]
     if last:
         part_in, lse_in, keep_ref, send_ref, key_ref, lse_ref = rest
+        lse_ref[...] = jnp.zeros_like(lse_ref)
     else:
         part_out, lse_out, key_ref = rest
-    step = pl.program_id(0)
-
-    @pl.when(step == 0)
-    def _():
-        qpos = qpos_ref[0:1, :]
-        start = 0
-        for ref in piece_refs:
-            rows = slice(start, start + ref.shape[0])
-            start += ref.shape[0]
-            key_ref[rows, :KEYW] = ref[...]
-            ext = ref[:, RANK:].astype(jnp.float32)
-            pos = ext[:, ROPE : ROPE + 1] * 128.0 + ext[:, ROPE + 1 : ROPE + 2]
-            key_ref[rows, KEYW:] = jnp.where(pos <= qpos, 0.0, NEG).astype(jnp.bfloat16)
+
+    qpos = qpos_ref[0:1, :]
+    start = 0
+    for ref in piece_refs:
+        rows = slice(start, start + ref.shape[0])
+        start += ref.shape[0]
+        key_ref[rows, :KEYW] = ref[...]
+        ext = ref[:, RANK:].astype(jnp.float32)
+        pos = ext[:, ROPE : ROPE + 1] * 128.0 + ext[:, ROPE + 1 : ROPE + 2]
+        key_ref[rows, KEYW:] = jnp.where(pos <= qpos, 0.0, NEG).astype(jnp.bfloat16)
+
+    half = ROWS // 2
+    heads = tile // ROWS
+
+    def body(step):
+        items = pl.ds(pl.multiple_of(step * tile, tile), tile)
+        scores = nt_dot(q_ref[items, :], key_ref[...]) * SCALE2
+        top = jnp.max(scores, axis=1, keepdims=True)
+        weights = jnp.exp2(scores - top)
+        total = jnp.sum(weights, axis=1, keepdims=True)
+        acc = jnp.dot(
+            weights.astype(jnp.bfloat16), key_ref[:, :RANK], preferred_element_type=jnp.float32
+        )
+        context = (acc * (1.0 / total)).astype(jnp.bfloat16)
+        lse = top + jnp.log2(total)
         if last:
-            lse_ref[...] = jnp.zeros_like(lse_ref)
-
-    tile = q_ref.shape[0]
-    scores = nt_dot(q_ref[...], key_ref[...]) * SCALE2
-    top = jnp.max(scores, axis=1, keepdims=True)
-    weights = jnp.exp2(scores - top)
-    total = jnp.sum(weights, axis=1, keepdims=True)
-    acc = jnp.dot(
-        weights.astype(jnp.bfloat16), key_ref[:, :RANK], preferred_element_type=jnp.float32
-    )
-    context = (acc * (1.0 / total)).astype(jnp.bfloat16)
-    lse = top + jnp.log2(total)
+            earlier = lse_in[items, 0:1]
+            top = jnp.maximum(lse, earlier)
+            here, there = jnp.exp2(lse - top), jnp.exp2(earlier - top)
+            total = here + there
+            lse = top + jnp.log2(total)
+            inverse = 1.0 / total
+            here, there = here * inverse, there * inverse
+        else:
+            lse_out[items, :] = jnp.broadcast_to(lse, (tile, 128))
+
+        lane = lax.broadcasted_iota(jnp.int32, (ROWS, 128), 1)
+        for i in range(heads):
+            rows = slice(i * ROWS, (i + 1) * ROWS)
+            head = step * heads + i
+            cols = pl.ds(pl.multiple_of(head * VDIM, VDIM), VDIM)
+            out = jnp.dot(context[rows], v_ref[head], preferred_element_type=jnp.float32)
+            if last:
+                out = out * here[rows] + part_in[:, cols] * there[rows]
+                out = out.astype(jnp.bfloat16)
+                keep_ref[:, cols] = out[:half]
+                send_ref[:, cols] = out[half:]
+                lse_ref[...] = jnp.where(lane == head, lse[rows], lse_ref[...])
+            else:
+                part_out[:, cols] = out
+
+    pl.loop(0, ITEMS // tile, unroll=unroll)(body)
+
     if last:
-        earlier = lse_in[:, 0:1]
-        top = jnp.maximum(lse, earlier)
-        here, there = jnp.exp2(lse - top), jnp.exp2(earlier - top)
-        total = here + there
-        lse = top + jnp.log2(total)
-        inverse = 1.0 / total
-        here, there = here * inverse, there * inverse
-    else:
-        lse_out[...] = jnp.broadcast_to(lse, lse_out.shape)
-
-    half = ROWS // 2
-    lane = lax.broadcasted_iota(jnp.int32, (ROWS, 128), 1)
-    for i in range(tile // ROWS):
-        rows = slice(i * ROWS, (i + 1) * ROWS)
-        head = step * (tile // ROWS) + i
-        cols = pl.ds(pl.multiple_of(head * VDIM, VDIM), VDIM)
-        out = jnp.dot(context[rows], v_ref[i], preferred_element_type=jnp.float32)
-        if last:
-            out = out * here[rows] + part_in[:, i * VDIM : (i + 1) * VDIM] * there[rows]
-            out = out.astype(jnp.bfloat16)
-            keep_ref[:, cols] = out[:half]
-            send_ref[:, cols] = out[half:]
-            lse_ref[...] = jnp.where(lane == head, lse[rows], lse_ref[...])
-        else:
-            part_out[:, i * VDIM : (i + 1) * VDIM] = out
-
-    if last:
-
-        @pl.when(step == pl.num_programs(0) - 1)
-        def _():
-            packed = pack_stats(lse_ref[...])
-            keep_ref[:, HG * VDIM :] = packed[:half]
-            send_ref[:, HG * VDIM :] = packed[half:]
-
-
-def attend(q, qpos, value_weight, pieces, earlier=None, tile=512):
+        packed = pack_stats(lse_ref[...])
+        keep_ref[:, HG * VDIM :] = packed[:half]
+        send_ref[:, HG * VDIM :] = packed[half:]
+
+
+def attend(q, qpos, value_weight, pieces, earlier=None, tile=512, unroll=4):
     n, keys = len(pieces), sum(piece.shape[0] for piece in pieces)
     last = earlier is not None
-    heads = tile // ROWS
-    whole = lambda shape: pl.BlockSpec(shape, lambda i: (0, 0))
-    part = lambda width: pl.BlockSpec((tile, width), lambda i: (i, 0))
-    carried = [pl.BlockSpec((ROWS, heads * VDIM), lambda i: (0, i)), part(128)]
-    in_specs = [part(ITEMW), whole((8, 128))]
-    in_specs += [pl.BlockSpec((heads, RANK, VDIM), lambda i: (i, 0, 0))]
-    in_specs += [whole(piece.shape) for piece in pieces]
     scratch = [pltpu.VMEM((keys, ITEMW), jnp.bfloat16)]
-    args = [q, qpos, value_weight, *pieces]
     if last:
-        in_specs += carried
-        args += earlier
         half = jax.ShapeDtypeStruct((ROWS // 2, SENDW), jnp.bfloat16)
-        out_shape, out_specs = (half, half), [whole((ROWS // 2, SENDW))] * 2
+        out_shape = (half, half)
         scratch.append(pltpu.VMEM((ROWS, 128), jnp.float32))
     else:
         out_shape = (
             jax.ShapeDtypeStruct((ROWS, HG * VDIM), jnp.float32),
             jax.ShapeDtypeStruct((ITEMS, 128), jnp.float32),
         )
-        out_specs = carried
     return call(
-        functools.partial(attend_kernel, n, last),
+        functools.partial(attend_kernel, n, last, tile, unroll),
         out_shape,
-        vmem=32,
-        grid=(ITEMS // tile,),
-        in_specs=in_specs,
-        out_specs=out_specs,
+        vmem=36,
         scratch_shapes=scratch,
-    )(*args)
+    )(q, qpos, value_weight, *pieces, *(earlier or ()))
 
 
 def merge(refs):
@@ -356,12 +340,12 @@
     z_keys = lax.ppermute(keys, "z", SWAP)
     up, down, across = (lax.ppermute(keys, "y", shift(d)) for d in (1, 3, 2))
     q_ring = [lax.ppermute(q_own, "x", shift(1)), lax.ppermute(q_own, "x", shift(3))]
-    q_ring, q_own, w_own = lax.optimization_barrier((q_ring, q_own, jnp.transpose(w_out)))
+    q_ring, q_own = lax.optimization_barrier((q_ring, q_own))
     q_ring.append(lax.ppermute(q_own, "x", shift(2)))
-    z_keys, up, down, across, q_ring[0] = lax.optimization_barrier((z_keys, up, down, across, q_ring[0]))
-    near = [keys, z_keys, up, down, across]
-    far = [lax.ppermute(z_keys, "y", shift(d)) for d in RING[1:]]
-    q_chip = join([q_own, *q_ring])
+    z_keys, up, down, across = lax.optimization_barrier((z_keys, up, down, across))
+    near = [keys, up, down, across]
+    far = [z_keys] + [lax.ppermute(z_keys, "y", shift(d)) for d in RING[1:]]
+    q_chip, w_own = lax.optimization_barrier((join([q_own, *q_ring]), jnp.transpose(w_out)))
     q_core = lax.ppermute(q_chip, "c", SWAP)
     z_w = lax.ppermute(w_own, "z", SWAP)
 

time: 115 us -> 107 us (0.930)
  waiting for transfers between devices: 25.6 us -> 18.8 us
  starting transfers between devices: 33.5 us -> 39.4 us
  Pallas kernels: 30.7 us -> 26.7 us
  blocking collectives: 21 us -> 17.5 us
    pallas_call x2, Pallas kernels: 20.9 us -> 16.8 us  [attend(): call(functools.partial(attend_kernel, n, last, tile, unroll), out_shape,...]
    ppermute x1, waiting for transfers between devices: 3.76 us -> 0.01 us  [local(): lax.ppermute(q_own, 'x', shift(1))]
    all_to_all x1, blocking collectives: 21 us -> 17.5 us  [local(): lax.all_to_all(sums.reshape(16, 4 * R, ncol), ('z', 'c', 'head'), 0, 0, t...]
    ppermute x1, waiting for transfers between devices: 0.65 us -> 3.73 us  [local(): q_ring.append(lax.ppermute(q_own, 'x', shift(2)))]
    ppermute x1, starting transfers between devices: 0.01 us -> 2.59 us  [local(): z_w = lax.ppermute(w_own, 'z', SWAP)]
    ppermute x1, waiting for transfers between devices: 2.49 us -> 0.01 us  [local(): lax.ppermute(q_own, 'x', shift(3))]
    ppermute x1, starting transfers between devices: 1.47 us -> 3.63 us  [local(): c_w = lax.ppermute(w_own, 'c', SWAP)]
    ppermute x3, waiting for transfers between devices: 3.08 us -> 1.02 us  [local(): up, down, across = (lax.ppermute(keys, 'y', shift(d)) for d in (1, 3, 2))]
  transfers between devices with their start and end apart: 19 -> 19, of which waited for: 8 -> 6; matrix products, arithmetic and copies ran while one was open for 0% -> 0% of each run, Pallas kernels for 23% -> 21%
where the time goes in v9:
time: 107 us; the launch traced here: 106 us
  starting transfers between devices  39.4 us (37%)
  Pallas kernels  26.7 us (25%)
  waiting for transfers between devices  18.8 us (18%)
  blocking collectives  17.5 us (16%)
  local copies, waits for them, and re-layouts  2.85 us (3%)
    all_to_all x1, blocking collectives, local(): lax.all_to_all(sums.reshape(16, 4 * R, ncol), ('z', 'c', 'head'), 0, 0, t...  17.5 us
    pallas_call x2, Pallas kernels, attend(): call(functools.partial(attend_kernel, n, last, tile, unroll), out_shape,...  16.8 us
    all_to_all x1, waiting for transfers between devices, local(): lax.all_to_all(heads, ('y', 'x'), 0, 0, tiled=True)  7.39 us
    ppermute x1, starting transfers between devices, local(): z_keys = lax.ppermute(keys, 'z', SWAP)  6.1 us
    ppermute x3, starting transfers between devices, local(): up, down, across = (lax.ppermute(keys, 'y', shift(d)) for d in (1, 3, 2))  5.21 us
    ppermute x3, starting transfers between devices, local(): far = [z_keys] + [lax.ppermute(z_keys, 'y', shift(d)) for d in RING[1:]]  4.67 us
    ppermute x3, starting transfers between devices, local(): lax.ppermute(part, 'x', shift(-d % 4))  4.32 us
    ppermute x3, waiting for transfers between devices, local(): lax.ppermute(part, 'x', shift(-d % 4))  3.76 us
  transfers between devices with their start and end apart: 19, of which 6 were waited for; matrix products, arithmetic and copies ran while one was open for 0% of the time, Pallas kernels for 21%

profile of v9, /device:TPU:33, one launch (start us, length us, event | category | flops | bytes accessed | tf_op | source)
XLA Modules:
  0.0 106.2 jit_solution(225000860179172571)
XLA Ops:
  0.0 1.0 shard_map.100
  1.0 6.1 %collective-permute-start.4 = (bf16[256,640]{1,0:T(8,128)(2,1)S(1)}, bf16[256,640]{1,0:T(8,128)(2,1)S(1)}, u32[]{:S(2)}, u32[]{:S(2)}) collective-permute-start(bf16[256,640]{1,0:T(8,128)(2,1)S(1)} %get-tuple-element.42.refs_3_), channel_id=1, source_target_pairs={{0,8},{8,0},{1,9},{9,1},{2,10},{10,2},{3,11},{11,3},{4,12},{12,4},... | collective-permute-start | bytes 983048 | tf_op jit(solution)/shard_map/ppermute | solution.py:340
  7.1 1.2 %collective-permute-start = (bf16[16,3072]{1,0:T(8,128)(2,1)S(1)}, bf16[16,3072]{1,0:T(8,128)(2,1)S(1)}, u32[]{:S(2)}, u32[]{:S(2)}) collective-permute-start(bf16[16,3072]{1,0:T(8,128)(2,1)S(1)} %get-tuple-element.38.refs_0_), channel_id=1, source_target_pairs={{0,16},{16,32},{32,48},{48,0},{1,17},{17,33},{33,49},{49,1},{2,18}... | collective-permute-start | bytes 294920 | tf_op jit(solution)/shard_map/ppermute | solution.py:342
  8.3 1.5 %collective-permute-start.1 = (bf16[16,3072]{1,0:T(8,128)(2,1)S(1)}, bf16[16,3072]{1,0:T(8,128)(2,1)S(1)}, u32[]{:S(2)}, u32[]{:S(2)}) collective-permute-start(bf16[16,3072]{1,0:T(8,128)(2,1)S(1)} %get-tuple-element.38.refs_0_), channel_id=1, source_target_pairs={{0,48},{16,0},{32,16},{48,32},{1,49},{17,1},{33,17},{49,33},{2,50}... | collective-permute-start | bytes 294920 | tf_op jit(solution)/shard_map/ppermute | solution.py:342
  9.8 1.3 %collective-permute-start.5 = (bf16[256,640]{1,0:T(8,128)(2,1)S(1)}, bf16[256,640]{1,0:T(8,128)(2,1)S(1)}, u32[]{:S(2)}, u32[]{:S(2)}) collective-permute-start(bf16[256,640]{1,0:T(8,128)(2,1)S(1)} %get-tuple-element.42.refs_3_), channel_id=1, source_target_pairs={{0,64},{64,128},{128,192},{192,0},{1,65},{65,129},{129,193},{193,1... | collective-permute-start | bytes 983048 | tf_op jit(solution)/shard_map/ppermute | solution.py:341
  11.1 1.4 %collective-permute-start.6 = (bf16[256,640]{1,0:T(8,128)(2,1)S(1)}, bf16[256,640]{1,0:T(8,128)(2,1)S(1)}, u32[]{:S(2)}, u32[]{:S(2)}) collective-permute-start(bf16[256,640]{1,0:T(8,128)(2,1)S(1)} %get-tuple-element.42.refs_3_), channel_id=1, source_target_pairs={{0,192},{64,0},{128,64},{192,128},{1,193},{65,1},{129,65},{193,129... | collective-permute-start | bytes 983048 | tf_op jit(solution)/shard_map/ppermute | solution.py:341
  12.6 0.0 collective-permute-done.refs_1_
  12.6 2.5 %collective-permute-start.7 = (bf16[256,640]{1,0:T(8,128)(2,1)S(1)}, bf16[256,640]{1,0:T(8,128)(2,1)S(1)}, u32[]{:S(2)}, u32[]{:S(2)}) collective-permute-start(bf16[256,640]{1,0:T(8,128)(2,1)S(1)} %get-tuple-element.42.refs_3_), channel_id=1, source_target_pairs={{0,128},{64,192},{128,0},{192,64},{1,129},{65,193},{129,1},{193,65... | collective-permute-start | bytes 983048 | tf_op jit(solution)/shard_map/ppermute | solution.py:341
  15.0 1.5 %collective-permute-start.2 = (bf16[16,3072]{1,0:T(8,128)(2,1)S(1)}, bf16[16,3072]{1,0:T(8,128)(2,1)S(1)}, u32[]{:S(2)}, u32[]{:S(2)}) collective-permute-start(bf16[16,3072]{1,0:T(8,128)(2,1)S(1)} %get-tuple-element.38.refs_0_), channel_id=1, source_target_pairs={{0,32},{16,48},{32,0},{48,16},{1,33},{17,49},{33,1},{49,17},{2,34}... | collective-permute-start | bytes 294920 | tf_op jit(solution)/shard_map/ppermute | solution.py:344
  16.6 3.7 %collective-permute-done.2.refs_3_ = bf16[16,3072]{1,0:T(8,128)(2,1)S(1)} collective-permute-done((bf16[16,3072]{1,0:T(8,128)(2,1)S(1)}, bf16[16,3072]{1,0:T(8,128)(2,1)S(1)}, u32[]{:S(2)}, u32[]{:S(2)}) %collective-permute-start.2) | collective-permute-done | bytes 98336 | tf_op jit(solution)/shard_map/ppermute | solution.py:344
  20.3 3.0 %collective-permute-start.3 = (bf16[64,3072]{1,0:T(8,128)(2,1)S(1)}, bf16[64,3072]{1,0:T(8,128)(2,1)S(1)}, u32[]{:S(2)}, u32[]{:S(2)}) collective-permute-start(bf16[64,3072]{1,0:T(8,128)(2,1)S(1)} %shard_map.101.refs_0_), channel_id=1, source_target_pairs={{0,4},{4,0},{1,5},{5,1},{2,6},{6,2},{3,7},{7,3},{8,12},{12,8},{9,1... | collective-permute-start | bytes 1179656 | tf_op jit(solution)/shard_map/ppermute | solution.py:349
  23.4 0.0 collective-permute-done.4.refs_3_
  23.4 2.6 %collective-permute-start.11 = (bf16[112,2048]{1,0:T(8,128)(2,1)}, bf16[112,2048]{1,0:T(8,128)(2,1)S(1)}, u32[]{:S(2)}, u32[]{:S(2)}) collective-permute-start(bf16[112,2048]{1,0:T(8,128)(2,1)} %bitcast.20), channel_id=1, source_target_pairs={{0,8},{8,0},{1,9},{9,1},{2,10},{10,2},{3,11},{11,3},{4,12},{12,4},... | collective-permute-start | bytes 1376264 | tf_op jit(solution)/shard_map/ppermute | solution.py:350
  25.9 0.0 collective-permute-done.5.refs_4_
  26.0 0.0 collective-permute-done.6.refs_5_
  26.0 1.0 collective-permute-done.7.refs_6_
  27.0 2.0 %collective-permute-start.10 = (bf16[256,640]{1,0:T(8,128)(2,1)S(1)}, bf16[256,640]{1,0:T(8,128)(2,1)S(1)}, u32[]{:S(2)}, u32[]{:S(2)}) collective-permute-start(bf16[256,640]{1,0:T(8,128)(2,1)S(1)} %collective-permute-done.4.refs_3_), channel_id=1, source_target_pairs={{0,128},{64,192},{128,0},{192,64},{1,129},{65,193},{129,1},{193,65... | collective-permute-start | bytes 983048 | tf_op jit(solution)/shard_map/ppermute | solution.py:347
  29.0 0.4 collective-permute-start.8
  29.4 2.3 %collective-permute-start.9 = (bf16[256,640]{1,0:T(8,128)(2,1)S(1)}, bf16[256,640]{1,0:T(8,128)(2,1)}, u32[]{:S(2)}, u32[]{:S(2)}) collective-permute-start(bf16[256,640]{1,0:T(8,128)(2,1)S(1)} %collective-permute-done.4.refs_3_), channel_id=1, source_target_pairs={{0,192},{64,0},{128,64},{192,128},{1,193},{65,1},{129,65},{193,129... | collective-permute-start | bytes 983048 | tf_op jit(solution)/shard_map/ppermute | solution.py:347
  32.3 0.0 collective-permute-done.3.refs_1_
  32.3 3.6 %collective-permute-start.16 = (bf16[112,2048]{1,0:T(8,128)(2,1)}, bf16[112,2048]{1,0:T(8,128)(2,1)S(1)}, u32[]{:S(2)}, u32[]{:S(2)}) collective-permute-start(bf16[112,2048]{1,0:T(8,128)(2,1)} %bitcast.21), channel_id=1, source_target_pairs={{0,4},{4,0},{1,5},{5,1},{2,6},{6,2},{3,7},{7,3},{8,12},{12,8},{9,1... | collective-permute-start | bytes 1376264 | tf_op jit(solution)/shard_map/ppermute | solution.py:371
  36.0 2.5 %shard_map.102.refs_0_ = bf16[2048,768]{1,0:T(8,128)(2,1)S(1)} custom-call(bf16[64,3072]{1,0:T(8,128)(2,1)S(1)} %shard_map.101.refs_0_, bf16[64,3072]{1,0:T(8,128)(2,1)S(1)} %collective-permute-done.3.refs_1_, bf16[16,128,512]{2,1,0:T(8,128)(2,1)} %refs_2_.3), custom_call_target="tpu_custom_call" | custom-call | flops 1 | bytes 1 | tf_op jit(solution)/shard_map/pallas_call | solution.py:142
  38.5 7.7 %shard_map.103 = (f32[128,2048]{1,0:T(8,128)S(1)}, f32[2048,128]{1,0:T(8,128)S(1)}) custom-call(bf16[2048,768]{1,0:T(8,128)(2,1)S(1)} %shard_map.102.refs_0_, f32[8,128]{1,0:T(8,128)S(1)} %broadcast_in_dim.17.refs_1_, bf16[16,512,128]{2,1,0:T(8,128)(2,1)S(1)} %copy-done, bf16[256,640]{1,0:T(8,128)(2,1)S(1)} %get-tuple-element.42.refs_3_, ...), custom_call_target="tpu_custom_call" | custom-call | flops 1 | bytes 1 | tf_op jit(solution)/shard_map/pallas_call | solution.py:248
  46.2 0.0 collective-permute-done.9.refs_5_
  46.2 9.2 %shard_map.104 = (bf16[64,2176]{1,0:T(8,128)(2,1)S(1)}, bf16[64,2176]{1,0:T(8,128)(2,1)S(1)}) custom-call(bf16[2048,768]{1,0:T(8,128)(2,1)S(1)} %shard_map.102.refs_0_, f32[8,128]{1,0:T(8,128)S(1)} %broadcast_in_dim.17.refs_1_, bf16[16,512,128]{2,1,0:T(8,128)(2,1)S(1)} %copy-done, bf16[256,640]{1,0:T(8,128)(2,1)S(1)} %collective-permute-done.4.refs_3_, ...), custom_call_target="tpu_custom_call" | custom-call | flops 1 | bytes 1 | tf_op jit(solution)/shard_map/pallas_call | solution.py:248
  55.3 0.0 collective-permute-done.11.refs_1_
  55.4 0.1 collective-permute-start.12
  55.5 1.5 %collective-permute-done.12.b_ref = bf16[64,2176]{1,0:T(8,128)(2,1)S(1)} collective-permute-done((bf16[64,2176]{1,0:T(8,128)(2,1)S(1)}, bf16[64,2176]{1,0:T(8,128)(2,1)S(1)}, u32[]{:S(2)}, u32[]{:S(2)}) %collective-permute-start.12) | collective-permute-done | bytes 278560 | tf_op jit(solution)/shard_map/ppermute | solution.py:367
  57.0 0.5 shard_map.105
  57.5 2.6 %collective-permute-start.13 = (bf16[16,2176]{1,0:T(8,128)(2,1)S(1)}, bf16[16,2176]{1,0:T(8,128)(2,1)S(1)}, u32[]{:S(2)}, u32[]{:S(2)}) collective-permute-start(bf16[16,2176]{1,0:T(8,128)(2,1)S(1)} %get-tuple-element.60), channel_id=1, source_target_pairs={{0,48},{16,0},{32,16},{48,32},{1,49},{17,1},{33,17},{49,33},{2,50}... | collective-permute-start | bytes 208904 | tf_op jit(solution)/shard_map/ppermute | solution.py:369
  60.1 1.8 %collective-permute-start.15 = (bf16[16,2176]{1,0:T(8,128)(2,1)S(1)}, bf16[16,2176]{1,0:T(8,128)(2,1)S(1)}, u32[]{:S(2)}, u32[]{:S(2)}) collective-permute-start(bf16[16,2176]{1,0:T(8,128)(2,1)S(1)} %get-tuple-element.62), channel_id=1, source_target_pairs={{0,32},{16,48},{32,0},{48,16},{1,33},{17,49},{33,1},{49,17},{2,34}... | collective-permute-start | bytes 208904 | tf_op jit(solution)/shard_map/ppermute | solution.py:369
  61.8 0.0 collective-permute-done.16.refs_2_
  61.8 0.8 copy-done.3
  62.6 0.0 collective-permute-done.13.refs_1_
  62.6 3.8 %collective-permute-done.14.refs_2_ = bf16[16,2176]{1,0:T(8,128)(2,1)S(1)} collective-permute-done((bf16[16,2176]{1,0:T(8,128)(2,1)S(1)}, bf16[16,2176]{1,0:T(8,128)(2,1)S(1)}, u32[]{:S(2)}, u32[]{:S(2)}) %collective-permute-start.14) | collective-permute-done | bytes 69664 | tf_op jit(solution)/shard_map/ppermute | solution.py:369
  66.4 0.0 collective-permute-done.15.refs_3_
  66.4 1.4 %shard_map.106 = bf16[16,16,2048]{2,1,0:T(8,128)(2,1)} custom-call(bf16[16,2176]{1,0:T(8,128)(2,1)S(1)} %get-tuple-element.63.refs_0_, bf16[16,2176]{1,0:T(8,128)(2,1)S(1)} %collective-permute-done.13.refs_1_, bf16[16,2176]{1,0:T(8,128)(2,1)S(1)} %collective-permute-done.14.refs_2_, bf16[16,2176]{1,0:T(8,128)(2,1)S(1)} %collective-permute-done.15.refs_3_), custom_call_target="tpu_custom_call" | custom-call | flops 1 | bytes 1 | tf_op jit(solution)/shard_map/pallas_call | solution.py:374
  67.8 3.7 %all-to-all-start = ((bf16[16,16,2048]{2,1,0:T(8,128)(2,1)}), bf16[16,16,2048]{2,1,0:T(8,128)(2,1)S(1)}, u32[]{:S(2)}, u32[]{:S(2)}) async-start(bf16[16,16,2048]{2,1,0:T(8,128)(2,1)} %shard_map.106), calls=%async_computation | async-start | bytes 2097152 | tf_op jit(solution)/shard_map/all_to_all | solution.py:378
  71.5 1.9 %collective-permute-start.17 = (bf16[112,2048]{1,0:T(8,128)(2,1)S(1)}, bf16[112,2048]{1,0:T(8,128)(2,1)S(1)}, u32[]{:S(2)}, u32[]{:S(2)}) collective-permute-start(bf16[112,2048]{1,0:T(8,128)(2,1)S(1)} %collective-permute-done.11.refs_1_), channel_id=1, source_target_pairs={{0,4},{4,0},{1,5},{5,1},{2,6},{6,2},{3,7},{7,3},{8,12},{12,8},{9,1... | collective-permute-start | bytes 1376264 | tf_op jit(solution)/shard_map/ppermute | solution.py:372
  73.4 0.1 pad_add_fusion.zc_ref
  73.5 1.4 %collective-permute-done.17.refs_3_ = bf16[112,2048]{1,0:T(8,128)(2,1)S(1)} collective-permute-done((bf16[112,2048]{1,0:T(8,128)(2,1)S(1)}, bf16[112,2048]{1,0:T(8,128)(2,1)S(1)}, u32[]{:S(2)}, u32[]{:S(2)}) %collective-permute-start.17) | collective-permute-done | bytes 458784 | tf_op jit(solution)/shard_map/ppermute | solution.py:372
  74.8 1.0 copy-done.2
  75.8 1.0 copy-done.4
  76.9 2.4 %shard_map.107.w_ref = bf16[4,2048,128]{2,1,0:T(8,128)(2,1)S(1)} custom-call(s32[2]{0:T(128)S(1)} %pad_add_fusion.zc_ref, bf16[112,2048]{1,0:T(8,128)(2,1)} %bitcast.22, bf16[112,2048]{1,0:T(8,128)(2,1)S(1)} %copy-done.2, bf16[112,2048]{1,0:T(8,128)(2,1)S(1)} %copy-done.4, bf16[112,2048]{1,0:T(8,128)(2,1)S(1)} %collective-permute-done.17.refs_3_), custom_call_target="tpu_custom_call" | custom-call | flops 1 | bytes 1 | tf_op jit(solution)/shard_map/pallas_call | solution.py:307
  79.3 7.4 %all-to-all-done = bf16[16,16,2048]{2,1,0:T(8,128)(2,1)S(1)} async-done(((bf16[16,16,2048]{2,1,0:T(8,128)(2,1)}), bf16[16,16,2048]{2,1,0:T(8,128)(2,1)S(1)}, u32[]{:S(2)}, u32[]{:S(2)}) %all-to-all-start) | async-done | bytes 1048608 | tf_op jit(solution)/shard_map/all_to_all | solution.py:378
  86.7 1.2 %shard_map.108 = bf16[4,256,112]{2,1,0:T(8,128)(2,1)S(1)} custom-call(bf16[256,2048]{1,0:T(8,128)(2,1)S(1)} %bitcast.18, bf16[4,2048,128]{2,1,0:T(8,128)(2,1)S(1)} %shard_map.107.w_ref), custom_call_target="tpu_custom_call" | custom-call | flops 1 | bytes 1 | tf_op jit(solution)/shard_map/pallas_call | solution.py:381
  87.9 17.5 %all_to_all.10.sums_ref = bf16[16,64,112]{2,1,0:T(8,128)(2,1)S(1)} all-to-all(bf16[16,64,112]{2,1,0:T(8,128)(2,1)S(1)} %bitcast.19), channel_id=1, replica_groups=mesh['y'=4,'x'=4,'z'=2,'c'=2,'head'=4] {'z','c','head'}, dimensions={0} | all-to-all | bytes 458752 | tf_op jit(solution)/shard_map/all_to_all | solution.py:384
  105.4 0.7 shard_map.109
  (14 shorter events, 0.1 us)
Async XLA Ops:
  1.0 22.3 %collective-permute-start.4 = (bf16[256,640]{1,0:T(8,128)(2,1)S(1)}, bf16[256,640]{1,0:T(8,128)(2,1)S(1)}, u32[]{:S(2)}, u32[]{:S(2)}) collective-permute-start(bf16[256,640]{1,0:T(8,128)(2,1)S(1)} %get-tuple-element.42.refs_3_), channel_id=1, source_target_pairs={{0,8},{8,0},{1,9},{9,1},{2,10},{10,2},{3,11},{11,3},{4,12},{12,4},... | collective-permute-start | bytes 983048 | tf_op jit(solution)/shard_map/ppermute | solution.py:340
  7.1 5.4 %collective-permute-start = (bf16[16,3072]{1,0:T(8,128)(2,1)S(1)}, bf16[16,3072]{1,0:T(8,128)(2,1)S(1)}, u32[]{:S(2)}, u32[]{:S(2)}) collective-permute-start(bf16[16,3072]{1,0:T(8,128)(2,1)S(1)} %get-tuple-element.38.refs_0_), channel_id=1, source_target_pairs={{0,16},{16,32},{32,48},{48,0},{1,17},{17,33},{33,49},{49,1},{2,18}... | collective-permute-start | bytes 294920 | tf_op jit(solution)/shard_map/ppermute | solution.py:342
  8.3 6.7 %collective-permute-start.1 = (bf16[16,3072]{1,0:T(8,128)(2,1)S(1)}, bf16[16,3072]{1,0:T(8,128)(2,1)S(1)}, u32[]{:S(2)}, u32[]{:S(2)}) collective-permute-start(bf16[16,3072]{1,0:T(8,128)(2,1)S(1)} %get-tuple-element.38.refs_0_), channel_id=1, source_target_pairs={{0,48},{16,0},{32,16},{48,32},{1,49},{17,1},{33,17},{49,33},{2,50}... | collective-permute-start | bytes 294920 | tf_op jit(solution)/shard_map/ppermute | solution.py:342
  9.8 16.1 %collective-permute-start.5 = (bf16[256,640]{1,0:T(8,128)(2,1)S(1)}, bf16[256,640]{1,0:T(8,128)(2,1)S(1)}, u32[]{:S(2)}, u32[]{:S(2)}) collective-permute-start(bf16[256,640]{1,0:T(8,128)(2,1)S(1)} %get-tuple-element.42.refs_3_), channel_id=1, source_target_pairs={{0,64},{64,128},{128,192},{192,0},{1,65},{65,129},{129,193},{193,1... | collective-permute-start | bytes 983048 | tf_op jit(solution)/shard_map/ppermute | solution.py:341
  11.1 14.8 %collective-permute-start.6 = (bf16[256,640]{1,0:T(8,128)(2,1)S(1)}, bf16[256,640]{1,0:T(8,128)(2,1)S(1)}, u32[]{:S(2)}, u32[]{:S(2)}) collective-permute-start(bf16[256,640]{1,0:T(8,128)(2,1)S(1)} %get-tuple-element.42.refs_3_), channel_id=1, source_target_pairs={{0,192},{64,0},{128,64},{192,128},{1,193},{65,1},{129,65},{193,129... | collective-permute-start | bytes 983048 | tf_op jit(solution)/shard_map/ppermute | solution.py:341
  12.6 14.4 %collective-permute-start.7 = (bf16[256,640]{1,0:T(8,128)(2,1)S(1)}, bf16[256,640]{1,0:T(8,128)(2,1)S(1)}, u32[]{:S(2)}, u32[]{:S(2)}) collective-permute-start(bf16[256,640]{1,0:T(8,128)(2,1)S(1)} %get-tuple-element.42.refs_3_), channel_id=1, source_target_pairs={{0,128},{64,192},{128,0},{192,64},{1,129},{65,193},{129,1},{193,65... | collective-permute-start | bytes 983048 | tf_op jit(solution)/shard_map/ppermute | solution.py:341
  15.0 5.3 %collective-permute-start.2 = (bf16[16,3072]{1,0:T(8,128)(2,1)S(1)}, bf16[16,3072]{1,0:T(8,128)(2,1)S(1)}, u32[]{:S(2)}, u32[]{:S(2)}) collective-permute-start(bf16[16,3072]{1,0:T(8,128)(2,1)S(1)} %get-tuple-element.38.refs_0_), channel_id=1, source_target_pairs={{0,32},{16,48},{32,0},{48,16},{1,33},{17,49},{33,1},{49,17},{2,34}... | collective-permute-start | bytes 294920 | tf_op jit(solution)/shard_map/ppermute | solution.py:344
  20.3 12.0 %collective-permute-start.3 = (bf16[64,3072]{1,0:T(8,128)(2,1)S(1)}, bf16[64,3072]{1,0:T(8,128)(2,1)S(1)}, u32[]{:S(2)}, u32[]{:S(2)}) collective-permute-start(bf16[64,3072]{1,0:T(8,128)(2,1)S(1)} %shard_map.101.refs_0_), channel_id=1, source_target_pairs={{0,4},{4,0},{1,5},{5,1},{2,6},{6,2},{3,7},{7,3},{8,12},{12,8},{9,1... | collective-permute-start | bytes 1179656 | tf_op jit(solution)/shard_map/ppermute | solution.py:349
  23.4 32.0 %collective-permute-start.11 = (bf16[112,2048]{1,0:T(8,128)(2,1)}, bf16[112,2048]{1,0:T(8,128)(2,1)S(1)}, u32[]{:S(2)}, u32[]{:S(2)}) collective-permute-start(bf16[112,2048]{1,0:T(8,128)(2,1)} %bitcast.20), channel_id=1, source_target_pairs={{0,8},{8,0},{1,9},{9,1},{2,10},{10,2},{3,11},{11,3},{4,12},{12,4},... | collective-permute-start | bytes 1376264 | tf_op jit(solution)/shard_map/ppermute | solution.py:350
  27.0 19.2 %collective-permute-start.10 = (bf16[256,640]{1,0:T(8,128)(2,1)S(1)}, bf16[256,640]{1,0:T(8,128)(2,1)S(1)}, u32[]{:S(2)}, u32[]{:S(2)}) collective-permute-start(bf16[256,640]{1,0:T(8,128)(2,1)S(1)} %collective-permute-done.4.refs_3_), channel_id=1, source_target_pairs={{0,128},{64,192},{128,0},{192,64},{1,129},{65,193},{129,1},{193,65... | collective-permute-start | bytes 983048 | tf_op jit(solution)/shard_map/ppermute | solution.py:347
  29.0 17.2 %collective-permute-start.8 = (bf16[256,640]{1,0:T(8,128)(2,1)S(1)}, bf16[256,640]{1,0:T(8,128)(2,1)S(1)}, u32[]{:S(2)}, u32[]{:S(2)}) collective-permute-start(bf16[256,640]{1,0:T(8,128)(2,1)S(1)} %collective-permute-done.4.refs_3_), channel_id=1, source_target_pairs={{0,64},{64,128},{128,192},{192,0},{1,65},{65,129},{129,193},{193,1... | collective-permute-start | bytes 983048 | tf_op jit(solution)/shard_map/ppermute | solution.py:347
  29.4 16.8 %collective-permute-start.9 = (bf16[256,640]{1,0:T(8,128)(2,1)S(1)}, bf16[256,640]{1,0:T(8,128)(2,1)}, u32[]{:S(2)}, u32[]{:S(2)}) collective-permute-start(bf16[256,640]{1,0:T(8,128)(2,1)S(1)} %collective-permute-done.4.refs_3_), channel_id=1, source_target_pairs={{0,192},{64,0},{128,64},{192,128},{1,193},{65,1},{129,65},{193,129... | collective-permute-start | bytes 983048 | tf_op jit(solution)/shard_map/ppermute | solution.py:347
  32.3 29.5 %collective-permute-start.16 = (bf16[112,2048]{1,0:T(8,128)(2,1)}, bf16[112,2048]{1,0:T(8,128)(2,1)S(1)}, u32[]{:S(2)}, u32[]{:S(2)}) collective-permute-start(bf16[112,2048]{1,0:T(8,128)(2,1)} %bitcast.21), channel_id=1, source_target_pairs={{0,4},{4,0},{1,5},{5,1},{2,6},{6,2},{3,7},{7,3},{8,12},{12,8},{9,1... | collective-permute-start | bytes 1376264 | tf_op jit(solution)/shard_map/ppermute | solution.py:371
  36.0 2.5 %copy-start = (bf16[16,512,128]{2,1,0:T(8,128)(2,1)S(1)}, bf16[16,512,128]{2,1,0:T(8,128)(2,1)}, u32[]{:S(2)}) copy-start(bf16[16,512,128]{2,1,0:T(8,128)(2,1)} %refs_2_.5) | copy-start | bytes 6291460
  55.4 18.1 %copy-start.1 = (bf16[112,2048]{1,0:T(8,128)(2,1)}, bf16[112,2048]{1,0:T(8,128)(2,1)S(1)}, u32[]{:S(2)}) copy-start(bf16[112,2048]{1,0:T(8,128)(2,1)S(1)} %collective-permute-done.11.refs_1_) | copy-start | bytes 1376260
  55.4 1.6 %collective-permute-start.12 = (bf16[64,2176]{1,0:T(8,128)(2,1)S(1)}, bf16[64,2176]{1,0:T(8,128)(2,1)S(1)}, u32[]{:S(2)}, u32[]{:S(2)}) collective-permute-start(bf16[64,2176]{1,0:T(8,128)(2,1)S(1)} %get-tuple-element.58), channel_id=1, source_target_pairs={{0,4},{4,0},{1,5},{5,1},{2,6},{6,2},{3,7},{7,3},{8,12},{12,8},{9,1... | collective-permute-start | bytes 835592 | tf_op jit(solution)/shard_map/ppermute | solution.py:367
  57.5 5.1 %collective-permute-start.13 = (bf16[16,2176]{1,0:T(8,128)(2,1)S(1)}, bf16[16,2176]{1,0:T(8,128)(2,1)S(1)}, u32[]{:S(2)}, u32[]{:S(2)}) collective-permute-start(bf16[16,2176]{1,0:T(8,128)(2,1)S(1)} %get-tuple-element.60), channel_id=1, source_target_pairs={{0,48},{16,0},{32,16},{48,32},{1,49},{17,1},{33,17},{49,33},{2,50}... | collective-permute-start | bytes 208904 | tf_op jit(solution)/shard_map/ppermute | solution.py:369
  60.1 6.3 %collective-permute-start.14 = (bf16[16,2176]{1,0:T(8,128)(2,1)S(1)}, bf16[16,2176]{1,0:T(8,128)(2,1)S(1)}, u32[]{:S(2)}, u32[]{:S(2)}) collective-permute-start(bf16[16,2176]{1,0:T(8,128)(2,1)S(1)} %get-tuple-element.61), channel_id=1, source_target_pairs={{0,16},{16,32},{32,48},{48,0},{1,17},{17,33},{33,49},{49,1},{2,18}... | collective-permute-start | bytes 208904 | tf_op jit(solution)/shard_map/ppermute | solution.py:369
  60.1 6.3 %collective-permute-start.15 = (bf16[16,2176]{1,0:T(8,128)(2,1)S(1)}, bf16[16,2176]{1,0:T(8,128)(2,1)S(1)}, u32[]{:S(2)}, u32[]{:S(2)}) collective-permute-start(bf16[16,2176]{1,0:T(8,128)(2,1)S(1)} %get-tuple-element.62), channel_id=1, source_target_pairs={{0,32},{16,48},{32,0},{48,16},{1,33},{17,49},{33,1},{49,17},{2,34}... | collective-permute-start | bytes 208904 | tf_op jit(solution)/shard_map/ppermute | solution.py:369
  61.8 0.8 copy-start.3
  67.8 18.8 %all-to-all-start = ((bf16[16,16,2048]{2,1,0:T(8,128)(2,1)}), bf16[16,16,2048]{2,1,0:T(8,128)(2,1)S(1)}, u32[]{:S(2)}, u32[]{:S(2)}) async-start(bf16[16,16,2048]{2,1,0:T(8,128)(2,1)} %shard_map.106), calls=%async_computation | async-start | bytes 2097152 | tf_op jit(solution)/shard_map/all_to_all | solution.py:378
  71.5 3.3 %collective-permute-start.17 = (bf16[112,2048]{1,0:T(8,128)(2,1)S(1)}, bf16[112,2048]{1,0:T(8,128)(2,1)S(1)}, u32[]{:S(2)}, u32[]{:S(2)}) collective-permute-start(bf16[112,2048]{1,0:T(8,128)(2,1)S(1)} %collective-permute-done.11.refs_1_), channel_id=1, source_target_pairs={{0,4},{4,0},{1,5},{5,1},{2,6},{6,2},{3,7},{7,3},{8,12},{12,8},{9,1... | collective-permute-start | bytes 1376264 | tf_op jit(solution)/shard_map/ppermute | solution.py:372
  74.8 1.0 copy-start.2
  75.8 1.0 copy-start.4

commit v10 on v9

--- a/solution.py
+++ b/solution.py
@@ -93,30 +93,28 @@
 
 
 def join_kernel(*refs):
-    start = 0
-    for ref in refs[:-1]:
-        refs[-1][start : start + ref.shape[0]] = ref[...]
-        start += ref.shape[0]
-
-
-def join(parts):
-    shape = (sum(part.shape[0] for part in parts), parts[0].shape[1])
-    return call(join_kernel, jax.ShapeDtypeStruct(shape, jnp.bfloat16))(*parts)
+    parts, (w_hbm, out_ref, w_ref, sem) = refs[:4], refs[4:]
+    copy = pltpu.make_async_copy(w_hbm, w_ref, sem)
+    copy.start()
+    for i, ref in enumerate(parts):
+        out_ref[i * R : (i + 1) * R] = ref[...]
+    copy.wait()
+
+
+def join(parts, w_uk):
+    return call(
+        join_kernel,
+        (
+            jax.ShapeDtypeStruct((4 * R, parts[0].shape[1]), jnp.bfloat16),
+            jax.ShapeDtypeStruct(w_uk.shape, jnp.bfloat16),
+        ),
+        in_specs=[pl.BlockSpec(memory_space=pltpu.VMEM)] * 4 + [HBM],
+        scratch_shapes=[pltpu.SemaphoreType.DMA],
+    )(*parts, *in_hbm(w_uk))
 
 
 def absorb_kernel(*refs):
-    q_refs, (w_hbm, out_ref, w_ref, sems) = refs[:2], refs[2:]
-    step = HG // 4
-    copies = [
-        pltpu.make_async_copy(
-            w_hbm.at[i * step : (i + 1) * step],
-            w_ref.at[i * step : (i + 1) * step],
-            sems.at[i],
-        )
-        for i in range(4)
-    ]
-    for copy in copies:
-        copy.start()
+    q_refs, (w_ref, out_ref) = refs[:2], refs[2:]
     lane = lax.broadcasted_iota(jnp.int32, (ROWS, 128), 1)
     row = lax.broadcasted_iota(jnp.int32, (ROWS, 128), 0)
     one_hot = (lane == row).astype(jnp.bfloat16)
@@ -125,8 +123,6 @@
         return jnp.concatenate([ref[:, start : start + 128] for ref in q_refs], axis=0)
 
     for h in range(HG):
-        if h % step == 0:
-            copies[h // step].wait()
         rows = slice(h * ROWS, (h + 1) * ROWS)
         latent = jnp.dot(columns(h * NOPE), w_ref[h], preferred_element_type=jnp.float32)
         out_ref[rows, :RANK] = latent.astype(jnp.bfloat16)
@@ -139,16 +135,9 @@
 
 
 def absorb(queries, w_uk):
-    return call(
-        absorb_kernel,
-        jax.ShapeDtypeStruct((ITEMS, ITEMW), jnp.bfloat16),
-        vmem=16,
-        in_specs=[pl.BlockSpec(memory_space=pltpu.VMEM)] * 2 + [HBM],
-        scratch_shapes=[
-            pltpu.VMEM(w_uk.shape, jnp.bfloat16),
-            pltpu.SemaphoreType.DMA((4,)),
-        ],
-    )(*queries, *in_hbm(w_uk))
+    return call(absorb_kernel, jax.ShapeDtypeStruct((ITEMS, ITEMW), jnp.bfloat16))(
+        *queries, w_uk
+    )
 
 
 def pack_stats(stats):
@@ -345,9 +334,10 @@
     z_keys, up, down, across = lax.optimization_barrier((z_keys, up, down, across))
     near = [keys, up, down, across]
     far = [z_keys] + [lax.ppermute(z_keys, "y", shift(d)) for d in RING[1:]]
-    q_chip, w_own = lax.optimization_barrier((join([q_own, *q_ring]), jnp.transpose(w_out)))
+    q_ring, w_own = lax.optimization_barrier((q_ring, jnp.transpose(w_out)))
+    z_w = lax.ppermute(w_own, "z", SWAP)
+    q_chip, w_absorb = join([q_own, *q_ring], w_uk)
     q_core = lax.ppermute(q_chip, "c", SWAP)
-    z_w = lax.ppermute(w_own, "z", SWAP)
 
     row = jnp.arange(ROWS, dtype=jnp.int32)
     part = row // R
@@ -356,10 +346,11 @@
     row = (((y * 4 + row_x) * 2 + z) * 2 + row_c) * R + row % R
     qpos = jnp.broadcast_to((offset[0] + row).astype(jnp.float32)[None, :], (8, ROWS))
 
-    q = absorb((q_chip, q_core), w_uk)
+    q = absorb((q_chip, q_core), w_absorb)
     earlier = attend(q, qpos, value_up_weight, near)
     earlier, far = lax.optimization_barrier((earlier, far))
     keep, send = attend(q, qpos, value_up_weight, far, earlier)
+    send, w_own = lax.optimization_barrier((send, w_own))
 
     z_w, send = lax.optimization_barrier((z_w, send))
     parts = call(
@@ -370,7 +361,6 @@
     ]
     c_w = lax.ppermute(w_own, "c", SWAP)
     zc_w = lax.ppermute(z_w, "c", SWAP)
-    parts, c_w = lax.optimization_barrier((parts, c_w))
     heads = call(merge_ring_kernel, jax.ShapeDtypeStruct((16, R, HG * VDIM), jnp.bfloat16))(
         *parts
     )

time: 107 us -> 114 us (1.065)
  blocking collectives: 17.5 us -> 22.2 us
  waiting for transfers between devices: 18.8 us -> 21.6 us
  starting transfers between devices: 39.4 us -> 37.6 us
  local copies, waits for them, and re-layouts: 2.85 us -> 4.28 us
    all_to_all x1, blocking collectives: 17.5 us -> 22.2 us  [local(): lax.all_to_all(sums.reshape(16, 4 * R, ncol), ('z', 'c', 'head'), 0, 0, t...]
    ppermute x1, starting transfers between devices: 3.63 us -> 0.11 us  [local(): c_w = lax.ppermute(w_own, 'c', SWAP)]
    ppermute x3, waiting for transfers between devices: 0.01 us -> 2.85 us  [local(): far = [z_keys] + [lax.ppermute(z_keys, 'y', shift(d)) for d in RING[1:]]]
    ppermute x1, starting transfers between devices: 2.59 us -> 0.01 us  [local(): z_w = lax.ppermute(w_own, 'z', SWAP)]
    ppermute x1, waiting for transfers between devices: 0.01 us -> 2.4 us  [local(): lax.ppermute(q_own, 'x', shift(3))]
    unnamed x10 -> x24, local copies, waits for them, and re-layouts: 2.85 us -> 4.27 us
    all_to_all x1, starting transfers between devices: 3.65 us -> 4.8 us  [local(): lax.all_to_all(heads, ('y', 'x'), 0, 0, tiled=True)]
  transfers between devices with their start and end apart: 19 -> 19, of which waited for: 6 -> 9; matrix products, arithmetic and copies ran while one was open for 0% -> 0% of each run, Pallas kernels for 21% -> 19%
where the time goes in v10:
time: 114 us; the launch traced here: 113 us
  starting transfers between devices  37.6 us (33%)
  Pallas kernels  26.7 us (23%)
  blocking collectives  22.2 us (19%)
  waiting for transfers between devices  21.6 us (19%)
  local copies, waits for them, and re-layouts  4.28 us (4%)
    all_to_all x1, blocking collectives, local(): lax.all_to_all(sums.reshape(16, 4 * R, ncol), ('z', 'c', 'head'), 0, 0, t...  22.2 us
    pallas_call x2, Pallas kernels, attend(): call(functools.partial(attend_kernel, n, last, tile, unroll), out_shape,...  17 us
    all_to_all x1, waiting for transfers between devices, local(): lax.all_to_all(heads, ('y', 'x'), 0, 0, tiled=True)  7.02 us
    ppermute x1, starting transfers between devices, local(): z_keys = lax.ppermute(keys, 'z', SWAP)  6.01 us
    ppermute x3, starting transfers between devices, local(): far = [z_keys] + [lax.ppermute(z_keys, 'y', shift(d)) for d in RING[1:]]  5.68 us
    all_to_all x1, starting transfers between devices, local(): lax.all_to_all(heads, ('y', 'x'), 0, 0, tiled=True)  4.8 us
    ppermute x3, starting transfers between devices, local(): lax.ppermute(part, 'x', shift(-d % 4))  4.43 us
    ppermute x3, starting transfers between devices, local(): up, down, across = (lax.ppermute(keys, 'y', shift(d)) for d in (1, 3, 2))  4.38 us
  transfers between devices with their start and end apart: 19, of which 9 were waited for; matrix products, arithmetic and copies ran while one was open for 0% of the time, Pallas kernels for 19%

profile of v10, /device:TPU:33, one launch (start us, length us, event | category | flops | bytes accessed | tf_op | source)
XLA Modules:
  0.0 113.4 jit_solution(17118496533253621806)
XLA Ops:
  0.0 1.0 shard_map.100
  1.1 1.3 %collective-permute-start = (bf16[16,3072]{1,0:T(8,128)(2,1)S(1)}, bf16[16,3072]{1,0:T(8,128)(2,1)S(1)}, u32[]{:S(2)}, u32[]{:S(2)}) collective-permute-start(bf16[16,3072]{1,0:T(8,128)(2,1)S(1)} %get-tuple-element.39.refs_0_), channel_id=1, source_target_pairs={{0,16},{16,32},{32,48},{48,0},{1,17},{17,33},{33,49},{49,1},{2,18}... | collective-permute-start | bytes 294920 | tf_op jit(solution)/shard_map/ppermute | solution.py:331
  2.3 6.0 %collective-permute-start.4 = (bf16[256,640]{1,0:T(8,128)(2,1)S(1)}, bf16[256,640]{1,0:T(8,128)(2,1)}, u32[]{:S(2)}, u32[]{:S(2)}) collective-permute-start(bf16[256,640]{1,0:T(8,128)(2,1)S(1)} %get-tuple-element.47.refs_3_), channel_id=1, source_target_pairs={{0,8},{8,0},{1,9},{9,1},{2,10},{10,2},{3,11},{11,3},{4,12},{12,4},... | collective-permute-start | bytes 983048 | tf_op jit(solution)/shard_map/ppermute | solution.py:329
  8.3 1.3 %collective-permute-start.5 = (bf16[256,640]{1,0:T(8,128)(2,1)S(1)}, bf16[256,640]{1,0:T(8,128)(2,1)S(1)}, u32[]{:S(2)}, u32[]{:S(2)}) collective-permute-start(bf16[256,640]{1,0:T(8,128)(2,1)S(1)} %get-tuple-element.47.refs_3_), channel_id=1, source_target_pairs={{0,64},{64,128},{128,192},{192,0},{1,65},{65,129},{129,193},{193,1... | collective-permute-start | bytes 983048 | tf_op jit(solution)/shard_map/ppermute | solution.py:330
  9.6 1.4 %collective-permute-start.6 = (bf16[256,640]{1,0:T(8,128)(2,1)S(1)}, bf16[256,640]{1,0:T(8,128)(2,1)S(1)}, u32[]{:S(2)}, u32[]{:S(2)}) collective-permute-start(bf16[256,640]{1,0:T(8,128)(2,1)S(1)} %get-tuple-element.47.refs_3_), channel_id=1, source_target_pairs={{0,192},{64,0},{128,64},{192,128},{1,193},{65,1},{129,65},{193,129... | collective-permute-start | bytes 983048 | tf_op jit(solution)/shard_map/ppermute | solution.py:330
  11.1 1.6 %collective-permute-start.7 = (bf16[256,640]{1,0:T(8,128)(2,1)S(1)}, bf16[256,640]{1,0:T(8,128)(2,1)S(1)}, u32[]{:S(2)}, u32[]{:S(2)}) collective-permute-start(bf16[256,640]{1,0:T(8,128)(2,1)S(1)} %get-tuple-element.47.refs_3_), channel_id=1, source_target_pairs={{0,128},{64,192},{128,0},{192,64},{1,129},{65,193},{129,1},{193,65... | collective-permute-start | bytes 983048 | tf_op jit(solution)/shard_map/ppermute | solution.py:330
  12.7 1.5 %collective-permute-start.1 = (bf16[16,3072]{1,0:T(8,128)(2,1)S(1)}, bf16[16,3072]{1,0:T(8,128)(2,1)S(1)}, u32[]{:S(2)}, u32[]{:S(2)}) collective-permute-start(bf16[16,3072]{1,0:T(8,128)(2,1)S(1)} %get-tuple-element.39.refs_0_), channel_id=1, source_target_pairs={{0,48},{16,0},{32,16},{48,32},{1,49},{17,1},{33,17},{49,33},{2,50}... | collective-permute-start | bytes 294920 | tf_op jit(solution)/shard_map/ppermute | solution.py:331
  14.2 2.4 %collective-permute-done.1.refs_2_ = bf16[16,3072]{1,0:T(8,128)(2,1)S(1)} collective-permute-done((bf16[16,3072]{1,0:T(8,128)(2,1)S(1)}, bf16[16,3072]{1,0:T(8,128)(2,1)S(1)}, u32[]{:S(2)}, u32[]{:S(2)}) %collective-permute-start.1) | collective-permute-done | bytes 98336 | tf_op jit(solution)/shard_map/ppermute | solution.py:331
  16.6 2.5 %collective-permute-start.2 = (bf16[16,3072]{1,0:T(8,128)(2,1)S(1)}, bf16[16,3072]{1,0:T(8,128)(2,1)S(1)}, u32[]{:S(2)}, u32[]{:S(2)}) collective-permute-start(bf16[16,3072]{1,0:T(8,128)(2,1)S(1)} %get-tuple-element.39.refs_0_), channel_id=1, source_target_pairs={{0,32},{16,48},{32,0},{48,16},{1,33},{17,49},{33,1},{49,17},{2,34}... | collective-permute-start | bytes 294920 | tf_op jit(solution)/shard_map/ppermute | solution.py:333
  19.1 2.9 %collective-permute-done.2.refs_3_ = bf16[16,3072]{1,0:T(8,128)(2,1)S(1)} collective-permute-done((bf16[16,3072]{1,0:T(8,128)(2,1)S(1)}, bf16[16,3072]{1,0:T(8,128)(2,1)S(1)}, u32[]{:S(2)}, u32[]{:S(2)}) %collective-permute-start.2) | collective-permute-done | bytes 98336 | tf_op jit(solution)/shard_map/ppermute | solution.py:333
  22.0 1.6 %shard_map.101 = (bf16[64,3072]{1,0:T(8,128)(2,1)S(1)}, bf16[16,128,512]{2,1,0:T(8,128)(2,1)S(1)}) custom-call(bf16[16,3072]{1,0:T(8,128)(2,1)S(1)} %get-tuple-element.39.refs_0_, bf16[16,3072]{1,0:T(8,128)(2,1)S(1)} %collective-permute-done.refs_1_, bf16[16,3072]{1,0:T(8,128)(2,1)S(1)} %collective-permute-done.1.refs_2_, ...), custom_call_target="tpu_custom_call" | custom-call | flops 1 | bytes 1 | tf_op jit(solution)/shard_map/pallas_call | solution.py:105
  23.6 3.7 %collective-permute-start.3 = (bf16[64,3072]{1,0:T(8,128)(2,1)S(1)}, bf16[64,3072]{1,0:T(8,128)(2,1)S(1)}, u32[]{:S(2)}, u32[]{:S(2)}) collective-permute-start(bf16[64,3072]{1,0:T(8,128)(2,1)S(1)} %get-tuple-element.45.refs_0_), channel_id=1, source_target_pairs={{0,4},{4,0},{1,5},{5,1},{2,6},{6,2},{3,7},{7,3},{8,12},{12,8},{9,1... | collective-permute-start | bytes 1179656 | tf_op jit(solution)/shard_map/ppermute | solution.py:340
  27.3 0.7 copy-done.5
  28.0 0.7 copy-done.7
  28.7 0.7 copy-done.9
  29.5 3.0 %collective-permute-start.10 = (bf16[256,640]{1,0:T(8,128)(2,1)}, bf16[256,640]{1,0:T(8,128)(2,1)}, u32[]{:S(2)}, u32[]{:S(2)}) collective-permute-start(bf16[256,640]{1,0:T(8,128)(2,1)} %collective-permute-done.4.refs_3_), channel_id=1, source_target_pairs={{0,128},{64,192},{128,0},{192,64},{1,129},{65,193},{129,1},{193,65... | collective-permute-start | bytes 983048 | tf_op jit(solution)/shard_map/ppermute | solution.py:336
  32.5 0.5 collective-permute-start.8
  33.0 2.1 %collective-permute-start.9 = (bf16[256,640]{1,0:T(8,128)(2,1)}, bf16[256,640]{1,0:T(8,128)(2,1)}, u32[]{:S(2)}, u32[]{:S(2)}) collective-permute-start(bf16[256,640]{1,0:T(8,128)(2,1)} %collective-permute-done.4.refs_3_), channel_id=1, source_target_pairs={{0,192},{64,0},{128,64},{192,128},{1,193},{65,1},{129,65},{193,129... | collective-permute-start | bytes 983048 | tf_op jit(solution)/shard_map/ppermute | solution.py:336
  35.9 0.8 shard_map.102.refs_0_
  36.7 0.7 copy-done
  37.5 0.0 copy-done.4
  37.5 0.1 copy-done.6
  37.6 0.1 copy-done.8
  37.7 0.1 copy-done.10
  37.8 7.7 %shard_map.103 = (f32[128,2048]{1,0:T(8,128)S(1)}, f32[2048,128]{1,0:T(8,128)S(1)}) custom-call(bf16[2048,768]{1,0:T(8,128)(2,1)S(1)} %shard_map.102.refs_0_, f32[8,128]{1,0:T(8,128)S(1)} %broadcast_in_dim.17.refs_1_, bf16[16,512,128]{2,1,0:T(8,128)(2,1)S(1)} %copy-done, bf16[256,640]{1,0:T(8,128)(2,1)S(1)} %copy-done.4, bf16[256,640]{1,0:T(8,128)(2,1)S(1)} %copy-done.6, ...), custom_call_target="tpu_custom_call" | custom-call | flops 1 | bytes 1 | tf_op jit(solution)/shard_map/pallas_call | solution.py:237
  45.4 2.6 %collective-permute-done.8.refs_4_ = bf16[256,640]{1,0:T(8,128)(2,1)} collective-permute-done((bf16[256,640]{1,0:T(8,128)(2,1)}, bf16[256,640]{1,0:T(8,128)(2,1)}, u32[]{:S(2)}, u32[]{:S(2)}) %collective-permute-start.8) | collective-permute-done | bytes 327712 | tf_op jit(solution)/shard_map/ppermute | solution.py:336
  48.0 0.3 collective-permute-done.9.refs_5_
  48.3 9.4 %shard_map.104 = (bf16[64,2176]{1,0:T(8,128)(2,1)S(1)}, bf16[64,2176]{1,0:T(8,128)(2,1)S(1)}) custom-call(bf16[2048,768]{1,0:T(8,128)(2,1)S(1)} %shard_map.102.refs_0_, f32[8,128]{1,0:T(8,128)S(1)} %broadcast_in_dim.17.refs_1_, bf16[16,512,128]{2,1,0:T(8,128)(2,1)S(1)} %copy-done, bf16[256,640]{1,0:T(8,128)(2,1)} %collective-permute-done.4.refs_3_, ...), custom_call_target="tpu_custom_call" | custom-call | flops 1 | bytes 1 | tf_op jit(solution)/shard_map/pallas_call | solution.py:237
  57.6 0.0 copy-start.11
  57.7 0.9 collective-permute-start.12
  58.6 1.2 %collective-permute-done.12.b_ref = bf16[64,2176]{1,0:T(8,128)(2,1)S(1)} collective-permute-done((bf16[64,2176]{1,0:T(8,128)(2,1)S(1)}, bf16[64,2176]{1,0:T(8,128)(2,1)S(1)}, u32[]{:S(2)}, u32[]{:S(2)}) %collective-permute-start.12) | collective-permute-done | bytes 278560 | tf_op jit(solution)/shard_map/ppermute | solution.py:358
  59.7 0.5 shard_map.105
  60.2 2.1 %collective-permute-start.13 = (bf16[16,2176]{1,0:T(8,128)(2,1)S(1)}, bf16[16,2176]{1,0:T(8,128)(2,1)S(1)}, u32[]{:S(2)}, u32[]{:S(2)}) collective-permute-start(bf16[16,2176]{1,0:T(8,128)(2,1)S(1)} %get-tuple-element.66), channel_id=1, source_target_pairs={{0,48},{16,0},{32,16},{48,32},{1,49},{17,1},{33,17},{49,33},{2,50}... | collective-permute-start | bytes 208904 | tf_op jit(solution)/shard_map/ppermute | solution.py:360
  62.4 2.3 %collective-permute-start.15 = (bf16[16,2176]{1,0:T(8,128)(2,1)S(1)}, bf16[16,2176]{1,0:T(8,128)(2,1)S(1)}, u32[]{:S(2)}, u32[]{:S(2)}) collective-permute-start(bf16[16,2176]{1,0:T(8,128)(2,1)S(1)} %get-tuple-element.68), channel_id=1, source_target_pairs={{0,32},{16,48},{32,0},{48,16},{1,33},{17,49},{33,1},{49,17},{2,34}... | collective-permute-start | bytes 208904 | tf_op jit(solution)/shard_map/ppermute | solution.py:360
  64.7 3.3 %collective-permute-done.14.refs_2_ = bf16[16,2176]{1,0:T(8,128)(2,1)S(1)} collective-permute-done((bf16[16,2176]{1,0:T(8,128)(2,1)S(1)}, bf16[16,2176]{1,0:T(8,128)(2,1)S(1)}, u32[]{:S(2)}, u32[]{:S(2)}) %collective-permute-start.14) | collective-permute-done | bytes 69664 | tf_op jit(solution)/shard_map/ppermute | solution.py:360
  68.0 1.4 %shard_map.106 = bf16[16,16,2048]{2,1,0:T(8,128)(2,1)} custom-call(bf16[16,2176]{1,0:T(8,128)(2,1)S(1)} %get-tuple-element.65.refs_0_, bf16[16,2176]{1,0:T(8,128)(2,1)S(1)} %collective-permute-done.13.refs_1_, bf16[16,2176]{1,0:T(8,128)(2,1)S(1)} %collective-permute-done.14.refs_2_, bf16[16,2176]{1,0:T(8,128)(2,1)S(1)} %collective-permute-done.15.refs_3_), custom_call_target="tpu_custom_call" | custom-call | flops 1 | bytes 1 | tf_op jit(solution)/shard_map/pallas_call | solution.py:364
  69.4 4.8 %all-to-all-start = ((bf16[16,16,2048]{2,1,0:T(8,128)(2,1)}), bf16[16,16,2048]{2,1,0:T(8,128)(2,1)S(1)}, u32[]{:S(2)}, u32[]{:S(2)}) async-start(bf16[16,16,2048]{2,1,0:T(8,128)(2,1)} %shard_map.106), calls=%async_computation | async-start | bytes 2097152 | tf_op jit(solution)/shard_map/all_to_all | solution.py:368
  74.2 2.5 %collective-permute-start.17 = (bf16[112,2048]{1,0:T(8,128)(2,1)S(1)}, bf16[112,2048]{1,0:T(8,128)(2,1)S(1)}, u32[]{:S(2)}, u32[]{:S(2)}) collective-permute-start(bf16[112,2048]{1,0:T(8,128)(2,1)S(1)} %collective-permute-done.11.refs_1_), channel_id=1, source_target_pairs={{0,4},{4,0},{1,5},{5,1},{2,6},{6,2},{3,7},{7,3},{8,12},{12,8},{9,1... | collective-permute-start | bytes 1376264 | tf_op jit(solution)/shard_map/ppermute | solution.py:363
  76.6 0.1 collective-permute-start.16
  76.7 0.1 pad_add_fusion.zc_ref
  76.8 1.3 %collective-permute-done.17.refs_3_ = bf16[112,2048]{1,0:T(8,128)(2,1)S(1)} collective-permute-done((bf16[112,2048]{1,0:T(8,128)(2,1)S(1)}, bf16[112,2048]{1,0:T(8,128)(2,1)S(1)}, u32[]{:S(2)}, u32[]{:S(2)}) %collective-permute-start.17) | collective-permute-done | bytes 458784 | tf_op jit(solution)/shard_map/ppermute | solution.py:363
  78.1 0.7 collective-permute-done.16.refs_2_
  78.7 1.0 copy-done.2
  79.7 2.4 %shard_map.107.w_ref = bf16[4,2048,128]{2,1,0:T(8,128)(2,1)S(1)} custom-call(s32[2]{0:T(128)S(1)} %pad_add_fusion.zc_ref, bf16[112,2048]{1,0:T(8,128)(2,1)} %bitcast.21, bf16[112,2048]{1,0:T(8,128)(2,1)S(1)} %copy-done.2, bf16[112,2048]{1,0:T(8,128)(2,1)S(1)} %collective-permute-done.16.refs_2_, bf16[112,2048]{1,0:T(8,128)(2,1)S(1)} %collective-permute-done.17.refs_3_), custom_call_target="tpu_custom_call" | custom-call | flops 1 | bytes 1 | tf_op jit(solution)/shard_map/pallas_call | solution.py:296
  82.2 7.0 %all-to-all-done = bf16[16,16,2048]{2,1,0:T(8,128)(2,1)S(1)} async-done(((bf16[16,16,2048]{2,1,0:T(8,128)(2,1)}), bf16[16,16,2048]{2,1,0:T(8,128)(2,1)S(1)}, u32[]{:S(2)}, u32[]{:S(2)}) %all-to-all-start) | async-done | bytes 1048608 | tf_op jit(solution)/shard_map/all_to_all | solution.py:368
  89.2 1.2 %shard_map.108 = bf16[4,256,112]{2,1,0:T(8,128)(2,1)S(1)} custom-call(bf16[256,2048]{1,0:T(8,128)(2,1)S(1)} %bitcast.18, bf16[4,2048,128]{2,1,0:T(8,128)(2,1)S(1)} %shard_map.107.w_ref), custom_call_target="tpu_custom_call" | custom-call | flops 1 | bytes 1 | tf_op jit(solution)/shard_map/pallas_call | solution.py:371
  90.4 22.2 %all_to_all.10.sums_ref = bf16[16,64,112]{2,1,0:T(8,128)(2,1)S(1)} all-to-all(bf16[16,64,112]{2,1,0:T(8,128)(2,1)S(1)} %bitcast.19), channel_id=1, replica_groups=mesh['y'=4,'x'=4,'z'=2,'c'=2,'head'=4] {'z','c','head'}, dimensions={0} | all-to-all | bytes 458752 | tf_op jit(solution)/shard_map/all_to_all | solution.py:374
  112.6 0.7 shard_map.109
  (28 shorter events, 0.1 us)
Async XLA Ops:
  1.0 22.6 %copy-start.3 = (bf16[256,640]{1,0:T(8,128)(2,1)}, bf16[256,640]{1,0:T(8,128)(2,1)S(1)}, u32[]{:S(2)}) copy-start(bf16[256,640]{1,0:T(8,128)(2,1)S(1)} %get-tuple-element.47.refs_3_) | copy-start | bytes 983044
  1.1 11.7 %collective-permute-start = (bf16[16,3072]{1,0:T(8,128)(2,1)S(1)}, bf16[16,3072]{1,0:T(8,128)(2,1)S(1)}, u32[]{:S(2)}, u32[]{:S(2)}) collective-permute-start(bf16[16,3072]{1,0:T(8,128)(2,1)S(1)} %get-tuple-element.39.refs_0_), channel_id=1, source_target_pairs={{0,16},{16,32},{32,48},{48,0},{1,17},{17,33},{33,49},{49,1},{2,18}... | collective-permute-start | bytes 294920 | tf_op jit(solution)/shard_map/ppermute | solution.py:331
  2.3 21.2 %collective-permute-start.4 = (bf16[256,640]{1,0:T(8,128)(2,1)S(1)}, bf16[256,640]{1,0:T(8,128)(2,1)}, u32[]{:S(2)}, u32[]{:S(2)}) collective-permute-start(bf16[256,640]{1,0:T(8,128)(2,1)S(1)} %get-tuple-element.47.refs_3_), channel_id=1, source_target_pairs={{0,8},{8,0},{1,9},{9,1},{2,10},{10,2},{3,11},{11,3},{4,12},{12,4},... | collective-permute-start | bytes 983048 | tf_op jit(solution)/shard_map/ppermute | solution.py:329
  8.3 18.9 %collective-permute-start.5 = (bf16[256,640]{1,0:T(8,128)(2,1)S(1)}, bf16[256,640]{1,0:T(8,128)(2,1)S(1)}, u32[]{:S(2)}, u32[]{:S(2)}) collective-permute-start(bf16[256,640]{1,0:T(8,128)(2,1)S(1)} %get-tuple-element.47.refs_3_), channel_id=1, source_target_pairs={{0,64},{64,128},{128,192},{192,0},{1,65},{65,129},{129,193},{193,1... | collective-permute-start | bytes 983048 | tf_op jit(solution)/shard_map/ppermute | solution.py:330
  9.6 18.3 %collective-permute-start.6 = (bf16[256,640]{1,0:T(8,128)(2,1)S(1)}, bf16[256,640]{1,0:T(8,128)(2,1)S(1)}, u32[]{:S(2)}, u32[]{:S(2)}) collective-permute-start(bf16[256,640]{1,0:T(8,128)(2,1)S(1)} %get-tuple-element.47.refs_3_), channel_id=1, source_target_pairs={{0,192},{64,0},{128,64},{192,128},{1,193},{65,1},{129,65},{193,129... | collective-permute-start | bytes 983048 | tf_op jit(solution)/shard_map/ppermute | solution.py:330
  11.1 17.6 %collective-permute-start.7 = (bf16[256,640]{1,0:T(8,128)(2,1)S(1)}, bf16[256,640]{1,0:T(8,128)(2,1)S(1)}, u32[]{:S(2)}, u32[]{:S(2)}) collective-permute-start(bf16[256,640]{1,0:T(8,128)(2,1)S(1)} %get-tuple-element.47.refs_3_), channel_id=1, source_target_pairs={{0,128},{64,192},{128,0},{192,64},{1,129},{65,193},{129,1},{193,65... | collective-permute-start | bytes 983048 | tf_op jit(solution)/shard_map/ppermute | solution.py:330
  12.7 3.9 %collective-permute-start.1 = (bf16[16,3072]{1,0:T(8,128)(2,1)S(1)}, bf16[16,3072]{1,0:T(8,128)(2,1)S(1)}, u32[]{:S(2)}, u32[]{:S(2)}) collective-permute-start(bf16[16,3072]{1,0:T(8,128)(2,1)S(1)} %get-tuple-element.39.refs_0_), channel_id=1, source_target_pairs={{0,48},{16,0},{32,16},{48,32},{1,49},{17,1},{33,17},{49,33},{2,50}... | collective-permute-start | bytes 294920 | tf_op jit(solution)/shard_map/ppermute | solution.py:331
  16.6 5.4 %collective-permute-start.2 = (bf16[16,3072]{1,0:T(8,128)(2,1)S(1)}, bf16[16,3072]{1,0:T(8,128)(2,1)S(1)}, u32[]{:S(2)}, u32[]{:S(2)}) collective-permute-start(bf16[16,3072]{1,0:T(8,128)(2,1)S(1)} %get-tuple-element.39.refs_0_), channel_id=1, source_target_pairs={{0,32},{16,48},{32,0},{48,16},{1,33},{17,49},{33,1},{49,17},{2,34}... | collective-permute-start | bytes 294920 | tf_op jit(solution)/shard_map/ppermute | solution.py:333
  22.0 35.7 %collective-permute-start.11 = (bf16[112,2048]{1,0:T(8,128)(2,1)}, bf16[112,2048]{1,0:T(8,128)(2,1)S(1)}, u32[]{:S(2)}, u32[]{:S(2)}) collective-permute-start(bf16[112,2048]{1,0:T(8,128)(2,1)} %bitcast.20), channel_id=1, source_target_pairs={{0,8},{8,0},{1,9},{9,1},{2,10},{10,2},{3,11},{11,3},{4,12},{12,4},... | collective-permute-start | bytes 1376264 | tf_op jit(solution)/shard_map/ppermute | solution.py:338
  23.6 12.2 %collective-permute-start.3 = (bf16[64,3072]{1,0:T(8,128)(2,1)S(1)}, bf16[64,3072]{1,0:T(8,128)(2,1)S(1)}, u32[]{:S(2)}, u32[]{:S(2)}) collective-permute-start(bf16[64,3072]{1,0:T(8,128)(2,1)S(1)} %get-tuple-element.45.refs_0_), channel_id=1, source_target_pairs={{0,4},{4,0},{1,5},{5,1},{2,6},{6,2},{3,7},{7,3},{8,12},{12,8},{9,1... | collective-permute-start | bytes 1179656 | tf_op jit(solution)/shard_map/ppermute | solution.py:340
  27.3 0.7 copy-start.5
  28.0 0.7 copy-start.7
  28.7 0.7 copy-start.9
  29.5 15.9 %collective-permute-start.10 = (bf16[256,640]{1,0:T(8,128)(2,1)}, bf16[256,640]{1,0:T(8,128)(2,1)}, u32[]{:S(2)}, u32[]{:S(2)}) collective-permute-start(bf16[256,640]{1,0:T(8,128)(2,1)} %collective-permute-done.4.refs_3_), channel_id=1, source_target_pairs={{0,128},{64,192},{128,0},{192,64},{1,129},{65,193},{129,1},{193,65... | collective-permute-start | bytes 983048 | tf_op jit(solution)/shard_map/ppermute | solution.py:336
  32.5 15.5 %collective-permute-start.8 = (bf16[256,640]{1,0:T(8,128)(2,1)}, bf16[256,640]{1,0:T(8,128)(2,1)}, u32[]{:S(2)}, u32[]{:S(2)}) collective-permute-start(bf16[256,640]{1,0:T(8,128)(2,1)} %collective-permute-done.4.refs_3_), channel_id=1, source_target_pairs={{0,64},{64,128},{128,192},{192,0},{1,65},{65,129},{129,193},{193,1... | collective-permute-start | bytes 983048 | tf_op jit(solution)/shard_map/ppermute | solution.py:336
  33.0 15.3 %collective-permute-start.9 = (bf16[256,640]{1,0:T(8,128)(2,1)}, bf16[256,640]{1,0:T(8,128)(2,1)}, u32[]{:S(2)}, u32[]{:S(2)}) collective-permute-start(bf16[256,640]{1,0:T(8,128)(2,1)} %collective-permute-done.4.refs_3_), channel_id=1, source_target_pairs={{0,192},{64,0},{128,64},{192,128},{1,193},{65,1},{129,65},{193,129... | collective-permute-start | bytes 983048 | tf_op jit(solution)/shard_map/ppermute | solution.py:336
  35.9 1.6 %copy-start = (bf16[16,512,128]{2,1,0:T(8,128)(2,1)S(1)}, bf16[16,512,128]{2,1,0:T(8,128)(2,1)}, u32[]{:S(2)}) copy-start(bf16[16,512,128]{2,1,0:T(8,128)(2,1)} %refs_2_.3) | copy-start | bytes 6291460
  35.9 1.6 %copy-start.4 = (bf16[256,640]{1,0:T(8,128)(2,1)S(1)}, bf16[256,640]{1,0:T(8,128)(2,1)}, u32[]{:S(2)}) copy-start(bf16[256,640]{1,0:T(8,128)(2,1)} %copy-done.3) | copy-start | bytes 983044
  35.9 1.7 %copy-start.6 = (bf16[256,640]{1,0:T(8,128)(2,1)S(1)}, bf16[256,640]{1,0:T(8,128)(2,1)}, u32[]{:S(2)}) copy-start(bf16[256,640]{1,0:T(8,128)(2,1)} %copy-done.5) | copy-start | bytes 983044
  35.9 1.8 %copy-start.8 = (bf16[256,640]{1,0:T(8,128)(2,1)S(1)}, bf16[256,640]{1,0:T(8,128)(2,1)}, u32[]{:S(2)}) copy-start(bf16[256,640]{1,0:T(8,128)(2,1)} %copy-done.7) | copy-start | bytes 983044
  35.9 1.9 %copy-start.10 = (bf16[256,640]{1,0:T(8,128)(2,1)S(1)}, bf16[256,640]{1,0:T(8,128)(2,1)}, u32[]{:S(2)}) copy-start(bf16[256,640]{1,0:T(8,128)(2,1)} %copy-done.9) | copy-start | bytes 983044
  57.6 19.0 %copy-start.11 = (bf16[2048,112]{0,1:T(8,128)(2,1)S(1)}, bf16[2048,112]{0,1:T(8,128)(2,1)}, u32[]{:S(2)}) copy-start(bf16[2048,112]{0,1:T(8,128)(2,1)} %param.18) | copy-start | bytes 1376260
  57.7 20.4 %copy-start.1 = (bf16[112,2048]{1,0:T(8,128)(2,1)}, bf16[112,2048]{1,0:T(8,128)(2,1)S(1)}, u32[]{:S(2)}) copy-start(bf16[112,2048]{1,0:T(8,128)(2,1)S(1)} %collective-permute-done.11.refs_1_) | copy-start | bytes 1376260
  57.7 2.1 %collective-permute-start.12 = (bf16[64,2176]{1,0:T(8,128)(2,1)S(1)}, bf16[64,2176]{1,0:T(8,128)(2,1)S(1)}, u32[]{:S(2)}, u32[]{:S(2)}) collective-permute-start(bf16[64,2176]{1,0:T(8,128)(2,1)S(1)} %get-tuple-element.64), channel_id=1, source_target_pairs={{0,4},{4,0},{1,5},{5,1},{2,6},{6,2},{3,7},{7,3},{8,12},{12,8},{9,1... | collective-permute-start | bytes 835592 | tf_op jit(solution)/shard_map/ppermute | solution.py:358
  60.2 4.4 %collective-permute-start.13 = (bf16[16,2176]{1,0:T(8,128)(2,1)S(1)}, bf16[16,2176]{1,0:T(8,128)(2,1)S(1)}, u32[]{:S(2)}, u32[]{:S(2)}) collective-permute-start(bf16[16,2176]{1,0:T(8,128)(2,1)S(1)} %get-tuple-element.66), channel_id=1, source_target_pairs={{0,48},{16,0},{32,16},{48,32},{1,49},{17,1},{33,17},{49,33},{2,50}... | collective-permute-start | bytes 208904 | tf_op jit(solution)/shard_map/ppermute | solution.py:360
  62.4 5.6 %collective-permute-start.14 = (bf16[16,2176]{1,0:T(8,128)(2,1)S(1)}, bf16[16,2176]{1,0:T(8,128)(2,1)S(1)}, u32[]{:S(2)}, u32[]{:S(2)}) collective-permute-start(bf16[16,2176]{1,0:T(8,128)(2,1)S(1)} %get-tuple-element.67), channel_id=1, source_target_pairs={{0,16},{16,32},{32,48},{48,0},{1,17},{17,33},{33,49},{49,1},{2,18}... | collective-permute-start | bytes 208904 | tf_op jit(solution)/shard_map/ppermute | solution.py:360
  62.4 5.6 %collective-permute-start.15 = (bf16[16,2176]{1,0:T(8,128)(2,1)S(1)}, bf16[16,2176]{1,0:T(8,128)(2,1)S(1)}, u32[]{:S(2)}, u32[]{:S(2)}) collective-permute-start(bf16[16,2176]{1,0:T(8,128)(2,1)S(1)} %get-tuple-element.68), channel_id=1, source_target_pairs={{0,32},{16,48},{32,0},{48,16},{1,33},{17,49},{33,1},{49,17},{2,34}... | collective-permute-start | bytes 208904 | tf_op jit(solution)/shard_map/ppermute | solution.py:360
  69.4 19.8 %all-to-all-start = ((bf16[16,16,2048]{2,1,0:T(8,128)(2,1)}), bf16[16,16,2048]{2,1,0:T(8,128)(2,1)S(1)}, u32[]{:S(2)}, u32[]{:S(2)}) async-start(bf16[16,16,2048]{2,1,0:T(8,128)(2,1)} %shard_map.106), calls=%async_computation | async-start | bytes 2097152 | tf_op jit(solution)/shard_map/all_to_all | solution.py:368
  74.2 3.9 %collective-permute-start.17 = (bf16[112,2048]{1,0:T(8,128)(2,1)S(1)}, bf16[112,2048]{1,0:T(8,128)(2,1)S(1)}, u32[]{:S(2)}, u32[]{:S(2)}) collective-permute-start(bf16[112,2048]{1,0:T(8,128)(2,1)S(1)} %collective-permute-done.11.refs_1_), channel_id=1, source_target_pairs={{0,4},{4,0},{1,5},{5,1},{2,6},{6,2},{3,7},{7,3},{8,12},{12,8},{9,1... | collective-permute-start | bytes 1376264 | tf_op jit(solution)/shard_map/ppermute | solution.py:363
  76.6 2.1 %collective-permute-start.16 = (bf16[112,2048]{1,0:T(8,128)(2,1)S(1)}, bf16[112,2048]{1,0:T(8,128)(2,1)S(1)}, u32[]{:S(2)}, u32[]{:S(2)}) collective-permute-start(bf16[112,2048]{1,0:T(8,128)(2,1)S(1)} %bitcast.22), channel_id=1, source_target_pairs={{0,4},{4,0},{1,5},{5,1},{2,6},{6,2},{3,7},{7,3},{8,12},{12,8},{9,1... | collective-permute-start | bytes 1376264 | tf_op jit(solution)/shard_map/ppermute | solution.py:362
  78.7 1.0 copy-start.2

commit v11 on v9

--- a/solution.py
+++ b/solution.py
@@ -59,9 +59,12 @@
         pltpu.make_async_copy(key_rope_ref, rope, sems.at[0]),
         pltpu.make_async_copy(pos_ref, pos, sems.at[1]),
         pltpu.make_async_copy(latent_ref, key_ref.at[:, :RANK], sems.at[2]),
-        pltpu.make_async_copy(query_ref, q_ref.at[:, : HG * NOPE], sems.at[3]),
-        pltpu.make_async_copy(q_rope_ref, q_ref.at[:, HG * NOPE :], sems.at[4]),
     ]
+    for i in range(4):
+        copies += [
+            pltpu.make_async_copy(query_ref, q_ref.at[i, :, : HG * NOPE], sems.at[3 + 2 * i]),
+            pltpu.make_async_copy(q_rope_ref, q_ref.at[i, :, HG * NOPE :], sems.at[4 + 2 * i]),
+        ]
     for copy in copies:
         copy.start()
     copies[0].wait()
@@ -81,27 +84,15 @@
         pack_kernel,
         (
             jax.ShapeDtypeStruct((latent.shape[0], KEYW), jnp.bfloat16),
-            jax.ShapeDtypeStruct((R, HG * (NOPE + ROPE)), jnp.bfloat16),
+            jax.ShapeDtypeStruct((4, R, HG * (NOPE + ROPE)), jnp.bfloat16),
         ),
         in_specs=[HBM] * 5,
         scratch_shapes=[
             pltpu.VMEM((k_rope.shape[1], k_rope.shape[0]), jnp.bfloat16),
             pltpu.VMEM(key_pos.shape, jnp.int32),
-            pltpu.SemaphoreType.DMA((5,)),
+            pltpu.SemaphoreType.DMA((11,)),
         ],
     )(*in_hbm(latent, jnp.transpose(k_rope), key_pos, query, q_rope))
-
-
-def join_kernel(*refs):
-    start = 0
-    for ref in refs[:-1]:
-        refs[-1][start : start + ref.shape[0]] = ref[...]
-        start += ref.shape[0]
-
-
-def join(parts):
-    shape = (sum(part.shape[0] for part in parts), parts[0].shape[1])
-    return call(join_kernel, jax.ShapeDtypeStruct(shape, jnp.bfloat16))(*parts)
 
 
 def absorb_kernel(*refs):
@@ -253,8 +244,8 @@
     )(q, qpos, value_weight, *pieces, *(earlier or ()))
 
 
-def merge(refs):
-    stats = [unpack_stats(ref[:, HG * VDIM :]) for ref in refs]
+def merge(refs, rows=slice(None)):
+    stats = [unpack_stats(ref[rows, HG * VDIM :]) for ref in refs]
     top = functools.reduce(jnp.maximum, stats)
     weights = [jnp.exp2(s - top) for s in stats]
     total = sum(weights)
@@ -263,19 +254,22 @@
     for h in range(HG):
         cols = slice(h * VDIM, (h + 1) * VDIM)
         head = sum(
-            ref[:, cols].astype(jnp.float32) * w[:, h : h + 1] for ref, w in zip(refs, weights)
+            ref[rows, cols].astype(jnp.float32) * w[:, h : h + 1]
+            for ref, w in zip(refs, weights)
         )
         out.append((cols, head.astype(jnp.bfloat16)))
     return out, top + jnp.log2(total)
 
 
-def merge_core_kernel(a_ref, b_ref, *out_refs):
-    heads, lse = merge((a_ref, b_ref))
-    lane = lax.broadcasted_iota(jnp.int32, lse.shape, 1)
-    packed = pack_stats(jnp.where(lane < HG, lse, 0.0))
-    for cols, head in heads + [(slice(HG * VDIM, SENDW), packed)]:
-        for i, ref in enumerate(out_refs):
-            ref[:, cols] = head[i * R : (i + 1) * R]
+def merge_core_kernel(x_ref, a_ref, b_ref, *out_refs):
+    for d, ref in enumerate(out_refs):
+        block = lax.rem(x_ref[0] + d, 4)
+        rows = pl.ds(pl.multiple_of(block * R, R), R)
+        heads, lse = merge((a_ref, b_ref), rows)
+        lane = lax.broadcasted_iota(jnp.int32, lse.shape, 1)
+        packed = pack_stats(jnp.where(lane < HG, lse, 0.0))
+        for cols, head in heads + [(slice(HG * VDIM, SENDW), packed)]:
+            ref[:, cols] = head
 
 
 def merge_ring_kernel(*refs):
@@ -339,19 +333,17 @@
     keys, q_own = pack(latent[0], k_rope[0], key_pos, query_unrotated, q_rope)
     z_keys = lax.ppermute(keys, "z", SWAP)
     up, down, across = (lax.ppermute(keys, "y", shift(d)) for d in (1, 3, 2))
-    q_ring = [lax.ppermute(q_own, "x", shift(1)), lax.ppermute(q_own, "x", shift(3))]
-    q_ring, q_own = lax.optimization_barrier((q_ring, q_own))
-    q_ring.append(lax.ppermute(q_own, "x", shift(2)))
+    q_chip = lax.all_to_all(q_own, "x", 0, 0, tiled=True).reshape(4 * R, -1)
     z_keys, up, down, across = lax.optimization_barrier((z_keys, up, down, across))
     near = [keys, up, down, across]
     far = [z_keys] + [lax.ppermute(z_keys, "y", shift(d)) for d in RING[1:]]
-    q_chip, w_own = lax.optimization_barrier((join([q_own, *q_ring]), jnp.transpose(w_out)))
+    q_chip, w_own = lax.optimization_barrier((q_chip, jnp.transpose(w_out)))
     q_core = lax.ppermute(q_chip, "c", SWAP)
     z_w = lax.ppermute(w_own, "z", SWAP)
 
     row = jnp.arange(ROWS, dtype=jnp.int32)
     part = row // R
-    row_x = (x - jnp.array(RING, jnp.int32)[part % 4]) % 4
+    row_x = part % 4
     row_c = jnp.where(part < 4, c, 1 - c)
     row = (((y * 4 + row_x) * 2 + z) * 2 + row_c) * R + row % R
     qpos = jnp.broadcast_to((offset[0] + row).astype(jnp.float32)[None, :], (8, ROWS))
@@ -361,20 +353,20 @@
     earlier, far = lax.optimization_barrier((earlier, far))
     keep, send = attend(q, qpos, value_up_weight, far, earlier)
 
-    z_w, send = lax.optimization_barrier((z_w, send))
     parts = call(
-        merge_core_kernel, [jax.ShapeDtypeStruct((R, SENDW), jnp.bfloat16)] * 4
-    )(keep, lax.ppermute(send, "c", SWAP))
-    parts = [parts[0]] + [
-        lax.ppermute(part, "x", shift(-d % 4)) for part, d in zip(parts[1:], RING[1:])
-    ]
-    c_w = lax.ppermute(w_own, "c", SWAP)
+        merge_core_kernel,
+        [jax.ShapeDtypeStruct((R, SENDW), jnp.bfloat16)] * 4,
+        in_specs=[pl.BlockSpec(memory_space=pltpu.SMEM)]
+        + [pl.BlockSpec(memory_space=pltpu.VMEM)] * 2,
+    )(x.reshape(1), keep, lax.ppermute(send, "c", SWAP))
+    parts = [parts[0]] + [lax.ppermute(parts[d], "x", shift(d)) for d in (1, 2, 3)]
     zc_w = lax.ppermute(z_w, "c", SWAP)
-    parts, c_w = lax.optimization_barrier((parts, c_w))
     heads = call(merge_ring_kernel, jax.ShapeDtypeStruct((16, R, HG * VDIM), jnp.bfloat16))(
         *parts
     )
 
+    heads, w_own = lax.optimization_barrier((heads, w_own))
+    c_w = lax.ppermute(w_own, "c", SWAP)
     rows = lax.all_to_all(heads, ("y", "x"), 0, 0, tiled=True).reshape(16 * R, HG * VDIM)
     ncol = w_out.shape[1]
     columns = columns_of(jnp.stack([z, c]), (w_own, z_w, c_w, zc_w))

time: 107 us -> 121 us (1.13)
  waiting for transfers between devices: 18.8 us -> 42.1 us
  starting transfers between devices: 39.4 us -> 36.1 us
  blocking collectives: 17.5 us -> 14.4 us
  local copies, waits for them, and re-layouts: 2.85 us -> 0.02 us
    ppermute x1, waiting for transfers between devices: 0.01 us -> 23.4 us  [local(): z_w = lax.ppermute(w_own, 'z', SWAP)]
    all_to_all x1, waiting for transfers between devices: 7.39 us -> 0.01 us  [local(): lax.all_to_all(heads, ('y', 'x'), 0, 0, tiled=True)]
    ppermute x1, waiting for transfers between devices: 0.01 us -> 7 us  [local(): z_keys = lax.ppermute(keys, 'z', SWAP)]
    ppermute x6 -> x3, starting transfers between devices: 8.53 us -> 4.24 us  [local(): lax.ppermute(parts[d], 'x', shift(d))]
    ppermute x1, starting transfers between devices: 0.11 us -> 4.18 us  [local(): lax.ppermute(send, 'c', SWAP)]
    all_to_all x0 -> x1, starting transfers between devices: none -> 4.02 us  [local(): q_chip = lax.all_to_all(q_own, 'x', 0, 0, tiled=True).reshape(4 * R, -1)]
    ppermute x6 -> x3, waiting for transfers between devices: 7.49 us -> 3.79 us  [local(): lax.ppermute(parts[d], 'x', shift(d))]
    ppermute x1, starting transfers between devices: 3.63 us -> 0.01 us  [local(): c_w = lax.ppermute(w_own, 'c', SWAP)]
  transfers between devices with their start and end apart: 19 -> 17, of which waited for: 6 -> 10; matrix products, arithmetic and copies ran while one was open for 0% -> 0% of each run, Pallas kernels for 21% -> 10%
where the time goes in v11:
time: 121 us; the launch traced here: 120 us
  waiting for transfers between devices  42.1 us (35%)
  starting transfers between devices  36.1 us (30%)
  Pallas kernels  27 us (22%)
  blocking collectives  14.4 us (12%)
    ppermute x1, waiting for transfers between devices, local(): z_w = lax.ppermute(w_own, 'z', SWAP)  23.4 us
    pallas_call x2, Pallas kernels, attend(): call(functools.partial(attend_kernel, n, last, tile, unroll), out_shape,...  15.9 us
    all_to_all x1, blocking collectives, local(): lax.all_to_all(sums.reshape(16, 4 * R, ncol), ('z', 'c', 'head'), 0, 0, t...  14.4 us
    ppermute x1, waiting for transfers between devices, local(): z_keys = lax.ppermute(keys, 'z', SWAP)  7 us
    ppermute x1, starting transfers between devices, local(): z_keys = lax.ppermute(keys, 'z', SWAP)  6.01 us
    all_to_all x1, starting transfers between devices, local(): lax.all_to_all(heads, ('y', 'x'), 0, 0, tiled=True)  5.16 us
    ppermute x3, starting transfers between devices, local(): up, down, across = (lax.ppermute(keys, 'y', shift(d)) for d in (1, 3, 2))  4.38 us
    ppermute x3, starting transfers between devices, local(): lax.ppermute(parts[d], 'x', shift(d))  4.24 us
  transfers between devices with their start and end apart: 17, of which 10 were waited for; matrix products, arithmetic and copies ran while one was open for 0% of the time, Pallas kernels for 10%

profile of v11, /device:TPU:33, one launch (start us, length us, event | category | flops | bytes accessed | tf_op | source)
XLA Modules:
  0.0 120.5 jit_solution(8259805568484677527)
XLA Ops:
  0.0 2.0 %shard_map.91 = (bf16[256,640]{1,0:T(8,128)(2,1)S(1)}, bf16[4,16,3072]{2,1,0:T(8,128)(2,1)}) custom-call(bf16[256,512]{1,0:T(8,128)(2,1)} %bitcast.21, bf16[64,256]{1,0:T(8,128)(2,1)} %bitcast.22, s32[1,256]{1,0:T(1,128)} %pos_ref.1, bf16[16,2048]{1,0:T(8,128)(2,1)} %query_ref.1, bf16[16,1024]{1,0:T(8,128)(2,1)} %q_rope_ref.1), custom_call_target="tpu_custom_call" | custom-call | flops 1 | bytes 1 | tf_op jit(solution)/shard_map/pallas_call | solution.py:83
  2.0 4.0 %all-to-all-start = ((bf16[4,16,3072]{2,1,0:T(8,128)(2,1)}), bf16[4,16,3072]{2,1,0:T(8,128)(2,1)S(1)}, u32[]{:S(2)}, u32[]{:S(2)}) async-start(bf16[4,16,3072]{2,1,0:T(8,128)(2,1)} %get-tuple-element.29), calls=%async_computation | async-start | bytes 786432 | tf_op jit(solution)/shard_map/all_to_all | solution.py:336
  6.0 6.0 %collective-permute-start.1 = (bf16[256,640]{1,0:T(8,128)(2,1)S(1)}, bf16[256,640]{1,0:T(8,128)(2,1)S(1)}, u32[]{:S(2)}, u32[]{:S(2)}) collective-permute-start(bf16[256,640]{1,0:T(8,128)(2,1)S(1)} %get-tuple-element.31.refs_3_), channel_id=1, source_target_pairs={{0,8},{8,0},{1,9},{9,1},{2,10},{10,2},{3,11},{11,3},{4,12},{12,4},... | collective-permute-start | bytes 983048 | tf_op jit(solution)/shard_map/ppermute | solution.py:334
  12.0 1.3 %collective-permute-start.2 = (bf16[256,640]{1,0:T(8,128)(2,1)S(1)}, bf16[256,640]{1,0:T(8,128)(2,1)S(1)}, u32[]{:S(2)}, u32[]{:S(2)}) collective-permute-start(bf16[256,640]{1,0:T(8,128)(2,1)S(1)} %get-tuple-element.31.refs_3_), channel_id=1, source_target_pairs={{0,64},{64,128},{128,192},{192,0},{1,65},{65,129},{129,193},{193,1... | collective-permute-start | bytes 983048 | tf_op jit(solution)/shard_map/ppermute | solution.py:335
  13.3 1.4 %collective-permute-start.3 = (bf16[256,640]{1,0:T(8,128)(2,1)S(1)}, bf16[256,640]{1,0:T(8,128)(2,1)S(1)}, u32[]{:S(2)}, u32[]{:S(2)}) collective-permute-start(bf16[256,640]{1,0:T(8,128)(2,1)S(1)} %get-tuple-element.31.refs_3_), channel_id=1, source_target_pairs={{0,192},{64,0},{128,64},{192,128},{1,193},{65,1},{129,65},{193,129... | collective-permute-start | bytes 983048 | tf_op jit(solution)/shard_map/ppermute | solution.py:335
  14.8 1.6 %collective-permute-start.4 = (bf16[256,640]{1,0:T(8,128)(2,1)S(1)}, bf16[256,640]{1,0:T(8,128)(2,1)S(1)}, u32[]{:S(2)}, u32[]{:S(2)}) collective-permute-start(bf16[256,640]{1,0:T(8,128)(2,1)S(1)} %get-tuple-element.31.refs_3_), channel_id=1, source_target_pairs={{0,128},{64,192},{128,0},{192,64},{1,129},{65,193},{129,1},{193,65... | collective-permute-start | bytes 983048 | tf_op jit(solution)/shard_map/ppermute | solution.py:335
  16.4 0.0 all-to-all-done
  16.4 2.1 %collective-permute-start = (bf16[64,3072]{1,0:T(8,128)(2,1)S(1)}, bf16[64,3072]{1,0:T(8,128)(2,1)S(1)}, u32[]{:S(2)}, u32[]{:S(2)}) collective-permute-start(bf16[64,3072]{1,0:T(8,128)(2,1)S(1)} %bitcast.15), channel_id=1, source_target_pairs={{0,4},{4,0},{1,5},{5,1},{2,6},{6,2},{3,7},{7,3},{8,12},{12,8},{9,1... | collective-permute-start | bytes 1179656 | tf_op jit(solution)/shard_map/ppermute | solution.py:341
  18.5 7.0 %collective-permute-done.1.refs_3_ = bf16[256,640]{1,0:T(8,128)(2,1)S(1)} collective-permute-done((bf16[256,640]{1,0:T(8,128)(2,1)S(1)}, bf16[256,640]{1,0:T(8,128)(2,1)S(1)}, u32[]{:S(2)}, u32[]{:S(2)}) %collective-permute-start.1) | collective-permute-done | bytes 327712 | tf_op jit(solution)/shard_map/ppermute | solution.py:334
  25.5 0.0 collective-permute-done.2.refs_4_
  25.5 0.0 collective-permute-done.3.refs_5_
  25.5 4.0 %collective-permute-done.4.refs_6_ = bf16[256,640]{1,0:T(8,128)(2,1)S(1)} collective-permute-done((bf16[256,640]{1,0:T(8,128)(2,1)S(1)}, bf16[256,640]{1,0:T(8,128)(2,1)S(1)}, u32[]{:S(2)}, u32[]{:S(2)}) %collective-permute-start.4) | collective-permute-done | bytes 327712 | tf_op jit(solution)/shard_map/ppermute | solution.py:335
  29.5 0.6 collective-permute-start.5
  30.1 2.1 %collective-permute-start.6 = (bf16[256,640]{1,0:T(8,128)(2,1)S(1)}, bf16[256,640]{1,0:T(8,128)(2,1)S(1)}, u32[]{:S(2)}, u32[]{:S(2)}) collective-permute-start(bf16[256,640]{1,0:T(8,128)(2,1)S(1)} %collective-permute-done.1.refs_3_), channel_id=1, source_target_pairs={{0,192},{64,0},{128,64},{192,128},{1,193},{65,1},{129,65},{193,129... | collective-permute-start | bytes 983048 | tf_op jit(solution)/shard_map/ppermute | solution.py:339
  32.2 0.0 collective-permute-start.7
  32.8 0.0 copy-start
  32.8 0.0 collective-permute-done.refs_1_
  32.9 2.5 %shard_map.92.refs_0_ = bf16[2048,768]{1,0:T(8,128)(2,1)S(1)} custom-call(bf16[64,3072]{1,0:T(8,128)(2,1)S(1)} %bitcast.16, bf16[64,3072]{1,0:T(8,128)(2,1)S(1)} %collective-permute-done.refs_1_, bf16[16,128,512]{2,1,0:T(8,128)(2,1)} %refs_2_.3), custom_call_target="tpu_custom_call" | custom-call | flops 1 | bytes 1 | tf_op jit(solution)/shard_map/pallas_call | solution.py:133
  35.4 7.7 %shard_map.93 = (f32[128,2048]{1,0:T(8,128)S(1)}, f32[2048,128]{1,0:T(8,128)S(1)}) custom-call(bf16[2048,768]{1,0:T(8,128)(2,1)S(1)} %shard_map.92.refs_0_, f32[8,128]{1,0:T(8,128)S(1)} %broadcast_in_dim.16.refs_1_, bf16[16,512,128]{2,1,0:T(8,128)(2,1)S(1)} %copy-done, bf16[256,640]{1,0:T(8,128)(2,1)S(1)} %get-tuple-element.31.refs_3_, ...), custom_call_target="tpu_custom_call" | custom-call | flops 1 | bytes 1 | tf_op jit(solution)/shard_map/pallas_call | solution.py:239
  43.0 0.0 collective-permute-done.5.refs_4_
  43.0 0.0 collective-permute-done.6.refs_5_
  43.1 0.7 collective-permute-done.7.refs_6_
  43.8 8.2 %shard_map.94 = (bf16[64,2176]{1,0:T(8,128)(2,1)S(1)}, bf16[64,2176]{1,0:T(8,128)(2,1)S(1)}) custom-call(bf16[2048,768]{1,0:T(8,128)(2,1)S(1)} %shard_map.92.refs_0_, f32[8,128]{1,0:T(8,128)S(1)} %broadcast_in_dim.16.refs_1_, bf16[16,512,128]{2,1,0:T(8,128)(2,1)S(1)} %copy-done, bf16[256,640]{1,0:T(8,128)(2,1)S(1)} %collective-permute-done.1.refs_3_, ...), custom_call_target="tpu_custom_call" | custom-call | flops 1 | bytes 1 | tf_op jit(solution)/shard_map/pallas_call | solution.py:239
  52.0 0.0 copy-start.1
  52.0 4.2 %collective-permute-start.8 = (bf16[64,2176]{1,0:T(8,128)(2,1)S(1)}, bf16[64,2176]{1,0:T(8,128)(2,1)S(1)}, u32[]{:S(2)}, u32[]{:S(2)}) collective-permute-start(bf16[64,2176]{1,0:T(8,128)(2,1)S(1)} %get-tuple-element.45), channel_id=1, source_target_pairs={{0,4},{4,0},{1,5},{5,1},{2,6},{6,2},{3,7},{7,3},{8,12},{12,8},{9,1... | collective-permute-start | bytes 835592 | tf_op jit(solution)/shard_map/ppermute | solution.py:361
  56.2 1.2 collective-permute-done.8.b_ref
  57.4 0.8 shard_map.95
  58.2 2.8 %collective-permute-start.10 = (bf16[16,2176]{1,0:T(8,128)(2,1)S(1)}, bf16[16,2176]{1,0:T(8,128)(2,1)S(1)}, u32[]{:S(2)}, u32[]{:S(2)}) collective-permute-start(bf16[16,2176]{1,0:T(8,128)(2,1)S(1)} %get-tuple-element.48), channel_id=1, source_target_pairs={{0,32},{16,48},{32,0},{48,16},{1,33},{17,49},{33,1},{49,17},{2,34}... | collective-permute-start | bytes 208904 | tf_op jit(solution)/shard_map/ppermute | solution.py:362
  61.0 0.9 collective-permute-start.11
  61.9 0.6 collective-permute-start.9
  62.4 0.5 collective-permute-done.10.refs_2_
  62.9 1.9 %collective-permute-done.11.refs_3_ = bf16[16,2176]{1,0:T(8,128)(2,1)S(1)} collective-permute-done((bf16[16,2176]{1,0:T(8,128)(2,1)S(1)}, bf16[16,2176]{1,0:T(8,128)(2,1)S(1)}, u32[]{:S(2)}, u32[]{:S(2)}) %collective-permute-start.11) | collective-permute-done | bytes 69664 | tf_op jit(solution)/shard_map/ppermute | solution.py:362
  64.8 1.4 %collective-permute-done.9.refs_1_ = bf16[16,2176]{1,0:T(8,128)(2,1)S(1)} collective-permute-done((bf16[16,2176]{1,0:T(8,128)(2,1)S(1)}, bf16[16,2176]{1,0:T(8,128)(2,1)S(1)}, u32[]{:S(2)}, u32[]{:S(2)}) %collective-permute-start.9) | collective-permute-done | bytes 69664 | tf_op jit(solution)/shard_map/ppermute | solution.py:362
  66.2 1.4 %shard_map.96 = bf16[16,16,2048]{2,1,0:T(8,128)(2,1)} custom-call(bf16[16,2176]{1,0:T(8,128)(2,1)S(1)} %get-tuple-element.46.refs_0_, bf16[16,2176]{1,0:T(8,128)(2,1)S(1)} %collective-permute-done.9.refs_1_, bf16[16,2176]{1,0:T(8,128)(2,1)S(1)} %collective-permute-done.10.refs_2_, bf16[16,2176]{1,0:T(8,128)(2,1)S(1)} %collective-permute-done.11.refs_3_), custom_call_target="tpu_custom_call" | custom-call | flops 1 | bytes 1 | tf_op jit(solution)/shard_map/pallas_call | solution.py:364
  67.7 5.2 %all-to-all-start.1 = ((bf16[16,16,2048]{2,1,0:T(8,128)(2,1)}), bf16[16,16,2048]{2,1,0:T(8,128)(2,1)S(1)}, u32[]{:S(2)}, u32[]{:S(2)}) async-start(bf16[16,16,2048]{2,1,0:T(8,128)(2,1)} %shard_map.96), calls=%async_computation.1 | async-start | bytes 2097152 | tf_op jit(solution)/shard_map/all_to_all | solution.py:370
  72.8 0.0 copy-done.1
  72.8 1.4 %collective-permute-start.12 = (bf16[112,2048]{1,0:T(8,128)(2,1)S(1)}, bf16[112,2048]{1,0:T(8,128)(2,1)S(1)}, u32[]{:S(2)}, u32[]{:S(2)}) collective-permute-start(bf16[112,2048]{1,0:T(8,128)(2,1)S(1)} %bitcast.19), channel_id=1, source_target_pairs={{0,8},{8,0},{1,9},{9,1},{2,10},{10,2},{3,11},{11,3},{4,12},{12,4},... | collective-permute-start | bytes 1376264 | tf_op jit(solution)/shard_map/ppermute | solution.py:342
  74.3 23.4 %collective-permute-done.12.refs_1_ = bf16[112,2048]{1,0:T(8,128)(2,1)S(1)} collective-permute-done((bf16[112,2048]{1,0:T(8,128)(2,1)S(1)}, bf16[112,2048]{1,0:T(8,128)(2,1)S(1)}, u32[]{:S(2)}, u32[]{:S(2)}) %collective-permute-start.12) | collective-permute-done | bytes 458784 | tf_op jit(solution)/shard_map/ppermute | solution.py:342
  97.7 1.9 %collective-permute-start.14 = (bf16[112,2048]{1,0:T(8,128)(2,1)S(1)}, bf16[112,2048]{1,0:T(8,128)(2,1)S(1)}, u32[]{:S(2)}, u32[]{:S(2)}) collective-permute-start(bf16[112,2048]{1,0:T(8,128)(2,1)S(1)} %collective-permute-done.12.refs_1_), channel_id=1, source_target_pairs={{0,4},{4,0},{1,5},{5,1},{2,6},{6,2},{3,7},{7,3},{8,12},{12,8},{9,1... | collective-permute-start | bytes 1376264 | tf_op jit(solution)/shard_map/ppermute | solution.py:363
  99.6 0.0 collective-permute-start.13
  99.6 0.1 pad_add_fusion.zc_ref
  99.7 1.4 %collective-permute-done.14.refs_3_ = bf16[112,2048]{1,0:T(8,128)(2,1)S(1)} collective-permute-done((bf16[112,2048]{1,0:T(8,128)(2,1)S(1)}, bf16[112,2048]{1,0:T(8,128)(2,1)S(1)}, u32[]{:S(2)}, u32[]{:S(2)}) %collective-permute-start.14) | collective-permute-done | bytes 458784 | tf_op jit(solution)/shard_map/ppermute | solution.py:363
  101.0 0.7 collective-permute-done.13.refs_2_
  101.7 2.4 %shard_map.97.w_ref = bf16[4,2048,128]{2,1,0:T(8,128)(2,1)S(1)} custom-call(s32[2]{0:T(128)S(1)} %pad_add_fusion.zc_ref, bf16[112,2048]{1,0:T(8,128)(2,1)} %bitcast.18, bf16[112,2048]{1,0:T(8,128)(2,1)S(1)} %collective-permute-done.12.refs_1_, bf16[112,2048]{1,0:T(8,128)(2,1)S(1)} %collective-permute-done.13.refs_2_, ...), custom_call_target="tpu_custom_call" | custom-call | flops 1 | bytes 1 | tf_op jit(solution)/shard_map/pallas_call | solution.py:301
  104.1 0.0 all-to-all-done.1
  104.1 1.2 %shard_map.98 = bf16[4,256,112]{2,1,0:T(8,128)(2,1)S(1)} custom-call(bf16[256,2048]{1,0:T(8,128)(2,1)S(1)} %bitcast.14, bf16[4,2048,128]{2,1,0:T(8,128)(2,1)S(1)} %shard_map.97.w_ref), custom_call_target="tpu_custom_call" | custom-call | flops 1 | bytes 1 | tf_op jit(solution)/shard_map/pallas_call | solution.py:373
  105.4 14.4 %all_to_all.15.sums_ref = bf16[16,64,112]{2,1,0:T(8,128)(2,1)S(1)} all-to-all(bf16[16,64,112]{2,1,0:T(8,128)(2,1)S(1)} %bitcast.17), channel_id=1, replica_groups=mesh['y'=4,'x'=4,'z'=2,'c'=2,'head'=4] {'z','c','head'}, dimensions={0} | all-to-all | bytes 458752 | tf_op jit(solution)/shard_map/all_to_all | solution.py:376
  119.7 0.7 shard_map.99
  (3 shorter events, 0.0 us)
Async XLA Ops:
  2.0 14.4 %all-to-all-start = ((bf16[4,16,3072]{2,1,0:T(8,128)(2,1)}), bf16[4,16,3072]{2,1,0:T(8,128)(2,1)S(1)}, u32[]{:S(2)}, u32[]{:S(2)}) async-start(bf16[4,16,3072]{2,1,0:T(8,128)(2,1)} %get-tuple-element.29), calls=%async_computation | async-start | bytes 786432 | tf_op jit(solution)/shard_map/all_to_all | solution.py:336
  6.0 19.5 %collective-permute-start.1 = (bf16[256,640]{1,0:T(8,128)(2,1)S(1)}, bf16[256,640]{1,0:T(8,128)(2,1)S(1)}, u32[]{:S(2)}, u32[]{:S(2)}) collective-permute-start(bf16[256,640]{1,0:T(8,128)(2,1)S(1)} %get-tuple-element.31.refs_3_), channel_id=1, source_target_pairs={{0,8},{8,0},{1,9},{9,1},{2,10},{10,2},{3,11},{11,3},{4,12},{12,4},... | collective-permute-start | bytes 983048 | tf_op jit(solution)/shard_map/ppermute | solution.py:334
  12.0 13.5 %collective-permute-start.2 = (bf16[256,640]{1,0:T(8,128)(2,1)S(1)}, bf16[256,640]{1,0:T(8,128)(2,1)S(1)}, u32[]{:S(2)}, u32[]{:S(2)}) collective-permute-start(bf16[256,640]{1,0:T(8,128)(2,1)S(1)} %get-tuple-element.31.refs_3_), channel_id=1, source_target_pairs={{0,64},{64,128},{128,192},{192,0},{1,65},{65,129},{129,193},{193,1... | collective-permute-start | bytes 983048 | tf_op jit(solution)/shard_map/ppermute | solution.py:335
  13.3 12.2 %collective-permute-start.3 = (bf16[256,640]{1,0:T(8,128)(2,1)S(1)}, bf16[256,640]{1,0:T(8,128)(2,1)S(1)}, u32[]{:S(2)}, u32[]{:S(2)}) collective-permute-start(bf16[256,640]{1,0:T(8,128)(2,1)S(1)} %get-tuple-element.31.refs_3_), channel_id=1, source_target_pairs={{0,192},{64,0},{128,64},{192,128},{1,193},{65,1},{129,65},{193,129... | collective-permute-start | bytes 983048 | tf_op jit(solution)/shard_map/ppermute | solution.py:335
  14.8 14.7 %collective-permute-start.4 = (bf16[256,640]{1,0:T(8,128)(2,1)S(1)}, bf16[256,640]{1,0:T(8,128)(2,1)S(1)}, u32[]{:S(2)}, u32[]{:S(2)}) collective-permute-start(bf16[256,640]{1,0:T(8,128)(2,1)S(1)} %get-tuple-element.31.refs_3_), channel_id=1, source_target_pairs={{0,128},{64,192},{128,0},{192,64},{1,129},{65,193},{129,1},{193,65... | collective-permute-start | bytes 983048 | tf_op jit(solution)/shard_map/ppermute | solution.py:335
  16.4 16.4 %collective-permute-start = (bf16[64,3072]{1,0:T(8,128)(2,1)S(1)}, bf16[64,3072]{1,0:T(8,128)(2,1)S(1)}, u32[]{:S(2)}, u32[]{:S(2)}) collective-permute-start(bf16[64,3072]{1,0:T(8,128)(2,1)S(1)} %bitcast.15), channel_id=1, source_target_pairs={{0,4},{4,0},{1,5},{5,1},{2,6},{6,2},{3,7},{7,3},{8,12},{12,8},{9,1... | collective-permute-start | bytes 1179656 | tf_op jit(solution)/shard_map/ppermute | solution.py:341
  29.5 13.6 %collective-permute-start.5 = (bf16[256,640]{1,0:T(8,128)(2,1)S(1)}, bf16[256,640]{1,0:T(8,128)(2,1)S(1)}, u32[]{:S(2)}, u32[]{:S(2)}) collective-permute-start(bf16[256,640]{1,0:T(8,128)(2,1)S(1)} %collective-permute-done.1.refs_3_), channel_id=1, source_target_pairs={{0,64},{64,128},{128,192},{192,0},{1,65},{65,129},{129,193},{193,1... | collective-permute-start | bytes 983048 | tf_op jit(solution)/shard_map/ppermute | solution.py:339
  30.1 13.0 %collective-permute-start.6 = (bf16[256,640]{1,0:T(8,128)(2,1)S(1)}, bf16[256,640]{1,0:T(8,128)(2,1)S(1)}, u32[]{:S(2)}, u32[]{:S(2)}) collective-permute-start(bf16[256,640]{1,0:T(8,128)(2,1)S(1)} %collective-permute-done.1.refs_3_), channel_id=1, source_target_pairs={{0,192},{64,0},{128,64},{192,128},{1,193},{65,1},{129,65},{193,129... | collective-permute-start | bytes 983048 | tf_op jit(solution)/shard_map/ppermute | solution.py:339
  32.2 11.6 %collective-permute-start.7 = (bf16[256,640]{1,0:T(8,128)(2,1)S(1)}, bf16[256,640]{1,0:T(8,128)(2,1)S(1)}, u32[]{:S(2)}, u32[]{:S(2)}) collective-permute-start(bf16[256,640]{1,0:T(8,128)(2,1)S(1)} %collective-permute-done.1.refs_3_), channel_id=1, source_target_pairs={{0,128},{64,192},{128,0},{192,64},{1,129},{65,193},{129,1},{193,65... | collective-permute-start | bytes 983048 | tf_op jit(solution)/shard_map/ppermute | solution.py:339
  32.8 2.5 %copy-start = (bf16[16,512,128]{2,1,0:T(8,128)(2,1)S(1)}, bf16[16,512,128]{2,1,0:T(8,128)(2,1)}, u32[]{:S(2)}) copy-start(bf16[16,512,128]{2,1,0:T(8,128)(2,1)} %refs_2_.5) | copy-start | bytes 6291460
  52.0 20.8 %copy-start.1 = (bf16[2048,112]{0,1:T(8,128)(2,1)S(1)}, bf16[2048,112]{0,1:T(8,128)(2,1)}, u32[]{:S(2)}) copy-start(bf16[2048,112]{0,1:T(8,128)(2,1)} %param.17) | copy-start | bytes 1376260
  52.0 5.4 %collective-permute-start.8 = (bf16[64,2176]{1,0:T(8,128)(2,1)S(1)}, bf16[64,2176]{1,0:T(8,128)(2,1)S(1)}, u32[]{:S(2)}, u32[]{:S(2)}) collective-permute-start(bf16[64,2176]{1,0:T(8,128)(2,1)S(1)} %get-tuple-element.45), channel_id=1, source_target_pairs={{0,4},{4,0},{1,5},{5,1},{2,6},{6,2},{3,7},{7,3},{8,12},{12,8},{9,1... | collective-permute-start | bytes 835592 | tf_op jit(solution)/shard_map/ppermute | solution.py:361
  58.2 4.8 %collective-permute-start.10 = (bf16[16,2176]{1,0:T(8,128)(2,1)S(1)}, bf16[16,2176]{1,0:T(8,128)(2,1)S(1)}, u32[]{:S(2)}, u32[]{:S(2)}) collective-permute-start(bf16[16,2176]{1,0:T(8,128)(2,1)S(1)} %get-tuple-element.48), channel_id=1, source_target_pairs={{0,32},{16,48},{32,0},{48,16},{1,33},{17,49},{33,1},{49,17},{2,34}... | collective-permute-start | bytes 208904 | tf_op jit(solution)/shard_map/ppermute | solution.py:362
  61.0 3.9 %collective-permute-start.11 = (bf16[16,2176]{1,0:T(8,128)(2,1)S(1)}, bf16[16,2176]{1,0:T(8,128)(2,1)S(1)}, u32[]{:S(2)}, u32[]{:S(2)}) collective-permute-start(bf16[16,2176]{1,0:T(8,128)(2,1)S(1)} %get-tuple-element.49), channel_id=1, source_target_pairs={{0,48},{16,0},{32,16},{48,32},{1,49},{17,1},{33,17},{49,33},{2,50}... | collective-permute-start | bytes 208904 | tf_op jit(solution)/shard_map/ppermute | solution.py:362
  61.9 4.4 %collective-permute-start.9 = (bf16[16,2176]{1,0:T(8,128)(2,1)S(1)}, bf16[16,2176]{1,0:T(8,128)(2,1)S(1)}, u32[]{:S(2)}, u32[]{:S(2)}) collective-permute-start(bf16[16,2176]{1,0:T(8,128)(2,1)S(1)} %get-tuple-element.47), channel_id=1, source_target_pairs={{0,16},{16,32},{32,48},{48,0},{1,17},{17,33},{33,49},{49,1},{2,18}... | collective-permute-start | bytes 208904 | tf_op jit(solution)/shard_map/ppermute | solution.py:362
  67.7 36.5 %all-to-all-start.1 = ((bf16[16,16,2048]{2,1,0:T(8,128)(2,1)}), bf16[16,16,2048]{2,1,0:T(8,128)(2,1)S(1)}, u32[]{:S(2)}, u32[]{:S(2)}) async-start(bf16[16,16,2048]{2,1,0:T(8,128)(2,1)} %shard_map.96), calls=%async_computation.1 | async-start | bytes 2097152 | tf_op jit(solution)/shard_map/all_to_all | solution.py:370
  72.8 24.8 %collective-permute-start.12 = (bf16[112,2048]{1,0:T(8,128)(2,1)S(1)}, bf16[112,2048]{1,0:T(8,128)(2,1)S(1)}, u32[]{:S(2)}, u32[]{:S(2)}) collective-permute-start(bf16[112,2048]{1,0:T(8,128)(2,1)S(1)} %bitcast.19), channel_id=1, source_target_pairs={{0,8},{8,0},{1,9},{9,1},{2,10},{10,2},{3,11},{11,3},{4,12},{12,4},... | collective-permute-start | bytes 1376264 | tf_op jit(solution)/shard_map/ppermute | solution.py:342
  97.7 3.4 %collective-permute-start.14 = (bf16[112,2048]{1,0:T(8,128)(2,1)S(1)}, bf16[112,2048]{1,0:T(8,128)(2,1)S(1)}, u32[]{:S(2)}, u32[]{:S(2)}) collective-permute-start(bf16[112,2048]{1,0:T(8,128)(2,1)S(1)} %collective-permute-done.12.refs_1_), channel_id=1, source_target_pairs={{0,4},{4,0},{1,5},{5,1},{2,6},{6,2},{3,7},{7,3},{8,12},{12,8},{9,1... | collective-permute-start | bytes 1376264 | tf_op jit(solution)/shard_map/ppermute | solution.py:363
  99.6 2.1 %collective-permute-start.13 = (bf16[112,2048]{1,0:T(8,128)(2,1)S(1)}, bf16[112,2048]{1,0:T(8,128)(2,1)S(1)}, u32[]{:S(2)}, u32[]{:S(2)}) collective-permute-start(bf16[112,2048]{1,0:T(8,128)(2,1)S(1)} %bitcast.20), channel_id=1, source_target_pairs={{0,4},{4,0},{1,5},{5,1},{2,6},{6,2},{3,7},{7,3},{8,12},{12,8},{9,1... | collective-permute-start | bytes 1376264 | tf_op jit(solution)/shard_map/ppermute | solution.py:369

commit v12 on v9

--- a/solution.py
+++ b/solution.py
@@ -125,17 +125,19 @@
         return jnp.concatenate([ref[:, start : start + 128] for ref in q_refs], axis=0)
 
     for h in range(HG):
-        if h % step == 0:
-            copies[h // step].wait()
         rows = slice(h * ROWS, (h + 1) * ROWS)
-        latent = jnp.dot(columns(h * NOPE), w_ref[h], preferred_element_type=jnp.float32)
-        out_ref[rows, :RANK] = latent.astype(jnp.bfloat16)
         pair = columns(HG * NOPE + (h // 2) * 128).astype(jnp.float32)
         if h % 2:
             pair = pltpu.roll(pair, ROPE, 1)
         rope = jnp.where(lane < ROPE, pair, 0.0)
         out_ref[rows, RANK : RANK + 128] = rope.astype(jnp.bfloat16)
         out_ref[rows, RANK + 128 :] = one_hot
+    for h in range(HG):
+        if h % step == 0:
+            copies[h // step].wait()
+        rows = slice(h * ROWS, (h + 1) * ROWS)
+        latent = jnp.dot(columns(h * NOPE), w_ref[h], preferred_element_type=jnp.float32)
+        out_ref[rows, :RANK] = latent.astype(jnp.bfloat16)
 
 
 def absorb(queries, w_uk):
@@ -232,7 +234,7 @@
         send_ref[:, HG * VDIM :] = packed[half:]
 
 
-def attend(q, qpos, value_weight, pieces, earlier=None, tile=512, unroll=4):
+def attend(q, qpos, value_weight, pieces, earlier=None, tile=1024, unroll=2):
     n, keys = len(pieces), sum(piece.shape[0] for piece in pieces)
     last = earlier is not None
     scratch = [pltpu.VMEM((keys, ITEMW), jnp.bfloat16)]
@@ -285,41 +287,43 @@
             refs[-1][i, :, cols] = head
 
 
-def columns_kernel(zc_ref, *refs):
+def columns_kernel(zc_ref, own_ref, *refs):
     z, c = zc_ref[0], zc_ref[1]
-    w_refs, (out_ref, held, sems) = refs[:4], refs[4:]
-    ncol, depth = w_refs[0].shape
-    copies = [pltpu.make_async_copy(w_refs[k], held.at[k], sems.at[k]) for k in range(4)]
-    for copy in copies:
-        copy.start()
-    for k in range(4):
+    w_refs, (out_ref, held, sem) = refs[:3], refs[3:]
+    ncol, depth = held.shape
+    copy = pltpu.make_async_copy(own_ref, held, sem)
+    copy.start()
+    for k in (1, 2, 3, 0):
         to_z = z if k % 2 == 0 else 1 - z
         to_c = c if k < 2 else 1 - c
-        copies[k].wait()
-        padded = jnp.concatenate(
-            [held[k], jnp.zeros((128 - ncol, depth), jnp.bfloat16)], axis=0
-        )
-        out_ref[to_z * 2 + to_c] = jnp.transpose(padded)
+        if k == 0:
+            copy.wait()
+        piece = held[...] if k == 0 else w_refs[k - 1][...]
+        padded = jnp.concatenate([piece, jnp.zeros((128 - ncol, depth), jnp.bfloat16)], axis=0)
+        lanes = pl.ds(pl.multiple_of((to_z * 2 + to_c) * 128, 128), 128)
+        out_ref[:, lanes] = jnp.transpose(padded)
 
 
 def columns_of(zc, pieces):
     ncol, depth = pieces[0].shape
     return call(
         columns_kernel,
-        jax.ShapeDtypeStruct((4, depth, 128), jnp.bfloat16),
+        jax.ShapeDtypeStruct((depth, 4 * 128), jnp.bfloat16),
         vmem=16,
-        in_specs=[pl.BlockSpec(memory_space=pltpu.SMEM)] + [HBM] * 4,
+        in_specs=[pl.BlockSpec(memory_space=pltpu.SMEM), HBM]
+        + [pl.BlockSpec(memory_space=pltpu.VMEM)] * 3,
         scratch_shapes=[
-            pltpu.VMEM((4, ncol, depth), jnp.bfloat16),
-            pltpu.SemaphoreType.DMA((4,)),
+            pltpu.VMEM((ncol, depth), jnp.bfloat16),
+            pltpu.SemaphoreType.DMA,
         ],
     )(zc, *in_hbm(pieces[0]), *pieces[1:])
 
 
 def project_kernel(x_ref, w_ref, out_ref):
+    ncol = out_ref.shape[2]
+    out = jnp.dot(x_ref[...], w_ref[...], preferred_element_type=jnp.float32)
     for k in range(4):
-        out = jnp.dot(x_ref[...], w_ref[k], preferred_element_type=jnp.float32)
-        out_ref[k] = out[:, : out_ref.shape[2]].astype(jnp.bfloat16)
+        out_ref[k] = out[:, k * 128 : k * 128 + ncol].astype(jnp.bfloat16)
 
 
 def finish_kernel(sums_ref, out_ref, row_ref):

time: 107 us -> 106 us (level)
  Pallas kernels: 26.7 us -> 25.4 us
  transfers between devices with their start and end apart: 19 -> 19, of which waited for: 6 -> 6; matrix products, arithmetic and copies ran while one was open for 0% -> 0% of each run, Pallas kernels for 21% -> 20%
where the time goes in v12:
time: 106 us; the launch traced here: 105 us
  starting transfers between devices  39.6 us (37%)
  Pallas kernels  25.4 us (24%)
  waiting for transfers between devices  18.6 us (18%)
  blocking collectives  18.1 us (17%)
  local copies, waits for them, and re-layouts  2.85 us (3%)
    all_to_all x1, blocking collectives, local(): lax.all_to_all(sums.reshape(16, 4 * R, ncol), ('z', 'c', 'head'), 0, 0, t...  18.1 us
    pallas_call x2, Pallas kernels, attend(): call(functools.partial(attend_kernel, n, last, tile, unroll), out_shape,...  16.4 us
    all_to_all x1, waiting for transfers between devices, local(): lax.all_to_all(heads, ('y', 'x'), 0, 0, tiled=True)  7.08 us
    ppermute x1, starting transfers between devices, local(): z_keys = lax.ppermute(keys, 'z', SWAP)  6.1 us
    ppermute x3, starting transfers between devices, local(): up, down, across = (lax.ppermute(keys, 'y', shift(d)) for d in (1, 3, 2))  5.21 us
    ppermute x3, starting transfers between devices, local(): far = [z_keys] + [lax.ppermute(z_keys, 'y', shift(d)) for d in RING[1:]]  4.67 us
    ppermute x3, starting transfers between devices, local(): lax.ppermute(part, 'x', shift(-d % 4))  4.28 us
    ppermute x3, waiting for transfers between devices, local(): lax.ppermute(part, 'x', shift(-d % 4))  3.84 us
  transfers between devices with their start and end apart: 19, of which 6 were waited for; matrix products, arithmetic and copies ran while one was open for 0% of the time, Pallas kernels for 20%

profile of v12, /device:TPU:33, one launch (start us, length us, event | category | flops | bytes accessed | tf_op | source)
XLA Modules:
  0.0 105.5 jit_solution(7786598809825331162)
XLA Ops:
  0.0 1.0 shard_map.100
  1.0 6.1 %collective-permute-start.4 = (bf16[256,640]{1,0:T(8,128)(2,1)S(1)}, bf16[256,640]{1,0:T(8,128)(2,1)S(1)}, u32[]{:S(2)}, u32[]{:S(2)}) collective-permute-start(bf16[256,640]{1,0:T(8,128)(2,1)S(1)} %get-tuple-element.42.refs_3_), channel_id=1, source_target_pairs={{0,8},{8,0},{1,9},{9,1},{2,10},{10,2},{3,11},{11,3},{4,12},{12,4},... | collective-permute-start | bytes 983048 | tf_op jit(solution)/shard_map/ppermute | solution.py:344
  7.1 1.2 %collective-permute-start = (bf16[16,3072]{1,0:T(8,128)(2,1)S(1)}, bf16[16,3072]{1,0:T(8,128)(2,1)S(1)}, u32[]{:S(2)}, u32[]{:S(2)}) collective-permute-start(bf16[16,3072]{1,0:T(8,128)(2,1)S(1)} %get-tuple-element.38.refs_0_), channel_id=1, source_target_pairs={{0,16},{16,32},{32,48},{48,0},{1,17},{17,33},{33,49},{49,1},{2,18}... | collective-permute-start | bytes 294920 | tf_op jit(solution)/shard_map/ppermute | solution.py:346
  8.3 1.5 %collective-permute-start.1 = (bf16[16,3072]{1,0:T(8,128)(2,1)S(1)}, bf16[16,3072]{1,0:T(8,128)(2,1)S(1)}, u32[]{:S(2)}, u32[]{:S(2)}) collective-permute-start(bf16[16,3072]{1,0:T(8,128)(2,1)S(1)} %get-tuple-element.38.refs_0_), channel_id=1, source_target_pairs={{0,48},{16,0},{32,16},{48,32},{1,49},{17,1},{33,17},{49,33},{2,50}... | collective-permute-start | bytes 294920 | tf_op jit(solution)/shard_map/ppermute | solution.py:346
  9.8 1.3 %collective-permute-start.5 = (bf16[256,640]{1,0:T(8,128)(2,1)S(1)}, bf16[256,640]{1,0:T(8,128)(2,1)S(1)}, u32[]{:S(2)}, u32[]{:S(2)}) collective-permute-start(bf16[256,640]{1,0:T(8,128)(2,1)S(1)} %get-tuple-element.42.refs_3_), channel_id=1, source_target_pairs={{0,64},{64,128},{128,192},{192,0},{1,65},{65,129},{129,193},{193,1... | collective-permute-start | bytes 983048 | tf_op jit(solution)/shard_map/ppermute | solution.py:345
  11.1 1.4 %collective-permute-start.6 = (bf16[256,640]{1,0:T(8,128)(2,1)S(1)}, bf16[256,640]{1,0:T(8,128)(2,1)S(1)}, u32[]{:S(2)}, u32[]{:S(2)}) collective-permute-start(bf16[256,640]{1,0:T(8,128)(2,1)S(1)} %get-tuple-element.42.refs_3_), channel_id=1, source_target_pairs={{0,192},{64,0},{128,64},{192,128},{1,193},{65,1},{129,65},{193,129... | collective-permute-start | bytes 983048 | tf_op jit(solution)/shard_map/ppermute | solution.py:345
  12.6 0.0 collective-permute-done.refs_1_
  12.6 2.5 %collective-permute-start.7 = (bf16[256,640]{1,0:T(8,128)(2,1)S(1)}, bf16[256,640]{1,0:T(8,128)(2,1)S(1)}, u32[]{:S(2)}, u32[]{:S(2)}) collective-permute-start(bf16[256,640]{1,0:T(8,128)(2,1)S(1)} %get-tuple-element.42.refs_3_), channel_id=1, source_target_pairs={{0,128},{64,192},{128,0},{192,64},{1,129},{65,193},{129,1},{193,65... | collective-permute-start | bytes 983048 | tf_op jit(solution)/shard_map/ppermute | solution.py:345
  15.0 1.5 %collective-permute-start.2 = (bf16[16,3072]{1,0:T(8,128)(2,1)S(1)}, bf16[16,3072]{1,0:T(8,128)(2,1)S(1)}, u32[]{:S(2)}, u32[]{:S(2)}) collective-permute-start(bf16[16,3072]{1,0:T(8,128)(2,1)S(1)} %get-tuple-element.38.refs_0_), channel_id=1, source_target_pairs={{0,32},{16,48},{32,0},{48,16},{1,33},{17,49},{33,1},{49,17},{2,34}... | collective-permute-start | bytes 294920 | tf_op jit(solution)/shard_map/ppermute | solution.py:348
  16.6 3.7 %collective-permute-done.2.refs_3_ = bf16[16,3072]{1,0:T(8,128)(2,1)S(1)} collective-permute-done((bf16[16,3072]{1,0:T(8,128)(2,1)S(1)}, bf16[16,3072]{1,0:T(8,128)(2,1)S(1)}, u32[]{:S(2)}, u32[]{:S(2)}) %collective-permute-start.2) | collective-permute-done | bytes 98336 | tf_op jit(solution)/shard_map/ppermute | solution.py:348
  20.3 3.0 %collective-permute-start.3 = (bf16[64,3072]{1,0:T(8,128)(2,1)S(1)}, bf16[64,3072]{1,0:T(8,128)(2,1)S(1)}, u32[]{:S(2)}, u32[]{:S(2)}) collective-permute-start(bf16[64,3072]{1,0:T(8,128)(2,1)S(1)} %shard_map.101.refs_0_), channel_id=1, source_target_pairs={{0,4},{4,0},{1,5},{5,1},{2,6},{6,2},{3,7},{7,3},{8,12},{12,8},{9,1... | collective-permute-start | bytes 1179656 | tf_op jit(solution)/shard_map/ppermute | solution.py:353
  23.4 0.0 collective-permute-done.4.refs_3_
  23.4 2.6 %collective-permute-start.11 = (bf16[112,2048]{1,0:T(8,128)(2,1)}, bf16[112,2048]{1,0:T(8,128)(2,1)S(1)}, u32[]{:S(2)}, u32[]{:S(2)}) collective-permute-start(bf16[112,2048]{1,0:T(8,128)(2,1)} %bitcast.20), channel_id=1, source_target_pairs={{0,8},{8,0},{1,9},{9,1},{2,10},{10,2},{3,11},{11,3},{4,12},{12,4},... | collective-permute-start | bytes 1376264 | tf_op jit(solution)/shard_map/ppermute | solution.py:354
  25.9 0.0 collective-permute-done.5.refs_4_
  26.0 0.0 collective-permute-done.6.refs_5_
  26.0 1.0 collective-permute-done.7.refs_6_
  27.0 2.0 %collective-permute-start.10 = (bf16[256,640]{1,0:T(8,128)(2,1)S(1)}, bf16[256,640]{1,0:T(8,128)(2,1)S(1)}, u32[]{:S(2)}, u32[]{:S(2)}) collective-permute-start(bf16[256,640]{1,0:T(8,128)(2,1)S(1)} %collective-permute-done.4.refs_3_), channel_id=1, source_target_pairs={{0,128},{64,192},{128,0},{192,64},{1,129},{65,193},{129,1},{193,65... | collective-permute-start | bytes 983048 | tf_op jit(solution)/shard_map/ppermute | solution.py:351
  29.0 0.4 collective-permute-start.8
  29.4 2.3 %collective-permute-start.9 = (bf16[256,640]{1,0:T(8,128)(2,1)S(1)}, bf16[256,640]{1,0:T(8,128)(2,1)}, u32[]{:S(2)}, u32[]{:S(2)}) collective-permute-start(bf16[256,640]{1,0:T(8,128)(2,1)S(1)} %collective-permute-done.4.refs_3_), channel_id=1, source_target_pairs={{0,192},{64,0},{128,64},{192,128},{1,193},{65,1},{129,65},{193,129... | collective-permute-start | bytes 983048 | tf_op jit(solution)/shard_map/ppermute | solution.py:351
  32.3 0.0 collective-permute-done.3.refs_1_
  32.3 3.6 %collective-permute-start.16 = (bf16[112,2048]{1,0:T(8,128)(2,1)}, bf16[112,2048]{1,0:T(8,128)(2,1)S(1)}, u32[]{:S(2)}, u32[]{:S(2)}) collective-permute-start(bf16[112,2048]{1,0:T(8,128)(2,1)} %bitcast.21), channel_id=1, source_target_pairs={{0,4},{4,0},{1,5},{5,1},{2,6},{6,2},{3,7},{7,3},{8,12},{12,8},{9,1... | collective-permute-start | bytes 1376264 | tf_op jit(solution)/shard_map/ppermute | solution.py:375
  36.0 2.4 %shard_map.102.refs_0_ = bf16[2048,768]{1,0:T(8,128)(2,1)S(1)} custom-call(bf16[64,3072]{1,0:T(8,128)(2,1)S(1)} %shard_map.101.refs_0_, bf16[64,3072]{1,0:T(8,128)(2,1)S(1)} %collective-permute-done.3.refs_1_, bf16[16,128,512]{2,1,0:T(8,128)(2,1)} %refs_2_.3), custom_call_target="tpu_custom_call" | custom-call | flops 1 | bytes 1 | tf_op jit(solution)/shard_map/pallas_call | solution.py:144
  38.4 7.4 %shard_map.103 = (f32[128,2048]{1,0:T(8,128)S(1)}, f32[2048,128]{1,0:T(8,128)S(1)}) custom-call(bf16[2048,768]{1,0:T(8,128)(2,1)S(1)} %shard_map.102.refs_0_, f32[8,128]{1,0:T(8,128)S(1)} %broadcast_in_dim.17.refs_1_, bf16[16,512,128]{2,1,0:T(8,128)(2,1)S(1)} %copy-done, bf16[256,640]{1,0:T(8,128)(2,1)S(1)} %get-tuple-element.42.refs_3_, ...), custom_call_target="tpu_custom_call" | custom-call | flops 1 | bytes 1 | tf_op jit(solution)/shard_map/pallas_call | solution.py:250
  45.8 0.0 collective-permute-done.10.refs_6_
  45.8 0.0 collective-permute-done.8.refs_4_
  45.8 9.0 %shard_map.104 = (bf16[64,2176]{1,0:T(8,128)(2,1)S(1)}, bf16[64,2176]{1,0:T(8,128)(2,1)S(1)}) custom-call(bf16[2048,768]{1,0:T(8,128)(2,1)S(1)} %shard_map.102.refs_0_, f32[8,128]{1,0:T(8,128)S(1)} %broadcast_in_dim.17.refs_1_, bf16[16,512,128]{2,1,0:T(8,128)(2,1)S(1)} %copy-done, bf16[256,640]{1,0:T(8,128)(2,1)S(1)} %collective-permute-done.4.refs_3_, ...), custom_call_target="tpu_custom_call" | custom-call | flops 1 | bytes 1 | tf_op jit(solution)/shard_map/pallas_call | solution.py:250
  54.9 0.1 collective-permute-start.12
  55.0 1.5 %collective-permute-done.12.b_ref = bf16[64,2176]{1,0:T(8,128)(2,1)S(1)} collective-permute-done((bf16[64,2176]{1,0:T(8,128)(2,1)S(1)}, bf16[64,2176]{1,0:T(8,128)(2,1)S(1)}, u32[]{:S(2)}, u32[]{:S(2)}) %collective-permute-start.12) | collective-permute-done | bytes 278560 | tf_op jit(solution)/shard_map/ppermute | solution.py:371
  56.5 0.5 shard_map.105
  57.0 2.6 %collective-permute-start.13 = (bf16[16,2176]{1,0:T(8,128)(2,1)S(1)}, bf16[16,2176]{1,0:T(8,128)(2,1)S(1)}, u32[]{:S(2)}, u32[]{:S(2)}) collective-permute-start(bf16[16,2176]{1,0:T(8,128)(2,1)S(1)} %get-tuple-element.60), channel_id=1, source_target_pairs={{0,48},{16,0},{32,16},{48,32},{1,49},{17,1},{33,17},{49,33},{2,50}... | collective-permute-start | bytes 208904 | tf_op jit(solution)/shard_map/ppermute | solution.py:373
  59.6 0.0 collective-permute-start.14
  59.6 1.7 %collective-permute-start.15 = (bf16[16,2176]{1,0:T(8,128)(2,1)S(1)}, bf16[16,2176]{1,0:T(8,128)(2,1)S(1)}, u32[]{:S(2)}, u32[]{:S(2)}) collective-permute-start(bf16[16,2176]{1,0:T(8,128)(2,1)S(1)} %get-tuple-element.62), channel_id=1, source_target_pairs={{0,32},{16,48},{32,0},{48,16},{1,33},{17,49},{33,1},{49,17},{2,34}... | collective-permute-start | bytes 208904 | tf_op jit(solution)/shard_map/ppermute | solution.py:373
  61.3 0.0 collective-permute-done.16.refs_1_
  61.3 0.8 copy-done.3
  62.1 0.0 collective-permute-done.13.refs_1_
  62.1 3.8 %collective-permute-done.14.refs_2_ = bf16[16,2176]{1,0:T(8,128)(2,1)S(1)} collective-permute-done((bf16[16,2176]{1,0:T(8,128)(2,1)S(1)}, bf16[16,2176]{1,0:T(8,128)(2,1)S(1)}, u32[]{:S(2)}, u32[]{:S(2)}) %collective-permute-start.14) | collective-permute-done | bytes 69664 | tf_op jit(solution)/shard_map/ppermute | solution.py:373
  65.9 1.4 %shard_map.106 = bf16[16,16,2048]{2,1,0:T(8,128)(2,1)} custom-call(bf16[16,2176]{1,0:T(8,128)(2,1)S(1)} %get-tuple-element.63.refs_0_, bf16[16,2176]{1,0:T(8,128)(2,1)S(1)} %collective-permute-done.13.refs_1_, bf16[16,2176]{1,0:T(8,128)(2,1)S(1)} %collective-permute-done.14.refs_2_, bf16[16,2176]{1,0:T(8,128)(2,1)S(1)} %collective-permute-done.15.refs_3_), custom_call_target="tpu_custom_call" | custom-call | flops 1 | bytes 1 | tf_op jit(solution)/shard_map/pallas_call | solution.py:378
  67.4 3.7 %all-to-all-start = ((bf16[16,16,2048]{2,1,0:T(8,128)(2,1)}), bf16[16,16,2048]{2,1,0:T(8,128)(2,1)S(1)}, u32[]{:S(2)}, u32[]{:S(2)}) async-start(bf16[16,16,2048]{2,1,0:T(8,128)(2,1)} %shard_map.106), calls=%async_computation | async-start | bytes 2097152 | tf_op jit(solution)/shard_map/all_to_all | solution.py:382
  71.0 2.2 %collective-permute-start.17 = (bf16[112,2048]{1,0:T(8,128)(2,1)S(1)}, bf16[112,2048]{1,0:T(8,128)(2,1)S(1)}, u32[]{:S(2)}, u32[]{:S(2)}) collective-permute-start(bf16[112,2048]{1,0:T(8,128)(2,1)S(1)} %collective-permute-done.11.refs_0_), channel_id=1, source_target_pairs={{0,4},{4,0},{1,5},{5,1},{2,6},{6,2},{3,7},{7,3},{8,12},{12,8},{9,1... | collective-permute-start | bytes 1376264 | tf_op jit(solution)/shard_map/ppermute | solution.py:376
  73.2 0.1 pad_add_fusion.zc_ref
  73.3 1.4 %collective-permute-done.17.refs_2_ = bf16[112,2048]{1,0:T(8,128)(2,1)S(1)} collective-permute-done((bf16[112,2048]{1,0:T(8,128)(2,1)S(1)}, bf16[112,2048]{1,0:T(8,128)(2,1)S(1)}, u32[]{:S(2)}, u32[]{:S(2)}) %collective-permute-start.17) | collective-permute-done | bytes 458784 | tf_op jit(solution)/shard_map/ppermute | solution.py:376
  74.7 1.0 copy-done.2
  75.7 1.0 copy-done.4
  76.7 2.2 %shard_map.107.w_ref = bf16[2048,512]{1,0:T(8,128)(2,1)S(1)} custom-call(s32[2]{0:T(128)S(1)} %pad_add_fusion.zc_ref, bf16[112,2048]{1,0:T(8,128)(2,1)} %bitcast.22, bf16[112,2048]{1,0:T(8,128)(2,1)S(1)} %copy-done.2, bf16[112,2048]{1,0:T(8,128)(2,1)S(1)} %copy-done.4, bf16[112,2048]{1,0:T(8,128)(2,1)S(1)} %collective-permute-done.17.refs_2_), custom_call_target="tpu_custom_call" | custom-call | flops 1 | bytes 1 | tf_op jit(solution)/shard_map/pallas_call | solution.py:309
  78.9 7.1 %all-to-all-done = bf16[16,16,2048]{2,1,0:T(8,128)(2,1)S(1)} async-done(((bf16[16,16,2048]{2,1,0:T(8,128)(2,1)}), bf16[16,16,2048]{2,1,0:T(8,128)(2,1)S(1)}, u32[]{:S(2)}, u32[]{:S(2)}) %all-to-all-start) | async-done | bytes 1048608 | tf_op jit(solution)/shard_map/all_to_all | solution.py:382
  85.9 0.7 shard_map.108
  86.7 18.1 %all_to_all.10.sums_ref = bf16[16,64,112]{2,1,0:T(8,128)(2,1)S(1)} all-to-all(bf16[16,64,112]{2,1,0:T(8,128)(2,1)S(1)} %bitcast.19), channel_id=1, replica_groups=mesh['y'=4,'x'=4,'z'=2,'c'=2,'head'=4] {'z','c','head'}, dimensions={0} | all-to-all | bytes 458752 | tf_op jit(solution)/shard_map/all_to_all | solution.py:388
  104.7 0.7 shard_map.109
  (14 shorter events, 0.1 us)
Async XLA Ops:
  1.0 22.3 %collective-permute-start.4 = (bf16[256,640]{1,0:T(8,128)(2,1)S(1)}, bf16[256,640]{1,0:T(8,128)(2,1)S(1)}, u32[]{:S(2)}, u32[]{:S(2)}) collective-permute-start(bf16[256,640]{1,0:T(8,128)(2,1)S(1)} %get-tuple-element.42.refs_3_), channel_id=1, source_target_pairs={{0,8},{8,0},{1,9},{9,1},{2,10},{10,2},{3,11},{11,3},{4,12},{12,4},... | collective-permute-start | bytes 983048 | tf_op jit(solution)/shard_map/ppermute | solution.py:344
  7.1 5.4 %collective-permute-start = (bf16[16,3072]{1,0:T(8,128)(2,1)S(1)}, bf16[16,3072]{1,0:T(8,128)(2,1)S(1)}, u32[]{:S(2)}, u32[]{:S(2)}) collective-permute-start(bf16[16,3072]{1,0:T(8,128)(2,1)S(1)} %get-tuple-element.38.refs_0_), channel_id=1, source_target_pairs={{0,16},{16,32},{32,48},{48,0},{1,17},{17,33},{33,49},{49,1},{2,18}... | collective-permute-start | bytes 294920 | tf_op jit(solution)/shard_map/ppermute | solution.py:346
  8.3 6.7 %collective-permute-start.1 = (bf16[16,3072]{1,0:T(8,128)(2,1)S(1)}, bf16[16,3072]{1,0:T(8,128)(2,1)S(1)}, u32[]{:S(2)}, u32[]{:S(2)}) collective-permute-start(bf16[16,3072]{1,0:T(8,128)(2,1)S(1)} %get-tuple-element.38.refs_0_), channel_id=1, source_target_pairs={{0,48},{16,0},{32,16},{48,32},{1,49},{17,1},{33,17},{49,33},{2,50}... | collective-permute-start | bytes 294920 | tf_op jit(solution)/shard_map/ppermute | solution.py:346
  9.8 16.1 %collective-permute-start.5 = (bf16[256,640]{1,0:T(8,128)(2,1)S(1)}, bf16[256,640]{1,0:T(8,128)(2,1)S(1)}, u32[]{:S(2)}, u32[]{:S(2)}) collective-permute-start(bf16[256,640]{1,0:T(8,128)(2,1)S(1)} %get-tuple-element.42.refs_3_), channel_id=1, source_target_pairs={{0,64},{64,128},{128,192},{192,0},{1,65},{65,129},{129,193},{193,1... | collective-permute-start | bytes 983048 | tf_op jit(solution)/shard_map/ppermute | solution.py:345
  11.1 14.8 %collective-permute-start.6 = (bf16[256,640]{1,0:T(8,128)(2,1)S(1)}, bf16[256,640]{1,0:T(8,128)(2,1)S(1)}, u32[]{:S(2)}, u32[]{:S(2)}) collective-permute-start(bf16[256,640]{1,0:T(8,128)(2,1)S(1)} %get-tuple-element.42.refs_3_), channel_id=1, source_target_pairs={{0,192},{64,0},{128,64},{192,128},{1,193},{65,1},{129,65},{193,129... | collective-permute-start | bytes 983048 | tf_op jit(solution)/shard_map/ppermute | solution.py:345
  12.6 14.4 %collective-permute-start.7 = (bf16[256,640]{1,0:T(8,128)(2,1)S(1)}, bf16[256,640]{1,0:T(8,128)(2,1)S(1)}, u32[]{:S(2)}, u32[]{:S(2)}) collective-permute-start(bf16[256,640]{1,0:T(8,128)(2,1)S(1)} %get-tuple-element.42.refs_3_), channel_id=1, source_target_pairs={{0,128},{64,192},{128,0},{192,64},{1,129},{65,193},{129,1},{193,65... | collective-permute-start | bytes 983048 | tf_op jit(solution)/shard_map/ppermute | solution.py:345
  15.0 5.3 %collective-permute-start.2 = (bf16[16,3072]{1,0:T(8,128)(2,1)S(1)}, bf16[16,3072]{1,0:T(8,128)(2,1)S(1)}, u32[]{:S(2)}, u32[]{:S(2)}) collective-permute-start(bf16[16,3072]{1,0:T(8,128)(2,1)S(1)} %get-tuple-element.38.refs_0_), channel_id=1, source_target_pairs={{0,32},{16,48},{32,0},{48,16},{1,33},{17,49},{33,1},{49,17},{2,34}... | collective-permute-start | bytes 294920 | tf_op jit(solution)/shard_map/ppermute | solution.py:348
  20.3 12.0 %collective-permute-start.3 = (bf16[64,3072]{1,0:T(8,128)(2,1)S(1)}, bf16[64,3072]{1,0:T(8,128)(2,1)S(1)}, u32[]{:S(2)}, u32[]{:S(2)}) collective-permute-start(bf16[64,3072]{1,0:T(8,128)(2,1)S(1)} %shard_map.101.refs_0_), channel_id=1, source_target_pairs={{0,4},{4,0},{1,5},{5,1},{2,6},{6,2},{3,7},{7,3},{8,12},{12,8},{9,1... | collective-permute-start | bytes 1179656 | tf_op jit(solution)/shard_map/ppermute | solution.py:353
  23.4 31.5 %collective-permute-start.11 = (bf16[112,2048]{1,0:T(8,128)(2,1)}, bf16[112,2048]{1,0:T(8,128)(2,1)S(1)}, u32[]{:S(2)}, u32[]{:S(2)}) collective-permute-start(bf16[112,2048]{1,0:T(8,128)(2,1)} %bitcast.20), channel_id=1, source_target_pairs={{0,8},{8,0},{1,9},{9,1},{2,10},{10,2},{3,11},{11,3},{4,12},{12,4},... | collective-permute-start | bytes 1376264 | tf_op jit(solution)/shard_map/ppermute | solution.py:354
  27.0 18.8 %collective-permute-start.10 = (bf16[256,640]{1,0:T(8,128)(2,1)S(1)}, bf16[256,640]{1,0:T(8,128)(2,1)S(1)}, u32[]{:S(2)}, u32[]{:S(2)}) collective-permute-start(bf16[256,640]{1,0:T(8,128)(2,1)S(1)} %collective-permute-done.4.refs_3_), channel_id=1, source_target_pairs={{0,128},{64,192},{128,0},{192,64},{1,129},{65,193},{129,1},{193,65... | collective-permute-start | bytes 983048 | tf_op jit(solution)/shard_map/ppermute | solution.py:351
  29.0 16.9 %collective-permute-start.8 = (bf16[256,640]{1,0:T(8,128)(2,1)S(1)}, bf16[256,640]{1,0:T(8,128)(2,1)S(1)}, u32[]{:S(2)}, u32[]{:S(2)}) collective-permute-start(bf16[256,640]{1,0:T(8,128)(2,1)S(1)} %collective-permute-done.4.refs_3_), channel_id=1, source_target_pairs={{0,64},{64,128},{128,192},{192,0},{1,65},{65,129},{129,193},{193,1... | collective-permute-start | bytes 983048 | tf_op jit(solution)/shard_map/ppermute | solution.py:351
  29.4 16.5 %collective-permute-start.9 = (bf16[256,640]{1,0:T(8,128)(2,1)S(1)}, bf16[256,640]{1,0:T(8,128)(2,1)}, u32[]{:S(2)}, u32[]{:S(2)}) collective-permute-start(bf16[256,640]{1,0:T(8,128)(2,1)S(1)} %collective-permute-done.4.refs_3_), channel_id=1, source_target_pairs={{0,192},{64,0},{128,64},{192,128},{1,193},{65,1},{129,65},{193,129... | collective-permute-start | bytes 983048 | tf_op jit(solution)/shard_map/ppermute | solution.py:351
  32.3 29.0 %collective-permute-start.16 = (bf16[112,2048]{1,0:T(8,128)(2,1)}, bf16[112,2048]{1,0:T(8,128)(2,1)S(1)}, u32[]{:S(2)}, u32[]{:S(2)}) collective-permute-start(bf16[112,2048]{1,0:T(8,128)(2,1)} %bitcast.21), channel_id=1, source_target_pairs={{0,4},{4,0},{1,5},{5,1},{2,6},{6,2},{3,7},{7,3},{8,12},{12,8},{9,1... | collective-permute-start | bytes 1376264 | tf_op jit(solution)/shard_map/ppermute | solution.py:375
  36.0 2.4 %copy-start = (bf16[16,512,128]{2,1,0:T(8,128)(2,1)S(1)}, bf16[16,512,128]{2,1,0:T(8,128)(2,1)}, u32[]{:S(2)}) copy-start(bf16[16,512,128]{2,1,0:T(8,128)(2,1)} %refs_2_.5) | copy-start | bytes 6291460
  54.9 18.4 %copy-start.1 = (bf16[112,2048]{1,0:T(8,128)(2,1)}, bf16[112,2048]{1,0:T(8,128)(2,1)S(1)}, u32[]{:S(2)}) copy-start(bf16[112,2048]{1,0:T(8,128)(2,1)S(1)} %collective-permute-done.11.refs_0_) | copy-start | bytes 1376260
  54.9 1.6 %collective-permute-start.12 = (bf16[64,2176]{1,0:T(8,128)(2,1)S(1)}, bf16[64,2176]{1,0:T(8,128)(2,1)S(1)}, u32[]{:S(2)}, u32[]{:S(2)}) collective-permute-start(bf16[64,2176]{1,0:T(8,128)(2,1)S(1)} %get-tuple-element.58), channel_id=1, source_target_pairs={{0,4},{4,0},{1,5},{5,1},{2,6},{6,2},{3,7},{7,3},{8,12},{12,8},{9,1... | collective-permute-start | bytes 835592 | tf_op jit(solution)/shard_map/ppermute | solution.py:371
  57.0 5.1 %collective-permute-start.13 = (bf16[16,2176]{1,0:T(8,128)(2,1)S(1)}, bf16[16,2176]{1,0:T(8,128)(2,1)S(1)}, u32[]{:S(2)}, u32[]{:S(2)}) collective-permute-start(bf16[16,2176]{1,0:T(8,128)(2,1)S(1)} %get-tuple-element.60), channel_id=1, source_target_pairs={{0,48},{16,0},{32,16},{48,32},{1,49},{17,1},{33,17},{49,33},{2,50}... | collective-permute-start | bytes 208904 | tf_op jit(solution)/shard_map/ppermute | solution.py:373
  59.6 6.4 %collective-permute-start.14 = (bf16[16,2176]{1,0:T(8,128)(2,1)S(1)}, bf16[16,2176]{1,0:T(8,128)(2,1)S(1)}, u32[]{:S(2)}, u32[]{:S(2)}) collective-permute-start(bf16[16,2176]{1,0:T(8,128)(2,1)S(1)} %get-tuple-element.61), channel_id=1, source_target_pairs={{0,16},{16,32},{32,48},{48,0},{1,17},{17,33},{33,49},{49,1},{2,18}... | collective-permute-start | bytes 208904 | tf_op jit(solution)/shard_map/ppermute | solution.py:373
  59.6 6.4 %collective-permute-start.15 = (bf16[16,2176]{1,0:T(8,128)(2,1)S(1)}, bf16[16,2176]{1,0:T(8,128)(2,1)S(1)}, u32[]{:S(2)}, u32[]{:S(2)}) collective-permute-start(bf16[16,2176]{1,0:T(8,128)(2,1)S(1)} %get-tuple-element.62), channel_id=1, source_target_pairs={{0,32},{16,48},{32,0},{48,16},{1,33},{17,49},{33,1},{49,17},{2,34}... | collective-permute-start | bytes 208904 | tf_op jit(solution)/shard_map/ppermute | solution.py:373
  61.3 0.8 copy-start.3
  67.4 18.6 %all-to-all-start = ((bf16[16,16,2048]{2,1,0:T(8,128)(2,1)}), bf16[16,16,2048]{2,1,0:T(8,128)(2,1)S(1)}, u32[]{:S(2)}, u32[]{:S(2)}) async-start(bf16[16,16,2048]{2,1,0:T(8,128)(2,1)} %shard_map.106), calls=%async_computation | async-start | bytes 2097152 | tf_op jit(solution)/shard_map/all_to_all | solution.py:382
  71.0 3.6 %collective-permute-start.17 = (bf16[112,2048]{1,0:T(8,128)(2,1)S(1)}, bf16[112,2048]{1,0:T(8,128)(2,1)S(1)}, u32[]{:S(2)}, u32[]{:S(2)}) collective-permute-start(bf16[112,2048]{1,0:T(8,128)(2,1)S(1)} %collective-permute-done.11.refs_0_), channel_id=1, source_target_pairs={{0,4},{4,0},{1,5},{5,1},{2,6},{6,2},{3,7},{7,3},{8,12},{12,8},{9,1... | collective-permute-start | bytes 1376264 | tf_op jit(solution)/shard_map/ppermute | solution.py:376
  74.7 1.0 copy-start.2
  75.7 1.0 copy-start.4

commit v13 on v12

--- a/solution.py
+++ b/solution.py
@@ -281,10 +281,23 @@
 
 
 def merge_ring_kernel(*refs):
-    heads, _ = merge(refs[:-1])
-    for cols, head in heads:
-        for i in range(refs[-1].shape[0]):
-            refs[-1][i, :, cols] = head
+    part_refs, (out_ref, held, sems) = refs[:4], refs[4:]
+    heads, _ = merge(part_refs)
+    half = HG * VDIM // 2
+    copies = []
+    for i, (cols, head) in enumerate(heads):
+        held[:, cols] = head
+        if (i + 1) % (HG // 2) == 0:
+            k = i // (HG // 2)
+            lanes = slice(k * half, (k + 1) * half)
+            for n in range(16):
+                copy = pltpu.make_async_copy(
+                    held.at[:, lanes], out_ref.at[n, :, lanes], sems.at[k, n]
+                )
+                copy.start()
+                copies.append(copy)
+    for copy in copies:
+        copy.wait()
 
 
 def columns_kernel(zc_ref, own_ref, *refs):
@@ -375,9 +388,15 @@
     c_w = lax.ppermute(w_own, "c", SWAP)
     zc_w = lax.ppermute(z_w, "c", SWAP)
     parts, c_w = lax.optimization_barrier((parts, c_w))
-    heads = call(merge_ring_kernel, jax.ShapeDtypeStruct((16, R, HG * VDIM), jnp.bfloat16))(
-        *parts
-    )
+    heads = call(
+        merge_ring_kernel,
+        jax.ShapeDtypeStruct((16, R, HG * VDIM), jnp.bfloat16),
+        out_specs=HBM,
+        scratch_shapes=[
+            pltpu.VMEM((R, HG * VDIM), jnp.bfloat16),
+            pltpu.SemaphoreType.DMA((2, 16)),
+        ],
+    )(*parts)
 
     rows = lax.all_to_all(heads, ("y", "x"), 0, 0, tiled=True).reshape(16 * R, HG * VDIM)
     ncol = w_out.shape[1]

time: 106 us -> 106 us (level)
  no operation moved by 1% of the time
where the time goes in v13:
time: 106 us
  starting transfers between devices  39.6 us (37%)
  Pallas kernels  25.5 us (24%)
  waiting for transfers between devices  18.6 us (18%)
  blocking collectives  18.1 us (17%)
  local copies, waits for them, and re-layouts  2.85 us (3%)
    all_to_all x1, blocking collectives, local(): lax.all_to_all(sums.reshape(16, 4 * R, ncol), ('z', 'c', 'head'), 0, 0, t...  18.1 us
    pallas_call x2, Pallas kernels, attend(): call(functools.partial(attend_kernel, n, last, tile, unroll), out_shape,...  16.4 us
    all_to_all x1, waiting for transfers between devices, local(): lax.all_to_all(heads, ('y', 'x'), 0, 0, tiled=True)  7.08 us
    ppermute x1, starting transfers between devices, local(): z_keys = lax.ppermute(keys, 'z', SWAP)  6.1 us
    ppermute x3, starting transfers between devices, local(): up, down, across = (lax.ppermute(keys, 'y', shift(d)) for d in (1, 3, 2))  5.21 us
    ppermute x3, starting transfers between devices, local(): far = [z_keys] + [lax.ppermute(z_keys, 'y', shift(d)) for d in RING[1:]]  4.67 us
    ppermute x3, starting transfers between devices, local(): lax.ppermute(part, 'x', shift(-d % 4))  4.28 us
    ppermute x3, waiting for transfers between devices, local(): lax.ppermute(part, 'x', shift(-d % 4))  3.84 us
  transfers between devices with their start and end apart: 19, of which 6 were waited for; matrix products, arithmetic and copies ran while one was open for 0% of the time, Pallas kernels for 20%

profile of v13, /device:TPU:33, one launch (start us, length us, event | category | flops | bytes accessed | tf_op | source)
XLA Modules:
  0.0 105.6 jit_solution(8313864354113571391)
XLA Ops:
  0.0 1.0 shard_map.100
  1.0 6.1 %collective-permute-start.4 = (bf16[256,640]{1,0:T(8,128)(2,1)S(1)}, bf16[256,640]{1,0:T(8,128)(2,1)S(1)}, u32[]{:S(2)}, u32[]{:S(2)}) collective-permute-start(bf16[256,640]{1,0:T(8,128)(2,1)S(1)} %get-tuple-element.42.refs_3_), channel_id=1, source_target_pairs={{0,8},{8,0},{1,9},{9,1},{2,10},{10,2},{3,11},{11,3},{4,12},{12,4},... | collective-permute-start | bytes 983048 | tf_op jit(solution)/shard_map/ppermute | solution.py:357
  7.1 1.2 %collective-permute-start = (bf16[16,3072]{1,0:T(8,128)(2,1)S(1)}, bf16[16,3072]{1,0:T(8,128)(2,1)S(1)}, u32[]{:S(2)}, u32[]{:S(2)}) collective-permute-start(bf16[16,3072]{1,0:T(8,128)(2,1)S(1)} %get-tuple-element.38.refs_0_), channel_id=1, source_target_pairs={{0,16},{16,32},{32,48},{48,0},{1,17},{17,33},{33,49},{49,1},{2,18}... | collective-permute-start | bytes 294920 | tf_op jit(solution)/shard_map/ppermute | solution.py:359
  8.3 1.5 %collective-permute-start.1 = (bf16[16,3072]{1,0:T(8,128)(2,1)S(1)}, bf16[16,3072]{1,0:T(8,128)(2,1)S(1)}, u32[]{:S(2)}, u32[]{:S(2)}) collective-permute-start(bf16[16,3072]{1,0:T(8,128)(2,1)S(1)} %get-tuple-element.38.refs_0_), channel_id=1, source_target_pairs={{0,48},{16,0},{32,16},{48,32},{1,49},{17,1},{33,17},{49,33},{2,50}... | collective-permute-start | bytes 294920 | tf_op jit(solution)/shard_map/ppermute | solution.py:359
  9.8 1.3 %collective-permute-start.5 = (bf16[256,640]{1,0:T(8,128)(2,1)S(1)}, bf16[256,640]{1,0:T(8,128)(2,1)S(1)}, u32[]{:S(2)}, u32[]{:S(2)}) collective-permute-start(bf16[256,640]{1,0:T(8,128)(2,1)S(1)} %get-tuple-element.42.refs_3_), channel_id=1, source_target_pairs={{0,64},{64,128},{128,192},{192,0},{1,65},{65,129},{129,193},{193,1... | collective-permute-start | bytes 983048 | tf_op jit(solution)/shard_map/ppermute | solution.py:358
  11.1 1.4 %collective-permute-start.6 = (bf16[256,640]{1,0:T(8,128)(2,1)S(1)}, bf16[256,640]{1,0:T(8,128)(2,1)S(1)}, u32[]{:S(2)}, u32[]{:S(2)}) collective-permute-start(bf16[256,640]{1,0:T(8,128)(2,1)S(1)} %get-tuple-element.42.refs_3_), channel_id=1, source_target_pairs={{0,192},{64,0},{128,64},{192,128},{1,193},{65,1},{129,65},{193,129... | collective-permute-start | bytes 983048 | tf_op jit(solution)/shard_map/ppermute | solution.py:358
  12.6 0.0 collective-permute-done.refs_1_
  12.6 2.5 %collective-permute-start.7 = (bf16[256,640]{1,0:T(8,128)(2,1)S(1)}, bf16[256,640]{1,0:T(8,128)(2,1)S(1)}, u32[]{:S(2)}, u32[]{:S(2)}) collective-permute-start(bf16[256,640]{1,0:T(8,128)(2,1)S(1)} %get-tuple-element.42.refs_3_), channel_id=1, source_target_pairs={{0,128},{64,192},{128,0},{192,64},{1,129},{65,193},{129,1},{193,65... | collective-permute-start | bytes 983048 | tf_op jit(solution)/shard_map/ppermute | solution.py:358
  15.0 1.5 %collective-permute-start.2 = (bf16[16,3072]{1,0:T(8,128)(2,1)S(1)}, bf16[16,3072]{1,0:T(8,128)(2,1)S(1)}, u32[]{:S(2)}, u32[]{:S(2)}) collective-permute-start(bf16[16,3072]{1,0:T(8,128)(2,1)S(1)} %get-tuple-element.38.refs_0_), channel_id=1, source_target_pairs={{0,32},{16,48},{32,0},{48,16},{1,33},{17,49},{33,1},{49,17},{2,34}... | collective-permute-start | bytes 294920 | tf_op jit(solution)/shard_map/ppermute | solution.py:361
  16.6 3.7 %collective-permute-done.2.refs_3_ = bf16[16,3072]{1,0:T(8,128)(2,1)S(1)} collective-permute-done((bf16[16,3072]{1,0:T(8,128)(2,1)S(1)}, bf16[16,3072]{1,0:T(8,128)(2,1)S(1)}, u32[]{:S(2)}, u32[]{:S(2)}) %collective-permute-start.2) | collective-permute-done | bytes 98336 | tf_op jit(solution)/shard_map/ppermute | solution.py:361
  20.3 3.0 %collective-permute-start.3 = (bf16[64,3072]{1,0:T(8,128)(2,1)S(1)}, bf16[64,3072]{1,0:T(8,128)(2,1)S(1)}, u32[]{:S(2)}, u32[]{:S(2)}) collective-permute-start(bf16[64,3072]{1,0:T(8,128)(2,1)S(1)} %shard_map.101.refs_0_), channel_id=1, source_target_pairs={{0,4},{4,0},{1,5},{5,1},{2,6},{6,2},{3,7},{7,3},{8,12},{12,8},{9,1... | collective-permute-start | bytes 1179656 | tf_op jit(solution)/shard_map/ppermute | solution.py:366
  23.4 0.0 collective-permute-done.4.refs_3_
  23.4 2.6 %collective-permute-start.11 = (bf16[112,2048]{1,0:T(8,128)(2,1)}, bf16[112,2048]{1,0:T(8,128)(2,1)S(1)}, u32[]{:S(2)}, u32[]{:S(2)}) collective-permute-start(bf16[112,2048]{1,0:T(8,128)(2,1)} %bitcast.20), channel_id=1, source_target_pairs={{0,8},{8,0},{1,9},{9,1},{2,10},{10,2},{3,11},{11,3},{4,12},{12,4},... | collective-permute-start | bytes 1376264 | tf_op jit(solution)/shard_map/ppermute | solution.py:367
  25.9 0.0 collective-permute-done.5.refs_4_
  26.0 0.0 collective-permute-done.6.refs_5_
  26.0 1.0 collective-permute-done.7.refs_6_
  27.0 2.0 %collective-permute-start.10 = (bf16[256,640]{1,0:T(8,128)(2,1)S(1)}, bf16[256,640]{1,0:T(8,128)(2,1)S(1)}, u32[]{:S(2)}, u32[]{:S(2)}) collective-permute-start(bf16[256,640]{1,0:T(8,128)(2,1)S(1)} %collective-permute-done.4.refs_3_), channel_id=1, source_target_pairs={{0,128},{64,192},{128,0},{192,64},{1,129},{65,193},{129,1},{193,65... | collective-permute-start | bytes 983048 | tf_op jit(solution)/shard_map/ppermute | solution.py:364
  29.0 0.4 collective-permute-start.8
  29.4 2.3 %collective-permute-start.9 = (bf16[256,640]{1,0:T(8,128)(2,1)S(1)}, bf16[256,640]{1,0:T(8,128)(2,1)}, u32[]{:S(2)}, u32[]{:S(2)}) collective-permute-start(bf16[256,640]{1,0:T(8,128)(2,1)S(1)} %collective-permute-done.4.refs_3_), channel_id=1, source_target_pairs={{0,192},{64,0},{128,64},{192,128},{1,193},{65,1},{129,65},{193,129... | collective-permute-start | bytes 983048 | tf_op jit(solution)/shard_map/ppermute | solution.py:364
  32.3 0.0 collective-permute-done.3.refs_1_
  32.3 3.6 %collective-permute-start.16 = (bf16[112,2048]{1,0:T(8,128)(2,1)}, bf16[112,2048]{1,0:T(8,128)(2,1)S(1)}, u32[]{:S(2)}, u32[]{:S(2)}) collective-permute-start(bf16[112,2048]{1,0:T(8,128)(2,1)} %bitcast.21), channel_id=1, source_target_pairs={{0,4},{4,0},{1,5},{5,1},{2,6},{6,2},{3,7},{7,3},{8,12},{12,8},{9,1... | collective-permute-start | bytes 1376264 | tf_op jit(solution)/shard_map/ppermute | solution.py:388
  36.0 2.4 %shard_map.102.refs_0_ = bf16[2048,768]{1,0:T(8,128)(2,1)S(1)} custom-call(bf16[64,3072]{1,0:T(8,128)(2,1)S(1)} %shard_map.101.refs_0_, bf16[64,3072]{1,0:T(8,128)(2,1)S(1)} %collective-permute-done.3.refs_1_, bf16[16,128,512]{2,1,0:T(8,128)(2,1)} %refs_2_.3), custom_call_target="tpu_custom_call" | custom-call | flops 1 | bytes 1 | tf_op jit(solution)/shard_map/pallas_call | solution.py:144
  38.4 7.4 %shard_map.103 = (f32[128,2048]{1,0:T(8,128)S(1)}, f32[2048,128]{1,0:T(8,128)S(1)}) custom-call(bf16[2048,768]{1,0:T(8,128)(2,1)S(1)} %shard_map.102.refs_0_, f32[8,128]{1,0:T(8,128)S(1)} %broadcast_in_dim.17.refs_1_, bf16[16,512,128]{2,1,0:T(8,128)(2,1)S(1)} %copy-done, bf16[256,640]{1,0:T(8,128)(2,1)S(1)} %get-tuple-element.42.refs_3_, ...), custom_call_target="tpu_custom_call" | custom-call | flops 1 | bytes 1 | tf_op jit(solution)/shard_map/pallas_call | solution.py:250
  45.8 0.0 collective-permute-done.10.refs_6_
  45.8 0.0 collective-permute-done.8.refs_4_
  45.8 9.0 %shard_map.104 = (bf16[64,2176]{1,0:T(8,128)(2,1)S(1)}, bf16[64,2176]{1,0:T(8,128)(2,1)S(1)}) custom-call(bf16[2048,768]{1,0:T(8,128)(2,1)S(1)} %shard_map.102.refs_0_, f32[8,128]{1,0:T(8,128)S(1)} %broadcast_in_dim.17.refs_1_, bf16[16,512,128]{2,1,0:T(8,128)(2,1)S(1)} %copy-done, bf16[256,640]{1,0:T(8,128)(2,1)S(1)} %collective-permute-done.4.refs_3_, ...), custom_call_target="tpu_custom_call" | custom-call | flops 1 | bytes 1 | tf_op jit(solution)/shard_map/pallas_call | solution.py:250
  54.9 0.1 collective-permute-start.12
  55.0 1.5 %collective-permute-done.12.b_ref = bf16[64,2176]{1,0:T(8,128)(2,1)S(1)} collective-permute-done((bf16[64,2176]{1,0:T(8,128)(2,1)S(1)}, bf16[64,2176]{1,0:T(8,128)(2,1)S(1)}, u32[]{:S(2)}, u32[]{:S(2)}) %collective-permute-start.12) | collective-permute-done | bytes 278560 | tf_op jit(solution)/shard_map/ppermute | solution.py:384
  56.5 0.5 shard_map.105
  57.0 2.6 %collective-permute-start.13 = (bf16[16,2176]{1,0:T(8,128)(2,1)S(1)}, bf16[16,2176]{1,0:T(8,128)(2,1)S(1)}, u32[]{:S(2)}, u32[]{:S(2)}) collective-permute-start(bf16[16,2176]{1,0:T(8,128)(2,1)S(1)} %get-tuple-element.60), channel_id=1, source_target_pairs={{0,48},{16,0},{32,16},{48,32},{1,49},{17,1},{33,17},{49,33},{2,50}... | collective-permute-start | bytes 208904 | tf_op jit(solution)/shard_map/ppermute | solution.py:386
  59.6 0.0 collective-permute-start.14
  59.6 1.7 %collective-permute-start.15 = (bf16[16,2176]{1,0:T(8,128)(2,1)S(1)}, bf16[16,2176]{1,0:T(8,128)(2,1)S(1)}, u32[]{:S(2)}, u32[]{:S(2)}) collective-permute-start(bf16[16,2176]{1,0:T(8,128)(2,1)S(1)} %get-tuple-element.62), channel_id=1, source_target_pairs={{0,32},{16,48},{32,0},{48,16},{1,33},{17,49},{33,1},{49,17},{2,34}... | collective-permute-start | bytes 208904 | tf_op jit(solution)/shard_map/ppermute | solution.py:386
  61.3 0.0 collective-permute-done.16.refs_1_
  61.3 0.8 copy-done.3
  62.1 0.0 collective-permute-done.13.refs_1_
  62.1 3.8 %collective-permute-done.14.refs_2_ = bf16[16,2176]{1,0:T(8,128)(2,1)S(1)} collective-permute-done((bf16[16,2176]{1,0:T(8,128)(2,1)S(1)}, bf16[16,2176]{1,0:T(8,128)(2,1)S(1)}, u32[]{:S(2)}, u32[]{:S(2)}) %collective-permute-start.14) | collective-permute-done | bytes 69664 | tf_op jit(solution)/shard_map/ppermute | solution.py:386
  65.9 1.5 %shard_map.106 = bf16[16,16,2048]{2,1,0:T(8,128)(2,1)} custom-call(bf16[16,2176]{1,0:T(8,128)(2,1)S(1)} %get-tuple-element.63.refs_0_, bf16[16,2176]{1,0:T(8,128)(2,1)S(1)} %collective-permute-done.13.refs_1_, bf16[16,2176]{1,0:T(8,128)(2,1)S(1)} %collective-permute-done.14.refs_2_, bf16[16,2176]{1,0:T(8,128)(2,1)S(1)} %collective-permute-done.15.refs_3_), custom_call_target="tpu_custom_call" | custom-call | flops 1 | bytes 1 | tf_op jit(solution)/shard_map/pallas_call | solution.py:391
  67.5 3.7 %all-to-all-start = ((bf16[16,16,2048]{2,1,0:T(8,128)(2,1)}), bf16[16,16,2048]{2,1,0:T(8,128)(2,1)S(1)}, u32[]{:S(2)}, u32[]{:S(2)}) async-start(bf16[16,16,2048]{2,1,0:T(8,128)(2,1)} %shard_map.106), calls=%async_computation | async-start | bytes 2097152 | tf_op jit(solution)/shard_map/all_to_all | solution.py:401
  71.2 2.2 %collective-permute-start.17 = (bf16[112,2048]{1,0:T(8,128)(2,1)S(1)}, bf16[112,2048]{1,0:T(8,128)(2,1)S(1)}, u32[]{:S(2)}, u32[]{:S(2)}) collective-permute-start(bf16[112,2048]{1,0:T(8,128)(2,1)S(1)} %collective-permute-done.11.refs_0_), channel_id=1, source_target_pairs={{0,4},{4,0},{1,5},{5,1},{2,6},{6,2},{3,7},{7,3},{8,12},{12,8},{9,1... | collective-permute-start | bytes 1376264 | tf_op jit(solution)/shard_map/ppermute | solution.py:389
  73.3 0.1 pad_add_fusion.zc_ref
  73.4 1.4 %collective-permute-done.17.refs_2_ = bf16[112,2048]{1,0:T(8,128)(2,1)S(1)} collective-permute-done((bf16[112,2048]{1,0:T(8,128)(2,1)S(1)}, bf16[112,2048]{1,0:T(8,128)(2,1)S(1)}, u32[]{:S(2)}, u32[]{:S(2)}) %collective-permute-start.17) | collective-permute-done | bytes 458784 | tf_op jit(solution)/shard_map/ppermute | solution.py:389
  74.8 1.0 copy-done.2
  75.8 1.0 copy-done.4
  76.8 2.2 %shard_map.107.w_ref = bf16[2048,512]{1,0:T(8,128)(2,1)S(1)} custom-call(s32[2]{0:T(128)S(1)} %pad_add_fusion.zc_ref, bf16[112,2048]{1,0:T(8,128)(2,1)} %bitcast.22, bf16[112,2048]{1,0:T(8,128)(2,1)S(1)} %copy-done.2, bf16[112,2048]{1,0:T(8,128)(2,1)S(1)} %copy-done.4, bf16[112,2048]{1,0:T(8,128)(2,1)S(1)} %collective-permute-done.17.refs_2_), custom_call_target="tpu_custom_call" | custom-call | flops 1 | bytes 1 | tf_op jit(solution)/shard_map/pallas_call | solution.py:322
  79.0 7.1 %all-to-all-done = bf16[16,16,2048]{2,1,0:T(8,128)(2,1)S(1)} async-done(((bf16[16,16,2048]{2,1,0:T(8,128)(2,1)}), bf16[16,16,2048]{2,1,0:T(8,128)(2,1)S(1)}, u32[]{:S(2)}, u32[]{:S(2)}) %all-to-all-start) | async-done | bytes 1048608 | tf_op jit(solution)/shard_map/all_to_all | solution.py:401
  86.1 0.7 shard_map.108
  86.8 18.1 %all_to_all.10.sums_ref = bf16[16,64,112]{2,1,0:T(8,128)(2,1)S(1)} all-to-all(bf16[16,64,112]{2,1,0:T(8,128)(2,1)S(1)} %bitcast.19), channel_id=1, replica_groups=mesh['y'=4,'x'=4,'z'=2,'c'=2,'head'=4] {'z','c','head'}, dimensions={0} | all-to-all | bytes 458752 | tf_op jit(solution)/shard_map/all_to_all | solution.py:407
  104.8 0.7 shard_map.109
  (14 shorter events, 0.1 us)
Async XLA Ops:
  1.0 22.3 %collective-permute-start.4 = (bf16[256,640]{1,0:T(8,128)(2,1)S(1)}, bf16[256,640]{1,0:T(8,128)(2,1)S(1)}, u32[]{:S(2)}, u32[]{:S(2)}) collective-permute-start(bf16[256,640]{1,0:T(8,128)(2,1)S(1)} %get-tuple-element.42.refs_3_), channel_id=1, source_target_pairs={{0,8},{8,0},{1,9},{9,1},{2,10},{10,2},{3,11},{11,3},{4,12},{12,4},... | collective-permute-start | bytes 983048 | tf_op jit(solution)/shard_map/ppermute | solution.py:357
  7.1 5.4 %collective-permute-start = (bf16[16,3072]{1,0:T(8,128)(2,1)S(1)}, bf16[16,3072]{1,0:T(8,128)(2,1)S(1)}, u32[]{:S(2)}, u32[]{:S(2)}) collective-permute-start(bf16[16,3072]{1,0:T(8,128)(2,1)S(1)} %get-tuple-element.38.refs_0_), channel_id=1, source_target_pairs={{0,16},{16,32},{32,48},{48,0},{1,17},{17,33},{33,49},{49,1},{2,18}... | collective-permute-start | bytes 294920 | tf_op jit(solution)/shard_map/ppermute | solution.py:359
  8.3 6.7 %collective-permute-start.1 = (bf16[16,3072]{1,0:T(8,128)(2,1)S(1)}, bf16[16,3072]{1,0:T(8,128)(2,1)S(1)}, u32[]{:S(2)}, u32[]{:S(2)}) collective-permute-start(bf16[16,3072]{1,0:T(8,128)(2,1)S(1)} %get-tuple-element.38.refs_0_), channel_id=1, source_target_pairs={{0,48},{16,0},{32,16},{48,32},{1,49},{17,1},{33,17},{49,33},{2,50}... | collective-permute-start | bytes 294920 | tf_op jit(solution)/shard_map/ppermute | solution.py:359
  9.8 16.1 %collective-permute-start.5 = (bf16[256,640]{1,0:T(8,128)(2,1)S(1)}, bf16[256,640]{1,0:T(8,128)(2,1)S(1)}, u32[]{:S(2)}, u32[]{:S(2)}) collective-permute-start(bf16[256,640]{1,0:T(8,128)(2,1)S(1)} %get-tuple-element.42.refs_3_), channel_id=1, source_target_pairs={{0,64},{64,128},{128,192},{192,0},{1,65},{65,129},{129,193},{193,1... | collective-permute-start | bytes 983048 | tf_op jit(solution)/shard_map/ppermute | solution.py:358
  11.1 14.8 %collective-permute-start.6 = (bf16[256,640]{1,0:T(8,128)(2,1)S(1)}, bf16[256,640]{1,0:T(8,128)(2,1)S(1)}, u32[]{:S(2)}, u32[]{:S(2)}) collective-permute-start(bf16[256,640]{1,0:T(8,128)(2,1)S(1)} %get-tuple-element.42.refs_3_), channel_id=1, source_target_pairs={{0,192},{64,0},{128,64},{192,128},{1,193},{65,1},{129,65},{193,129... | collective-permute-start | bytes 983048 | tf_op jit(solution)/shard_map/ppermute | solution.py:358
  12.6 14.4 %collective-permute-start.7 = (bf16[256,640]{1,0:T(8,128)(2,1)S(1)}, bf16[256,640]{1,0:T(8,128)(2,1)S(1)}, u32[]{:S(2)}, u32[]{:S(2)}) collective-permute-start(bf16[256,640]{1,0:T(8,128)(2,1)S(1)} %get-tuple-element.42.refs_3_), channel_id=1, source_target_pairs={{0,128},{64,192},{128,0},{192,64},{1,129},{65,193},{129,1},{193,65... | collective-permute-start | bytes 983048 | tf_op jit(solution)/shard_map/ppermute | solution.py:358
  15.0 5.3 %collective-permute-start.2 = (bf16[16,3072]{1,0:T(8,128)(2,1)S(1)}, bf16[16,3072]{1,0:T(8,128)(2,1)S(1)}, u32[]{:S(2)}, u32[]{:S(2)}) collective-permute-start(bf16[16,3072]{1,0:T(8,128)(2,1)S(1)} %get-tuple-element.38.refs_0_), channel_id=1, source_target_pairs={{0,32},{16,48},{32,0},{48,16},{1,33},{17,49},{33,1},{49,17},{2,34}... | collective-permute-start | bytes 294920 | tf_op jit(solution)/shard_map/ppermute | solution.py:361
  20.3 12.0 %collective-permute-start.3 = (bf16[64,3072]{1,0:T(8,128)(2,1)S(1)}, bf16[64,3072]{1,0:T(8,128)(2,1)S(1)}, u32[]{:S(2)}, u32[]{:S(2)}) collective-permute-start(bf16[64,3072]{1,0:T(8,128)(2,1)S(1)} %shard_map.101.refs_0_), channel_id=1, source_target_pairs={{0,4},{4,0},{1,5},{5,1},{2,6},{6,2},{3,7},{7,3},{8,12},{12,8},{9,1... | collective-permute-start | bytes 1179656 | tf_op jit(solution)/shard_map/ppermute | solution.py:366
  23.4 31.5 %collective-permute-start.11 = (bf16[112,2048]{1,0:T(8,128)(2,1)}, bf16[112,2048]{1,0:T(8,128)(2,1)S(1)}, u32[]{:S(2)}, u32[]{:S(2)}) collective-permute-start(bf16[112,2048]{1,0:T(8,128)(2,1)} %bitcast.20), channel_id=1, source_target_pairs={{0,8},{8,0},{1,9},{9,1},{2,10},{10,2},{3,11},{11,3},{4,12},{12,4},... | collective-permute-start | bytes 1376264 | tf_op jit(solution)/shard_map/ppermute | solution.py:367
  27.0 18.8 %collective-permute-start.10 = (bf16[256,640]{1,0:T(8,128)(2,1)S(1)}, bf16[256,640]{1,0:T(8,128)(2,1)S(1)}, u32[]{:S(2)}, u32[]{:S(2)}) collective-permute-start(bf16[256,640]{1,0:T(8,128)(2,1)S(1)} %collective-permute-done.4.refs_3_), channel_id=1, source_target_pairs={{0,128},{64,192},{128,0},{192,64},{1,129},{65,193},{129,1},{193,65... | collective-permute-start | bytes 983048 | tf_op jit(solution)/shard_map/ppermute | solution.py:364
  29.0 16.9 %collective-permute-start.8 = (bf16[256,640]{1,0:T(8,128)(2,1)S(1)}, bf16[256,640]{1,0:T(8,128)(2,1)S(1)}, u32[]{:S(2)}, u32[]{:S(2)}) collective-permute-start(bf16[256,640]{1,0:T(8,128)(2,1)S(1)} %collective-permute-done.4.refs_3_), channel_id=1, source_target_pairs={{0,64},{64,128},{128,192},{192,0},{1,65},{65,129},{129,193},{193,1... | collective-permute-start | bytes 983048 | tf_op jit(solution)/shard_map/ppermute | solution.py:364
  29.4 16.5 %collective-permute-start.9 = (bf16[256,640]{1,0:T(8,128)(2,1)S(1)}, bf16[256,640]{1,0:T(8,128)(2,1)}, u32[]{:S(2)}, u32[]{:S(2)}) collective-permute-start(bf16[256,640]{1,0:T(8,128)(2,1)S(1)} %collective-permute-done.4.refs_3_), channel_id=1, source_target_pairs={{0,192},{64,0},{128,64},{192,128},{1,193},{65,1},{129,65},{193,129... | collective-permute-start | bytes 983048 | tf_op jit(solution)/shard_map/ppermute | solution.py:364
  32.3 29.0 %collective-permute-start.16 = (bf16[112,2048]{1,0:T(8,128)(2,1)}, bf16[112,2048]{1,0:T(8,128)(2,1)S(1)}, u32[]{:S(2)}, u32[]{:S(2)}) collective-permute-start(bf16[112,2048]{1,0:T(8,128)(2,1)} %bitcast.21), channel_id=1, source_target_pairs={{0,4},{4,0},{1,5},{5,1},{2,6},{6,2},{3,7},{7,3},{8,12},{12,8},{9,1... | collective-permute-start | bytes 1376264 | tf_op jit(solution)/shard_map/ppermute | solution.py:388
  36.0 2.4 %copy-start = (bf16[16,512,128]{2,1,0:T(8,128)(2,1)S(1)}, bf16[16,512,128]{2,1,0:T(8,128)(2,1)}, u32[]{:S(2)}) copy-start(bf16[16,512,128]{2,1,0:T(8,128)(2,1)} %refs_2_.5) | copy-start | bytes 6291460
  54.9 18.5 %copy-start.1 = (bf16[112,2048]{1,0:T(8,128)(2,1)}, bf16[112,2048]{1,0:T(8,128)(2,1)S(1)}, u32[]{:S(2)}) copy-start(bf16[112,2048]{1,0:T(8,128)(2,1)S(1)} %collective-permute-done.11.refs_0_) | copy-start | bytes 1376260
  54.9 1.6 %collective-permute-start.12 = (bf16[64,2176]{1,0:T(8,128)(2,1)S(1)}, bf16[64,2176]{1,0:T(8,128)(2,1)S(1)}, u32[]{:S(2)}, u32[]{:S(2)}) collective-permute-start(bf16[64,2176]{1,0:T(8,128)(2,1)S(1)} %get-tuple-element.58), channel_id=1, source_target_pairs={{0,4},{4,0},{1,5},{5,1},{2,6},{6,2},{3,7},{7,3},{8,12},{12,8},{9,1... | collective-permute-start | bytes 835592 | tf_op jit(solution)/shard_map/ppermute | solution.py:384
  57.0 5.1 %collective-permute-start.13 = (bf16[16,2176]{1,0:T(8,128)(2,1)S(1)}, bf16[16,2176]{1,0:T(8,128)(2,1)S(1)}, u32[]{:S(2)}, u32[]{:S(2)}) collective-permute-start(bf16[16,2176]{1,0:T(8,128)(2,1)S(1)} %get-tuple-element.60), channel_id=1, source_target_pairs={{0,48},{16,0},{32,16},{48,32},{1,49},{17,1},{33,17},{49,33},{2,50}... | collective-permute-start | bytes 208904 | tf_op jit(solution)/shard_map/ppermute | solution.py:386
  59.6 6.4 %collective-permute-start.14 = (bf16[16,2176]{1,0:T(8,128)(2,1)S(1)}, bf16[16,2176]{1,0:T(8,128)(2,1)S(1)}, u32[]{:S(2)}, u32[]{:S(2)}) collective-permute-start(bf16[16,2176]{1,0:T(8,128)(2,1)S(1)} %get-tuple-element.61), channel_id=1, source_target_pairs={{0,16},{16,32},{32,48},{48,0},{1,17},{17,33},{33,49},{49,1},{2,18}... | collective-permute-start | bytes 208904 | tf_op jit(solution)/shard_map/ppermute | solution.py:386
  59.6 6.4 %collective-permute-start.15 = (bf16[16,2176]{1,0:T(8,128)(2,1)S(1)}, bf16[16,2176]{1,0:T(8,128)(2,1)S(1)}, u32[]{:S(2)}, u32[]{:S(2)}) collective-permute-start(bf16[16,2176]{1,0:T(8,128)(2,1)S(1)} %get-tuple-element.62), channel_id=1, source_target_pairs={{0,32},{16,48},{32,0},{48,16},{1,33},{17,49},{33,1},{49,17},{2,34}... | collective-permute-start | bytes 208904 | tf_op jit(solution)/shard_map/ppermute | solution.py:386
  61.3 0.8 copy-start.3
  67.5 18.6 %all-to-all-start = ((bf16[16,16,2048]{2,1,0:T(8,128)(2,1)}), bf16[16,16,2048]{2,1,0:T(8,128)(2,1)S(1)}, u32[]{:S(2)}, u32[]{:S(2)}) async-start(bf16[16,16,2048]{2,1,0:T(8,128)(2,1)} %shard_map.106), calls=%async_computation | async-start | bytes 2097152 | tf_op jit(solution)/shard_map/all_to_all | solution.py:401
  71.2 3.6 %collective-permute-start.17 = (bf16[112,2048]{1,0:T(8,128)(2,1)S(1)}, bf16[112,2048]{1,0:T(8,128)(2,1)S(1)}, u32[]{:S(2)}, u32[]{:S(2)}) collective-permute-start(bf16[112,2048]{1,0:T(8,128)(2,1)S(1)} %collective-permute-done.11.refs_0_), channel_id=1, source_target_pairs={{0,4},{4,0},{1,5},{5,1},{2,6},{6,2},{3,7},{7,3},{8,12},{12,8},{9,1... | collective-permute-start | bytes 1376264 | tf_op jit(solution)/shard_map/ppermute | solution.py:389
  74.8 1.0 copy-start.2
  75.8 1.0 copy-start.4
